TPU v7x, 32 devices: a whole 2x2x4 slice. The times are simulated.
32 devices in a mesh: fsdp: 4 (over x, core), heads: 2 (over y), tensor: 4 (over z).
Axes of the slice: x: 2, y: 2, z: 4, core: 2. Of those that a mesh axis runs over, the one named last changes fastest.
Arguments:
- tokens: bfloat16 [32768, 2048], P(('fsdp', 'heads', 'tensor')), may hold values from -6 to 6
- cotangent: bfloat16 [32768, 2048], P(('fsdp', 'heads', 'tensor')), may hold values from -6 to 6
- seq_lens: int32 [16, 3], P(('fsdp', 'tensor')), may hold values from 129 to 1024, as said below
- block_pos: int32 [16, 16], P(('fsdp', 'tensor')), may hold values from 0 to 15, as said below
- norm1_gain: float32 [2048], replicated, may hold values from 0.5 to 1.5
- w_query: bfloat16 [2048, 2048], P(None, ('heads', 'fsdp', 'tensor')), may hold values from -0.125 to 0.125
- key_matrix: bfloat16 [2048, 1024], P(None, ('heads', 'fsdp', 'tensor')), may hold values from -0.125 to 0.125
- value_matrix: bfloat16 [2048, 1024], P(None, ('heads', 'fsdp', 'tensor')), may hold values from -0.125 to 0.125
- query_gain: float32 [128], replicated, may hold values from 0.5 to 1.5
- key_gain: float32 [128], replicated, may hold values from 0.5 to 1.5
- w_out: bfloat16 [2048, 2048], P(('heads', 'fsdp', 'tensor')), may hold values from -0.75 to 0.75
- norm2_gain: float32 [2048], replicated, may hold values from 0.5 to 1.5
- w_gate: bfloat16 [2048, 6144], P(('fsdp', 'heads'), 'tensor'), may hold values from -0.125 to 0.125
- w_up: bfloat16 [2048, 6144], P(('fsdp', 'heads'), 'tensor'), may hold values from -0.125 to 0.125
- w_down: bfloat16 [6144, 2048], P('tensor', ('fsdp', 'heads')), may hold values from -0.078125 to 0.078125
Outputs:
- output: bfloat16 [32768, 2048], P(('fsdp', 'heads', 'tensor'))
- tokens_grad: float32 [32768, 2048], P(('fsdp', 'heads', 'tensor'))
- norm1_gain_grad: float32 [2048], replicated
- w_query_grad: float32 [2048, 2048], P(None, ('heads', 'fsdp', 'tensor'))
- w_key_grad: float32 [2048, 1024], P(None, ('heads', 'fsdp', 'tensor'))
- w_value_grad: float32 [2048, 1024], P(None, ('heads', 'fsdp', 'tensor'))
- query_gain_grad: float32 [128], replicated
- key_gain_grad: float32 [128], replicated
- w_out_grad: float32 [2048, 2048], P(('heads', 'fsdp', 'tensor'))
- norm2_gain_grad: float32 [2048], replicated
- w_gate_grad: float32 [2048, 6144], P(('fsdp', 'heads'), 'tensor')
- w_up_grad: float32 [2048, 6144], P(('fsdp', 'heads'), 'tensor')
- w_down_grad: float32 [6144, 2048], P('tensor', ('fsdp', 'heads'))
Inputs may be any that keep to these rules, and one draw needn't show every extreme that they name: `seq_lens`: in each row one sequence, at a place drawn from the seed, has exactly 1024 tokens; every other one has at most (8) // 2 * 128, so that all sequences of a group, padded to whole blocks, fit in its 16 blocks. `block_pos`: each row is a permutation: the block at position p lies on heads index (p + c) mod 2 as its local block p // 2, with c drawn for each row; entry h * 8 + j is the position of local block j of heads index h.
All inputs are finite; a program needn't handle non-finite values.
Results may differ from a plain program's by a relative error of at most 0.017.
Values may be sent and summed in bfloat16 or wider, within the bound.
A program may use at most 384 MiB of HBM per device.

v0:
```python
import math

import jax
import jax.numpy as jnp
from jax import lax
from jax.sharding import PartitionSpec as P

QUERY_HEADS = 16
KEY_VALUE_HEADS = 8
HEAD_SIZE = 128
BLK = 128


EPS_NORM = 1e-06
ROPE_BASE = 1000000.0
NEG_FILL = -1e30


def row_info(lengths, positions):
    block_count = (lengths + BLK - 1) // BLK
    ends = jnp.cumsum(block_count)
    starts = ends - block_count
    used = ends[-1]
    column = positions[:, None]
    inside = (column >= starts[None, :]) & (column < ends[None, :])
    past = positions >= used
    seq_block = jnp.sum((column >= ends[None, :]).astype(jnp.int32), axis=1)
    first_block = jnp.sum(jnp.where(inside, starts[None, :], 0), axis=1) + jnp.where(past, used, 0)
    limit = jnp.sum(jnp.where(inside, lengths[None, :], 0), axis=1)
    offsets = jnp.arange(BLK, dtype=jnp.int32)[None, :]
    pos_rows = (positions - first_block)[:, None] * BLK + offsets
    seq_rows = jnp.broadcast_to(seq_block[:, None], pos_rows.shape)
    valid_rows = jnp.logical_not(past)[:, None] & (pos_rows < limit[:, None])
    return (seq_rows.reshape(-1), pos_rows.reshape(-1), valid_rows.reshape(-1))


def rope_tables(pos_rows):
    half_dim = HEAD_SIZE // 2
    freq = jnp.exp(
        jnp.arange(half_dim, dtype=jnp.float32) * (-2.0 * math.log(ROPE_BASE) / HEAD_SIZE)
    )
    angles = pos_rows.astype(jnp.float32)[:, None] * freq[None, :]
    return (jnp.cos(angles)[:, None, :], jnp.sin(angles)[:, None, :])


def rotate(value_rows, cos_tab, sin_tab):
    half_dim = value_rows.shape[-1] // 2
    first_half, second_half = (value_rows[..., :half_dim], value_rows[..., half_dim:])
    return jnp.concatenate(
        [
            first_half * cos_tab - second_half * sin_tab,
            second_half * cos_tab + first_half * sin_tab,
        ],
        axis=-1,
    )


def unrotate(upstream, cos_tab, sin_tab):
    half_dim = upstream.shape[-1] // 2
    first_half, second_half = (upstream[..., :half_dim], upstream[..., half_dim:])
    return jnp.concatenate(
        [
            first_half * cos_tab + second_half * sin_tab,
            second_half * cos_tab - first_half * sin_tab,
        ],
        axis=-1,
    )


def rms_parts(value_rows, gain_vec):
    scales = lax.rsqrt(jnp.mean(value_rows * value_rows, axis=-1, keepdims=True) + EPS_NORM)
    return (value_rows * scales * gain_vec, scales)


def norm_back(value_rows, scales, gain_vec, upstream):
    weighted = upstream * gain_vec
    inner = jnp.sum(value_rows * weighted, axis=-1, keepdims=True) / value_rows.shape[-1]
    return scales * weighted - value_rows * scales * scales * scales * inner


def matrix_product(left, right):
    return jnp.dot(left, right, preferred_element_type=jnp.float32)


def dot_rows(left, right):
    return lax.dot_general(
        left, right, (((0,), (0,)), ((), ())), preferred_element_type=jnp.float32
    )


def dot_cols(left, right):
    return lax.dot_general(
        left, right, (((1,), (1,)), ((), ())), preferred_element_type=jnp.float32
    )


def swap_cols(array, outer, inner):
    lead = array.shape[0]
    return jnp.swapaxes(array.reshape(lead, outer, inner, -1), 1, 2).reshape(lead, -1)


def swap_rows(array, outer, inner):
    width = array.shape[1]
    return jnp.swapaxes(array.reshape(outer, inner, -1, width), 0, 1).reshape(-1, width)


def spread_rows(local_rows):
    return lax.all_gather(local_rows, "tensor", axis=0, tiled=True)


def to_heads(packed):
    return lax.all_to_all(packed, "heads", split_axis=1, concat_axis=0, tiled=True)


def to_rows(packed):
    return lax.all_to_all(packed, "heads", split_axis=0, concat_axis=1, tiled=True)


def tensor_sum(term, row_count):
    total = lax.psum(
        term(0, row_count * lax.axis_size("tensor")).astype(jnp.bfloat16), "tensor"
    ).astype(jnp.float32)
    return lax.dynamic_slice_in_dim(total, lax.axis_index("tensor") * row_count, row_count)


def block_scores(query_blk, key_all, seq_blk, pos_blk, seq_all, pos_all):
    scores = jnp.einsum(
        "qkgd,pkd->kgqp", query_blk, key_all, preferred_element_type=jnp.float32
    ) * HEAD_SIZE ** (-0.5)
    allowed = (seq_blk[:, None] == seq_all[None, :]) & (pos_all[None, :] <= pos_blk[:, None])
    return jnp.where(allowed[None, None], scores, NEG_FILL)


def attend_forward(query_grp, key_grp, value_grp, seq_all, pos_all):
    group_factor = QUERY_HEADS // KEY_VALUE_HEADS
    group_len = query_grp.shape[0]
    kv_local = key_grp.shape[1] // HEAD_SIZE
    query_four = query_grp.reshape(group_len, kv_local, group_factor, HEAD_SIZE)
    key_three = key_grp.reshape(group_len, kv_local, HEAD_SIZE)
    value_three = value_grp.reshape(group_len, kv_local, HEAD_SIZE)
    block_rows = min(512, group_len)

    def forward_block(block_idx):
        first_row = block_idx * block_rows
        query_blk = lax.dynamic_slice_in_dim(query_four, first_row, block_rows)
        seq_blk = lax.dynamic_slice_in_dim(seq_all, first_row, block_rows)
        pos_blk = lax.dynamic_slice_in_dim(pos_all, first_row, block_rows)
        scores = block_scores(query_blk, key_three, seq_blk, pos_blk, seq_all, pos_all)
        peak = jnp.max(scores, axis=-1, keepdims=True)
        expo = jnp.exp(scores - peak)
        total = jnp.sum(expo, axis=-1, keepdims=True)
        probs_b = (expo / total).astype(jnp.bfloat16)
        attended = jnp.einsum(
            "kgqp,pkd->qkgd", probs_b, value_three, preferred_element_type=jnp.float32
        )
        return (attended, (peak + jnp.log(total))[..., 0])

    attended, log_sums = lax.map(forward_block, jnp.arange(group_len // block_rows))
    return (
        attended.reshape(group_len, kv_local * group_factor * HEAD_SIZE).astype(jnp.bfloat16),
        log_sums,
    )


def attend_backward(query_grp, key_grp, value_grp, grad_grp, log_sums, seq_all, pos_all):
    group_factor = QUERY_HEADS // KEY_VALUE_HEADS
    scale = HEAD_SIZE ** (-0.5)
    group_len = query_grp.shape[0]
    kv_local = key_grp.shape[1] // HEAD_SIZE
    query_four = query_grp.reshape(group_len, kv_local, group_factor, HEAD_SIZE)
    key_three = key_grp.reshape(group_len, kv_local, HEAD_SIZE)
    value_three = value_grp.reshape(group_len, kv_local, HEAD_SIZE)
    grad_four = grad_grp.reshape(group_len, kv_local, group_factor, HEAD_SIZE)
    block_rows = min(512, group_len)

    def backward_block(carry, block_idx):
        key_acc, value_acc = carry
        first_row = block_idx * block_rows
        query_blk = lax.dynamic_slice_in_dim(query_four, first_row, block_rows)
        grad_blk = lax.dynamic_slice_in_dim(grad_four, first_row, block_rows)
        seq_blk = lax.dynamic_slice_in_dim(seq_all, first_row, block_rows)
        pos_blk = lax.dynamic_slice_in_dim(pos_all, first_row, block_rows)
        scores = block_scores(query_blk, key_three, seq_blk, pos_blk, seq_all, pos_all)
        probs = jnp.exp(scores - log_sums[block_idx][..., None])
        probs_b = probs.astype(jnp.bfloat16)
        prob_grad = jnp.einsum(
            "qkgd,pkd->kgqp", grad_blk, value_three, preferred_element_type=jnp.float32
        )
        score_grad_b = (
            probs * (prob_grad - jnp.sum(probs * prob_grad, axis=-1, keepdims=True))
        ).astype(jnp.bfloat16)
        query_grad = (
            jnp.einsum(
                "kgqp,pkd->qkgd", score_grad_b, key_three, preferred_element_type=jnp.float32
            )
            * scale
        )
        key_acc = (
            key_acc
            + jnp.einsum(
                "kgqp,qkgd->pkd", score_grad_b, query_blk, preferred_element_type=jnp.float32
            )
            * scale
        )
        value_acc = value_acc + jnp.einsum(
            "kgqp,qkgd->pkd", probs_b, grad_blk, preferred_element_type=jnp.float32
        )
        return ((key_acc, value_acc), query_grad)

    empty = jnp.zeros((group_len, kv_local, HEAD_SIZE), jnp.float32)
    (key_acc, value_acc), query_blocks = lax.scan(
        backward_block, (empty, empty), jnp.arange(group_len // block_rows)
    )
    query_grad_b = query_blocks.reshape(group_len, kv_local * group_factor * HEAD_SIZE).astype(
        jnp.bfloat16
    )
    key_grad_b = key_acc.reshape(group_len, kv_local * HEAD_SIZE).astype(jnp.bfloat16)
    value_grad_b = value_acc.reshape(group_len, kv_local * HEAD_SIZE).astype(jnp.bfloat16)
    return (query_grad_b, key_grad_b, value_grad_b)


def project_heads(normed_b, query_w, key_w, value_w, query_gain, key_gain, pos_rows):
    lines = normed_b.shape[0]
    q_raw = matrix_product(normed_b, query_w).reshape(lines, -1, HEAD_SIZE)
    key_unnormed = matrix_product(normed_b, key_w).reshape(lines, -1, HEAD_SIZE)
    value_b = matrix_product(normed_b, value_w).astype(jnp.bfloat16)
    cos_tab, sin_tab = rope_tables(pos_rows)
    q_normed, q_scale = rms_parts(q_raw, query_gain)
    k_normed, k_scale = rms_parts(key_unnormed, key_gain)
    query_b = rotate(q_normed, cos_tab, sin_tab).astype(jnp.bfloat16).reshape(lines, -1)
    key_b = rotate(k_normed, cos_tab, sin_tab).astype(jnp.bfloat16).reshape(lines, -1)
    return (query_b, key_b, value_b, (q_raw, q_scale, key_unnormed, k_scale, cos_tab, sin_tab))


def heads_back(query_back, key_back, kept, query_gain, key_gain):
    q_raw, q_scale, key_unnormed, k_scale, cos_tab, sin_tab = kept
    lines = q_raw.shape[0]
    q_turned = unrotate(query_back.astype(jnp.float32).reshape(q_raw.shape), cos_tab, sin_tab)
    k_turned = unrotate(key_back.astype(jnp.float32).reshape(key_unnormed.shape), cos_tab, sin_tab)
    q_raw_grad = (
        norm_back(q_raw, q_scale, query_gain, q_turned).reshape(lines, -1).astype(jnp.bfloat16)
    )
    k_raw_grad = (
        norm_back(key_unnormed, k_scale, key_gain, k_turned).reshape(lines, -1).astype(jnp.bfloat16)
    )
    qgain_part = jnp.sum(q_turned * q_raw * q_scale, axis=(0, 1))
    kgain_part = jnp.sum(k_turned * key_unnormed * k_scale, axis=(0, 1))
    return (q_raw_grad, k_raw_grad, qgain_part, kgain_part)


def local(
    tokens,
    cotangent,
    seq_lens,
    block_pos,
    norm1_gain,
    w_query,
    key_matrix,
    value_matrix,
    query_gain,
    key_gain,
    w_out,
    norm2_gain,
    w_gate,
    w_up,
    w_down,
):
    row_count = tokens.shape[0]
    fsdp_count = lax.axis_size("fsdp")
    heads_count = lax.axis_size("heads")
    gate_full, up_full, down_full = (
        lax.all_gather(w_gate, ("fsdp", "heads"), axis=0, tiled=True),
        lax.all_gather(w_up, ("fsdp", "heads"), axis=0, tiled=True),
        lax.all_gather(w_down, ("fsdp", "heads"), axis=1, tiled=True),
    )
    seq_all, pos_all, valid_all = row_info(seq_lens[0], block_pos[0])
    own_first = lax.axis_index("heads") * row_count
    pos_own = lax.dynamic_slice_in_dim(pos_all, own_first, row_count)
    valid_own = lax.dynamic_slice_in_dim(valid_all, own_first, row_count).astype(jnp.float32)[
        :, None
    ]
    inputs = tokens.astype(jnp.float32)
    first_normed, scale1 = rms_parts(inputs, norm1_gain)
    normed1_b = first_normed.astype(jnp.bfloat16)
    query_all, key_all, value_all, out_all = (
        lax.all_gather(w_query, ("fsdp", "heads", "tensor"), axis=1, tiled=True),
        lax.all_gather(key_matrix, ("fsdp", "heads", "tensor"), axis=1, tiled=True),
        lax.all_gather(value_matrix, ("fsdp", "heads", "tensor"), axis=1, tiled=True),
        lax.all_gather(w_out, ("fsdp", "heads", "tensor"), axis=0, tiled=True),
    )
    query_full = swap_cols(query_all, fsdp_count, heads_count)
    key_full = swap_cols(key_all, fsdp_count, heads_count)
    value_full = swap_cols(value_all, fsdp_count, heads_count)
    out_full = swap_rows(out_all, fsdp_count, heads_count)
    query_b, key_b, value_b, kept = project_heads(
        normed1_b, query_full, key_full, value_full, query_gain, key_gain, pos_own
    )
    q_width = query_b.shape[1] // heads_count
    k_width = key_b.shape[1] // heads_count
    packed = jnp.concatenate(
        [
            query_b.reshape(row_count, heads_count, q_width),
            key_b.reshape(row_count, heads_count, k_width),
            value_b.reshape(row_count, heads_count, k_width),
        ],
        axis=2,
    )
    grouped = to_heads(packed.reshape(row_count, -1))
    query_grp = grouped[:, :q_width]
    key_grp = grouped[:, q_width : q_width + k_width]
    value_grp = grouped[:, q_width + k_width :]
    attended_b, log_sums = attend_forward(query_grp, key_grp, value_grp, seq_all, pos_all)
    attn_tok = to_rows(attended_b)
    resid = inputs + matrix_product(attn_tok, out_full)
    normed2, scale2 = rms_parts(resid, norm2_gain)
    normed2_b = normed2.astype(jnp.bfloat16)
    wide_in = spread_rows(normed2_b)
    gate_pre = matrix_product(wide_in, gate_full)
    up_pre = matrix_product(wide_in, up_full)
    sigmoid_gate = jax.nn.sigmoid(gate_pre)
    silu_gate = gate_pre * sigmoid_gate
    act_b = (silu_gate * up_pre).astype(jnp.bfloat16)

    def forward_term(first_row, span):
        return matrix_product(act_b, down_full)

    mixed = tensor_sum(forward_term, row_count)
    output = (valid_own * (resid + mixed)).astype(jnp.bfloat16)
    grad_out = valid_own * cotangent.astype(jnp.float32)
    wide_grad = spread_rows(grad_out.astype(jnp.bfloat16))
    act_grad = dot_cols(wide_grad, down_full)
    down_grad = dot_rows(act_b, wide_grad)
    gate_grad_b = (
        act_grad * up_pre * sigmoid_gate * (1.0 + gate_pre * (1.0 - sigmoid_gate))
    ).astype(jnp.bfloat16)
    up_grad_b = (act_grad * silu_gate).astype(jnp.bfloat16)
    gate_wgrad = dot_rows(wide_in, gate_grad_b)
    up_wgrad = dot_rows(wide_in, up_grad_b)

    def backward_term(first_row, span):
        return dot_cols(gate_grad_b, gate_full) + dot_cols(up_grad_b, up_full)

    normed2_grad = tensor_sum(backward_term, row_count)
    gate_sum, up_sum, down_sum = (
        lax.psum_scatter(
            gate_wgrad.astype(jnp.bfloat16), ("fsdp", "heads"), scatter_dimension=0, tiled=True
        ).astype(jnp.float32),
        lax.psum_scatter(
            up_wgrad.astype(jnp.bfloat16), ("fsdp", "heads"), scatter_dimension=0, tiled=True
        ).astype(jnp.float32),
        lax.psum_scatter(
            down_grad.astype(jnp.bfloat16), ("fsdp", "heads"), scatter_dimension=1, tiled=True
        ).astype(jnp.float32),
    )
    resid_grad = grad_out + norm_back(resid, scale2, norm2_gain, normed2_grad)
    gain2_part = jnp.sum(normed2_grad * resid * scale2, axis=0)
    resid_grad_b = resid_grad.astype(jnp.bfloat16)
    out_wgrad = dot_rows(attn_tok, resid_grad_b)
    attn_grad_b = dot_cols(resid_grad_b, out_full).astype(jnp.bfloat16)
    attn_grad_grp = to_heads(attn_grad_b)
    query_grad_b, key_grad_b, value_grad_b = attend_backward(
        query_grp, key_grp, value_grp, attn_grad_grp, log_sums, seq_all, pos_all
    )
    back_packed = to_rows(jnp.concatenate([query_grad_b, key_grad_b, value_grad_b], axis=1))
    back_three = back_packed.reshape(row_count, heads_count, -1)
    query_back = back_three[:, :, :q_width].reshape(row_count, -1)
    key_back = back_three[:, :, q_width : q_width + k_width].reshape(row_count, -1)
    value_back = back_three[:, :, q_width + k_width :].reshape(row_count, -1)
    q_raw_grad, k_raw_grad, qgain_part, kgain_part = heads_back(
        query_back, key_back, kept, query_gain, key_gain
    )
    query_wgrad = swap_cols(dot_rows(normed1_b, q_raw_grad), heads_count, fsdp_count)
    key_wgrad = swap_cols(dot_rows(normed1_b, k_raw_grad), heads_count, fsdp_count)
    value_wgrad = swap_cols(dot_rows(normed1_b, value_back), heads_count, fsdp_count)
    out_wgrad = swap_rows(out_wgrad, heads_count, fsdp_count)
    normed1_grad = (
        dot_cols(q_raw_grad, query_full)
        + dot_cols(k_raw_grad, key_full)
        + dot_cols(value_back, value_full)
    )
    query_sum, key_sum, value_sum, out_sum = (
        lax.psum_scatter(query_wgrad, ("fsdp", "heads", "tensor"), scatter_dimension=1, tiled=True),
        lax.psum_scatter(key_wgrad, ("fsdp", "heads", "tensor"), scatter_dimension=1, tiled=True),
        lax.psum_scatter(value_wgrad, ("fsdp", "heads", "tensor"), scatter_dimension=1, tiled=True),
        lax.psum_scatter(out_wgrad, ("fsdp", "heads", "tensor"), scatter_dimension=0, tiled=True),
    )
    tokens_grad = resid_grad + norm_back(inputs, scale1, norm1_gain, normed1_grad)
    gain1_part = jnp.sum(normed1_grad * inputs * scale1, axis=0)
    gain1_sum, qgain_sum, kgain_sum, gain2_sum = lax.psum(
        (gain1_part, qgain_part, kgain_part, gain2_part), ("fsdp", "heads", "tensor")
    )
    return (
        output,
        tokens_grad,
        gain1_sum,
        query_sum,
        key_sum,
        value_sum,
        qgain_sum,
        kgain_sum,
        out_sum,
        gain2_sum,
        gate_sum,
        up_sum,
        down_sum,
    )


def solution(mesh):
    return jax.shard_map(
        local,
        mesh=mesh,
        in_specs=(
            P(("fsdp", "heads", "tensor"), None),
            P(("fsdp", "heads", "tensor"), None),
            P(("fsdp", "tensor"), None),
            P(("fsdp", "tensor"), None),
            P(),
            P(None, ("heads", "fsdp", "tensor")),
            P(None, ("heads", "fsdp", "tensor")),
            P(None, ("heads", "fsdp", "tensor")),
            P(),
            P(),
            P(("heads", "fsdp", "tensor"), None),
            P(),
            P(("fsdp", "heads"), "tensor"),
            P(("fsdp", "heads"), "tensor"),
            P("tensor", ("fsdp", "heads")),
        ),
        out_specs=(
            P(("fsdp", "heads", "tensor"), None),
            P(("fsdp", "heads", "tensor"), None),
            P(),
            P(None, ("heads", "fsdp", "tensor")),
            P(None, ("heads", "fsdp", "tensor")),
            P(None, ("heads", "fsdp", "tensor")),
            P(),
            P(),
            P(("heads", "fsdp", "tensor"), None),
            P(),
            P(("fsdp", "heads"), "tensor"),
            P(("fsdp", "heads"), "tensor"),
            P("tensor", ("fsdp", "heads")),
        ),
        check_vma=False,
    )
```

profile of v0, /device:TPU:0, one launch (start us, length us, event | category | flops | bytes accessed | tf_op | source)
XLA Modules:
  0.0 4478.9 jit_solution(15250095937784842616)
XLA Ops:
  18.9 56.9 %all-gather.12.cloned.1.call-done = bf16[2048,1024]{0,1:T(8,128)(2,1)} async-done(((bf16[2048,32]{0,1:T(8,128)(2,1)}), bf16[2048,1024]{0,1:T(8,128)(2,1)}) %all-gather.12.cloned.1.call-update) | async-done | bytes 4194320 | tf_op jit(solution)/shard_map/all_gather | solution.py:287
  80.6 58.9 %all-gather.14.cloned.1.call-done = bf16[2048,1024]{0,1:T(8,128)(2,1)} async-done(((bf16[2048,32]{0,1:T(8,128)(2,1)}), bf16[2048,1024]{0,1:T(8,128)(2,1)}) %all-gather.14.cloned.1.call-update) | async-done | bytes 4194320 | tf_op jit(solution)/shard_map/all_gather | solution.py:288
  163.9 54.7 %all-gather.10.cloned.1.call-done = bf16[2048,2048]{0,1:T(8,128)(2,1)} async-done(((bf16[2048,64]{0,1:T(8,128)(2,1)}), bf16[2048,2048]{0,1:T(8,128)(2,1)}) %all-gather.10.cloned.1.call-update) | async-done | bytes 8388624 | tf_op jit(solution)/shard_map/all_gather | solution.py:286
  268.7 131.0 %all-to-all-done = bf16[1024,2,2048]{2,0,1:T(8,128)(2,1)} async-done(((bf16[1024,2,2048]{2,0,1:T(8,128)(2,1)}), bf16[1024,2,2048]{2,0,1:T(8,128)(2,1)}, u32[]{:S(2)}, u32[]{:S(2)}) %all-to-all-start) | async-done | bytes 8388640 | tf_op jit(solution)/shard_map/all_to_all | solution.py:112
  437.3 195.8 %while.28 = (s32[]{:T(128)}, bf16[4,512,4,2,128]{4,1,3,2,0:T(8,128)(2,1)}, f32[4,4,2,512]{3,2,1,0:T(2,128)}, s32[4]{0:T(128)S(1)}, s32[2048]{0:T(1024)S(1)}, /*i...) while((s32[]{:T(128)}, ...), condition=%wide.region_10.11_spmd.clone, body=%wide.region_7.10_spmd.clone.sunk | while | flops 4398774272 | bytes 112374112 | solution.py:158
  664.0 39.3 all-to-all-done.1
  738.3 278.7 %all-gather.18.cloned.1.call-done = bf16[4096,2048]{1,0:T(8,128)(2,1)} async-done(((bf16[1024,2048]{1,0:T(8,128)(2,1)}), bf16[4096,2048]{1,0:T(8,128)(2,1)}) %all-gather.18.cloned.1.call-update) | async-done | bytes 16777232 | tf_op jit(solution)/shard_map/all_gather | solution.py:108
  1017.1 33.3 fusion.86
  1062.7 33.3 fusion.85
  1111.3 288.4 %all-gather.26.cloned.1.call-done = bf16[4096,2048]{1,0:T(8,128)(2,1)} async-done(((bf16[1024,2048]{1,0:T(8,128)(2,1)}), bf16[4096,2048]{1,0:T(8,128)(2,1)}) %all-gather.26.cloned.1.call-update) | async-done | bytes 16777232 | tf_op jit(solution)/shard_map/all_gather | solution.py:108
  1399.6 45.8 %multiply_convert_fusion = (bf16[4096,1536]{1,0:T(8,128)(2,1)}, bf16[4096,1536]{1,0:T(8,128)(2,1)}, bf16[4096,1536]{1,0:T(8,128)(2,1)}) fusion(f32[4096,1536]{1,0:T(8,128)} %fusion.85, f32[4096,1536]{1,0:T(8,128)} %fusion.86, bf16[4096,2048]{1,0:T(8,128)(2,1)} %all-gather.26.cloned.1.call-done, bf16[1536,2048]{1,0:T(8,128)(2,1)} %all-gather.24.cloned.1.call-done), kind=kOutput, calls=%fused_computation.53 | convolution fusion | flops 25864175616 | bytes 111149056 | tf_op jit(solution)/shard_map/dot_general | solution.py:92
  1445.5 32.9 convolution_convert_fusion
  1478.4 31.9 fusion.87
  1510.3 36.8 add_convert_fusion
  1547.2 35.6 convolution_convert_fusion.1
  1582.9 34.2 convolution_convert_fusion.2
  1617.2 1033.9 %all-reduce.4.cloned.1.call-done = (bf16[4096,2048]{1,0:T(8,128)(2,1)}, bf16[4096,2048]{1,0:T(8,128)(2,1)}) async-done(((bf16[4096,2048]{1,0:T(8,128)(2,1)}, bf16[4096,2048]{1,0:T(8,128)(2,1)}), (bf16[4096,2048]{1,0:T(8,128)(2,1)}, bf16[4096,2048]{1,0:T(8,128)(2,1)})) %all-reduce.4.cloned.1.call-update) | async-done | bytes 33554448 | tf_op jit(solution)/shard_map/psum | solution.py:120
  2692.8 34.1 convolution_convert_fusion.3
  2760.8 452.3 %while.29 = (s32[]{:T(128)}, f32[2048,4,128]{0,2,1:T(8,128)}, f32[2048,4,128]{0,2,1:T(8,128)}, bf16[4,512,4,2,128]{4,1,3,2,0:T(8,128)(2,1)}, s32[4]{0:T(128)S(1)...) while((s32[]{:T(128)}, f32[2048,4,128]{0,2,1:T(8,128)}, ...), condition=%wide.region_17.18_spmd.clone, body=%wide.region_15.17_spmd.clone.sunk | while | flops 10821826560 | bytes 335671872 | solution.py:211
  2783.1 25.6 fusion.150
  2808.7 29.8 fusion.151
  2897.3 24.4 fusion.150
  2921.7 27.4 fusion.151
  3009.6 24.4 fusion.150
  3034.0 27.4 fusion.151
  3121.9 24.4 fusion.150
  3146.3 27.4 fusion.151
  3254.5 95.0 %all_to_all.61 = bf16[2,1024,2048]{2,1,0:T(8,128)(2,1)S(1)} all-to-all(bf16[2,1024,2048]{2,1,0:T(8,128)(2,1)S(1)} %pad_maximum_fusion.1), channel_id=1, replica_groups=mesh['fsdp'=4,'heads'=2,'tensor'=4] {'heads'}, dimensions={0} | all-to-all | bytes 16777216 | tf_op jit(solution)/shard_map/all_to_all | solution.py:116
  3507.2 42.9 all-reduce
  3562.1 180.3 %reduce-scatter.10.cloned.1.call-done = f32[2048,32]{0,1:T(8,128)} async-done(((f32[2048,1024]{0,1:T(8,128)}), f32[2048,32]{0,1:T(8,128)}) %reduce-scatter.10.cloned.1.call-update) | async-done | bytes 262160 | tf_op jit(solution)/shard_map/reduce_scatter | solution.py:383
  3742.3 364.7 %reduce-scatter.14.cloned.1.call-done = f32[64,2048]{1,0:T(8,128)} async-done(((f32[2048,2048]{1,0:T(8,128)}), f32[64,2048]{1,0:T(8,128)}) %reduce-scatter.14.cloned.1.call-update) | async-done | bytes 524304 | tf_op jit(solution)/shard_map/reduce_scatter | solution.py:385
  4107.0 364.9 %reduce-scatter.8.cloned.1.call-done = f32[2048,64]{0,1:T(8,128)} async-done(((f32[2048,2048]{0,1:T(8,128)}), f32[2048,64]{0,1:T(8,128)}) %reduce-scatter.8.cloned.1.call-update) | async-done | bytes 524304 | tf_op jit(solution)/shard_map/reduce_scatter | solution.py:382
  (368 shorter events, 931.4 us)
Async XLA Ops:
  7.2 68.7 %all-gather.12.cloned.1.call-start = ((), (), s32[]{:S(2)}) async-start(), calls=%async_computation.12 | async-start | bytes 4325376 | tf_op jit(solution)/shard_map/all_gather | solution.py:287
  7.9 131.6 %all-gather.14.cloned.1.call-start = ((), (), s32[]{:S(2)}) async-start(), calls=%async_computation.13 | async-start | bytes 4325376 | tf_op jit(solution)/shard_map/all_gather | solution.py:288
  8.7 209.9 %all-gather.10.cloned.1.call-start = ((), (), s32[]{:S(2)}) async-start(), calls=%async_computation.11 | async-start | bytes 8650752 | tf_op jit(solution)/shard_map/all_gather | solution.py:286
  9.4 646.3 %all-gather.16.cloned.1.call-start = ((), (), s32[]{:S(2)}) async-start(), calls=%async_computation.14 | async-start | bytes 8650752 | tf_op jit(solution)/shard_map/all_gather | solution.py:289
  17.9 209.2 %copy-start.46 = (f32[1024]{0:T(1024)}, f32[1024]{0:T(1024)S(1)}, u32[]{:S(2)}) copy-start(f32[1024]{0:T(1024)S(1)} %add_rsqrt_fusion.3) | copy-start | bytes 12292
  18.9 223.3 %copy-start.19 = (f32[1024,64]{0,1:T(8,128)}, f32[1024,64]{0,1:T(8,128)S(1)}, u32[]{:S(2)}) copy-start(f32[1024,64]{0,1:T(8,128)S(1)} %get-tuple-element.395) | copy-start | bytes 786436
  18.9 223.3 %copy-start.21 = (f32[1024,64]{0,1:T(8,128)}, f32[1024,64]{0,1:T(8,128)S(1)}, u32[]{:S(2)}) copy-start(f32[1024,64]{0,1:T(8,128)S(1)} %get-tuple-element.396) | copy-start | bytes 786436
  75.8 66.3 %copy-start.48 = (f32[2048]{0:T(1024)S(1)}, f32[2048]{0:T(1024)}, u32[]{:S(2)}) copy-start(f32[2048]{0:T(1024)} %param.23) | copy-start | bytes 24580
  261.0 138.8 %all-to-all-start = ((bf16[1024,2,2048]{2,0,1:T(8,128)(2,1)}), bf16[1024,2,2048]{2,0,1:T(8,128)(2,1)}, u32[]{:S(2)}, u32[]{:S(2)}) async-start(bf16[1024,2,2048]{2,0,1:T(8,128)(2,1)} %pad_maximum_fusion), calls=%async_computation | async-start | bytes 16777216 | tf_op jit(solution)/shard_map/all_to_all | solution.py:112
  268.0 470.3 %all-gather.22.cloned.1.call-start = ((), (), s32[]{:S(2)}) async-start(), calls=%async_computation.17 | async-start | bytes 7077888 | tf_op jit(solution)/shard_map/all_gather | solution.py:273
  633.2 99.4 %copy-start.32 = (s32[2048]{0:T(1024)}, s32[2048]{0:T(1024)S(1)}, u32[]{:S(2)}) copy-start(s32[2048]{0:T(1024)S(1)} %get-tuple-element.746) | copy-start | bytes 24580
  650.1 53.3 %all-to-all-start.1 = ((bf16[2,1024,1024]{2,1,0:T(8,128)(2,1)}), bf16[2,1024,1024]{2,1,0:T(8,128)(2,1)}, u32[]{:S(2)}, u32[]{:S(2)}) async-start(bf16[2,1024,1024]{2,1,0:T(8,128)(2,1)} %convert_element_type.159), calls=%async_computation.1 | async-start | bytes 8388608 | tf_op jit(solution)/shard_map/all_to_all | solution.py:116
  655.7 361.4 %all-gather.18.cloned.1.call-start = ((), (), s32[]{:S(2)}) async-start(), calls=%async_computation.15 | async-start | bytes 20971520 | tf_op jit(solution)/shard_map/all_gather | solution.py:108
  730.1 332.6 %all-gather.20.cloned.1.call-start = ((), (), s32[]{:S(2)}) async-start(), calls=%async_computation.16 | async-start | bytes 7077888 | tf_op jit(solution)/shard_map/all_gather | solution.py:272
  730.8 380.4 %all-gather.24.cloned.1.call-start = ((), (), s32[]{:S(2)}) async-start(), calls=%async_computation.18 | async-start | bytes 7077888 | tf_op jit(solution)/shard_map/all_gather | solution.py:274
  731.6 668.1 %all-gather.26.cloned.1.call-start = ((), (), s32[]{:S(2)}) async-start(), calls=%async_computation.19 | async-start | bytes 20971520 | tf_op jit(solution)/shard_map/all_gather | solution.py:108
  738.3 1912.8 %all-reduce.4.cloned.1.call-start = ((), (), s32[]{:S(2)}) async-start(), calls=%async_computation.27 | async-start | bytes 67108864 | tf_op jit(solution)/shard_map/psum | solution.py:120
  1445.5 32.9 copy-start.55
  1547.1 1919.0 %reduce-scatter.20.cloned.1.call-start = ((), (), s32[]{:S(2)}) async-start(), calls=%async_computation.26 | async-start | bytes 7077888 | tf_op jit(solution)/shard_map/reduce_scatter | solution.py:351
  1582.8 1068.3 %copy-start.39 = (f32[2048]{0:T(1024)S(1)}, f32[2048]{0:T(1024)}, u32[]{:S(2)}) copy-start(f32[2048]{0:T(1024)} %param.30) | copy-start | bytes 24580
  1582.8 1068.3 %copy-start.41 = (f32[1024]{0:T(1024)S(1)}, f32[1024]{0:T(1024)}, u32[]{:S(2)}) copy-start(f32[1024]{0:T(1024)} %copy-done.40) | copy-start | bytes 12292
  1582.8 1885.7 %reduce-scatter.18.cloned.1.call-start = ((), (), s32[]{:S(2)}) async-start(), calls=%async_computation.25 | async-start | bytes 7077888 | tf_op jit(solution)/shard_map/reduce_scatter | solution.py:348
  1617.1 1040.8 %copy-start.43 = (f32[1024]{0:T(1024)S(1)}, f32[1024]{0:T(1024)}, u32[]{:S(2)}) copy-start(f32[1024]{0:T(1024)} %copy-done.42) | copy-start | bytes 12292
  2687.0 62.9 %all-to-all-start.2 = ((bf16[1024,2,1024]{2,0,1:T(8,128)(2,1)}), bf16[1024,2,1024]{2,0,1:T(8,128)(2,1)}, u32[]{:S(2)}, u32[]{:S(2)}) async-start(bf16[1024,2,1024]{2,0,1:T(8,128)(2,1)} %bitcast.307), calls=%async_computation.2 | async-start | bytes 8388608 | tf_op jit(solution)/shard_map/all_to_all | solution.py:112
  2692.7 778.3 %reduce-scatter.16.cloned.1.call-start = ((), (), s32[]{:S(2)}) async-start(), calls=%async_computation.24 | async-start | bytes 7077888 | tf_op jit(solution)/shard_map/reduce_scatter | solution.py:345
  2726.9 33.9 copy-start.1
  2726.9 33.9 copy-start.35
  2726.9 33.9 copy-start.37
  2726.9 835.1 %reduce-scatter.12.cloned.1.call-start = ((), (), s32[]{:S(2)}) async-start(), calls=%async_computation.22 | async-start | bytes 8650752 | tf_op jit(solution)/shard_map/reduce_scatter | solution.py:384
  3369.3 373.1 %reduce-scatter.10.cloned.1.call-start = ((), (), s32[]{:S(2)}) async-start(), calls=%async_computation.21 | async-start | bytes 8650752 | tf_op jit(solution)/shard_map/reduce_scatter | solution.py:383
  3390.7 716.3 %reduce-scatter.14.cloned.1.call-start = ((), (), s32[]{:S(2)}) async-start(), calls=%async_computation.23 | async-start | bytes 17301504 | tf_op jit(solution)/shard_map/reduce_scatter | solution.py:385
  3410.2 1061.7 %reduce-scatter.8.cloned.1.call-start = ((), (), s32[]{:S(2)}) async-start(), calls=%async_computation.20 | async-start | bytes 17301504 | tf_op jit(solution)/shard_map/reduce_scatter | solution.py:382
  (58 other events, 497.9 us)
Sparse Core Ops, SparseCore 0:
  11.0 64.7 all-gather.11
  78.8 60.6 all-gather.13
  142.5 76.0 all-gather.9
  221.4 88.3 all-gather.15
  311.6 72.1 all-gather.21
  730.2 286.8 all-gather.17
  1018.9 43.6 all-gather.19
  1064.5 46.6 all-gather.23
  1112.8 286.7 all-gather.25
  1547.2 1103.7 all-reduce.3
  2654.8 74.4 reduce-scatter.19
  2732.5 61.7 reduce-scatter.17
  2798.1 61.7 reduce-scatter.15
  3369.4 186.6 reduce-scatter.11
  3558.8 183.4 reduce-scatter.9
  3745.0 361.9 reduce-scatter.13
  4109.7 362.1 reduce-scatter.7
where the time goes:
time: 4490 us; the launch traced here: 4480 us
  waiting for transfers between devices  2910 us (65%)
  matrix products  865 us (19%)
  other arithmetic  293 us (7%)
  local copies, waits for them, and re-layouts  228 us (5%)
  blocking collectives  138 us (3%)
    psum x1, waiting for transfers between devices, tensor_sum(): lax.psum(term(0, row_count * lax.axis_size('tensor')).astype(jnp.bfloat16...  1030 us
    all_gather x2, waiting for transfers between devices, spread_rows(): return lax.all_gather(local_rows, 'tensor', axis=0, tiled=True)  567 us
    reduce_scatter x1, waiting for transfers between devices, local(): lax.psum_scatter(query_wgrad, ('fsdp', 'heads', 'tensor'), scatter_dimens...  365 us
    reduce_scatter x1, waiting for transfers between devices, local(): lax.psum_scatter(out_wgrad, ('fsdp', 'heads', 'tensor'), scatter_dimensio...  365 us
    reduce_scatter x1, waiting for transfers between devices, local(): lax.psum_scatter(key_wgrad, ('fsdp', 'heads', 'tensor'), scatter_dimensio...  180 us
    dot_general x7, matrix products, dot_cols(): lax.dot_general(left, right, (((1,), (1,)), ((), ())), preferred_element_...  163 us
    dot_general x8, matrix products, block_scores(): jnp.einsum('qkgd,pkd->kgqp', query_blk, key_all, preferred_element_type=j...  161 us
    all_to_all x2, waiting for transfers between devices, to_heads(): lax.all_to_all(packed, 'heads', split_axis=1, concat_axis=0, tiled=True)  154 us
  transfers between devices with their start and end apart: 20, of which 14 were waited for; matrix products, arithmetic and copies ran while one was open for 27% of the time, Pallas kernels for 0%

commit v1 on v0

--- a/solution.py
+++ b/solution.py
@@ -1,8 +1,12 @@
+import functools
 import math
 
 import jax
 import jax.numpy as jnp
 from jax import lax
+from jax.experimental import pallas as pl
+from jax.experimental.pallas import tpu as pltpu
+from jax.sharding import Mesh
 from jax.sharding import PartitionSpec as P
 
 QUERY_HEADS = 16
@@ -248,7 +252,7 @@
     return (q_raw_grad, k_raw_grad, qgain_part, kgain_part)
 
 
-def local(
+def plain_layer(
     tokens,
     cotangent,
     seq_lens,
@@ -406,9 +410,9 @@
     )
 
 
-def solution(mesh):
+def plain_solution(mesh):
     return jax.shard_map(
-        local,
+        plain_layer,
         mesh=mesh,
         in_specs=(
             P(("fsdp", "heads", "tensor"), None),
@@ -444,3 +448,710 @@
         ),
         check_vma=False,
     )
+
+
+VMEM_LIMIT = 56 * 1024 * 1024
+SWAP = ((0, 1), (1, 0))
+ROW_TILE = 256
+SCALE = HEAD_SIZE ** (-0.5)
+
+
+def dot_t(left, right):
+    return lax.dot_general(
+        left, right, (((1,), (1,)), ((), ())), preferred_element_type=jnp.float32
+    )
+
+
+def swap(array, axis):
+    return lax.ppermute(array, axis, SWAP)
+
+
+def pick(first, second, index):
+    return jnp.where(index == 0, first, second)
+
+
+def join(mine, other, index, axis):
+    return pick(
+        jnp.concatenate([mine, other], axis=axis),
+        jnp.concatenate([other, mine], axis=axis),
+        index,
+    )
+
+
+def gather_z(array):
+    return lax.all_gather(array, "z", axis=0, tiled=True)
+
+
+def scatter_z(array):
+    return lax.psum_scatter(array, "z", scatter_dimension=0, tiled=True)
+
+
+def four_pieces(own, via):
+    along_x, along_y = swap(own, "x"), swap(own, "y")
+    corner = swap(along_y, "x") if via == "x" else swap(along_x, "y")
+    return [own, along_x, along_y, corner]
+
+
+def add_pieces(pieces, via):
+    own, along_x, along_y, corner = pieces
+    if via == "x":
+        along_y = along_y + swap(corner, "x")
+    else:
+        along_x = along_x + swap(corner, "y")
+    return own + swap(along_x, "x") + swap(along_y, "y")
+
+
+def to_core(array, core):
+    half = array.shape[0] // 2
+    first, second = array[:half], array[half:]
+    other = swap(pick(second, first, core), "c")
+    return join(pick(first, second, core), other, core, 1)
+
+
+def from_core(array, core):
+    half = array.shape[1] // 2
+    first, second = array[:, :half], array[:, half:]
+    other = swap(pick(second, first, core), "c")
+    return join(pick(first, second, core), other, core, 0)
+
+
+def params(flops, bytes_accessed):
+    return dict(
+        compiler_params=pltpu.CompilerParams(vmem_limit_bytes=VMEM_LIMIT),
+        cost_estimate=pl.CostEstimate(
+            flops=flops, bytes_accessed=bytes_accessed, transcendentals=0
+        ),
+    )
+
+
+def reorder_kernel(order_ref, in_ref, out_ref):
+    out_ref[...] = in_ref[...]
+
+
+def reorder(array, order):
+    rows, width = array.shape
+    parts = order.shape[0]
+    return pl.pallas_call(
+        reorder_kernel,
+        grid_spec=pltpu.PrefetchScalarGridSpec(
+            num_scalar_prefetch=1,
+            grid=(parts,),
+            in_specs=[pl.BlockSpec((rows, width // parts), lambda i, o: (0, o[i]))],
+            out_specs=pl.BlockSpec((rows, width // parts), lambda i, o: (0, i)),
+        ),
+        out_shape=jax.ShapeDtypeStruct(array.shape, array.dtype),
+        name="reorder",
+        **params(0, 2 * array.size * array.dtype.itemsize),
+    )(order, array)
+
+
+def head_norm(raw, gain):
+    scale = lax.rsqrt(jnp.mean(raw * raw, axis=-1, keepdims=True) + EPS_NORM)
+    return raw * scale * gain
+
+
+def turn(value, cos_tab, sin_tab):
+    return value * cos_tab + pltpu.roll(value, HEAD_SIZE // 2, 1) * sin_tab
+
+
+def heads_kernel(raw_ref, cos_ref, sin_ref, qgain_ref, kgain_ref, q_ref, k_ref, v_ref):
+    raw = raw_ref[...]
+    cos_tab, sin_tab = cos_ref[...], sin_ref[...]
+    for head in range(2):
+        at = slice(head * HEAD_SIZE, (head + 1) * HEAD_SIZE)
+        q_ref[:, at] = turn(head_norm(raw[:, at], qgain_ref[...]), cos_tab, sin_tab).astype(
+            jnp.bfloat16
+        )
+    k_raw = raw[:, 2 * HEAD_SIZE : 3 * HEAD_SIZE]
+    k_ref[...] = turn(head_norm(k_raw, kgain_ref[...]), cos_tab, sin_tab).astype(jnp.bfloat16)
+    v_ref[...] = raw[:, 3 * HEAD_SIZE :].astype(jnp.bfloat16)
+
+
+def make_heads(raw, cos_tab, sin_tab, query_gain, key_gain):
+    rows, width = raw.shape
+    count = width // (4 * HEAD_SIZE)
+    table = pl.BlockSpec((ROW_TILE, HEAD_SIZE), lambda i, r: (i, 0))
+    gain = pl.BlockSpec((1, HEAD_SIZE), lambda i, r: (0, 0))
+    one = pl.BlockSpec((ROW_TILE, HEAD_SIZE), lambda i, r: (i, r))
+    return pl.pallas_call(
+        heads_kernel,
+        grid=(rows // ROW_TILE, count),
+        in_specs=[
+            pl.BlockSpec((ROW_TILE, 4 * HEAD_SIZE), lambda i, r: (i, r)),
+            table,
+            table,
+            gain,
+            gain,
+        ],
+        out_specs=[pl.BlockSpec((ROW_TILE, 2 * HEAD_SIZE), lambda i, r: (i, r)), one, one],
+        out_shape=[
+            jax.ShapeDtypeStruct((rows, count * 2 * HEAD_SIZE), jnp.bfloat16),
+            jax.ShapeDtypeStruct((rows, count * HEAD_SIZE), jnp.bfloat16),
+            jax.ShapeDtypeStruct((rows, count * HEAD_SIZE), jnp.bfloat16),
+        ],
+        name="make_heads",
+        **params(0, raw.size * 6),
+    )(raw, cos_tab, sin_tab, query_gain[None, :], key_gain[None, :])
+
+
+def heads_back_kernel(
+    raw_ref,
+    dq_ref,
+    dk_ref,
+    dk_far_ref,
+    dv_ref,
+    dv_far_ref,
+    cos_ref,
+    sin_ref,
+    qgain_ref,
+    kgain_ref,
+    out_ref,
+    gain_ref,
+):
+    raw = raw_ref[...]
+    cos_tab, sin_tab = cos_ref[...], sin_ref[...]
+
+    @pl.when((pl.program_id(0) == 0) & (pl.program_id(1) == 0))
+    def _():
+        gain_ref[...] = jnp.zeros_like(gain_ref)
+
+    def back(value, upstream, gain):
+        turned = upstream * cos_tab - pltpu.roll(upstream, HEAD_SIZE // 2, 1) * sin_tab
+        scale = lax.rsqrt(jnp.mean(value * value, axis=-1, keepdims=True) + EPS_NORM)
+        hat = value * scale
+        weighted = turned * gain
+        inner = jnp.mean(hat * weighted, axis=-1, keepdims=True)
+        grad = scale * (weighted - hat * inner)
+        return grad.astype(jnp.bfloat16), jnp.sum(turned * hat, axis=0, keepdims=True)
+
+    q_sum = jnp.zeros((1, HEAD_SIZE), jnp.float32)
+    for head in range(2):
+        at = slice(head * HEAD_SIZE, (head + 1) * HEAD_SIZE)
+        grad, part = back(raw[:, at], dq_ref[:, at].astype(jnp.float32), qgain_ref[...])
+        out_ref[:, at] = grad
+        q_sum = q_sum + part
+    key_up = dk_ref[...].astype(jnp.float32) + dk_far_ref[...].astype(jnp.float32)
+    grad, k_sum = back(raw[:, 2 * HEAD_SIZE : 3 * HEAD_SIZE], key_up, kgain_ref[...])
+    out_ref[:, 2 * HEAD_SIZE : 3 * HEAD_SIZE] = grad
+    out_ref[:, 3 * HEAD_SIZE :] = (
+        dv_ref[...].astype(jnp.float32) + dv_far_ref[...].astype(jnp.float32)
+    ).astype(jnp.bfloat16)
+    gain_ref[0:1, :] += q_sum
+    gain_ref[1:2, :] += k_sum
+
+
+def heads_return(raw, dq, dk, dk_far, dv, dv_far, cos_tab, sin_tab, query_gain, key_gain):
+    rows, width = raw.shape
+    count = width // (4 * HEAD_SIZE)
+    table = pl.BlockSpec((ROW_TILE, HEAD_SIZE), lambda i, r: (i, 0))
+    gain = pl.BlockSpec((1, HEAD_SIZE), lambda i, r: (0, 0))
+    one = pl.BlockSpec((ROW_TILE, HEAD_SIZE), lambda i, r: (i, r))
+    far = pl.BlockSpec((ROW_TILE, HEAD_SIZE), lambda i, r: (i, (r + 2) % 4))
+    full = pl.BlockSpec((ROW_TILE, 4 * HEAD_SIZE), lambda i, r: (i, r))
+    return pl.pallas_call(
+        heads_back_kernel,
+        grid=(rows // ROW_TILE, count),
+        in_specs=[
+            full,
+            pl.BlockSpec((ROW_TILE, 2 * HEAD_SIZE), lambda i, r: (i, r)),
+            one,
+            far,
+            one,
+            far,
+            table,
+            table,
+            gain,
+            gain,
+        ],
+        out_specs=[full, pl.BlockSpec((8, HEAD_SIZE), lambda i, r: (0, 0))],
+        out_shape=[
+            jax.ShapeDtypeStruct((rows, width), jnp.bfloat16),
+            jax.ShapeDtypeStruct((8, HEAD_SIZE), jnp.float32),
+        ],
+        name="heads_return",
+        **params(0, raw.size * 8),
+    )(raw, dq, dk, dk_far, dv, dv_far, cos_tab, sin_tab, query_gain[None, :], key_gain[None, :])
+
+
+def stack_heads(block):
+    return jnp.concatenate([block[:, :HEAD_SIZE], block[:, HEAD_SIZE:]], axis=0)
+
+
+def pair_mask(first_key, row_block, pair, parity):
+    rows = lax.broadcasted_iota(jnp.int32, (2 * BLK, 2 * BLK), 0)
+    cols = lax.broadcasted_iota(jnp.int32, (2 * BLK, 2 * BLK), 1)
+    row_at = row_block * BLK + lax.rem(rows, BLK)
+    key_block = 2 * pair + jnp.where(cols < BLK, parity, 1 - parity)
+    key_at = key_block * BLK + lax.rem(cols, BLK)
+    return (key_at <= row_at) & (key_at >= first_key * BLK)
+
+
+def attend_kernel(info_ref, q_ref, ko_ref, vo_ref, kf_ref, vf_ref, o_ref, l_ref):
+    group = pl.program_id(0)
+    blocks = q_ref.shape[0] // BLK
+    parity = info_ref[group, blocks]
+
+    def one_block(j, _):
+        first_key = info_ref[group, j]
+        rows = pl.ds(pl.multiple_of(j * BLK, BLK), BLK)
+        query = stack_heads(q_ref[rows, :])
+
+        def one_pair(m, carry):
+            total, acc = carry
+            at = pl.ds(pl.multiple_of(m * BLK, BLK), BLK)
+            key = jnp.concatenate([ko_ref[at, :], kf_ref[at, :]], axis=0)
+            value = jnp.concatenate([vo_ref[at, :], vf_ref[at, :]], axis=0)
+            score = dot_t(query, key) * SCALE
+            expo = jnp.where(
+                pair_mask(first_key, 2 * j + parity, m, parity), jnp.exp(score), 0.0
+            )
+            total = total + jnp.sum(expo, axis=1, keepdims=True)
+            acc = acc + matrix_product(expo.astype(jnp.bfloat16), value)
+            return total, acc
+
+        total, acc = lax.fori_loop(
+            lax.div(first_key, 2),
+            j + 1,
+            one_pair,
+            (jnp.zeros((2 * BLK, 1), jnp.float32), jnp.zeros((2 * BLK, HEAD_SIZE), jnp.float32)),
+        )
+        out = (acc / total).astype(jnp.bfloat16)
+        o_ref[rows, :HEAD_SIZE] = out[:BLK]
+        o_ref[rows, HEAD_SIZE:] = out[BLK:]
+        lane = lax.broadcasted_iota(jnp.int32, (BLK, HEAD_SIZE), 1)
+        l_ref[rows, :] = jnp.where(lane == 0, total[:BLK], total[BLK:])
+        return 0
+
+    lax.fori_loop(0, blocks, one_block, 0)
+
+
+def attend(info, query, key, value, key_far, value_far):
+    groups = 2
+    rows = query.shape[0] // groups
+    count = key.shape[1] // HEAD_SIZE
+    own = pl.BlockSpec((rows, HEAD_SIZE), lambda g, r, s: (g, r))
+    far = pl.BlockSpec((rows, HEAD_SIZE), lambda g, r, s: (g, (r + 2) % 4))
+    wide = pl.BlockSpec((rows, 2 * HEAD_SIZE), lambda g, r, s: (g, r))
+    return pl.pallas_call(
+        attend_kernel,
+        grid_spec=pltpu.PrefetchScalarGridSpec(
+            num_scalar_prefetch=1,
+            grid=(groups, count),
+            in_specs=[wide, own, own, far, far],
+            out_specs=[wide, own],
+        ),
+        out_shape=[
+            jax.ShapeDtypeStruct(query.shape, jnp.bfloat16),
+            jax.ShapeDtypeStruct(key.shape, jnp.float32),
+        ],
+        name="attend",
+        **params(20_000_000_000, 40_000_000),
+    )(info, query, key, value, key_far, value_far)
+
+
+def attend_back_kernel(
+    info_ref,
+    q_ref,
+    do_ref,
+    o_ref,
+    l_ref,
+    ko_ref,
+    vo_ref,
+    kf_ref,
+    vf_ref,
+    dq_ref,
+    dko_ref,
+    dvo_ref,
+    dkf_ref,
+    dvf_ref,
+    kacc_ref,
+    vacc_ref,
+):
+    group = pl.program_id(0)
+    blocks = q_ref.shape[0] // BLK
+    parity = info_ref[group, blocks]
+    kacc_ref[...] = jnp.zeros_like(kacc_ref)
+    vacc_ref[...] = jnp.zeros_like(vacc_ref)
+
+    def one_block(j, _):
+        first_key = info_ref[group, j]
+        rows = pl.ds(pl.multiple_of(j * BLK, BLK), BLK)
+        query = stack_heads(q_ref[rows, :])
+        attn = stack_heads(o_ref[rows, :]).astype(jnp.float32)
+        grad = stack_heads(do_ref[rows, :]).astype(jnp.float32)
+        total = jnp.concatenate([l_ref[rows, 0:1], l_ref[rows, 1:2]], axis=0)
+        grad_b = (grad / total).astype(jnp.bfloat16)
+        inner = jnp.sum(grad_b.astype(jnp.float32) * attn, axis=1, keepdims=True)
+
+        def one_pair(m, dq):
+            at = pl.ds(pl.multiple_of(m * BLK, BLK), BLK)
+            key = jnp.concatenate([ko_ref[at, :], kf_ref[at, :]], axis=0)
+            value = jnp.concatenate([vo_ref[at, :], vf_ref[at, :]], axis=0)
+            score = dot_t(query, key) * SCALE
+            expo = jnp.where(
+                pair_mask(first_key, 2 * j + parity, m, parity), jnp.exp(score), 0.0
+            )
+            d_score = (expo * (dot_t(grad_b, value) - inner)).astype(jnp.bfloat16)
+            d_key = dot_rows(d_score, query)
+            d_value = dot_rows(expo.astype(jnp.bfloat16), grad_b)
+            kacc_ref[0, at, :] += d_key[:BLK]
+            kacc_ref[1, at, :] += d_key[BLK:]
+            vacc_ref[0, at, :] += d_value[:BLK]
+            vacc_ref[1, at, :] += d_value[BLK:]
+            return dq + matrix_product(d_score, key)
+
+        dq = lax.fori_loop(
+            lax.div(first_key, 2), j + 1, one_pair, jnp.zeros((2 * BLK, HEAD_SIZE), jnp.float32)
+        )
+        dq = (dq * SCALE).astype(jnp.bfloat16)
+        dq_ref[rows, :HEAD_SIZE] = dq[:BLK]
+        dq_ref[rows, HEAD_SIZE:] = dq[BLK:]
+        return 0
+
+    lax.fori_loop(0, blocks, one_block, 0)
+    dko_ref[...] = (kacc_ref[0] * SCALE).astype(jnp.bfloat16)
+    dkf_ref[...] = (kacc_ref[1] * SCALE).astype(jnp.bfloat16)
+    dvo_ref[...] = vacc_ref[0].astype(jnp.bfloat16)
+    dvf_ref[...] = vacc_ref[1].astype(jnp.bfloat16)
+
+
+def attend_back(info, query, d_attn, attn, total, key, value, key_far, value_far):
+    groups = 2
+    rows = query.shape[0] // groups
+    count = key.shape[1] // HEAD_SIZE
+    own = pl.BlockSpec((rows, HEAD_SIZE), lambda g, r, s: (g, r))
+    far = pl.BlockSpec((rows, HEAD_SIZE), lambda g, r, s: (g, (r + 2) % 4))
+    wide = pl.BlockSpec((rows, 2 * HEAD_SIZE), lambda g, r, s: (g, r))
+    narrow = jax.ShapeDtypeStruct(key.shape, jnp.bfloat16)
+    return pl.pallas_call(
+        attend_back_kernel,
+        grid_spec=pltpu.PrefetchScalarGridSpec(
+            num_scalar_prefetch=1,
+            grid=(groups, count),
+            in_specs=[wide, wide, wide, own, own, own, far, far],
+            out_specs=[wide, own, own, own, own],
+            scratch_shapes=[
+                pltpu.VMEM((2, rows, HEAD_SIZE), jnp.float32),
+                pltpu.VMEM((2, rows, HEAD_SIZE), jnp.float32),
+            ],
+        ),
+        out_shape=[
+            jax.ShapeDtypeStruct(query.shape, jnp.bfloat16),
+            narrow,
+            narrow,
+            narrow,
+            narrow,
+        ],
+        name="attend_back",
+        **params(50_000_000_000, 60_000_000),
+    )(info, query, d_attn, attn, total, key, value, key_far, value_far)
+
+
+HIDDEN_TILE = 256
+ROW_STEP = 512
+
+
+def ffn_up_kernel(x_ref, g0, g1, g2, g3, u0, u1, u2, u3, act_ref, dgate_ref, silu_ref):
+    depth = g0.shape[1]
+    for first in range(0, x_ref.shape[0], ROW_STEP):
+        rows = slice(first, first + ROW_STEP)
+        gate = jnp.zeros((ROW_STEP, HIDDEN_TILE), jnp.float32)
+        upper = jnp.zeros((ROW_STEP, HIDDEN_TILE), jnp.float32)
+        for i, (g, u) in enumerate(((g0, u0), (g1, u1), (g2, u2), (g3, u3))):
+            x = x_ref[rows, i * depth : (i + 1) * depth]
+            gate = gate + dot_t(x, g[...])
+            upper = upper + dot_t(x, u[...])
+        sig = 1.0 / (1.0 + jnp.exp(-gate))
+        silu = gate * sig
+        act_ref[rows, :] = (silu * upper).astype(jnp.bfloat16)
+        silu_ref[rows, :] = silu.astype(jnp.bfloat16)
+        dgate_ref[rows, :] = (upper * sig * (1.0 + gate * (1.0 - sig))).astype(jnp.bfloat16)
+
+
+def ffn_up(x, gates, ups):
+    rows, width = x.shape
+    hidden, depth = gates[0].shape
+    weight = pl.BlockSpec((HIDDEN_TILE, depth), lambda j: (j, 0))
+    out = pl.BlockSpec((rows, HIDDEN_TILE), lambda j: (0, j))
+    shape = jax.ShapeDtypeStruct((rows, hidden), jnp.bfloat16)
+    return pl.pallas_call(
+        ffn_up_kernel,
+        grid=(hidden // HIDDEN_TILE,),
+        in_specs=[pl.BlockSpec((rows, width), lambda j: (0, 0))] + [weight] * 8,
+        out_specs=[out] * 3,
+        out_shape=[shape] * 3,
+        name="ffn_up",
+        **params(4 * rows * width * hidden, 70_000_000),
+    )(x, *gates, *ups)
+
+
+def ffn_back_kernel(dy_ref, w_ref, dgate_ref, silu_ref, gate_ref, up_ref):
+    for first in range(0, dy_ref.shape[0], ROW_STEP):
+        rows = slice(first, first + ROW_STEP)
+        d_act = dot_t(dy_ref[rows, :], w_ref[...])
+        gate_ref[rows, :] = (d_act * dgate_ref[rows, :].astype(jnp.float32)).astype(jnp.bfloat16)
+        up_ref[rows, :] = (d_act * silu_ref[rows, :].astype(jnp.float32)).astype(jnp.bfloat16)
+
+
+def ffn_back(dy, w_down, dgate, silu):
+    rows, width = dy.shape
+    hidden = w_down.shape[0]
+    out = pl.BlockSpec((rows, HIDDEN_TILE), lambda j: (0, j))
+    shape = jax.ShapeDtypeStruct((rows, hidden), jnp.bfloat16)
+    return pl.pallas_call(
+        ffn_back_kernel,
+        grid=(hidden // HIDDEN_TILE,),
+        in_specs=[
+            pl.BlockSpec((rows, width), lambda j: (0, 0)),
+            pl.BlockSpec((HIDDEN_TILE, width), lambda j: (j, 0)),
+            out,
+            out,
+        ],
+        out_specs=[out] * 2,
+        out_shape=[shape] * 2,
+        name="ffn_back",
+        **params(2 * rows * width * hidden, 70_000_000),
+    )(dy, w_down, dgate, silu)
+
+
+def block_info(lengths, positions, first):
+    count = (lengths + BLK - 1) // BLK
+    ends = jnp.cumsum(count)
+    starts = jnp.concatenate([jnp.zeros((1,), jnp.int32), ends])
+    own = lax.dynamic_slice_in_dim(positions, first, 8)
+    first_keys = jnp.max(jnp.where(starts[None, :] <= own[:, None], starts[None, :], 0), axis=1)
+    limits = jnp.concatenate([lengths, jnp.zeros((1,), jnp.int32)])
+    seq = jnp.sum((own[:, None] >= ends[None, :]).astype(jnp.int32), axis=1)
+    limit = jnp.sum(jnp.where(seq[:, None] == jnp.arange(4)[None, :], limits[None, :], 0), axis=1)
+    pos = ((own - first_keys)[:, None] * BLK + jnp.arange(BLK)[None, :]).astype(jnp.int32)
+    valid = pos < limit[:, None]
+    return first_keys, own, pos.reshape(-1), valid.reshape(-1)
+
+
+def chip_layer(
+    tokens,
+    cotangent,
+    seq_lens,
+    block_pos,
+    norm1_gain,
+    w_query,
+    key_matrix,
+    value_matrix,
+    query_gain,
+    key_gain,
+    w_out,
+    norm2_gain,
+    w_gate,
+    w_up,
+    w_down,
+):
+    xi, core, yi = lax.axis_index("x"), lax.axis_index("c"), lax.axis_index("y")
+    rows, width = tokens.shape
+    bf16, f32 = jnp.bfloat16, jnp.float32
+
+    q_in, k_in = w_query.shape[1], key_matrix.shape[1]
+    attn_shard = jnp.concatenate([w_query.T, key_matrix.T, value_matrix.T, w_out], axis=0)
+    attn_w = four_pieces(gather_z(attn_shard), "x")
+    attn_w = [a.reshape(4, attn_shard.shape[0], width) for a in attn_w]
+
+    def part(first, last):
+        return [a[:, first:last].reshape(-1, width) for a in attn_w]
+
+    q_w, k_w = part(0, q_in), part(q_in, q_in + k_in)
+    v_w, o_w = part(q_in + k_in, q_in + 2 * k_in), part(q_in + 2 * k_in, attn_shard.shape[0])
+    qkv_w = jnp.concatenate([w for trio in zip(q_w, k_w, v_w) for w in trio], axis=0)
+    out_w = jnp.concatenate(o_w, axis=0)
+    gate_w = four_pieces(gather_z(to_core(w_gate.T, core)), "y")
+    up_w = four_pieces(gather_z(to_core(w_up.T, core)), "x")
+    down_w = gather_z(jnp.concatenate(four_pieces(to_core(w_down, core), "y"), axis=1))
+
+    lengths_here = jnp.concatenate([seq_lens[0], block_pos[0]]).astype(f32)
+    lengths_there = swap(lengths_here[None, :], "c")[0].astype(jnp.int32)
+    first_own = yi * 8
+    keys_here, at_here, pos_here, valid_here = block_info(seq_lens[0], block_pos[0], first_own)
+    keys_there, at_there, pos_there, _ = block_info(
+        lengths_there[:3], lengths_there[3:], first_own
+    )
+    info = jnp.stack(
+        [
+            jnp.concatenate([keys_here, at_here[:1]]),
+            jnp.concatenate([keys_there, at_there[:1]]),
+        ]
+    ).astype(jnp.int32)
+    freq = jnp.exp(
+        jnp.arange(HEAD_SIZE // 2, dtype=f32) * (-2.0 * math.log(ROPE_BASE) / HEAD_SIZE)
+    )
+    angles = jnp.concatenate([pos_here, pos_there]).astype(f32)[:, None] * freq[None, :]
+    cos_half, sin_half = jnp.cos(angles), jnp.sin(angles)
+    cos_tab = jnp.concatenate([cos_half, cos_half], axis=1)
+    sin_tab = jnp.concatenate([-sin_half, sin_half], axis=1)
+    valid = valid_here.astype(f32)[:, None]
+
+    blocks = jnp.arange(8)
+    ry, rx, rc = blocks // 4, (blocks // 2) % 2, blocks % 2
+    order = ((rx ^ xi) * 4 + rc * 2 + (ry ^ yi)).astype(jnp.int32)
+    nx, nc, ny = blocks // 4, (blocks // 2) % 2, blocks % 2
+    order_back = ((ny ^ yi) * 4 + (nx ^ xi) * 2 + nc).astype(jnp.int32)
+
+    def both(own):
+        return jnp.concatenate([own, swap(own, "c")], axis=0)
+
+    inputs = tokens.astype(f32)
+    first_normed, scale1 = rms_parts(inputs, norm1_gain)
+    normed1 = both(first_normed.astype(bf16))
+    grad_out = valid * cotangent.astype(f32)
+    dy = both(reorder(grad_out.astype(bf16), order))
+
+    raw = dot_t(normed1, qkv_w)
+    query, key, value = make_heads(raw, cos_tab, sin_tab, query_gain, key_gain)
+    key_far, value_far = swap(key, "y"), swap(value, "y")
+    attn, totals = attend(info, query, key, value, key_far, value_far)
+    out_there = swap(matrix_product(attn[rows:], out_w).astype(bf16), "c")
+    resid = inputs + matrix_product(attn[:rows], out_w) + out_there.astype(f32)
+    normed2, scale2 = rms_parts(resid, norm2_gain)
+    normed2_b = both(reorder(normed2.astype(bf16), order))
+
+    act, dgate, silu = ffn_up(normed2_b, gate_w, up_w)
+    mixed_there = swap(matrix_product(act[rows:], down_w).astype(bf16), "c")
+    mixed = (matrix_product(act[:rows], down_w) + mixed_there.astype(f32)).astype(bf16)
+    output = (valid * (resid + reorder(mixed, order_back).astype(f32))).astype(bf16)
+
+    down_sum = scatter_z(dot_rows(act, dy).astype(bf16))
+    fourth = width // 4
+    down_sum = add_pieces([down_sum[:, i * fourth : (i + 1) * fourth] for i in range(4)], "x")
+    gate_grad, up_grad = ffn_back(dy, down_w, dgate, silu)
+    pieces = [normed2_b[:, i * fourth : (i + 1) * fourth] for i in range(4)]
+    gate_sum = scatter_z(add_pieces([dot_rows(gate_grad, p).astype(bf16) for p in pieces], "y"))
+    up_sum = scatter_z(add_pieces([dot_rows(up_grad, p).astype(bf16) for p in pieces], "x"))
+
+    def back_term(first):
+        g, u = gate_grad[first : first + rows], up_grad[first : first + rows]
+        return jnp.concatenate(
+            [(matrix_product(g, a) + matrix_product(u, b)).astype(bf16) for a, b in zip(gate_w, up_w)],
+            axis=1,
+        )
+
+    normed2_there = swap(back_term(rows), "c")
+    normed2_grad = reorder(
+        (back_term(0).astype(f32) + normed2_there.astype(f32)).astype(bf16), order_back
+    ).astype(f32)
+    resid_grad = grad_out + norm_back(resid, scale2, norm2_gain, normed2_grad)
+    gain2_part = jnp.sum(normed2_grad * resid * scale2, axis=0)
+    resid_grad_b = both(resid_grad.astype(bf16))
+    d_attn = dot_t(resid_grad_b, out_w).astype(bf16)
+    dq, dk, dv, dk_far, dv_far = attend_back(
+        info, query, d_attn, attn, totals, key, value, key_far, value_far
+    )
+    dk_back, dv_back = swap(dk_far, "y"), swap(dv_far, "y")
+    raw_grad, head_gains = heads_return(
+        raw, dq, dk, dk_back, dv, dv_back, cos_tab, sin_tab, query_gain, key_gain
+    )
+
+    out_span, qkv_span = out_w.shape[0] // 4, qkv_w.shape[0] // 4
+    out_sum = scatter_z(
+        add_pieces(
+            [
+                dot_rows(attn[:, i * out_span : (i + 1) * out_span], resid_grad_b).astype(bf16)
+                for i in range(4)
+            ],
+            "y",
+        )
+    )
+    qkv_sum = add_pieces(
+        [
+            dot_rows(raw_grad[:, i * qkv_span : (i + 1) * qkv_span], normed1).astype(bf16)
+            for i in range(4)
+        ],
+        "x",
+    )
+    q_rows, k_rows = 4 * q_in, 4 * k_in
+    qkv_sum = scatter_z(
+        jnp.concatenate(
+            [
+                qkv_sum[:q_rows].reshape(4, q_in, width),
+                qkv_sum[q_rows : q_rows + k_rows].reshape(4, k_in, width),
+                qkv_sum[q_rows + k_rows :].reshape(4, k_in, width),
+            ],
+            axis=1,
+        ).reshape(-1, width)
+    ).astype(f32)
+
+    normed1_there = swap(matrix_product(raw_grad[rows:], qkv_w).astype(bf16), "c")
+    normed1_grad = matrix_product(raw_grad[:rows], qkv_w) + normed1_there.astype(f32)
+    tokens_grad = resid_grad + norm_back(inputs, scale1, norm1_gain, normed1_grad)
+    gain1_part = jnp.sum(normed1_grad * inputs * scale1, axis=0)
+    gains = jnp.concatenate([gain1_part, gain2_part, head_gains[0], head_gains[1]])[None, :]
+    for axis in ("c", "x", "y"):
+        gains = gains + swap(gains, axis)
+    for step in (1, 2):
+        gains = gains + lax.ppermute(gains, "z", [(i, i ^ step) for i in range(4)])
+    gains = gains[0]
+
+    return (
+        output,
+        tokens_grad,
+        gains[:width],
+        qkv_sum[:q_in].T,
+        qkv_sum[q_in : q_in + k_in].T,
+        qkv_sum[q_in + k_in :].T,
+        gains[2 * width : 2 * width + HEAD_SIZE],
+        gains[2 * width + HEAD_SIZE :],
+        out_sum.astype(f32),
+        gains[width : 2 * width],
+        from_core(gate_sum, core).astype(f32).T,
+        from_core(up_sum, core).astype(f32).T,
+        from_core(down_sum, core).astype(f32),
+    )
+
+
+def chip_solution(mesh):
+    fine = Mesh(mesh.devices.reshape(2, 2, 2, 4), ("x", "c", "y", "z"))
+    row_spec = P(("x", "c", "y", "z"), None)
+    group_spec = P(("x", "c", "z"), None)
+    head_cols = P(None, ("y", "x", "c", "z"))
+    head_rows = P(("y", "x", "c", "z"), None)
+    up_spec, down_spec = P(("x", "c", "y"), "z"), P("z", ("x", "c", "y"))
+    return jax.shard_map(
+        chip_layer,
+        mesh=fine,
+        in_specs=(
+            row_spec,
+            row_spec,
+            group_spec,
+            group_spec,
+            P(),
+            head_cols,
+            head_cols,
+            head_cols,
+            P(),
+            P(),
+            head_rows,
+            P(),
+            up_spec,
+            up_spec,
+            down_spec,
+        ),
+        out_specs=(
+            row_spec,
+            row_spec,
+            P(),
+            head_cols,
+            head_cols,
+            head_cols,
+            P(),
+            P(),
+            head_rows,
+            P(),
+            up_spec,
+            up_spec,
+            down_spec,
+        ),
+        check_vma=False,
+    )
+
+
+def solution(mesh):
+    sizes = dict(mesh.shape)
+    if sizes == {"fsdp": 4, "heads": 2, "tensor": 4}:
+        return chip_solution(mesh)
+    return plain_solution(mesh)

time: 4490 us -> 1680 us (0.37)
  waiting for transfers between devices: 2910 us -> 698 us
  matrix products: 865 us -> 418 us
  Pallas kernels: 0 us -> 335 us
  local copies, waits for them, and re-layouts: 228 us -> 30.8 us
  other arithmetic: 293 us -> 102 us
  blocking collectives: 138 us -> 0 us
  starting transfers between devices: 19.3 us -> 70.6 us
    psum x1 -> x0, waiting for transfers between devices: 1030 us -> none  [tensor_sum(): lax.psum(term(0, row_count * lax.axis_size('tensor')).astype(jnp.bfloat16...]
    reduce_scatter x7 -> x5, waiting for transfers between devices: 910 us -> 0.01 us  [scatter_z(): return lax.psum_scatter(array, 'z', scatter_dimension=0, tiled=True)]
    all_gather x9 -> x4, waiting for transfers between devices: 765 us -> 51.5 us  [gather_z(): return lax.all_gather(array, 'z', axis=0, tiled=True)]
    ppermute x0 -> x51, waiting for transfers between devices: none -> 646 us  [the longest x49 643 us: swap(): return lax.ppermute(array, axis, SWAP)]
    dot_general x35 -> x2, matrix products: 584 us -> 38.1 us  [dot_t(): lax.dot_general(left, right, (((1,), (1,)), ((), ())), preferred_element_...]
    pallas_call x0 -> x10, Pallas kernels: none -> 335 us  [the longest x1 90.8 us: attend_back(): pl.pallas_call(attend_back_kernel, grid_spec=pltpu.PrefetchScalarGridSpec...]
    all_to_all x3 -> x0, waiting for transfers between devices: 193 us -> none  [the longest x2 154 us: to_heads(): lax.all_to_all(packed, 'heads', split_axis=1, concat_axis=0, tiled=True)]
    convert_element_type x16 -> x12, other arithmetic: 145 us -> 24.9 us  [the longest x1 5.47 us: chip_layer(): resid_grad_b = both(resid_grad.astype(bf16))]
  transfers between devices with their start and end apart: 20 -> 60, of which waited for: 14 -> 25; matrix products, arithmetic and copies ran while one was open for 27% -> 31% of each run, Pallas kernels for 0% -> 18%
where the time goes in v1:
time: 1680 us; the launch traced here: 1670 us
  waiting for transfers between devices  698 us (42%)
  matrix products  418 us (25%)
  Pallas kernels  335 us (20%)
  other arithmetic  102 us (6%)
  starting transfers between devices  70.6 us (4%)
  local copies, waits for them, and re-layouts  30.8 us (2%)
    ppermute x49, waiting for transfers between devices, swap(): return lax.ppermute(array, axis, SWAP)  643 us
    dot_general x22, matrix products, matrix_product(): return jnp.dot(left, right, preferred_element_type=jnp.float32)  191 us
    dot_general x17, matrix products, dot_rows(): lax.dot_general(left, right, (((0,), (0,)), ((), ())), preferred_element_...  189 us
    pallas_call x1, Pallas kernels, attend_back(): pl.pallas_call(attend_back_kernel, grid_spec=pltpu.PrefetchScalarGridSpec...  90.8 us
    pallas_call x1, Pallas kernels, ffn_up(): pl.pallas_call(ffn_up_kernel, grid=(hidden // HIDDEN_TILE,), in_specs=[pl...  66.8 us
    all_gather x4, waiting for transfers between devices, gather_z(): return lax.all_gather(array, 'z', axis=0, tiled=True)  51.5 us
    pallas_call x1, Pallas kernels, attend(): pl.pallas_call(attend_kernel, grid_spec=pltpu.PrefetchScalarGridSpec(num_...  49.3 us
    ppermute x49, starting transfers between devices, swap(): return lax.ppermute(array, axis, SWAP)  45.2 us
  transfers between devices with their start and end apart: 60, of which 25 were waited for; matrix products, arithmetic and copies ran while one was open for 31% of the time, Pallas kernels for 18%

profile of v1, /device:TPU:0, one launch (start us, length us, event | category | flops | bytes accessed | tf_op | source)
XLA Modules:
  0.0 1670.6 jit_solution(17171698388038980717)
XLA Ops:
  24.9 51.5 %all-gather.5.cloned.1.call-done = bf16[768,2048]{1,0:T(8,128)(2,1)} async-done(((bf16[192,2048]{1,0:T(8,128)(2,1)}), bf16[768,2048]{1,0:T(8,128)(2,1)}) %all-gather.5.cloned.1.call-update) | async-done | bytes 3145744 | tf_op jit(solution)/shard_map/all_gather | solution.py:482
  89.7 58.0 %collective-permute-done.3 = bf16[768,2048]{1,0:T(8,128)(2,1)} collective-permute-done((bf16[768,2048]{1,0:T(8,128)(2,1)}, bf16[768,2048]{1,0:T(8,128)(2,1)}, u32[]{:S(2)}, u32[]{:S(2)}) %collective-permute-start.3) | collective-permute-done | bytes 3145760 | tf_op jit(solution)/shard_map/ppermute | solution.py:466
  155.1 61.4 %collective-permute-done.4 = bf16[768,2048]{1,0:T(8,128)(2,1)S(1)} collective-permute-done((bf16[768,2048]{1,0:T(8,128)(2,1)}, bf16[768,2048]{1,0:T(8,128)(2,1)S(1)}, u32[]{:S(2)}, u32[]{:S(2)}) %collective-permute-start.4) | collective-permute-done | bytes 3145760 | tf_op jit(solution)/shard_map/ppermute | solution.py:466
  218.0 23.4 %fusion.126.raw_ref = f32[2048,2048]{1,0:T(8,128)} fusion(bf16[2048,2048]{1,0:T(8,128)(2,1)S(1)} %constant_dynamic-update-slice_fusion, bf16[1024,2048]{1,0:T(8,128)(2,1)} %collective-permute-done.1, bf16[1024,2048]{1,0:T(8,128)(2,1)} %fusion.4), kind=kOutput, calls=%fused_computation.245 | convolution fusion | flops 17196646400 | bytes 33554432 | tf_op jit(solution)/shard_map/dot_general | solution.py:460
  241.4 28.0 %make_heads.1 = (bf16[2048,1024]{1,0:T(8,128)(2,1)}, bf16[2048,512]{1,0:T(8,128)(2,1)}, bf16[2048,512]{1,0:T(8,128)(2,1)}) custom-call(f32[2048,2048]{1,0:T(8,128)} %fusion.126.raw_ref, f32[2048,128]{1,0:T(8,128)} %pad_maximum_fusion.8.cos_ref, f32[2048,128]{1,0:T(8,128)} %pad_maximum_fusion.9.sin_ref, f32[1,128]{1,0:T(1,128)} %bitcast.169, f32[1,128]{1,0:T(1,128)} %bitcast.171), custom_call_target="tpu_custom_call" | custom-call | bytes 25165824 | tf_op jit(solution)/shard_map/make_heads/pallas_call | solution.py:576
  274.8 14.5 collective-permute-done.18
  291.8 88.2 %collective-permute-done.19 = bf16[768,512]{1,0:T(8,128)(2,1)S(1)} collective-permute-done((bf16[768,512]{1,0:T(8,128)(2,1)S(1)}, bf16[768,512]{1,0:T(8,128)(2,1)S(1)}, u32[]{:S(2)}, u32[]{:S(2)}) %collective-permute-start.19) | collective-permute-done | bytes 786464 | tf_op jit(solution)/shard_map/ppermute | solution.py:466
  380.0 13.5 collective-permute-done.20
  395.9 49.3 %attend.1 = (bf16[2048,1024]{1,0:T(8,128)(2,1)}, f32[2048,512]{1,0:T(8,128)}) custom-call(s32[2,9]{1,0:T(2,128)} %pad_add_fusion.info_ref, bf16[2048,1024]{1,0:T(8,128)(2,1)} %get-tuple-element.30.q_ref, bf16[2048,512]{1,0:T(8,128)(2,1)} %get-tuple-element.31.ko_ref, bf16[2048,512]{1,0:T(8,128)(2,1)} %get-tuple-element.32.vo_ref, ...), custom_call_target="tpu_custom_call" | custom-call | flops 20000000000 | bytes 40000000 | tf_op jit(solution)/shard_map/attend/pallas_call | solution.py:735
  494.3 44.1 %collective-permute-done.10.g1 = bf16[3072,512]{1,0:T(8,128)(2,1)} collective-permute-done((bf16[3072,512]{1,0:T(8,128)(2,1)}, bf16[3072,512]{1,0:T(8,128)(2,1)}, u32[]{:S(2)}, u32[]{:S(2)}) %collective-permute-start.10) | collective-permute-done | bytes 3145760 | tf_op jit(solution)/shard_map/ppermute | solution.py:466
  559.3 48.6 %collective-permute-done.11.g2 = bf16[3072,512]{1,0:T(8,128)(2,1)} collective-permute-done((bf16[3072,512]{1,0:T(8,128)(2,1)S(1)}, bf16[3072,512]{1,0:T(8,128)(2,1)}, u32[]{:S(2)}, u32[]{:S(2)}) %collective-permute-start.11) | collective-permute-done | bytes 3145760 | tf_op jit(solution)/shard_map/ppermute | solution.py:466
  607.9 66.2 %collective-permute-done.12.g3 = bf16[3072,512]{1,0:T(8,128)(2,1)} collective-permute-done((bf16[3072,512]{1,0:T(8,128)(2,1)}, bf16[3072,512]{1,0:T(8,128)(2,1)}, u32[]{:S(2)}, u32[]{:S(2)}) %collective-permute-start.12) | collective-permute-done | bytes 3145760 | tf_op jit(solution)/shard_map/ppermute | solution.py:466
  674.1 66.8 %ffn_up.1 = (bf16[2048,3072]{1,0:T(8,128)(2,1)}, bf16[2048,3072]{1,0:T(8,128)(2,1)}, bf16[2048,3072]{1,0:T(8,128)(2,1)}) custom-call(bf16[2048,2048]{1,0:T(8,128)(2,1)} %pad_maximum_fusion.x_ref, bf16[3072,512]{1,0:T(8,128)(2,1)} %all-gather.7.cloned.1.call-done.g0, bf16[3072,512]{1,0:T(8,128)(2,1)} %collective-permute-done.10.g1, ...), custom_call_target="tpu_custom_call" | custom-call | flops 51539607552 | bytes 70000000 | tf_op jit(solution)/shard_map/ffn_up/pallas_call | solution.py:877
  741.0 37.1 %ffn_back.1 = (bf16[2048,3072]{1,0:T(8,128)(2,1)}, bf16[2048,3072]{1,0:T(8,128)(2,1)}) custom-call(bf16[2048,2048]{1,0:T(8,128)(2,1)} %pad_maximum_fusion.2.dy_ref, bf16[3072,2048]{1,0:T(8,128)(2,1)} %all-gather.11.cloned.1.call-done.w_ref, bf16[2048,3072]{1,0:T(8,128)(2,1)} %get-tuple-element.35.dgate_ref, bf16[2048,3072]{1,0:T(8,128)(2,1)} %get-tuple-element.36.silu_ref), custom_call_target="tpu_custom_call" | custom-call | flops 25769803776 | bytes 70000000 | tf_op jit(solution)/shard_map/ffn_back/pallas_call | solution.py:901
  904.2 21.7 %collective-permute-done.44 = bf16[3072,512]{1,0:T(8,128)(2,1)S(1)} collective-permute-done((bf16[3072,512]{1,0:T(8,128)(2,1)S(1)}, bf16[3072,512]{1,0:T(8,128)(2,1)S(1)}, u32[]{:S(2)}, u32[]{:S(2)}) %collective-permute-start.44) | collective-permute-done | bytes 3145760 | tf_op jit(solution)/shard_map/ppermute | solution.py:466
  965.9 48.7 %collective-permute-done.45 = bf16[3072,512]{1,0:T(8,128)(2,1)S(1)} collective-permute-done((bf16[3072,512]{1,0:T(8,128)(2,1)S(1)}, bf16[3072,512]{1,0:T(8,128)(2,1)S(1)}, u32[]{:S(2)}, u32[]{:S(2)}) %collective-permute-start.45) | collective-permute-done | bytes 3145760 | tf_op jit(solution)/shard_map/ppermute | solution.py:466
  1026.5 14.5 fusion.70
  1068.8 40.0 %collective-permute-done.40 = bf16[3072,512]{1,0:T(8,128)(2,1)} collective-permute-done((bf16[3072,512]{1,0:T(8,128)(2,1)}, bf16[3072,512]{1,0:T(8,128)(2,1)}, u32[]{:S(2)}, u32[]{:S(2)}) %collective-permute-start.40) | collective-permute-done | bytes 3145760 | tf_op jit(solution)/shard_map/ppermute | solution.py:466
  1135.6 18.2 %collective-permute-done.36 = bf16[256,2048]{1,0:T(8,128)(2,1)S(1)} collective-permute-done((bf16[256,2048]{1,0:T(8,128)(2,1)S(1)}, bf16[256,2048]{1,0:T(8,128)(2,1)S(1)}, u32[]{:S(2)}, u32[]{:S(2)}) %collective-permute-start.36) | collective-permute-done | bytes 1048608 | tf_op jit(solution)/shard_map/ppermute | solution.py:466
  1183.5 32.9 %convolution_convert_fusion = bf16[3072,2048]{1,0:T(8,128)(2,1)} fusion(bf16[2048,3072]{1,0:T(8,128)(2,1)} %get-tuple-element.34, bf16[1024,2048]{1,0:T(8,128)(2,1)} %collective-permute-done.22, bf16[1024,2048]{1,0:T(8,128)(2,1)} %reorder.6), kind=kOutput, calls=%fused_computation.14 | convolution fusion | flops 25792872448 | bytes 33554432 | tf_op jit(solution)/shard_map/dot_general | solution.py:90
  1218.3 14.7 convolution_convert_fusion.9.do_ref
  1233.0 90.8 %attend_back.1 = (bf16[2048,1024]{1,0:T(8,128)(2,1)}, bf16[2048,512]{1,0:T(8,128)(2,1)}, bf16[2048,512]{1,0:T(8,128)(2,1)}, bf16[2048,512]{1,0:T(8,128)(2,1)}, bf16[2048,512]{1,0:T(8,128)(2,1)}) custom-call(s32[2,9]{1,0:T(2,128)} %pad_add_fusion.info_ref, bf16[2048,1024]{1,0:T(8,128)(2,1)} %get-tuple-element.30.q_ref, ...), custom_call_target="tpu_custom_call" | custom-call | flops 49999998976 | bytes 60000000 | tf_op jit(solution)/shard_map/attend_back/pallas_call | solution.py:826
  1327.2 19.4 %fusion.62 = bf16[1024,2048]{1,0:T(8,128)(2,1)} fusion(bf16[3072,2048]{1,0:T(8,128)(2,1)} %all-gather.11.cloned.1.call-done.w_ref, bf16[2048,3072]{1,0:T(8,128)(2,1)} %get-tuple-element.34), kind=kOutput, calls=%fused_computation.97 | convolution fusion | flops 12886999040 | bytes 23068672 | tf_op jit(solution)/shard_map/dot_general | solution.py:86
  1346.7 27.3 %collective-permute-done.25.dk_far_ref = bf16[2048,512]{1,0:T(8,128)(2,1)S(1)} collective-permute-done((bf16[2048,512]{1,0:T(8,128)(2,1)}, bf16[2048,512]{1,0:T(8,128)(2,1)S(1)}, u32[]{:S(2)}, u32[]{:S(2)}) %collective-permute-start.25) | collective-permute-done | bytes 2097184 | tf_op jit(solution)/shard_map/ppermute | solution.py:466
  1373.9 35.2 %collective-permute-done.26.dv_far_ref = bf16[2048,512]{1,0:T(8,128)(2,1)S(1)} collective-permute-done((bf16[2048,512]{1,0:T(8,128)(2,1)}, bf16[2048,512]{1,0:T(8,128)(2,1)S(1)}, u32[]{:S(2)}, u32[]{:S(2)}) %collective-permute-start.26) | collective-permute-done | bytes 2097184 | tf_op jit(solution)/shard_map/ppermute | solution.py:466
  1410.5 32.4 %heads_return.1 = (bf16[2048,2048]{1,0:T(8,128)(2,1)}, f32[8,128]{1,0:T(8,128)}) custom-call(f32[2048,2048]{1,0:T(8,128)} %fusion.126.raw_ref, bf16[2048,1024]{1,0:T(8,128)(2,1)} %get-tuple-element.40.dq_ref, bf16[2048,512]{1,0:T(8,128)(2,1)} %get-tuple-element.41.dk_ref, bf16[2048,512]{1,0:T(8,128)(2,1)} %copy-done.8, ...), custom_call_target="tpu_custom_call" | custom-call | bytes 33554432 | tf_op jit(solution)/shard_map/heads_return/pallas_call | solution.py:651
  1455.9 14.0 fusion.65
  1470.0 17.2 %add_convert_fusion.1.in_ref = bf16[1024,2048]{1,0:T(8,128)(2,1)} fusion(bf16[1024,2048]{1,0:T(8,128)(2,1)} %collective-permute-done.21, bf16[3072,2048]{1,0:T(8,128)(2,1)S(1)} %bitcast.177, bf16[2048,3072]{1,0:T(8,128)(2,1)} %get-tuple-element.34), kind=kOutput, calls=%fused_computation.44 | convolution fusion | flops 12891193344 | bytes 27262976 | tf_op jit(solution)/shard_map/dot_general | solution.py:86
  1522.2 18.9 %fusion.18 = (f32[2048]{0:T(1024)S(1)}, f32[1024]{0:T(1024)S(1)}, f32[1024,2048]{1,0:T(8,128)}) fusion(bf16[1024,2048]{1,0:T(8,128)(2,1)} %param.15, f32[1024]{0:T(1024)S(1)} %copy-done.33, f32[2048]{0:T(1024)S(1)} %copy-done.38, bf16[1024,2048]{1,0:T(8,128)(2,1)} %collective-permute-done.27, bf16[2048,2048]{1,0:T(8,128)(2,1)} %copy-done.22, ...), kind=kOutput, calls=%fused_computation.35 | convolution fusion | flops 8608805888 | bytes 29384704 | tf_op jit(solution)/shard_map/dot_general | solution.py:86
  1553.1 14.5 collective-permute-done.35
  1594.5 23.9 %collective-permute-start.32 = (f32[1,4352]{1,0:T(1,128)S(1)}, f32[1,4352]{1,0:T(1,128)S(1)}, u32[]{:S(2)}, u32[]{:S(2)}) collective-permute-start(f32[1,4352]{1,0:T(1,128)S(1)} %add.276), channel_id=1, source_target_pairs={{0,2},{1,3},{2,0},{3,1},{4,6},{5,7},{6,4},{7,5},{8,10},{9,11},{10,... | collective-permute-start | bytes 52232 | tf_op jit(solution)/shard_map/ppermute | solution.py:1087
  1622.5 18.8 %fusion.8 = (f32[1024,2048]{1,0:T(8,128)}, bf16[1024,2048]{1,0:T(8,128)(2,1)}) fusion(bf16[1024,2048]{1,0:T(8,128)(2,1)} %param.15, f32[1024,2048]{1,0:T(8,128)} %get-tuple-element.124, f32[1024]{0:T(1024)S(1)} %broadcast_multiply_fusion, f32[2048]{0:T(1024)S(1)} %copy-done.38, f32[1024]{0:T(1024)S(1)} %copy-done.33, f32[1024]{0:T(1024)S(1)} %copy-done.35, ...), kind=kLoop, calls=%fused_computation.25 | loop fusion | flops 50331648 | bytes 46174208 | tf_op jit(solution)/shard_map/add | solution.py:1081
  (369 shorter events, 501.4 us)
Async XLA Ops:
  9.4 457.8 %all-gather.7.cloned.1.call-start = ((), (), s32[]{:S(2)}) async-start(), calls=%async_computation.6 | async-start | bytes 3932160 | tf_op jit(solution)/shard_map/all_gather | solution.py:482
  13.9 455.2 %all-gather.9.cloned.1.call-start = ((), (), s32[]{:S(2)}) async-start(), calls=%async_computation.7 | async-start | bytes 3932160 | tf_op jit(solution)/shard_map/all_gather | solution.py:482
  20.5 197.5 %collective-permute-start.1 = (bf16[1024,2048]{1,0:T(8,128)(2,1)}, bf16[1024,2048]{1,0:T(8,128)(2,1)}, u32[]{:S(2)}, u32[]{:S(2)}) collective-permute-start(bf16[1024,2048]{1,0:T(8,128)(2,1)} %fusion.4), channel_id=1, source_target_pairs={{0,8},{8,0},{1,9},{9,1},{2,10},{10,2},{3,11},{11,3},{4,12},{12,4},... | collective-permute-start | bytes 12582920 | tf_op jit(solution)/shard_map/ppermute | solution.py:466
  23.0 248.4 %collective-permute-start.17 = (bf16[768,256]{1,0:T(8,128)(2,1)}, bf16[768,256]{1,0:T(8,128)(2,1)}, u32[]{:S(2)}, u32[]{:S(2)}) collective-permute-start(bf16[768,256]{1,0:T(8,128)(2,1)} %get-tuple-element.112), channel_id=1, source_target_pairs={{0,8},{8,0},{1,9},{9,1},{2,10},{10,2},{3,11},{11,3},{4,12},{12,4},... | collective-permute-start | bytes 1179656 | tf_op jit(solution)/shard_map/ppermute | solution.py:466
  76.4 71.9 %collective-permute-start.2 = (bf16[768,2048]{1,0:T(8,128)(2,1)}, bf16[768,2048]{1,0:T(8,128)(2,1)}, u32[]{:S(2)}, u32[]{:S(2)}) collective-permute-start(bf16[768,2048]{1,0:T(8,128)(2,1)} %all-gather.5.cloned.1.call-done), channel_id=1, source_target_pairs={{0,16},{16,0},{1,17},{17,1},{2,18},{18,2},{3,19},{19,3},{4,20},{20... | collective-permute-start | bytes 9437192 | tf_op jit(solution)/shard_map/ppermute | solution.py:466
  77.9 69.8 %collective-permute-start.3 = (bf16[768,2048]{1,0:T(8,128)(2,1)}, bf16[768,2048]{1,0:T(8,128)(2,1)}, u32[]{:S(2)}, u32[]{:S(2)}) collective-permute-start(bf16[768,2048]{1,0:T(8,128)(2,1)} %all-gather.5.cloned.1.call-done), channel_id=1, source_target_pairs={{0,4},{4,0},{1,5},{5,1},{2,6},{6,2},{3,7},{7,3},{8,12},{12,8},{9,1... | collective-permute-start | bytes 9437192 | tf_op jit(solution)/shard_map/ppermute | solution.py:466
  88.0 652.9 %all-gather.11.cloned.1.call-start = ((), (), s32[]{:S(2)}) async-start(), calls=%async_computation.8 | async-start | bytes 15728640 | tf_op jit(solution)/shard_map/all_gather | solution.py:482
  269.4 126.5 %collective-permute-start.5 = (bf16[2048,512]{1,0:T(8,128)(2,1)}, bf16[2048,512]{1,0:T(8,128)(2,1)}, u32[]{:S(2)}, u32[]{:S(2)}) collective-permute-start(bf16[2048,512]{1,0:T(8,128)(2,1)} %get-tuple-element.31.ko_ref), channel_id=1, source_target_pairs={{0,4},{4,0},{1,5},{5,1},{2,6},{6,2},{3,7},{7,3},{8,12},{12,8},{9,1... | collective-permute-start | bytes 6291464 | tf_op jit(solution)/shard_map/ppermute | solution.py:466
  270.9 125.0 %collective-permute-start.6 = (bf16[2048,512]{1,0:T(8,128)(2,1)}, bf16[2048,512]{1,0:T(8,128)(2,1)}, u32[]{:S(2)}, u32[]{:S(2)}) collective-permute-start(bf16[2048,512]{1,0:T(8,128)(2,1)} %get-tuple-element.32.vo_ref), channel_id=1, source_target_pairs={{0,4},{4,0},{1,5},{5,1},{2,6},{6,2},{3,7},{7,3},{8,12},{12,8},{9,1... | collective-permute-start | bytes 6291464 | tf_op jit(solution)/shard_map/ppermute | solution.py:466
  273.4 106.6 %collective-permute-start.19 = (bf16[768,512]{1,0:T(8,128)(2,1)S(1)}, bf16[768,512]{1,0:T(8,128)(2,1)S(1)}, u32[]{:S(2)}, u32[]{:S(2)}) collective-permute-start(bf16[768,512]{1,0:T(8,128)(2,1)S(1)} %maximum_select_fusion.2), channel_id=1, source_target_pairs={{0,4},{4,0},{1,5},{5,1},{2,6},{6,2},{3,7},{7,3},{8,12},{12,8},{9,1... | collective-permute-start | bytes 2359304 | tf_op jit(solution)/shard_map/ppermute | solution.py:466
  289.4 104.1 %collective-permute-start.20 = (bf16[768,512]{1,0:T(8,128)(2,1)S(1)}, bf16[768,512]{1,0:T(8,128)(2,1)S(1)}, u32[]{:S(2)}, u32[]{:S(2)}) collective-permute-start(bf16[768,512]{1,0:T(8,128)(2,1)S(1)} %collective-permute-done.18), channel_id=1, source_target_pairs={{0,4},{4,0},{1,5},{5,1},{2,6},{6,2},{3,7},{7,3},{8,12},{12,8},{9,1... | collective-permute-start | bytes 2359304 | tf_op jit(solution)/shard_map/ppermute | solution.py:466
  395.4 1110.2 %reduce-scatter.12.cloned.1.call-start = ((), (), s32[]{:S(2)}) async-start(), calls=%async_computation.12 | async-start | bytes 3932160 | tf_op jit(solution)/shard_map/reduce_scatter | solution.py:486
  467.2 71.2 %collective-permute-start.10 = (bf16[3072,512]{1,0:T(8,128)(2,1)}, bf16[3072,512]{1,0:T(8,128)(2,1)}, u32[]{:S(2)}, u32[]{:S(2)}) collective-permute-start(bf16[3072,512]{1,0:T(8,128)(2,1)} %all-gather.7.cloned.1.call-done.g0), channel_id=1, source_target_pairs={{0,16},{16,0},{1,17},{17,1},{2,18},{18,2},{3,19},{19,3},{4,20},{20... | collective-permute-start | bytes 9437192 | tf_op jit(solution)/shard_map/ppermute | solution.py:466
  469.1 72.2 %collective-permute-start.15 = (bf16[3072,512]{1,0:T(8,128)(2,1)}, bf16[3072,512]{1,0:T(8,128)(2,1)}, u32[]{:S(2)}, u32[]{:S(2)}) collective-permute-start(bf16[3072,512]{1,0:T(8,128)(2,1)} %all-gather.9.cloned.1.call-done.u0), channel_id=1, source_target_pairs={{0,4},{4,0},{1,5},{5,1},{2,6},{6,2},{3,7},{7,3},{8,12},{12,8},{9,1... | collective-permute-start | bytes 9437192 | tf_op jit(solution)/shard_map/ppermute | solution.py:466
  492.7 115.1 %collective-permute-start.11 = (bf16[3072,512]{1,0:T(8,128)(2,1)S(1)}, bf16[3072,512]{1,0:T(8,128)(2,1)}, u32[]{:S(2)}, u32[]{:S(2)}) collective-permute-start(bf16[3072,512]{1,0:T(8,128)(2,1)S(1)} %copy-done.44), channel_id=1, source_target_pairs={{0,4},{4,0},{1,5},{5,1},{2,6},{6,2},{3,7},{7,3},{8,12},{12,8},{9,1... | collective-permute-start | bytes 9437192 | tf_op jit(solution)/shard_map/ppermute | solution.py:466
  493.3 114.6 %collective-permute-start.14 = (bf16[3072,512]{1,0:T(8,128)(2,1)}, bf16[3072,512]{1,0:T(8,128)(2,1)}, u32[]{:S(2)}, u32[]{:S(2)}) collective-permute-start(bf16[3072,512]{1,0:T(8,128)(2,1)} %all-gather.9.cloned.1.call-done.u0), channel_id=1, source_target_pairs={{0,16},{16,0},{1,17},{17,1},{2,18},{18,2},{3,19},{19,3},{4,20},{20... | collective-permute-start | bytes 9437192 | tf_op jit(solution)/shard_map/ppermute | solution.py:466
  538.4 135.7 %collective-permute-start.12 = (bf16[3072,512]{1,0:T(8,128)(2,1)}, bf16[3072,512]{1,0:T(8,128)(2,1)}, u32[]{:S(2)}, u32[]{:S(2)}) collective-permute-start(bf16[3072,512]{1,0:T(8,128)(2,1)} %collective-permute-done.10.g1), channel_id=1, source_target_pairs={{0,4},{4,0},{1,5},{5,1},{2,6},{6,2},{3,7},{7,3},{8,12},{12,8},{9,1... | collective-permute-start | bytes 9437192 | tf_op jit(solution)/shard_map/ppermute | solution.py:466
  541.3 132.8 %collective-permute-start.16 = (bf16[3072,512]{1,0:T(8,128)(2,1)}, bf16[3072,512]{1,0:T(8,128)(2,1)}, u32[]{:S(2)}, u32[]{:S(2)}) collective-permute-start(bf16[3072,512]{1,0:T(8,128)(2,1)} %collective-permute-done.15.u2), channel_id=1, source_target_pairs={{0,16},{16,0},{1,17},{17,1},{2,18},{18,2},{3,19},{19,3},{4,20},{20... | collective-permute-start | bytes 9437192 | tf_op jit(solution)/shard_map/ppermute | solution.py:466
  789.3 176.5 %collective-permute-start.43 = (bf16[3072,512]{1,0:T(8,128)(2,1)}, bf16[3072,512]{1,0:T(8,128)(2,1)}, u32[]{:S(2)}, u32[]{:S(2)}) collective-permute-start(bf16[3072,512]{1,0:T(8,128)(2,1)} %convolution_convert_fusion.3), channel_id=1, source_target_pairs={{0,16},{16,0},{1,17},{17,1},{2,18},{18,2},{3,19},{19,3},{4,20},{20... | collective-permute-start | bytes 9437192 | tf_op jit(solution)/shard_map/ppermute | solution.py:466
  799.1 126.8 %collective-permute-start.44 = (bf16[3072,512]{1,0:T(8,128)(2,1)S(1)}, bf16[3072,512]{1,0:T(8,128)(2,1)S(1)}, u32[]{:S(2)}, u32[]{:S(2)}) collective-permute-start(bf16[3072,512]{1,0:T(8,128)(2,1)S(1)} %convolution_convert_fusion.1), channel_id=1, source_target_pairs={{0,16},{16,0},{1,17},{17,1},{2,18},{18,2},{3,19},{19,3},{4,20},{20... | collective-permute-start | bytes 9437192 | tf_op jit(solution)/shard_map/ppermute | solution.py:466
  811.2 215.3 %collective-permute-start.39 = (bf16[3072,512]{1,0:T(8,128)(2,1)}, bf16[3072,512]{1,0:T(8,128)(2,1)}, u32[]{:S(2)}, u32[]{:S(2)}) collective-permute-start(bf16[3072,512]{1,0:T(8,128)(2,1)} %convolution_convert_fusion.6), channel_id=1, source_target_pairs={{0,4},{4,0},{1,5},{5,1},{2,6},{6,2},{3,7},{7,3},{8,12},{12,8},{9,1... | collective-permute-start | bytes 9437192 | tf_op jit(solution)/shard_map/ppermute | solution.py:466
  824.0 244.8 %collective-permute-start.41 = (bf16[3072,512]{1,0:T(8,128)(2,1)}, bf16[3072,512]{1,0:T(8,128)(2,1)}, u32[]{:S(2)}, u32[]{:S(2)}) collective-permute-start(bf16[3072,512]{1,0:T(8,128)(2,1)} %convolution_convert_fusion.5), channel_id=1, source_target_pairs={{0,4},{4,0},{1,5},{5,1},{2,6},{6,2},{3,7},{7,3},{8,12},{12,8},{9,1... | collective-permute-start | bytes 9437192 | tf_op jit(solution)/shard_map/ppermute | solution.py:466
  880.2 162.3 %collective-permute-start.23 = (bf16[1024,2048]{1,0:T(8,128)(2,1)}, bf16[1024,2048]{1,0:T(8,128)(2,1)}, u32[]{:S(2)}, u32[]{:S(2)}) collective-permute-start(bf16[1024,2048]{1,0:T(8,128)(2,1)} %pad_maximum_fusion.5), channel_id=1, source_target_pairs={{0,8},{8,0},{1,9},{9,1},{2,10},{10,2},{3,11},{11,3},{4,12},{12,4},... | collective-permute-start | bytes 12582920 | tf_op jit(solution)/shard_map/ppermute | solution.py:466
  936.0 78.6 %collective-permute-start.45 = (bf16[3072,512]{1,0:T(8,128)(2,1)S(1)}, bf16[3072,512]{1,0:T(8,128)(2,1)S(1)}, u32[]{:S(2)}, u32[]{:S(2)}) collective-permute-start(bf16[3072,512]{1,0:T(8,128)(2,1)S(1)} %fusion.73), channel_id=1, source_target_pairs={{0,4},{4,0},{1,5},{5,1},{2,6},{6,2},{3,7},{7,3},{8,12},{12,8},{9,1... | collective-permute-start | bytes 9437192 | tf_op jit(solution)/shard_map/ppermute | solution.py:466
  1026.4 480.8 %reduce-scatter.10.cloned.1.call-start = ((), (), s32[]{:S(2)}) async-start(), calls=%async_computation.11 | async-start | bytes 3932160 | tf_op jit(solution)/shard_map/reduce_scatter | solution.py:486
  1121.1 399.3 %reduce-scatter.8.cloned.1.call-start = ((), (), s32[]{:S(2)}) async-start(), calls=%async_computation.10 | async-start | bytes 1310720 | tf_op jit(solution)/shard_map/reduce_scatter | solution.py:486
  1183.5 434.9 %reduce-scatter.14.cloned.1.call-start = ((), (), s32[]{:S(2)}) async-start(), calls=%async_computation.13 | async-start | bytes 15728640 | tf_op jit(solution)/shard_map/reduce_scatter | solution.py:486
  1216.5 428.9 %reduce-scatter.6.cloned.1.call-start = ((), (), s32[]{:S(2)}) async-start(), calls=%async_computation.9 | async-start | bytes 2621440 | tf_op jit(solution)/shard_map/reduce_scatter | solution.py:486
  1327.2 82.0 %collective-permute-start.26 = (bf16[2048,512]{1,0:T(8,128)(2,1)}, bf16[2048,512]{1,0:T(8,128)(2,1)S(1)}, u32[]{:S(2)}, u32[]{:S(2)}) collective-permute-start(bf16[2048,512]{1,0:T(8,128)(2,1)} %get-tuple-element.44), channel_id=1, source_target_pairs={{0,4},{4,0},{1,5},{5,1},{2,6},{6,2},{3,7},{7,3},{8,12},{12,8},{9,1... | collective-permute-start | bytes 6291464 | tf_op jit(solution)/shard_map/ppermute | solution.py:466
  1346.7 123.3 %collective-permute-start.21 = (bf16[1024,2048]{1,0:T(8,128)(2,1)}, bf16[1024,2048]{1,0:T(8,128)(2,1)}, u32[]{:S(2)}, u32[]{:S(2)}) collective-permute-start(bf16[1024,2048]{1,0:T(8,128)(2,1)} %fusion.62), channel_id=1, source_target_pairs={{0,8},{8,0},{1,9},{9,1},{2,10},{10,2},{3,11},{11,3},{4,12},{12,4},... | collective-permute-start | bytes 12582920 | tf_op jit(solution)/shard_map/ppermute | solution.py:466
  1506.8 74.1 %collective-permute-start.46 = (bf16[768,256]{1,0:T(8,128)(2,1)S(1)}, bf16[768,256]{1,0:T(8,128)(2,1)S(1)}, u32[]{:S(2)}, u32[]{:S(2)}) collective-permute-start(bf16[768,256]{1,0:T(8,128)(2,1)S(1)} %get-tuple-element.104), channel_id=1, source_target_pairs={{0,8},{8,0},{1,9},{9,1},{2,10},{10,2},{3,11},{11,3},{4,12},{12,4},... | collective-permute-start | bytes 1179656 | tf_op jit(solution)/shard_map/ppermute | solution.py:466
  1508.4 76.1 %collective-permute-start.42 = (bf16[768,256]{1,0:T(8,128)(2,1)S(1)}, bf16[768,256]{1,0:T(8,128)(2,1)S(1)}, u32[]{:S(2)}, u32[]{:S(2)}) collective-permute-start(bf16[768,256]{1,0:T(8,128)(2,1)S(1)} %get-tuple-element.106), channel_id=1, source_target_pairs={{0,8},{8,0},{1,9},{9,1},{2,10},{10,2},{3,11},{11,3},{4,12},{12,4},... | collective-permute-start | bytes 1179656 | tf_op jit(solution)/shard_map/ppermute | solution.py:466
  (85 other events, 2460.5 us)
Sparse Core Ops, SparseCore 0:
  10.2 66.1 all-gather.4
  78.0 62.1 all-gather.6
  141.7 62.1 all-gather.8
  395.5 216.7 all-gather.10
  1026.5 67.2 reduce-scatter.11
  1121.3 67.4 reduce-scatter.9
  1191.1 27.8 reduce-scatter.7
  1221.4 215.1 reduce-scatter.13
  1579.2 65.6 reduce-scatter.5

commit v2 on v0

--- a/solution.py
+++ b/solution.py
@@ -1,8 +1,12 @@
+import functools
 import math
 
 import jax
 import jax.numpy as jnp
 from jax import lax
+from jax.experimental import pallas as pl
+from jax.experimental.pallas import tpu as pltpu
+from jax.sharding import Mesh
 from jax.sharding import PartitionSpec as P
 
 QUERY_HEADS = 16
@@ -248,7 +252,7 @@
     return (q_raw_grad, k_raw_grad, qgain_part, kgain_part)
 
 
-def local(
+def plain_layer(
     tokens,
     cotangent,
     seq_lens,
@@ -406,9 +410,9 @@
     )
 
 
-def solution(mesh):
+def plain_solution(mesh):
     return jax.shard_map(
-        local,
+        plain_layer,
         mesh=mesh,
         in_specs=(
             P(("fsdp", "heads", "tensor"), None),
@@ -444,3 +448,939 @@
         ),
         check_vma=False,
     )
+
+
+VMEM_LIMIT = 56 * 1024 * 1024
+LOG2_E = 1.4426950408889634
+SWAP = ((0, 1), (1, 0))
+ROW_TILE = 1024
+SCALE = HEAD_SIZE ** (-0.5)
+
+
+def dot_t(left, right):
+    return lax.dot_general(
+        left, right, (((1,), (1,)), ((), ())), preferred_element_type=jnp.float32
+    )
+
+
+def swap(array, axis):
+    return lax.ppermute(array, axis, SWAP)
+
+
+def pick(first, second, index):
+    return jnp.where(index == 0, first, second)
+
+
+def join(mine, other, index, axis):
+    return pick(
+        jnp.concatenate([mine, other], axis=axis),
+        jnp.concatenate([other, mine], axis=axis),
+        index,
+    )
+
+
+def gather_z(array):
+    return lax.all_gather(array, "z", axis=0, tiled=True)
+
+
+def scatter_z(array):
+    return lax.psum_scatter(array, "z", scatter_dimension=0, tiled=True)
+
+
+def after(array, *done):
+    return lax.optimization_barrier((array, *done))[0]
+
+
+def sync(*arrays):
+    return lax.optimization_barrier(arrays)
+
+
+def to_core(array, core):
+    half = array.shape[0] // 2
+    first, second = array[:half], array[half:]
+    other = swap(pick(second, first, core), "c")
+    return join(pick(first, second, core), other, core, 1)
+
+
+def from_core(array, core, count):
+    half = array.shape[1] // 2
+    span = array.shape[0] // count
+    first, second = array[:, :half], array[:, half:]
+    other = swap(pick(second, first, core), "c").reshape(count, span, half)
+    mine = pick(first, second, core).reshape(count, span, half)
+    return join(mine, other, core, 1).reshape(-1, half)
+
+
+def call(kernel, inputs, in_specs, out_specs, out_shape, grid, after=(), prefetch=None, **more):
+    lead = 0 if prefetch is None else 1
+    count, extra = lead + len(inputs), len(after)
+
+    def body(*refs):
+        kernel(*refs[:count], *refs[count + extra :])
+
+    if prefetch is not None:
+        prefetched, inputs = [prefetch], list(inputs)
+    else:
+        prefetched, inputs = [], list(inputs)
+    scratch = more.pop("scratch_shapes", ())
+    return pl.pallas_call(
+        body,
+        grid_spec=pltpu.PrefetchScalarGridSpec(
+            num_scalar_prefetch=lead,
+            grid=grid,
+            in_specs=list(in_specs) + [pl.BlockSpec(memory_space=pl.ANY)] * extra,
+            out_specs=out_specs,
+            scratch_shapes=scratch,
+        ),
+        out_shape=out_shape,
+        compiler_params=pltpu.CompilerParams(vmem_limit_bytes=VMEM_LIMIT),
+        cost_estimate=pl.CostEstimate(flops=1000, bytes_accessed=1000, transcendentals=0),
+        **more,
+    )(*prefetched, *inputs, *after)
+
+
+def reorder_kernel(order_ref, in_ref, out_ref):
+    out_ref[...] = in_ref[...]
+
+
+def reorder(array, order, after=()):
+    rows, width = array.shape
+    parts = order.shape[0]
+    return call(
+        reorder_kernel,
+        [array],
+        [pl.BlockSpec((rows, width // parts), lambda i, o: (0, o[i]))],
+        pl.BlockSpec((rows, width // parts), lambda i, o: (0, i)),
+        jax.ShapeDtypeStruct(array.shape, array.dtype),
+        (parts,),
+        after,
+        order,
+        name="reorder",
+    )
+
+
+def lane_mean(value):
+    ones = jnp.full((HEAD_SIZE, HEAD_SIZE), 1.0 / HEAD_SIZE, jnp.bfloat16)
+    high = value.astype(jnp.bfloat16)
+    low = (value - high.astype(jnp.float32)).astype(jnp.bfloat16)
+    return matrix_product(high, ones) + matrix_product(low, ones)
+
+
+def heads_kernel(count, raw_ref, cos_ref, sin_ref, gain_ref, out_ref):
+    raw = raw_ref[:, :HEAD_SIZE]
+    value = raw * lax.rsqrt(lane_mean(raw * raw) + EPS_NORM) * gain_ref[...]
+    out_ref[:, :HEAD_SIZE] = (
+        value * cos_ref[...] + pltpu.roll(value, HEAD_SIZE // 2, 1) * sin_ref[...]
+    ).astype(jnp.bfloat16)
+    if count == 2:
+        out_ref[:, HEAD_SIZE:] = raw_ref[:, HEAD_SIZE:].astype(jnp.bfloat16)
+
+
+def make_heads(raw, cos_tab, sin_tab, gain, count, first, rows, after=()):
+    width = raw.shape[1]
+    skip = first // ROW_TILE
+    table = pl.BlockSpec((ROW_TILE, HEAD_SIZE), lambda i, r: (i + skip, 0))
+    return call(
+        functools.partial(heads_kernel, count),
+        [raw, cos_tab, sin_tab, gain[None, :]],
+        [
+            pl.BlockSpec((ROW_TILE, count * HEAD_SIZE), lambda i, r: (i + skip, r)),
+            table,
+            table,
+            pl.BlockSpec((1, HEAD_SIZE), lambda i, r: (0, 0)),
+        ],
+        pl.BlockSpec((ROW_TILE, count * HEAD_SIZE), lambda i, r: (i, r)),
+        jax.ShapeDtypeStruct((rows, width), jnp.bfloat16),
+        (rows // ROW_TILE, width // (count * HEAD_SIZE)),
+        after,
+        name="make_heads",
+    )
+
+
+def heads_back_kernel(count, raw_ref, cos_ref, sin_ref, gain_ref, *rest):
+    *up_refs, out_ref, sum_ref = rest
+
+    @pl.when((pl.program_id(0) == 0) & (pl.program_id(1) == 0))
+    def _():
+        sum_ref[...] = jnp.zeros_like(sum_ref)
+
+    raw = raw_ref[:, :HEAD_SIZE]
+    upstream = up_refs[0][...].astype(jnp.float32)
+    for ref in up_refs[1:]:
+        upstream = upstream + ref[...].astype(jnp.float32)
+    if count == 2:
+        out_ref[:, HEAD_SIZE:] = upstream[:, HEAD_SIZE:].astype(jnp.bfloat16)
+        upstream = upstream[:, :HEAD_SIZE]
+    turned = upstream * cos_ref[...] - pltpu.roll(upstream, HEAD_SIZE // 2, 1) * sin_ref[...]
+    scale = lax.rsqrt(lane_mean(raw * raw) + EPS_NORM)
+    hat = raw * scale
+    weighted = turned * gain_ref[...]
+    out_ref[:, :HEAD_SIZE] = (scale * (weighted - hat * lane_mean(hat * weighted))).astype(
+        jnp.bfloat16
+    )
+    sum_ref[0:1, :] += jnp.sum(turned * hat, axis=0, keepdims=True)
+
+
+def heads_return(raw, upstream, far, cos_tab, sin_tab, gain, count, after=()):
+    rows, width = raw.shape
+    heads = width // (count * HEAD_SIZE)
+    table = pl.BlockSpec((ROW_TILE, HEAD_SIZE), lambda i, r: (i, 0))
+    one = pl.BlockSpec((ROW_TILE, count * HEAD_SIZE), lambda i, r: (i, r))
+    across = pl.BlockSpec(
+        (ROW_TILE, count * HEAD_SIZE), lambda i, r: (i, (r + heads // 2) % heads)
+    )
+    return call(
+        functools.partial(heads_back_kernel, count),
+        [raw, cos_tab, sin_tab, gain[None, :], upstream] + far,
+        [one, table, table, pl.BlockSpec((1, HEAD_SIZE), lambda i, r: (0, 0)), one]
+        + [across] * len(far),
+        [one, pl.BlockSpec((8, HEAD_SIZE), lambda i, r: (0, 0))],
+        [
+            jax.ShapeDtypeStruct((rows, width), jnp.bfloat16),
+            jax.ShapeDtypeStruct((8, HEAD_SIZE), jnp.float32),
+        ],
+        (rows // ROW_TILE, heads),
+        after,
+        name="heads_return",
+    )
+
+
+def stack_heads(block):
+    return jnp.concatenate([block[:, :HEAD_SIZE], block[:, HEAD_SIZE:]], axis=0)
+
+
+def key_bias(first_key, pair, parity):
+    cols = lax.broadcasted_iota(jnp.int32, (1, 2 * BLK), 1)
+    block = 2 * pair + jnp.where(cols < BLK, parity, 1 - parity)
+    return jnp.where(block >= first_key, 0.0, NEG_FILL)
+
+
+def last_bias(first_key, pair, parity):
+    rows = lax.broadcasted_iota(jnp.int32, (2 * BLK, 2 * BLK), 0)
+    cols = lax.broadcasted_iota(jnp.int32, (2 * BLK, 2 * BLK), 1)
+    far = (parity == 1) & (2 * pair >= first_key)
+    own = lax.rem(cols, BLK) <= lax.rem(rows, BLK)
+    far_bias = jnp.where(far, 0.0, NEG_FILL)
+    return jnp.where(cols < BLK, jnp.where(own, 0.0, NEG_FILL), far_bias)
+
+
+def pair_of(own_ref, far_ref, m, first):
+    at = pl.ds(pl.multiple_of(m * BLK, BLK), BLK)
+    lanes = slice(first, first + HEAD_SIZE)
+    return jnp.concatenate([own_ref[at, lanes], far_ref[at, lanes]], axis=0)
+
+
+def attend_kernel(group, info_ref, q_ref, own_ref, far_ref, o_ref, l_ref):
+    blocks = q_ref.shape[0] // BLK
+    parity = info_ref[group, blocks]
+
+    def one_block(j, _):
+        first_key = info_ref[group, j]
+        rows = pl.ds(pl.multiple_of(j * BLK, BLK), BLK)
+        query = stack_heads(q_ref[rows, :])
+
+        def step(m, bias, carry):
+            total, acc = carry
+            score = dot_t(query, pair_of(own_ref, far_ref, m, 0))
+            expo = jnp.exp2(score * (SCALE * LOG2_E) + bias)
+            total = total + jnp.sum(expo, axis=1, keepdims=True)
+            value = pair_of(own_ref, far_ref, m, HEAD_SIZE)
+            acc = acc + matrix_product(expo.astype(jnp.bfloat16), value)
+            return total, acc
+
+        carry = step(
+            j,
+            last_bias(first_key, j, parity),
+            (jnp.zeros((2 * BLK, 1), jnp.float32), jnp.zeros((2 * BLK, HEAD_SIZE), jnp.float32)),
+        )
+        total, acc = lax.fori_loop(
+            lax.div(first_key, 2),
+            j,
+            lambda m, c: step(m, key_bias(first_key, m, parity), c),
+            carry,
+        )
+        out = (acc / total).astype(jnp.bfloat16)
+        o_ref[rows, :HEAD_SIZE] = out[:BLK]
+        o_ref[rows, HEAD_SIZE:] = out[BLK:]
+        lane = lax.broadcasted_iota(jnp.int32, (BLK, HEAD_SIZE), 1)
+        l_ref[rows, :] = jnp.where(lane == 0, total[:BLK], total[BLK:])
+        return 0
+
+    lax.fori_loop(0, blocks, one_block, 0)
+
+
+def attend(group, info, query, own, far, after=()):
+    rows = query.shape[0] // 2
+    count = query.shape[1] // (2 * HEAD_SIZE)
+    wide = pl.BlockSpec((rows, 2 * HEAD_SIZE), lambda r, s: (group, r))
+    here = pl.BlockSpec((rows, 2 * HEAD_SIZE), lambda r, s: (0, r))
+    return call(
+        functools.partial(attend_kernel, group),
+        [query, own, far],
+        [wide, here, pl.BlockSpec((rows, 2 * HEAD_SIZE), lambda r, s: (0, (r + 2) % 4))],
+        [here, pl.BlockSpec((rows, HEAD_SIZE), lambda r, s: (0, r))],
+        [
+            jax.ShapeDtypeStruct((rows, query.shape[1]), jnp.bfloat16),
+            jax.ShapeDtypeStruct((rows, count * HEAD_SIZE), jnp.float32),
+        ],
+        (count,),
+        after,
+        info,
+        name="attend",
+    )
+
+
+def attend_back_kernel(
+    group,
+    info_ref,
+    q_ref,
+    do_ref,
+    o_ref,
+    l_ref,
+    own_ref,
+    far_ref,
+    dq_ref,
+    down_ref,
+    dfar_ref,
+    kacc_ref,
+    vacc_ref,
+):
+    blocks = q_ref.shape[0] // BLK
+    parity = info_ref[group, blocks]
+    kacc_ref[...] = jnp.zeros_like(kacc_ref)
+    vacc_ref[...] = jnp.zeros_like(vacc_ref)
+
+    def one_block(j, _):
+        first_key = info_ref[group, j]
+        rows = pl.ds(pl.multiple_of(j * BLK, BLK), BLK)
+        query = stack_heads(q_ref[rows, :])
+        attn = stack_heads(o_ref[rows, :]).astype(jnp.float32)
+        grad = stack_heads(do_ref[rows, :]).astype(jnp.float32)
+        total = jnp.concatenate([l_ref[rows, 0:1], l_ref[rows, 1:2]], axis=0)
+        grad_b = (grad / total).astype(jnp.bfloat16)
+        inner = jnp.sum(grad_b.astype(jnp.float32) * attn, axis=1, keepdims=True)
+
+        def step(m, bias, dq):
+            at = pl.ds(pl.multiple_of(m * BLK, BLK), BLK)
+            key = pair_of(own_ref, far_ref, m, 0)
+            expo = jnp.exp2(dot_t(query, key) * (SCALE * LOG2_E) + bias)
+            d_prob = dot_t(grad_b, pair_of(own_ref, far_ref, m, HEAD_SIZE))
+            d_score = (expo * (d_prob - inner)).astype(jnp.bfloat16)
+            d_key = dot_rows(d_score, query)
+            d_value = dot_rows(expo.astype(jnp.bfloat16), grad_b)
+            kacc_ref[0, at, :] += d_key[:BLK]
+            kacc_ref[1, at, :] += d_key[BLK:]
+            vacc_ref[0, at, :] += d_value[:BLK]
+            vacc_ref[1, at, :] += d_value[BLK:]
+            return dq + matrix_product(d_score, key)
+
+        dq = step(
+            j, last_bias(first_key, j, parity), jnp.zeros((2 * BLK, HEAD_SIZE), jnp.float32)
+        )
+        dq = lax.fori_loop(
+            lax.div(first_key, 2),
+            j,
+            lambda m, c: step(m, key_bias(first_key, m, parity), c),
+            dq,
+        )
+        dq = (dq * SCALE).astype(jnp.bfloat16)
+        dq_ref[rows, :HEAD_SIZE] = dq[:BLK]
+        dq_ref[rows, HEAD_SIZE:] = dq[BLK:]
+        return 0
+
+    lax.fori_loop(0, blocks, one_block, 0)
+    for half, ref in enumerate((down_ref, dfar_ref)):
+        ref[:, :HEAD_SIZE] = (kacc_ref[half] * SCALE).astype(jnp.bfloat16)
+        ref[:, HEAD_SIZE:] = vacc_ref[half].astype(jnp.bfloat16)
+
+
+def attend_back(group, info, query, d_attn, attn, total, own, far, after=()):
+    rows = query.shape[0] // 2
+    count = query.shape[1] // (2 * HEAD_SIZE)
+    wide = pl.BlockSpec((rows, 2 * HEAD_SIZE), lambda r, s: (group, r))
+    here = pl.BlockSpec((rows, 2 * HEAD_SIZE), lambda r, s: (0, r))
+    shape = jax.ShapeDtypeStruct((rows, query.shape[1]), jnp.bfloat16)
+    return call(
+        functools.partial(attend_back_kernel, group),
+        [query, d_attn, attn, total, own, far],
+        [
+            wide,
+            here,
+            here,
+            pl.BlockSpec((rows, HEAD_SIZE), lambda r, s: (0, r)),
+            here,
+            pl.BlockSpec((rows, 2 * HEAD_SIZE), lambda r, s: (0, (r + 2) % 4)),
+        ],
+        [here] * 3,
+        [shape] * 3,
+        (count,),
+        after,
+        info,
+        scratch_shapes=[
+            pltpu.VMEM((2, rows, HEAD_SIZE), jnp.float32),
+            pltpu.VMEM((2, rows, HEAD_SIZE), jnp.float32),
+        ],
+        name="attend_back",
+    )
+
+
+HIDDEN_TILE = 512
+ROW_STEP = 512
+
+
+def ffn_up_kernel(x_ref, g0, g1, g2, g3, u0, u1, u2, u3, act_ref, dgate_ref, silu_ref):
+    gate_w = jnp.concatenate([g0[...], g1[...], g2[...], g3[...]], axis=1).T
+    up_w = jnp.concatenate([u0[...], u1[...], u2[...], u3[...]], axis=1).T
+    for first in range(0, x_ref.shape[0], ROW_STEP):
+        rows = slice(first, first + ROW_STEP)
+        gate = matrix_product(x_ref[rows, :], gate_w)
+        upper = matrix_product(x_ref[rows, :], up_w)
+        sig = 0.5 * jnp.tanh(0.5 * gate) + 0.5
+        silu = gate * sig
+        act_ref[rows, :] = (silu * upper).astype(jnp.bfloat16)
+        silu_ref[rows, :] = silu.astype(jnp.bfloat16)
+        dgate_ref[rows, :] = (upper * (sig + silu * (1.0 - sig))).astype(jnp.bfloat16)
+
+
+def ffn_up(x, gates, ups, after=()):
+    rows, width = x.shape
+    hidden, depth = gates[0].shape
+    weight = pl.BlockSpec((HIDDEN_TILE, depth), lambda j: (j, 0))
+    out = pl.BlockSpec((rows, HIDDEN_TILE), lambda j: (0, j))
+    shape = jax.ShapeDtypeStruct((rows, hidden), jnp.bfloat16)
+    return call(
+        ffn_up_kernel,
+        [x, *gates, *ups],
+        [pl.BlockSpec((rows, width), lambda j: (0, 0))] + [weight] * 8,
+        [out] * 3,
+        [shape] * 3,
+        (hidden // HIDDEN_TILE,),
+        after,
+        name="ffn_up",
+    )
+
+
+def ffn_back_kernel(dy_ref, wa_ref, wb_ref, dgate_ref, silu_ref, gate_ref, up_ref):
+    weight = jnp.concatenate([wa_ref[...], wb_ref[...]], axis=1).T
+    for first in range(0, dy_ref.shape[0], ROW_STEP):
+        rows = slice(first, first + ROW_STEP)
+        d_act = matrix_product(dy_ref[rows, :], weight)
+        gate_ref[rows, :] = (d_act * dgate_ref[rows, :].astype(jnp.float32)).astype(jnp.bfloat16)
+        up_ref[rows, :] = (d_act * silu_ref[rows, :].astype(jnp.float32)).astype(jnp.bfloat16)
+
+
+def ffn_back(dy, downs, dgate, silu, after=()):
+    rows, width = dy.shape
+    hidden = downs[0].shape[0]
+    out = pl.BlockSpec((rows, HIDDEN_TILE), lambda j: (0, j))
+    shape = jax.ShapeDtypeStruct((rows, hidden), jnp.bfloat16)
+    return call(
+        ffn_back_kernel,
+        [dy, *downs, dgate, silu],
+        [
+            pl.BlockSpec((rows, width), lambda j: (0, 0)),
+            pl.BlockSpec((HIDDEN_TILE, width // 2), lambda j: (j, 0)),
+            pl.BlockSpec((HIDDEN_TILE, width // 2), lambda j: (j, 0)),
+            out,
+            out,
+        ],
+        [out] * 2,
+        [shape] * 2,
+        (hidden // HIDDEN_TILE,),
+        after,
+        name="ffn_back",
+    )
+
+
+def weight_grad_kernel(left_ref, right_ref, *out_refs):
+    left = left_ref[...].T
+    span = out_refs[0].shape[1]
+    for i, out_ref in enumerate(out_refs):
+        right = right_ref[:, i * span : (i + 1) * span]
+        out_ref[...] = matrix_product(left, right).astype(jnp.bfloat16)
+
+
+def weight_grad(left, right, first, last, count, after=()):
+    rows, hidden = left.shape
+    width = last - first
+    shape = jax.ShapeDtypeStruct((hidden, width // count), jnp.bfloat16)
+    return call(
+        weight_grad_kernel,
+        [left, right],
+        [
+            pl.BlockSpec((rows, HIDDEN_TILE), lambda j: (0, j)),
+            pl.BlockSpec((rows, width), lambda j: (0, first // width)),
+        ],
+        [pl.BlockSpec((HIDDEN_TILE, width // count), lambda j: (j, 0))] * count,
+        [shape] * count,
+        (hidden // HIDDEN_TILE,),
+        after,
+        name="weight_grad",
+    )
+
+
+def to_model_kernel(terms, order_ref, *refs):
+    left_refs, weight_refs = refs[:terms], refs[terms:-2]
+    out_ref, acc_ref = refs[-2:]
+    pieces = len(weight_refs) // terms
+    span = weight_refs[0].shape[1]
+
+    @pl.when(pl.program_id(0) == 0)
+    def _():
+        acc_ref[...] = jnp.zeros_like(acc_ref)
+
+    left = jnp.concatenate([ref[...] for ref in left_refs], axis=1)
+    for i in range(pieces):
+        weight = jnp.concatenate([weight_refs[t * pieces + i][...] for t in range(terms)], axis=0)
+        acc_ref[:, i * span : (i + 1) * span] += matrix_product(left, weight)
+
+    @pl.when(pl.program_id(0) == pl.num_programs(0) - 1)
+    def _():
+        block = acc_ref.shape[1] // order_ref.shape[0]
+        for i in range(order_ref.shape[0]):
+            at = pl.ds(pl.multiple_of(order_ref[i] * block, block), block)
+            out_ref[:, at] = acc_ref[:, i * block : (i + 1) * block].astype(jnp.bfloat16)
+
+
+def to_model(lefts, weights, order, half, rows, after=()):
+    hidden = lefts[0].shape[1]
+    span, pieces = weights[0][0].shape[1], len(weights[0])
+    return call(
+        functools.partial(to_model_kernel, len(lefts)),
+        [*lefts, *(w for group in weights for w in group)],
+        [pl.BlockSpec((rows, HIDDEN_TILE), lambda j, o: (half, j))] * len(lefts)
+        + [pl.BlockSpec((HIDDEN_TILE, span), lambda j, o: (j, 0))] * (len(lefts) * pieces),
+        pl.BlockSpec((rows, span * pieces), lambda j, o: (0, 0)),
+        jax.ShapeDtypeStruct((rows, span * pieces), jnp.bfloat16),
+        (hidden // HIDDEN_TILE,),
+        after,
+        order,
+        scratch_shapes=[pltpu.VMEM((rows, span * pieces), jnp.float32)],
+        name="to_model",
+    )
+
+
+def to_hidden_kernel(x_ref, weight_ref, out_ref):
+    out_ref[...] = matrix_product(x_ref[...], weight_ref[...].T).astype(jnp.bfloat16)
+
+
+def to_hidden(x, weight, after=()):
+    rows, width = x.shape
+    hidden = weight.shape[0]
+    return call(
+        to_hidden_kernel,
+        [x, weight],
+        [
+            pl.BlockSpec((rows, width), lambda j: (0, 0)),
+            pl.BlockSpec((HIDDEN_TILE, width), lambda j: (j, 0)),
+        ],
+        pl.BlockSpec((rows, HIDDEN_TILE), lambda j: (0, j)),
+        jax.ShapeDtypeStruct((rows, hidden), jnp.bfloat16),
+        (hidden // HIDDEN_TILE,),
+        after,
+        name="to_hidden",
+    )
+
+
+NORM_TILE = 128
+
+
+def resid_kernel(order_ref, tokens_ref, own_ref, there_ref, gain_ref, resid_ref, normed_ref):
+    resid = (
+        tokens_ref[...].astype(jnp.float32)
+        + own_ref[...].astype(jnp.float32)
+        + there_ref[...].astype(jnp.float32)
+    )
+    resid_ref[...] = resid
+    scale = lax.rsqrt(jnp.mean(resid * resid, axis=-1, keepdims=True) + EPS_NORM)
+    normed = (resid * scale * gain_ref[...]).astype(jnp.bfloat16)
+    block = normed.shape[1] // order_ref.shape[0]
+    for i in range(order_ref.shape[0]):
+        at = pl.ds(pl.multiple_of(order_ref[i] * block, block), block)
+        normed_ref[:, at] = normed[:, i * block : (i + 1) * block]
+
+
+def resid_norm(tokens, own, there, gain, order, after=()):
+    rows, width = tokens.shape
+    tile = pl.BlockSpec((NORM_TILE, width), lambda i, o: (i, 0))
+    return call(
+        resid_kernel,
+        [tokens, own, there, gain[None, :]],
+        [tile, tile, tile, pl.BlockSpec((1, width), lambda i, o: (0, 0))],
+        [tile, tile],
+        [
+            jax.ShapeDtypeStruct((rows, width), jnp.float32),
+            jax.ShapeDtypeStruct((rows, width), jnp.bfloat16),
+        ],
+        (rows // NORM_TILE,),
+        after,
+        order,
+        name="resid_norm",
+    )
+
+
+def norm_back_kernel(value_ref, base_ref, own_ref, there_ref, gain_ref, *out_refs):
+    *grad_refs, sum_ref = out_refs
+
+    @pl.when(pl.program_id(0) == 0)
+    def _():
+        sum_ref[...] = jnp.zeros_like(sum_ref)
+
+    value = value_ref[...].astype(jnp.float32)
+    upstream = own_ref[...].astype(jnp.float32) + there_ref[...].astype(jnp.float32)
+    scale = lax.rsqrt(jnp.mean(value * value, axis=-1, keepdims=True) + EPS_NORM)
+    hat = value * scale
+    weighted = upstream * gain_ref[...]
+    inner = jnp.mean(hat * weighted, axis=-1, keepdims=True)
+    grad = base_ref[...].astype(jnp.float32) + scale * (weighted - hat * inner)
+    for ref in grad_refs:
+        ref[...] = grad.astype(ref.dtype)
+    sum_ref[0:1, :] += jnp.sum(upstream * hat, axis=0, keepdims=True)
+
+
+def norm_return(value, base, own, there, gain, dtypes, after=()):
+    rows, width = value.shape
+    tile = pl.BlockSpec((NORM_TILE, width), lambda i: (i, 0))
+    return call(
+        norm_back_kernel,
+        [value, base, own, there, gain[None, :]],
+        [tile, tile, tile, tile, pl.BlockSpec((1, width), lambda i: (0, 0))],
+        [tile] * len(dtypes) + [pl.BlockSpec((8, width), lambda i: (0, 0))],
+        [jax.ShapeDtypeStruct((rows, width), d) for d in dtypes]
+        + [jax.ShapeDtypeStruct((8, width), jnp.float32)],
+        (rows // NORM_TILE,),
+        after,
+        name="norm_return",
+    )
+
+
+def block_info(lengths, positions, first):
+    count = (lengths + BLK - 1) // BLK
+    ends = jnp.cumsum(count)
+    starts = jnp.concatenate([jnp.zeros((1,), jnp.int32), ends])
+    own = lax.dynamic_slice_in_dim(positions, first, 8)
+    first_keys = jnp.max(jnp.where(starts[None, :] <= own[:, None], starts[None, :], 0), axis=1)
+    limits = jnp.concatenate([lengths, jnp.zeros((1,), jnp.int32)])
+    seq = jnp.sum((own[:, None] >= ends[None, :]).astype(jnp.int32), axis=1)
+    limit = jnp.sum(jnp.where(seq[:, None] == jnp.arange(4)[None, :], limits[None, :], 0), axis=1)
+    pos = ((own - first_keys)[:, None] * BLK + jnp.arange(BLK)[None, :]).astype(jnp.int32)
+    valid = pos < limit[:, None]
+    return first_keys, own, pos.reshape(-1), valid.reshape(-1)
+
+
+def chip_layer(
+    tokens,
+    cotangent,
+    seq_lens,
+    block_pos,
+    norm1_gain,
+    w_query,
+    key_matrix,
+    value_matrix,
+    query_gain,
+    key_gain,
+    w_out,
+    norm2_gain,
+    w_gate,
+    w_up,
+    w_down,
+):
+    xi, core, yi = lax.axis_index("x"), lax.axis_index("c"), lax.axis_index("y")
+    rows, width = tokens.shape
+    bf16, f32 = jnp.bfloat16, jnp.float32
+    half, fourth = width // 2, width // 4
+
+    q_in, k_in = w_query.shape[1], key_matrix.shape[1]
+    down_0 = to_core(w_down, core)
+    down_x, down_y = swap(down_0, "x"), swap(down_0, "y")
+    down_c = swap(down_x, "y")
+    qkv_0 = gather_z(jnp.concatenate([w_query.T, key_matrix.T, value_matrix.T], axis=0))
+    gate_0 = gather_z(to_core(after(w_gate, down_0).T, core))
+    out_0 = gather_z(w_out)
+    up_0 = gather_z(to_core(after(w_up, down_0).T, core))
+    down_w = [
+        gather_z(jnp.concatenate([down_0, down_x], axis=1)),
+        gather_z(jnp.concatenate([down_y, down_c], axis=1)),
+    ]
+    qkv_start = after(qkv_0, down_x, down_y, down_c)
+    qkv_x, qkv_y = swap(qkv_start, "x"), swap(qkv_start, "y")
+    middle = qkv_0.shape[0] // 2
+    qkv_y_top, qkv_x_low, _, _ = lax.optimization_barrier(
+        (qkv_y[:middle], qkv_x[middle:], qkv_x, qkv_y)
+    )
+    qkv_c = jnp.concatenate([swap(qkv_y_top, "x"), swap(qkv_x_low, "y")], axis=0)
+    qkv_p = [
+        a.reshape(4, q_in + 2 * k_in, width) for a in (qkv_0, qkv_x, qkv_y, qkv_c)
+    ]
+    q_w = jnp.concatenate([a[:, :q_in].reshape(-1, width) for a in qkv_p], axis=0)
+    kv_w = jnp.concatenate(
+        [
+            part.reshape(-1, width)
+            for a in qkv_p
+            for part in (a[:, q_in : q_in + k_in], a[:, q_in + k_in :])
+        ],
+        axis=0,
+    )
+    split = gate_0.shape[0] // 2
+    gate_send = after(gate_0, qkv_c)
+    gate_x, gate_y = swap(gate_send, "x"), swap(gate_send, "y")
+    out_send = after(out_0, qkv_c)
+    out_x, out_y = swap(out_send, "x"), swap(out_send, "y")
+
+    lengths_here = jnp.concatenate([seq_lens[0], block_pos[0]]).astype(f32)
+    lengths_there = swap(lengths_here[None, :], "c")[0].astype(jnp.int32)
+    first_own = yi * 8
+    keys_here, at_here, pos_here, valid_here = block_info(seq_lens[0], block_pos[0], first_own)
+    keys_there, at_there, pos_there, _ = block_info(
+        lengths_there[:3], lengths_there[3:], first_own
+    )
+    info = jnp.stack(
+        [
+            jnp.concatenate([keys_here, at_here[:1]]),
+            jnp.concatenate([keys_there, at_there[:1]]),
+        ]
+    ).astype(jnp.int32)
+    freq = jnp.exp(
+        jnp.arange(HEAD_SIZE // 2, dtype=f32) * (-2.0 * math.log(ROPE_BASE) / HEAD_SIZE)
+    )
+    angles = jnp.concatenate([pos_here, pos_there]).astype(f32)[:, None] * freq[None, :]
+    cos_half, sin_half = jnp.cos(angles), jnp.sin(angles)
+    cos_tab = jnp.concatenate([cos_half, cos_half], axis=1)
+    sin_tab = jnp.concatenate([-sin_half, sin_half], axis=1)
+    valid = valid_here.astype(f32)[:, None]
+
+    blocks = jnp.arange(8)
+    ry, rx, rc = blocks // 4, (blocks // 2) % 2, blocks % 2
+    order = ((rx ^ xi) * 4 + rc * 2 + (ry ^ yi)).astype(jnp.int32)
+    nx, nc, ny = blocks // 4, (blocks // 2) % 2, blocks % 2
+    order_back = ((ny ^ yi) * 4 + (nx ^ xi) * 2 + nc).astype(jnp.int32)
+
+    def both(own):
+        return jnp.concatenate([own, swap(own, "c")], axis=0)
+
+    inputs = tokens.astype(f32)
+    first_normed, scale1 = rms_parts(inputs, norm1_gain)
+    normed1 = both(first_normed.astype(bf16))
+    dy_own = (valid * cotangent.astype(f32)).astype(bf16)
+    dy = both(reorder(dy_own, order))
+
+    q_raw = dot_t(normed1, q_w)
+    query = make_heads(q_raw, cos_tab, sin_tab, query_gain, 1, 0, 2 * rows)
+    kv_raw = dot_t(after(normed1, query), kv_w)
+    kv0 = make_heads(kv_raw, cos_tab, sin_tab, key_gain, 2, 0, rows)
+    kv1 = make_heads(kv_raw, cos_tab, sin_tab, key_gain, 2, rows, rows, [kv0])
+    kv0, kv1, gate_x, gate_y, out_x, out_y, up_0 = sync(
+        kv0, kv1, gate_x, gate_y, out_x, out_y, up_0
+    )
+    kv_far0 = swap(kv0, "y")
+    kv_far1 = swap(after(kv1, kv_far0), "y")
+    out_c = swap(out_y, "x")
+    up_x = swap(up_0, "x")
+    attn0, totals0 = attend(0, info, query, kv0, kv_far0, [dy])
+    kv_far1, attn0, up_0, up_x, gate_y, out_c = sync(kv_far1, attn0, up_0, up_x, gate_y, out_c)
+    out_w = jnp.concatenate([out_0, out_x, out_y, out_c], axis=0)
+    up_y, gate_c = swap(up_0, "y"), swap(gate_y, "x")
+    attn1, totals1 = attend(1, info, query, kv1, kv_far1)
+    same = jnp.arange(8, dtype=jnp.int32)
+    out_term = to_model([attn1], [[out_w]], same, 0, rows)
+    out_there = swap(out_term, "c")
+    out_here = to_model([attn0], [[out_w]], same, 0, rows, [out_term])
+    resid, normed2_own = resid_norm(
+        tokens, out_here, out_there, norm2_gain, order_back, [down_w[0]]
+    )
+    normed2_b = both(normed2_own)
+    up_y_top, up_x_low, *_ = sync(up_y[:split], up_x[split:], up_y, gate_c, normed2_own)
+    up_c = jnp.concatenate([swap(up_y_top, "x"), swap(up_x_low, "y")], axis=0)
+    gate_w, up_w = [gate_0, gate_x, gate_y, gate_c], [up_0, up_x, up_y, up_c]
+    act, dgate, silu = ffn_up(normed2_b, gate_w, up_w, [dy])
+
+    def stacked(first, second):
+        return jnp.concatenate([first, second], axis=0)
+
+    def corner_start(corner):
+        span = corner.shape[0] // 2
+        return swap(corner[:span], "x"), swap(corner[span:], "y")
+
+    def corner_add(along_x, along_y, from_x, from_y):
+        span = from_x.shape[0]
+        return (
+            stacked(along_x[:span], along_x[span:] + from_y),
+            stacked(along_y[:span] + from_x, along_y[span:]),
+        )
+
+    (down_first,) = weight_grad(act, dy, 0, half, 1)
+    (down_second,) = weight_grad(act, dy, half, width, 1, [down_first])
+    down_a, down_b = scatter_z(down_first), scatter_z(down_second)
+    gate_grad, up_grad = ffn_back(dy, down_w, dgate, silu, [down_second])
+    g_own, g_x, g_y, g_c = weight_grad(gate_grad, normed2_b, 0, width, 4)
+    g_from = corner_start(g_c)
+    u_own, u_x, u_y, u_c = weight_grad(up_grad, normed2_b, 0, width, 4, [g_own])
+    g_x, g_y, _ = sync(*corner_add(g_x, g_y, *g_from), u_own)
+    got_gx, got_gy = swap(g_x, "x"), swap(g_y, "y")
+    there = to_model([gate_grad, up_grad], [gate_w, up_w], order, 1, rows, [g_x, g_y, down_a])
+    normed2_there = swap(there, "c")
+    normed2_own = to_model([gate_grad, up_grad], [gate_w, up_w], order, 0, rows, [there])
+    g_own, got_gx, got_gy, normed2_own, u_c = sync(g_own, got_gx, got_gy, normed2_own, u_c)
+    gate_sum = scatter_z(g_own + got_gx + got_gy)
+    u_from = corner_start(u_c)
+    resid_grad, resid_here, gain2_sum = norm_return(
+        resid, dy_own, normed2_own, normed2_there, norm2_gain, (f32, bf16)
+    )
+    resid_there = swap(resid_here, "c")
+    mixed_term = to_model([act], [down_w], order, 1, rows, [resid_here])
+    mixed_there = swap(mixed_term, "c")
+    resid_here, mixed_term, down_b, *u_from = sync(resid_here, mixed_term, down_b, *u_from)
+    u_x, u_y = corner_add(u_x, u_y, *u_from)
+    d_own, d_x = down_a[:, :fourth], down_a[:, fourth:]
+    d_y, d_c = down_b[:, :fourth], down_b[:, fourth:]
+    resid_here, u_x, u_y, d_c = sync(resid_here, u_x, u_y, d_c)
+    got_ux, got_uy = swap(u_x, "x"), swap(u_y, "y")
+    got_dc = swap(d_c, "x")
+
+    d_attn0 = to_hidden(resid_here, out_w)
+    dq0, dkv0, dkv0_far = attend_back(0, info, query, d_attn0, attn0, totals0, kv0, kv_far0)
+    dkv0_back = swap(dkv0_far, "y")
+    mixed_own = to_model([act], [down_w], order, 0, rows, [dkv0_far])
+    mixed_own, resid_there, u_own, got_ux, got_uy, got_dc = sync(
+        mixed_own, resid_there, u_own, got_ux, got_uy, got_dc
+    )
+    up_sum = scatter_z(u_own + got_ux + got_uy)
+    d_y = d_y + got_dc
+    d_x, d_y, resid_there = sync(d_x, d_y, resid_there)
+    got_dx, got_dy = swap(d_x, "x"), swap(d_y, "y")
+    d_attn1 = to_hidden(resid_there, out_w)
+    dq1, dkv1, dkv1_far = attend_back(1, info, query, d_attn1, attn1, totals1, kv1, kv_far1)
+    dkv1_far, dkv0_back, d_own, got_dx, got_dy, dq1 = sync(
+        dkv1_far, dkv0_back, d_own, got_dx, got_dy, dq1
+    )
+    dkv1_back = swap(dkv1_far, "y")
+    q_grad, q_gains = heads_return(
+        q_raw, stacked(dq0, dq1), [], cos_tab, sin_tab, query_gain, 1
+    )
+    (o_grad,) = weight_grad(
+        stacked(attn0, attn1), stacked(after(resid_here, q_grad), resid_there), 0, width, 1
+    )
+    (w_grad,) = weight_grad(q_grad, normed1, 0, width, 1)
+    a_own, a_x, a_y, a_c = (
+        stacked(*pair) for pair in zip(jnp.split(w_grad, 4), jnp.split(o_grad, 4))
+    )
+    dkv1_back, a_own, a_x, a_y, a_c = sync(dkv1_back, a_own, a_x, a_y, a_c)
+    a_from = corner_start(a_c)
+    kv_grad, k_gains = heads_return(
+        kv_raw,
+        stacked(dkv0, dkv1),
+        [stacked(dkv0_back, dkv1_back)],
+        cos_tab,
+        sin_tab,
+        key_gain,
+        2,
+    )
+    (w_grad,) = weight_grad(kv_grad, normed1, 0, width, 1)
+    kv_own, kv_x, kv_y, kv_c, *a_from = sync(*jnp.split(w_grad, 4), *a_from)
+    kv_from = corner_start(kv_c)
+    a_x, a_y = corner_add(a_x, a_y, *a_from)
+    got_ax, got_ay = swap(a_x, "x"), swap(a_y, "y")
+    term_there = to_model([q_grad, kv_grad], [[q_w], [kv_w]], same, 1, rows, [a_x, a_y])
+    normed1_there = swap(term_there, "c")
+    q_grad, kv_x, kv_y, term_there, *kv_from = sync(q_grad, kv_x, kv_y, term_there, *kv_from)
+    kv_x, kv_y = corner_add(kv_x, kv_y, *kv_from)
+    got_kvx, got_kvy = swap(kv_x, "x"), swap(kv_y, "y")
+    term_own = to_model([q_grad, kv_grad], [[q_w], [kv_w]], same, 0, rows)
+    tokens_grad, gain1_sum = norm_return(
+        tokens, resid_grad, term_own, normed1_there, norm1_gain, (f32,), [kv_x, kv_y]
+    )
+    gain1_part, gain2_part = gain1_sum[0], gain2_sum[0]
+    a_near = after(a_own, term_own) + got_ax + got_ay
+    a_sum = scatter_z(
+        jnp.concatenate(
+            [a.reshape(4, q_in, width) for a in jnp.split(a_near, 2)], axis=1
+        ).reshape(8 * q_in, width)
+    )
+    kv_near = kv_own + got_kvx + got_kvy
+    kv_sum = scatter_z(
+        kv_near.reshape(2, 4, k_in, width).swapaxes(0, 1).reshape(8 * k_in, width)
+    )
+    output = (
+        valid * (resid + mixed_own.astype(f32) + mixed_there.astype(f32))
+    ).astype(bf16)
+
+    down_sum = after(d_own, term_own) + got_dx + got_dy
+    gate_sum, up_sum, down_sum = jnp.split(
+        from_core(jnp.concatenate([gate_sum, up_sum, down_sum], axis=0), core, 3), 3
+    )
+
+    gains = jnp.concatenate([gain1_part, gain2_part, q_gains[0], k_gains[0]])[None, :]
+    for axis in ("c", "x", "y"):
+        gains = gains + swap(gains, axis)
+    for step in (1, 2):
+        gains = gains + lax.ppermute(gains, "z", [(i, i ^ step) for i in range(4)])
+    gains = gains[0]
+
+    return (
+        output,
+        tokens_grad,
+        gains[:width],
+        a_sum[:q_in].astype(f32).T,
+        kv_sum[:k_in].astype(f32).T,
+        kv_sum[k_in:].astype(f32).T,
+        gains[2 * width : 2 * width + HEAD_SIZE],
+        gains[2 * width + HEAD_SIZE :],
+        a_sum[q_in:].astype(f32),
+        gains[width : 2 * width],
+        gate_sum.astype(f32).T,
+        up_sum.astype(f32).T,
+        down_sum.astype(f32),
+    )
+
+
+def chip_solution(mesh):
+    fine = Mesh(mesh.devices.reshape(2, 2, 2, 4), ("x", "c", "y", "z"))
+    row_spec = P(("x", "c", "y", "z"), None)
+    group_spec = P(("x", "c", "z"), None)
+    head_cols = P(None, ("y", "x", "c", "z"))
+    head_rows = P(("y", "x", "c", "z"), None)
+    up_spec, down_spec = P(("x", "c", "y"), "z"), P("z", ("x", "c", "y"))
+    return jax.shard_map(
+        chip_layer,
+        mesh=fine,
+        in_specs=(
+            row_spec,
+            row_spec,
+            group_spec,
+            group_spec,
+            P(),
+            head_cols,
+            head_cols,
+            head_cols,
+            P(),
+            P(),
+            head_rows,
+            P(),
+            up_spec,
+            up_spec,
+            down_spec,
+        ),
+        out_specs=(
+            row_spec,
+            row_spec,
+            P(),
+            head_cols,
+            head_cols,
+            head_cols,
+            P(),
+            P(),
+            head_rows,
+            P(),
+            up_spec,
+            up_spec,
+            down_spec,
+        ),
+        check_vma=False,
+    )
+
+
+def solution(mesh):
+    sizes = dict(mesh.shape)
+    if sizes == {"fsdp": 4, "heads": 2, "tensor": 4}:
+        return chip_solution(mesh)
+    return plain_solution(mesh)

time: 4490 us -> 1300 us (0.29)
  waiting for transfers between devices: 2910 us -> 277 us
  matrix products: 865 us -> 32 us
  Pallas kernels: 0 us -> 686 us
  other arithmetic: 293 us -> 131 us
  local copies, waits for them, and re-layouts: 228 us -> 74 us
  blocking collectives: 138 us -> 0 us
  starting transfers between devices: 19.3 us -> 79.5 us
    psum x1 -> x0, waiting for transfers between devices: 1030 us -> none  [tensor_sum(): lax.psum(term(0, row_count * lax.axis_size('tensor')).astype(jnp.bfloat16...]
    reduce_scatter x7 -> x6, waiting for transfers between devices: 910 us -> 0.07 us  [scatter_z(): return lax.psum_scatter(array, 'z', scatter_dimension=0, tiled=True)]
    dot_general x49 -> x2, matrix products: 865 us -> 32 us  [dot_t(): lax.dot_general(left, right, (((1,), (1,)), ((), ())), preferred_element_...]
    all_gather x9 -> x6, waiting for transfers between devices: 765 us -> 0.03 us  [gather_z(): return lax.all_gather(array, 'z', axis=0, tiled=True)]
    pallas_call x0 -> x32, Pallas kernels: none -> 686 us  [call(): pl.pallas_call(body, grid_spec=pltpu.PrefetchScalarGridSpec(num_scalar_pr...]
    ppermute x0 -> x58, waiting for transfers between devices: none -> 276 us  [the longest x56 273 us: swap(): return lax.ppermute(array, axis, SWAP)]
    all_to_all x3 -> x0, waiting for transfers between devices: 193 us -> none  [the longest x2 154 us: to_heads(): lax.all_to_all(packed, 'heads', split_axis=1, concat_axis=0, tiled=True)]
    convert_element_type x16 -> x9, other arithmetic: 145 us -> 21.9 us  [the longest x1 7.81 us: chip_layer(): output = (valid * (resid + mixed_own.astype(f32) + mixed_there.astype(f32...]
  transfers between devices with their start and end apart: 20 -> 70, of which waited for: 14 -> 23; matrix products, arithmetic and copies ran while one was open for 27% -> 17% of each run, Pallas kernels for 0% -> 53%
where the time goes in v2:
time: 1300 us; the launch traced here: 1290 us
  Pallas kernels  686 us (53%)
  waiting for transfers between devices  277 us (21%)
  other arithmetic  131 us (10%)
  starting transfers between devices  79.5 us (6%)
  local copies, waits for them, and re-layouts  74 us (6%)
  matrix products  32 us (2%)
  between operations  15.5 us (1%)
    pallas_call x32, Pallas kernels, call(): pl.pallas_call(body, grid_spec=pltpu.PrefetchScalarGridSpec(num_scalar_pr...  686 us
    ppermute x56, waiting for transfers between devices, swap(): return lax.ppermute(array, axis, SWAP)  273 us
    ppermute x56, starting transfers between devices, swap(): return lax.ppermute(array, axis, SWAP)  58.9 us
    concatenate x17, other arithmetic, stacked(): return jnp.concatenate([first, second], axis=0)  32.6 us
    dot_general x2, matrix products, dot_t(): lax.dot_general(left, right, (((1,), (1,)), ((), ())), preferred_element_...  32 us
    unnamed x107, local copies, waits for them, and re-layouts  28.9 us
  transfers between devices with their start and end apart: 70, of which 23 were waited for; matrix products, arithmetic and copies ran while one was open for 17% of the time, Pallas kernels for 53%

profile of v2, /device:TPU:0, one launch (start us, length us, event | category | flops | bytes accessed | tf_op | source)
XLA Modules:
  0.0 1294.2 jit_solution(2331098647670928430)
XLA Ops:
  63.4 15.1 %collective-permute-done.4 = bf16[768,512]{1,0:T(8,128)(2,1)} collective-permute-done((bf16[768,512]{1,0:T(8,128)(2,1)S(1)}, bf16[768,512]{1,0:T(8,128)(2,1)}, u32[]{:S(2)}, u32[]{:S(2)}) %collective-permute-start.4) | collective-permute-done | bytes 786464 | tf_op jit(solution)/shard_map/ppermute | solution.py:467
  108.1 17.4 %collective-permute-done.6 = bf16[512,2048]{1,0:T(8,128)(2,1)S(1)} collective-permute-done((bf16[512,2048]{1,0:T(8,128)(2,1)}, bf16[512,2048]{1,0:T(8,128)(2,1)S(1)}, u32[]{:S(2)}, u32[]{:S(2)}) %collective-permute-start.6) | collective-permute-done | bytes 2097184 | tf_op jit(solution)/shard_map/ppermute | solution.py:467
  158.9 17.4 %fusion.8.refs_0_ = f32[2048,1024]{1,0:T(8,128)} fusion(bf16[1024,2048]{1,0:T(8,128)(2,1)} %collective-permute-done, bf16[1024,2048]{1,0:T(8,128)(2,1)} %fusion.2, bf16[256,2048]{1,0:T(8,128)(2,1)S(1)} %bitcast.134, bf16[256,2048]{1,0:T(8,128)(2,1)} %bitcast.130, bf16[256,2048]{1,0:T(8,128)(2,1)} %bitcast.132, bf16[256,2048]{1,0:T(8,128)(2,1)} %bitcast.128), kind=kOutput, calls=%fused_computation.143 | convolution fusion | flops 8623489024 | bytes 20971520 | tf_op jit(solution)/shard_map/dot_general | solution.py:461
  176.2 14.6 %make_heads.3.refs_1_ = bf16[2048,1024]{1,0:T(8,128)(2,1)} custom-call(f32[2048,1024]{1,0:T(8,128)} %fusion.8.refs_0_, f32[2048,128]{1,0:T(8,128)} %pad_maximum_fusion.22.refs_1_, f32[2048,128]{1,0:T(8,128)} %pad_maximum_fusion.23.refs_2_, f32[1,128]{1,0:T(1,128)} %bitcast.162), custom_call_target="tpu_custom_call" | custom-call | flops 1000 | bytes 1000 | tf_op jit(solution)/shard_map/make_heads/pallas_call | solution.py:526
  193.7 14.7 %fusion.27.refs_0_ = f32[2048,1024]{1,0:T(8,128)} fusion(bf16[2048,2048]{1,0:T(8,128)(2,1)} %pad_maximum_fusion.refs_1_, bf16[1024,2048]{1,0:T(8,128)(2,1)} %constant_dynamic-update-slice_fusion.2.refs_4_), kind=kOutput, calls=%fused_computation.162 | convolution fusion | flops 8589934592 | bytes 20971520 | tf_op jit(solution)/shard_map/dot_general | solution.py:461
  219.0 24.4 %collective-permute-done.13 = bf16[256,2048]{1,0:T(8,128)(2,1)} collective-permute-done((bf16[256,2048]{1,0:T(8,128)(2,1)}, bf16[256,2048]{1,0:T(8,128)(2,1)}, u32[]{:S(2)}, u32[]{:S(2)}) %collective-permute-start.13) | collective-permute-done | bytes 1048608 | tf_op jit(solution)/shard_map/ppermute | solution.py:467
  247.7 43.2 %collective-permute-done.16.refs_3_.refs_6_ = bf16[1024,1024]{1,0:T(8,128)(2,1)} collective-permute-done((bf16[1024,1024]{1,0:T(8,128)(2,1)}, bf16[1024,1024]{1,0:T(8,128)(2,1)}, u32[]{:S(2)}, u32[]{:S(2)}) %collective-permute-start.16) | collective-permute-done | bytes 2097184 | tf_op jit(solution)/shard_map/ppermute | solution.py:467
  312.8 33.9 %attend.2 = (bf16[1024,1024]{1,0:T(8,128)(2,1)}, f32[1024,512]{1,0:T(8,128)}) custom-call(s32[2,9]{1,0:T(2,128)} %pad_add_fusion.refs_0_, bf16[2048,1024]{1,0:T(8,128)(2,1)} %make_heads.3.refs_1_, bf16[1024,1024]{1,0:T(8,128)(2,1)} %make_heads.4.refs_4_.refs_2_.refs_5_, bf16[1024,1024]{1,0:T(8,128)(2,1)} %collective-permute-done.16.refs_3_.refs_6_, ...), custom_call_target="tpu_custom_call" | custom-call | flops 1000 | bytes 1000 | tf_op jit(solution)/shard_map/attend/pallas_call | solution.py:526
  346.7 25.5 %attend.3 = (bf16[1024,1024]{1,0:T(8,128)(2,1)}, f32[1024,512]{1,0:T(8,128)}) custom-call(s32[2,9]{1,0:T(2,128)} %pad_add_fusion.refs_0_, bf16[2048,1024]{1,0:T(8,128)(2,1)} %make_heads.3.refs_1_, bf16[1024,1024]{1,0:T(8,128)(2,1)} %make_heads.5.refs_2_.refs_5_, bf16[1024,1024]{1,0:T(8,128)(2,1)} %collective-permute-done.17.refs_3_.refs_6_), custom_call_target="tpu_custom_call" | custom-call | flops 1000 | bytes 1000 | tf_op jit(solution)/shard_map/attend/pallas_call | solution.py:526
  411.0 45.3 %collective-permute-done.24.refs_7_.refs_9_ = bf16[3072,512]{1,0:T(8,128)(2,1)} collective-permute-done((bf16[3072,512]{1,0:T(8,128)(2,1)}, bf16[3072,512]{1,0:T(8,128)(2,1)}, u32[]{:S(2)}, u32[]{:S(2)}) %collective-permute-start.24) | collective-permute-done | bytes 3145760 | tf_op jit(solution)/shard_map/ppermute | solution.py:467
  461.5 32.5 %collective-permute-done.25 = bf16[1536,512]{1,0:T(8,128)(2,1)S(1)} collective-permute-done((bf16[1536,512]{1,0:T(8,128)(2,1)S(1)}, bf16[1536,512]{1,0:T(8,128)(2,1)S(1)}, u32[]{:S(2)}, u32[]{:S(2)}) %collective-permute-start.25) | collective-permute-done | bytes 1572896 | tf_op jit(solution)/shard_map/ppermute | solution.py:467
  497.8 63.5 %ffn_up.1 = (bf16[2048,3072]{1,0:T(8,128)(2,1)}, bf16[2048,3072]{1,0:T(8,128)(2,1)}, bf16[2048,3072]{1,0:T(8,128)(2,1)}) custom-call(bf16[2048,2048]{1,0:T(8,128)(2,1)} %constant_dynamic-update-slice_fusion.14.refs_0_.refs_1_, bf16[3072,512]{1,0:T(8,128)(2,1)} %all-gather.9.cloned.1.call-done.refs_1_.refs_3_, bf16[3072,512]{1,0:T(8,128)(2,1)} %copy-done.2, ...), custom_call_target="tpu_custom_call" | custom-call | flops 1000 | bytes 1000 | tf_op jit(solution)/shard_map/ffn_up/pallas_call | solution.py:526
  561.2 18.1 %weight_grad.7.refs_2_ = bf16[3072,1024]{1,0:T(8,128)(2,1)} custom-call(bf16[2048,3072]{1,0:T(8,128)(2,1)} %get-tuple-element.148.refs_0_.refs_1_, bf16[2048,2048]{1,0:T(8,128)(2,1)} %pad_maximum_fusion.1.refs_4_.refs_9_.refs_1_.refs_0_), custom_call_target="tpu_custom_call" | custom-call | flops 1000 | bytes 1000 | tf_op jit(solution)/shard_map/weight_grad/pallas_call | solution.py:526
  579.4 18.1 %weight_grad.8.refs_5_ = bf16[3072,1024]{1,0:T(8,128)(2,1)} custom-call(bf16[2048,3072]{1,0:T(8,128)(2,1)} %get-tuple-element.148.refs_0_.refs_1_, bf16[2048,2048]{1,0:T(8,128)(2,1)} %pad_maximum_fusion.1.refs_4_.refs_9_.refs_1_.refs_0_, bf16[3072,1024]{1,0:T(8,128)(2,1)} %weight_grad.7.refs_2_), custom_call_target="tpu_custom_call" | custom-call | flops 1000 | bytes 1000 | tf_op jit(solution)/shard_map/weight_grad/pallas_call | solution.py:526
  597.6 36.9 %ffn_back.1 = (bf16[2048,3072]{1,0:T(8,128)(2,1)}, bf16[2048,3072]{1,0:T(8,128)(2,1)}) custom-call(bf16[2048,2048]{1,0:T(8,128)(2,1)} %pad_maximum_fusion.1.refs_4_.refs_9_.refs_1_.refs_0_, bf16[3072,1024]{1,0:T(8,128)(2,1)} %all-gather.15.cloned.1.call-done.refs_5_.refs_1_.refs_2_, bf16[3072,1024]{1,0:T(8,128)(2,1)} %all-gather.17.cloned.1.call-done.refs_2_.refs_3_, ...), custom_call_target="tpu_custom_call" | custom-call | flops 1000 | bytes 1000 | tf_op jit(solution)/shard_map/ffn_back/pallas_call | solution.py:526
  634.5 32.1 %weight_grad.9 = (bf16[3072,512]{1,0:T(8,128)(2,1)}, bf16[3072,512]{1,0:T(8,128)(2,1)}, bf16[3072,512]{1,0:T(8,128)(2,1)}, bf16[3072,512]{1,0:T(8,128)(2,1)}) custom-call(bf16[2048,3072]{1,0:T(8,128)(2,1)} %get-tuple-element.151.refs_0_.refs_1_, bf16[2048,2048]{1,0:T(8,128)(2,1)} %constant_dynamic-update-slice_fusion.14.refs_0_.refs_1_), custom_call_target="tpu_custom_call" | custom-call | flops 1000 | bytes 1000 | tf_op jit(solution)/shard_map/weight_grad/pallas_call | solution.py:526
  670.5 32.3 %weight_grad.10 = (bf16[3072,512]{1,0:T(8,128)(2,1)}, bf16[3072,512]{1,0:T(8,128)(2,1)}, bf16[3072,512]{1,0:T(8,128)(2,1)}, bf16[3072,512]{1,0:T(8,128)(2,1)}) custom-call(bf16[2048,3072]{1,0:T(8,128)(2,1)} %get-tuple-element.156.refs_0_.refs_2_, bf16[2048,2048]{1,0:T(8,128)(2,1)} %constant_dynamic-update-slice_fusion.14.refs_0_.refs_1_, ...), custom_call_target="tpu_custom_call" | custom-call | flops 1000 | bytes 1000 | tf_op jit(solution)/shard_map/weight_grad/pallas_call | solution.py:526
  712.9 34.3 %to_model.10.refs_11_ = bf16[1024,2048]{1,0:T(8,128)(2,1)} custom-call(s32[8]{0:T(128)} %xor_add_fusion.refs_0_, bf16[2048,3072]{1,0:T(8,128)(2,1)} %get-tuple-element.151.refs_0_.refs_1_, bf16[2048,3072]{1,0:T(8,128)(2,1)} %get-tuple-element.156.refs_0_.refs_2_, bf16[3072,512]{1,0:T(8,128)(2,1)} %all-gather.9.cloned.1.call-done.refs_1_.refs_3_, ...), custom_call_target="tpu_custom_call" | custom-call | flops 1000 | bytes 1000 | tf_op jit(solution)/shard_map/to_model/pallas_call | solution.py:526
  747.3 34.5 %to_model.11.refs_2_ = bf16[1024,2048]{1,0:T(8,128)(2,1)} custom-call(s32[8]{0:T(128)} %xor_add_fusion.refs_0_, bf16[2048,3072]{1,0:T(8,128)(2,1)} %get-tuple-element.151.refs_0_.refs_1_, bf16[2048,3072]{1,0:T(8,128)(2,1)} %get-tuple-element.156.refs_0_.refs_2_, bf16[3072,512]{1,0:T(8,128)(2,1)} %all-gather.9.cloned.1.call-done.refs_1_.refs_3_, ...), custom_call_target="tpu_custom_call" | custom-call | flops 1000 | bytes 1000 | tf_op jit(solution)/shard_map/to_model/pallas_call | solution.py:526
  790.1 15.8 %norm_return.2 = (f32[1024,2048]{1,0:T(8,128)}, bf16[1024,2048]{1,0:T(8,128)(2,1)}, f32[8,2048]{1,0:T(8,128)}) custom-call(f32[1024,2048]{1,0:T(8,128)} %get-tuple-element.140.refs_0_, bf16[1024,2048]{1,0:T(8,128)(2,1)} %multiply_convert_fusion.1.refs_1_, bf16[1024,2048]{1,0:T(8,128)(2,1)} %to_model.11.refs_2_, ...), custom_call_target="tpu_custom_call" | custom-call | flops 1000 | bytes 1000 | tf_op jit(solution)/shard_map/norm_return/pallas_call | solution.py:526
  806.1 20.4 %to_model.12 = bf16[1024,2048]{1,0:T(8,128)(2,1)} custom-call(s32[8]{0:T(128)} %xor_add_fusion.refs_0_, bf16[2048,3072]{1,0:T(8,128)(2,1)} %get-tuple-element.148.refs_0_.refs_1_, bf16[3072,1024]{1,0:T(8,128)(2,1)} %all-gather.15.cloned.1.call-done.refs_5_.refs_1_.refs_2_, bf16[3072,1024]{1,0:T(8,128)(2,1)} %all-gather.17.cloned.1.call-done.refs_2_.refs_3_, ...), custom_call_target="tpu_custom_call" | custom-call | flops 1000 | bytes 1000 | tf_op jit(solution)/shard_map/to_model/pallas_call | solution.py:526
  846.0 54.9 %attend_back.2 = (bf16[1024,1024]{1,0:T(8,128)(2,1)}, bf16[1024,1024]{1,0:T(8,128)(2,1)}, bf16[1024,1024]{1,0:T(8,128)(2,1)}) custom-call(s32[2,9]{1,0:T(2,128)} %pad_add_fusion.refs_0_, bf16[2048,1024]{1,0:T(8,128)(2,1)} %make_heads.3.refs_1_, bf16[1024,1024]{1,0:T(8,128)(2,1)} %to_hidden.2.refs_2_, bf16[1024,1024]{1,0:T(8,128)(2,1)} %get-tuple-element.135.refs_1_.refs_3_, ...), custom_call_target="tpu_custom_call" | custom-call | flops 1000 | bytes 1000 | tf_op jit(solution)/shard_map/attend_back/pallas_call | solution.py:526
  904.7 20.5 %to_model.13 = bf16[1024,2048]{1,0:T(8,128)(2,1)} custom-call(s32[8]{0:T(128)} %xor_add_fusion.refs_0_, bf16[2048,3072]{1,0:T(8,128)(2,1)} %get-tuple-element.148.refs_0_.refs_1_, bf16[3072,1024]{1,0:T(8,128)(2,1)} %all-gather.15.cloned.1.call-done.refs_5_.refs_1_.refs_2_, bf16[3072,1024]{1,0:T(8,128)(2,1)} %all-gather.17.cloned.1.call-done.refs_2_.refs_3_, ...), custom_call_target="tpu_custom_call" | custom-call | flops 1000 | bytes 1000 | tf_op jit(solution)/shard_map/to_model/pallas_call | solution.py:526
  938.7 40.9 %attend_back.3 = (bf16[1024,1024]{1,0:T(8,128)(2,1)}, bf16[1024,1024]{1,0:T(8,128)(2,1)}, bf16[1024,1024]{1,0:T(8,128)(2,1)}) custom-call(s32[2,9]{1,0:T(2,128)} %pad_add_fusion.refs_0_, bf16[2048,1024]{1,0:T(8,128)(2,1)} %make_heads.3.refs_1_, bf16[1024,1024]{1,0:T(8,128)(2,1)} %to_hidden.3.refs_2_, bf16[1024,1024]{1,0:T(8,128)(2,1)} %get-tuple-element.139.refs_1_.refs_3_, ...), custom_call_target="tpu_custom_call" | custom-call | flops 1000 | bytes 1000 | tf_op jit(solution)/shard_map/attend_back/pallas_call | solution.py:526
  993.5 18.2 %heads_return.2 = (bf16[2048,1024]{1,0:T(8,128)(2,1)}, f32[8,128]{1,0:T(8,128)}) custom-call(f32[2048,1024]{1,0:T(8,128)} %fusion.8.refs_0_, f32[2048,128]{1,0:T(8,128)} %pad_maximum_fusion.22.refs_1_, f32[2048,128]{1,0:T(8,128)} %pad_maximum_fusion.23.refs_2_, f32[1,128]{1,0:T(1,128)} %bitcast.163, bf16[2048,1024]{1,0:T(8,128)(2,1)} %pad_maximum_fusion.4.refs_4_), custom_call_target="tpu_custom_call" | custom-call | flops 1000 | bytes 1000 | tf_op jit(solution)/shard_map/heads_return/pallas_call | solution.py:526
  1011.7 14.4 %weight_grad.11 = bf16[1024,2048]{1,0:T(8,128)(2,1)} custom-call(bf16[2048,1024]{1,0:T(8,128)(2,1)} %get-tuple-element.204.refs_0_.refs_1_, bf16[2048,2048]{1,0:T(8,128)(2,1)} %pad_maximum_fusion.refs_1_), custom_call_target="tpu_custom_call" | custom-call | flops 1000 | bytes 1000 | tf_op jit(solution)/shard_map/weight_grad/pallas_call | solution.py:526
  1056.3 21.6 %collective-permute-done.42 = bf16[1024,1024]{1,0:T(8,128)(2,1)} collective-permute-done((bf16[1024,1024]{1,0:T(8,128)(2,1)}, bf16[1024,1024]{1,0:T(8,128)(2,1)}, u32[]{:S(2)}, u32[]{:S(2)}) %collective-permute-start.42) | collective-permute-done | bytes 2097184 | tf_op jit(solution)/shard_map/ppermute | solution.py:467
  1101.5 14.6 %weight_grad.13 = bf16[1024,2048]{1,0:T(8,128)(2,1)} custom-call(bf16[2048,1024]{1,0:T(8,128)(2,1)} %get-tuple-element.195.refs_0_.refs_2_, bf16[2048,2048]{1,0:T(8,128)(2,1)} %pad_maximum_fusion.refs_1_), custom_call_target="tpu_custom_call" | custom-call | flops 1000 | bytes 1000 | tf_op jit(solution)/shard_map/weight_grad/pallas_call | solution.py:526
  1129.9 16.0 %to_model.14 = bf16[1024,2048]{1,0:T(8,128)(2,1)} custom-call(s32[8]{0:T(128)} %iota.45.refs_0_, bf16[2048,1024]{1,0:T(8,128)(2,1)} %get-tuple-element.204.refs_0_.refs_1_, bf16[2048,1024]{1,0:T(8,128)(2,1)} %get-tuple-element.195.refs_0_.refs_2_, bf16[1024,2048]{1,0:T(8,128)(2,1)} %pad_maximum_fusion.3.refs_3_, ...), custom_call_target="tpu_custom_call" | custom-call | flops 1000 | bytes 1000 | tf_op jit(solution)/shard_map/to_model/pallas_call | solution.py:526
  1180.1 16.2 %to_model.15.refs_2_ = bf16[1024,2048]{1,0:T(8,128)(2,1)} custom-call(s32[8]{0:T(128)} %iota.44.refs_0_, bf16[2048,1024]{1,0:T(8,128)(2,1)} %get-tuple-element.204.refs_0_.refs_1_, bf16[2048,1024]{1,0:T(8,128)(2,1)} %get-tuple-element.195.refs_0_.refs_2_, bf16[1024,2048]{1,0:T(8,128)(2,1)} %pad_maximum_fusion.3.refs_3_, ...), custom_call_target="tpu_custom_call" | custom-call | flops 1000 | bytes 1000 | tf_op jit(solution)/shard_map/to_model/pallas_call | solution.py:526
  1197.6 17.4 %collective-permute-done.54 = bf16[512,2048]{1,0:T(8,128)(2,1)} collective-permute-done((bf16[512,2048]{1,0:T(8,128)(2,1)}, bf16[512,2048]{1,0:T(8,128)(2,1)}, u32[]{:S(2)}, u32[]{:S(2)}) %collective-permute-start.54) | collective-permute-done | bytes 2097184 | tf_op jit(solution)/shard_map/ppermute | solution.py:467
  1254.1 19.8 %collective-permute-start.51 = (f32[1,4352]{1,0:T(1,128)S(1)}, f32[1,4352]{1,0:T(1,128)S(1)}, u32[]{:S(2)}, u32[]{:S(2)}) collective-permute-start(f32[1,4352]{1,0:T(1,128)S(1)} %add.237), channel_id=1, source_target_pairs={{0,1},{1,0},{2,3},{3,2},{4,5},{5,4},{6,7},{7,6},{8,9},{9,8},{10,11... | collective-permute-start | bytes 52232 | tf_op jit(solution)/shard_map/ppermute | solution.py:1316
  (395 shorter events, 434.1 us)
Async XLA Ops:
  7.2 71.3 %all-gather.7.cloned.1.call-start = ((), (), s32[]{:S(2)}) async-start(), calls=%async_computation.6 | async-start | bytes 2621440 | tf_op jit(solution)/shard_map/all_gather | solution.py:483
  9.2 144.2 %all-gather.9.cloned.1.call-start = ((), (), s32[]{:S(2)}) async-start(), calls=%async_computation.7 | async-start | bytes 3932160 | tf_op jit(solution)/shard_map/all_gather | solution.py:483
  15.8 139.0 %all-gather.11.cloned.1.call-start = ((), (), s32[]{:S(2)}) async-start(), calls=%async_computation.8 | async-start | bytes 1310720 | tf_op jit(solution)/shard_map/all_gather | solution.py:483
  16.6 202.4 %all-gather.13.cloned.1.call-start = ((), (), s32[]{:S(2)}) async-start(), calls=%async_computation.9 | async-start | bytes 3932160 | tf_op jit(solution)/shard_map/all_gather | solution.py:483
  25.9 73.7 %collective-permute-start = (bf16[1024,2048]{1,0:T(8,128)(2,1)}, bf16[1024,2048]{1,0:T(8,128)(2,1)}, u32[]{:S(2)}, u32[]{:S(2)}) collective-permute-start(bf16[1024,2048]{1,0:T(8,128)(2,1)} %fusion.2), channel_id=1, source_target_pairs={{0,8},{8,0},{1,9},{9,1},{2,10},{10,2},{3,11},{11,3},{4,12},{12,4},... | collective-permute-start | bytes 12582920 | tf_op jit(solution)/shard_map/ppermute | solution.py:467
  27.2 370.9 %all-gather.15.cloned.1.call-start = ((), (), s32[]{:S(2)}) async-start(), calls=%async_computation.10 | async-start | bytes 7864320 | tf_op jit(solution)/shard_map/all_gather | solution.py:483
  91.0 208.6 %collective-permute-start.18 = (bf16[1024,2048]{1,0:T(8,128)(2,1)}, bf16[1024,2048]{1,0:T(8,128)(2,1)}, u32[]{:S(2)}, u32[]{:S(2)}) collective-permute-start(bf16[1024,2048]{1,0:T(8,128)(2,1)} %reorder.1), channel_id=1, source_target_pairs={{0,8},{8,0},{1,9},{9,1},{2,10},{10,2},{3,11},{11,3},{4,12},{12,4},... | collective-permute-start | bytes 12582920 | tf_op jit(solution)/shard_map/ppermute | solution.py:467
  94.0 503.6 %all-gather.17.cloned.1.call-start = ((), (), s32[]{:S(2)}) async-start(), calls=%async_computation.11 | async-start | bytes 7864320 | tf_op jit(solution)/shard_map/all_gather | solution.py:483
  153.4 90.2 %collective-permute-start.11 = (bf16[3072,512]{1,0:T(8,128)(2,1)}, bf16[3072,512]{1,0:T(8,128)(2,1)S(1)}, u32[]{:S(2)}, u32[]{:S(2)}) collective-permute-start(bf16[3072,512]{1,0:T(8,128)(2,1)} %all-gather.9.cloned.1.call-done.refs_1_.refs_3_), channel_id=1, source_target_pairs={{0,16},{16,0},{1,17},{17,1},{2,18},{18,2},{3,19},{19,3},{4,20},{20... | collective-permute-start | bytes 9437192 | tf_op jit(solution)/shard_map/ppermute | solution.py:467
  154.1 89.5 %collective-permute-start.12 = (bf16[3072,512]{1,0:T(8,128)(2,1)}, bf16[3072,512]{1,0:T(8,128)(2,1)}, u32[]{:S(2)}, u32[]{:S(2)}) collective-permute-start(bf16[3072,512]{1,0:T(8,128)(2,1)} %all-gather.9.cloned.1.call-done.refs_1_.refs_3_), channel_id=1, source_target_pairs={{0,4},{4,0},{1,5},{5,1},{2,6},{6,2},{3,7},{7,3},{8,12},{12,8},{9,1... | collective-permute-start | bytes 9437192 | tf_op jit(solution)/shard_map/ppermute | solution.py:467
  154.9 88.5 %collective-permute-start.13 = (bf16[256,2048]{1,0:T(8,128)(2,1)}, bf16[256,2048]{1,0:T(8,128)(2,1)}, u32[]{:S(2)}, u32[]{:S(2)}) collective-permute-start(bf16[256,2048]{1,0:T(8,128)(2,1)} %all-gather.11.cloned.1.call-done), channel_id=1, source_target_pairs={{0,16},{16,0},{1,17},{17,1},{2,18},{18,2},{3,19},{19,3},{4,20},{20... | collective-permute-start | bytes 3145736 | tf_op jit(solution)/shard_map/ppermute | solution.py:467
  156.1 87.5 %collective-permute-start.14 = (bf16[256,2048]{1,0:T(8,128)(2,1)}, bf16[256,2048]{1,0:T(8,128)(2,1)}, u32[]{:S(2)}, u32[]{:S(2)}) collective-permute-start(bf16[256,2048]{1,0:T(8,128)(2,1)} %all-gather.11.cloned.1.call-done), channel_id=1, source_target_pairs={{0,4},{4,0},{1,5},{5,1},{2,6},{6,2},{3,7},{7,3},{8,12},{12,8},{9,1... | collective-permute-start | bytes 3145736 | tf_op jit(solution)/shard_map/ppermute | solution.py:467
  246.6 100.0 %collective-permute-start.19 = (bf16[3072,512]{1,0:T(8,128)(2,1)}, bf16[3072,512]{1,0:T(8,128)(2,1)S(1)}, u32[]{:S(2)}, u32[]{:S(2)}) collective-permute-start(bf16[3072,512]{1,0:T(8,128)(2,1)} %all-gather.13.cloned.1.call-done.refs_5_.refs_7_), channel_id=1, source_target_pairs={{0,16},{16,0},{1,17},{17,1},{2,18},{18,2},{3,19},{19,3},{4,20},{20... | collective-permute-start | bytes 9437192 | tf_op jit(solution)/shard_map/ppermute | solution.py:467
  298.4 414.5 %reduce-scatter.7.cloned.1.call-start = ((), (), s32[]{:S(2)}) async-start(), calls=%async_computation.12 | async-start | bytes 7864320 | tf_op jit(solution)/shard_map/reduce_scatter | solution.py:487
  385.5 70.8 %collective-permute-start.24 = (bf16[3072,512]{1,0:T(8,128)(2,1)}, bf16[3072,512]{1,0:T(8,128)(2,1)}, u32[]{:S(2)}, u32[]{:S(2)}) collective-permute-start(bf16[3072,512]{1,0:T(8,128)(2,1)} %all-gather.13.cloned.1.call-done.refs_5_.refs_7_), channel_id=1, source_target_pairs={{0,4},{4,0},{1,5},{5,1},{2,6},{6,2},{3,7},{7,3},{8,12},{12,8},{9,1... | collective-permute-start | bytes 9437192 | tf_op jit(solution)/shard_map/ppermute | solution.py:467
  385.5 72.3 %collective-permute-start.23 = (bf16[3072,512]{1,0:T(8,128)(2,1)}, bf16[3072,512]{1,0:T(8,128)(2,1)}, u32[]{:S(2)}, u32[]{:S(2)}) collective-permute-start(bf16[3072,512]{1,0:T(8,128)(2,1)} %collective-permute-done.12.refs_3_.refs_5_), channel_id=1, source_target_pairs={{0,16},{16,0},{1,17},{17,1},{2,18},{18,2},{3,19},{19,3},{4,20},{20... | collective-permute-start | bytes 9437192 | tf_op jit(solution)/shard_map/ppermute | solution.py:467
  410.8 84.0 %collective-permute-start.22 = (bf16[1024,2048]{1,0:T(8,128)(2,1)}, bf16[1024,2048]{1,0:T(8,128)(2,1)S(1)}, u32[]{:S(2)}, u32[]{:S(2)}) collective-permute-start(bf16[1024,2048]{1,0:T(8,128)(2,1)} %get-tuple-element.141), channel_id=1, source_target_pairs={{0,8},{8,0},{1,9},{9,1},{2,10},{10,2},{3,11},{11,3},{4,12},{12,4},... | collective-permute-start | bytes 12582920 | tf_op jit(solution)/shard_map/ppermute | solution.py:467
  579.4 247.1 %reduce-scatter.9.cloned.1.call-start = ((), (), s32[]{:S(2)}) async-start(), calls=%async_computation.13 | async-start | bytes 7864320 | tf_op jit(solution)/shard_map/reduce_scatter | solution.py:487
  597.6 624.3 %reduce-scatter.15.cloned.1.call-start = ((), (), s32[]{:S(2)}) async-start(), calls=%async_computation.16 | async-start | bytes 3932160 | tf_op jit(solution)/shard_map/reduce_scatter | solution.py:487
  710.9 70.9 %collective-permute-start.29 = (bf16[3072,512]{1,0:T(8,128)(2,1)S(1)}, bf16[3072,512]{1,0:T(8,128)(2,1)}, u32[]{:S(2)}, u32[]{:S(2)}) collective-permute-start(bf16[3072,512]{1,0:T(8,128)(2,1)S(1)} %pad_maximum_fusion.8.refs_11_), channel_id=1, source_target_pairs={{0,16},{16,0},{1,17},{17,1},{2,18},{18,2},{3,19},{19,3},{4,20},{20... | collective-permute-start | bytes 9437192 | tf_op jit(solution)/shard_map/ppermute | solution.py:467
  712.0 69.9 %collective-permute-start.30 = (bf16[3072,512]{1,0:T(8,128)(2,1)}, bf16[3072,512]{1,0:T(8,128)(2,1)}, u32[]{:S(2)}, u32[]{:S(2)}) collective-permute-start(bf16[3072,512]{1,0:T(8,128)(2,1)} %pad_maximum_fusion.9.refs_12_), channel_id=1, source_target_pairs={{0,4},{4,0},{1,5},{5,1},{2,6},{6,2},{3,7},{7,3},{8,12},{12,8},{9,1... | collective-permute-start | bytes 9437192 | tf_op jit(solution)/shard_map/ppermute | solution.py:467
  790.1 431.9 %reduce-scatter.17.cloned.1.call-start = ((), (), s32[]{:S(2)}) async-start(), calls=%async_computation.17 | async-start | bytes 3932160 | tf_op jit(solution)/shard_map/reduce_scatter | solution.py:487
  805.9 119.3 %collective-permute-start.34 = (bf16[1024,2048]{1,0:T(8,128)(2,1)}, bf16[1024,2048]{1,0:T(8,128)(2,1)}, u32[]{:S(2)}, u32[]{:S(2)}) collective-permute-start(bf16[1024,2048]{1,0:T(8,128)(2,1)} %get-tuple-element.193.refs_4_.refs_0_), channel_id=1, source_target_pairs={{0,8},{8,0},{1,9},{9,1},{2,10},{10,2},{3,11},{11,3},{4,12},{12,4},... | collective-permute-start | bytes 12582920 | tf_op jit(solution)/shard_map/ppermute | solution.py:467
  834.2 91.0 %collective-permute-start.35 = (bf16[3072,512]{1,0:T(8,128)(2,1)S(1)}, bf16[3072,512]{1,0:T(8,128)(2,1)}, u32[]{:S(2)}, u32[]{:S(2)}) collective-permute-start(bf16[3072,512]{1,0:T(8,128)(2,1)S(1)} %pad_maximum_fusion.10), channel_id=1, source_target_pairs={{0,16},{16,0},{1,17},{17,1},{2,18},{18,2},{3,19},{19,3},{4,20},{20... | collective-permute-start | bytes 9437192 | tf_op jit(solution)/shard_map/ppermute | solution.py:467
  835.6 89.7 %collective-permute-start.36 = (bf16[3072,512]{1,0:T(8,128)(2,1)}, bf16[3072,512]{1,0:T(8,128)(2,1)}, u32[]{:S(2)}, u32[]{:S(2)}) collective-permute-start(bf16[3072,512]{1,0:T(8,128)(2,1)} %pad_maximum_fusion.11), channel_id=1, source_target_pairs={{0,4},{4,0},{1,5},{5,1},{2,6},{6,2},{3,7},{7,3},{8,12},{12,8},{9,1... | collective-permute-start | bytes 9437192 | tf_op jit(solution)/shard_map/ppermute | solution.py:467
  836.5 88.7 %collective-permute-start.37 = (bf16[768,512]{1,0:T(8,128)(2,1)S(1)}, bf16[768,512]{1,0:T(8,128)(2,1)}, u32[]{:S(2)}, u32[]{:S(2)}) collective-permute-start(bf16[768,512]{1,0:T(8,128)(2,1)S(1)} %slice.267), channel_id=1, source_target_pairs={{0,16},{16,0},{1,17},{17,1},{2,18},{18,2},{3,19},{19,3},{4,20},{20... | collective-permute-start | bytes 2359304 | tf_op jit(solution)/shard_map/ppermute | solution.py:467
  900.9 88.1 %collective-permute-start.39 = (bf16[1024,1024]{1,0:T(8,128)(2,1)}, bf16[1024,1024]{1,0:T(8,128)(2,1)}, u32[]{:S(2)}, u32[]{:S(2)}) collective-permute-start(bf16[1024,1024]{1,0:T(8,128)(2,1)} %get-tuple-element.172.refs_4_), channel_id=1, source_target_pairs={{0,4},{4,0},{1,5},{5,1},{2,6},{6,2},{3,7},{7,3},{8,12},{12,8},{9,1... | collective-permute-start | bytes 6291464 | tf_op jit(solution)/shard_map/ppermute | solution.py:467
  993.4 285.4 %reduce-scatter.13.cloned.1.call-start = ((), (), s32[]{:S(2)}) async-start(), calls=%async_computation.15 | async-start | bytes 1310720 | tf_op jit(solution)/shard_map/reduce_scatter | solution.py:487
  1149.4 74.1 %collective-permute-start.47 = (bf16[1024,2048]{1,0:T(8,128)(2,1)}, bf16[1024,2048]{1,0:T(8,128)(2,1)}, u32[]{:S(2)}, u32[]{:S(2)}) collective-permute-start(bf16[1024,2048]{1,0:T(8,128)(2,1)} %to_model.14), channel_id=1, source_target_pairs={{0,8},{8,0},{1,9},{9,1},{2,10},{10,2},{3,11},{11,3},{4,12},{12,4},... | collective-permute-start | bytes 12582920 | tf_op jit(solution)/shard_map/ppermute | solution.py:467
  1154.5 63.1 %collective-permute-start.53 = (bf16[512,2048]{1,0:T(8,128)(2,1)}, bf16[512,2048]{1,0:T(8,128)(2,1)}, u32[]{:S(2)}, u32[]{:S(2)}) collective-permute-start(bf16[512,2048]{1,0:T(8,128)(2,1)} %pad_maximum_fusion.17.refs_5_), channel_id=1, source_target_pairs={{0,16},{16,0},{1,17},{17,1},{2,18},{18,2},{3,19},{19,3},{4,20},{20... | collective-permute-start | bytes 6291464 | tf_op jit(solution)/shard_map/ppermute | solution.py:467
  1169.9 72.5 %collective-permute-start.38 = (bf16[1024,2048]{1,0:T(8,128)(2,1)}, bf16[1024,2048]{1,0:T(8,128)(2,1)}, u32[]{:S(2)}, u32[]{:S(2)}) collective-permute-start(bf16[1024,2048]{1,0:T(8,128)(2,1)} %to_model.12), channel_id=1, source_target_pairs={{0,8},{8,0},{1,9},{9,1},{2,10},{10,2},{3,11},{11,3},{4,12},{12,4},... | collective-permute-start | bytes 12582920 | tf_op jit(solution)/shard_map/ppermute | solution.py:467
  1178.2 106.6 %reduce-scatter.11.cloned.1.call-start = ((), (), s32[]{:S(2)}) async-start(), calls=%async_computation.14 | async-start | bytes 2621440 | tf_op jit(solution)/shard_map/reduce_scatter | solution.py:487
  (84 other events, 1784.6 us)
Sparse Core Ops, SparseCore 0:
  10.2 48.6 all-gather.6
  60.4 62.2 all-gather.8
  124.2 26.6 all-gather.10
  152.3 62.9 all-gather.12
  217.3 113.9 all-gather.14
  333.4 113.6 all-gather.16
  579.5 116.7 reduce-scatter.6
  698.6 111.2 reduce-scatter.8
  812.3 60.7 reduce-scatter.14
  993.5 79.2 reduce-scatter.16
  1178.3 45.7 reduce-scatter.12
  1226.3 58.2 reduce-scatter.10

commit v3 on v2

--- a/solution.py
+++ b/solution.py
@@ -499,16 +499,15 @@
     half = array.shape[0] // 2
     first, second = array[:half], array[half:]
     other = swap(pick(second, first, core), "c")
-    return join(pick(first, second, core), other, core, 1)
-
-
-def from_core(array, core, count):
-    half = array.shape[1] // 2
-    span = array.shape[0] // count
-    first, second = array[:, :half], array[:, half:]
-    other = swap(pick(second, first, core), "c").reshape(count, span, half)
-    mine = pick(first, second, core).reshape(count, span, half)
-    return join(mine, other, core, 1).reshape(-1, half)
+    mine = pick(first, second, core)
+    return join(mine, other, core, 1)
+
+
+def from_core(pairs, core):
+    mine = [pick(a, b, core) for a, b in pairs]
+    send = jnp.concatenate([pick(b, a, core) for a, b in pairs], axis=0)
+    others = jnp.split(swap(send, "c"), len(pairs))
+    return [join(m, o, core, 0) for m, o in zip(mine, others)]
 
 
 def call(kernel, inputs, in_specs, out_specs, out_shape, grid, after=(), prefetch=None, **more):
@@ -576,15 +575,15 @@
         out_ref[:, HEAD_SIZE:] = raw_ref[:, HEAD_SIZE:].astype(jnp.bfloat16)
 
 
-def make_heads(raw, cos_tab, sin_tab, gain, count, first, rows, after=()):
-    width = raw.shape[1]
-    skip = first // ROW_TILE
+def make_heads(group, raw, cos_tab, sin_tab, gain, count, after=()):
+    rows, width = raw.shape
+    skip = group * (rows // ROW_TILE)
     table = pl.BlockSpec((ROW_TILE, HEAD_SIZE), lambda i, r: (i + skip, 0))
     return call(
         functools.partial(heads_kernel, count),
         [raw, cos_tab, sin_tab, gain[None, :]],
         [
-            pl.BlockSpec((ROW_TILE, count * HEAD_SIZE), lambda i, r: (i + skip, r)),
+            pl.BlockSpec((ROW_TILE, count * HEAD_SIZE), lambda i, r: (i, r)),
             table,
             table,
             pl.BlockSpec((1, HEAD_SIZE), lambda i, r: (0, 0)),
@@ -621,10 +620,11 @@
     sum_ref[0:1, :] += jnp.sum(turned * hat, axis=0, keepdims=True)
 
 
-def heads_return(raw, upstream, far, cos_tab, sin_tab, gain, count, after=()):
+def heads_return(group, raw, upstream, far, cos_tab, sin_tab, gain, count, after=()):
     rows, width = raw.shape
     heads = width // (count * HEAD_SIZE)
-    table = pl.BlockSpec((ROW_TILE, HEAD_SIZE), lambda i, r: (i, 0))
+    skip = group * (rows // ROW_TILE)
+    table = pl.BlockSpec((ROW_TILE, HEAD_SIZE), lambda i, r: (i + skip, 0))
     one = pl.BlockSpec((ROW_TILE, count * HEAD_SIZE), lambda i, r: (i, r))
     across = pl.BlockSpec(
         (ROW_TILE, count * HEAD_SIZE), lambda i, r: (i, (r + heads // 2) % heads)
@@ -645,6 +645,10 @@
     )
 
 
+GROUP_WIDTH = 2 * HEAD_SIZE
+TOGETHER = 2
+
+
 def stack_heads(block):
     return jnp.concatenate([block[:, :HEAD_SIZE], block[:, HEAD_SIZE:]], axis=0)
 
@@ -670,6 +674,10 @@
     return jnp.concatenate([own_ref[at, lanes], far_ref[at, lanes]], axis=0)
 
 
+def head_lanes(head):
+    return slice(head * GROUP_WIDTH, (head + 1) * GROUP_WIDTH)
+
+
 def attend_kernel(group, info_ref, q_ref, own_ref, far_ref, o_ref, l_ref):
     blocks = q_ref.shape[0] // BLK
     parity = info_ref[group, blocks]
@@ -677,53 +685,58 @@
     def one_block(j, _):
         first_key = info_ref[group, j]
         rows = pl.ds(pl.multiple_of(j * BLK, BLK), BLK)
-        query = stack_heads(q_ref[rows, :])
+        queries = [stack_heads(q_ref[rows, head_lanes(h)]) for h in range(TOGETHER)]
 
         def step(m, bias, carry):
-            total, acc = carry
-            score = dot_t(query, pair_of(own_ref, far_ref, m, 0))
-            expo = jnp.exp2(score * (SCALE * LOG2_E) + bias)
-            total = total + jnp.sum(expo, axis=1, keepdims=True)
-            value = pair_of(own_ref, far_ref, m, HEAD_SIZE)
-            acc = acc + matrix_product(expo.astype(jnp.bfloat16), value)
-            return total, acc
-
-        carry = step(
-            j,
-            last_bias(first_key, j, parity),
-            (jnp.zeros((2 * BLK, 1), jnp.float32), jnp.zeros((2 * BLK, HEAD_SIZE), jnp.float32)),
+            out = []
+            for h in range(TOGETHER):
+                total, acc = carry[h]
+                score = dot_t(queries[h], pair_of(own_ref, far_ref, m, h * GROUP_WIDTH))
+                expo = jnp.exp2(score * (SCALE * LOG2_E) + bias)
+                total = total + jnp.sum(expo, axis=1, keepdims=True)
+                value = pair_of(own_ref, far_ref, m, h * GROUP_WIDTH + HEAD_SIZE)
+                acc = acc + matrix_product(expo.astype(jnp.bfloat16), value)
+                out.append((total, acc))
+            return tuple(out)
+
+        empty = (
+            jnp.zeros((2 * BLK, 1), jnp.float32),
+            jnp.zeros((2 * BLK, HEAD_SIZE), jnp.float32),
         )
-        total, acc = lax.fori_loop(
+        carry = step(j, last_bias(first_key, j, parity), (empty,) * TOGETHER)
+        carry = lax.fori_loop(
             lax.div(first_key, 2),
             j,
             lambda m, c: step(m, key_bias(first_key, m, parity), c),
             carry,
         )
-        out = (acc / total).astype(jnp.bfloat16)
-        o_ref[rows, :HEAD_SIZE] = out[:BLK]
-        o_ref[rows, HEAD_SIZE:] = out[BLK:]
         lane = lax.broadcasted_iota(jnp.int32, (BLK, HEAD_SIZE), 1)
-        l_ref[rows, :] = jnp.where(lane == 0, total[:BLK], total[BLK:])
+        for h, (total, acc) in enumerate(carry):
+            out = (acc / total).astype(jnp.bfloat16)
+            o_ref[rows, head_lanes(h)] = jnp.concatenate([out[:BLK], out[BLK:]], axis=1)
+            l_ref[rows, h * HEAD_SIZE : (h + 1) * HEAD_SIZE] = jnp.where(
+                lane == 0, total[:BLK], total[BLK:]
+            )
         return 0
 
     lax.fori_loop(0, blocks, one_block, 0)
 
 
 def attend(group, info, query, own, far, after=()):
-    rows = query.shape[0] // 2
-    count = query.shape[1] // (2 * HEAD_SIZE)
-    wide = pl.BlockSpec((rows, 2 * HEAD_SIZE), lambda r, s: (group, r))
-    here = pl.BlockSpec((rows, 2 * HEAD_SIZE), lambda r, s: (0, r))
+    rows, width = query.shape
+    span = TOGETHER * GROUP_WIDTH
+    here = pl.BlockSpec((rows, span), lambda r, s: (0, r))
+    there = pl.BlockSpec((rows, span), lambda r, s: (0, (r + 1) % 2))
     return call(
         functools.partial(attend_kernel, group),
         [query, own, far],
-        [wide, here, pl.BlockSpec((rows, 2 * HEAD_SIZE), lambda r, s: (0, (r + 2) % 4))],
-        [here, pl.BlockSpec((rows, HEAD_SIZE), lambda r, s: (0, r))],
+        [here, here, there],
+        [here, pl.BlockSpec((rows, span // 2), lambda r, s: (0, r))],
         [
-            jax.ShapeDtypeStruct((rows, query.shape[1]), jnp.bfloat16),
-            jax.ShapeDtypeStruct((rows, count * HEAD_SIZE), jnp.float32),
+            jax.ShapeDtypeStruct((rows, width), jnp.bfloat16),
+            jax.ShapeDtypeStruct((rows, width // 2), jnp.float32),
         ],
-        (count,),
+        (width // span,),
         after,
         info,
         name="attend",
@@ -753,72 +766,78 @@
     def one_block(j, _):
         first_key = info_ref[group, j]
         rows = pl.ds(pl.multiple_of(j * BLK, BLK), BLK)
-        query = stack_heads(q_ref[rows, :])
-        attn = stack_heads(o_ref[rows, :]).astype(jnp.float32)
-        grad = stack_heads(do_ref[rows, :]).astype(jnp.float32)
-        total = jnp.concatenate([l_ref[rows, 0:1], l_ref[rows, 1:2]], axis=0)
-        grad_b = (grad / total).astype(jnp.bfloat16)
-        inner = jnp.sum(grad_b.astype(jnp.float32) * attn, axis=1, keepdims=True)
-
-        def step(m, bias, dq):
+        held = []
+        for h in range(TOGETHER):
+            query = stack_heads(q_ref[rows, head_lanes(h)])
+            attn = stack_heads(o_ref[rows, head_lanes(h)]).astype(jnp.float32)
+            grad = stack_heads(do_ref[rows, head_lanes(h)]).astype(jnp.float32)
+            at = h * HEAD_SIZE
+            total = jnp.concatenate(
+                [l_ref[rows, at : at + 1], l_ref[rows, at + 1 : at + 2]], axis=0
+            )
+            grad_b = (grad / total).astype(jnp.bfloat16)
+            inner = jnp.sum(grad_b.astype(jnp.float32) * attn, axis=1, keepdims=True)
+            held.append((query, grad_b, inner))
+
+        def step(m, bias, carry):
             at = pl.ds(pl.multiple_of(m * BLK, BLK), BLK)
-            key = pair_of(own_ref, far_ref, m, 0)
-            expo = jnp.exp2(dot_t(query, key) * (SCALE * LOG2_E) + bias)
-            d_prob = dot_t(grad_b, pair_of(own_ref, far_ref, m, HEAD_SIZE))
-            d_score = (expo * (d_prob - inner)).astype(jnp.bfloat16)
-            d_key = dot_rows(d_score, query)
-            d_value = dot_rows(expo.astype(jnp.bfloat16), grad_b)
-            kacc_ref[0, at, :] += d_key[:BLK]
-            kacc_ref[1, at, :] += d_key[BLK:]
-            vacc_ref[0, at, :] += d_value[:BLK]
-            vacc_ref[1, at, :] += d_value[BLK:]
-            return dq + matrix_product(d_score, key)
-
-        dq = step(
-            j, last_bias(first_key, j, parity), jnp.zeros((2 * BLK, HEAD_SIZE), jnp.float32)
-        )
-        dq = lax.fori_loop(
+            out = []
+            for h in range(TOGETHER):
+                query, grad_b, inner = held[h]
+                key = pair_of(own_ref, far_ref, m, h * GROUP_WIDTH)
+                value = pair_of(own_ref, far_ref, m, h * GROUP_WIDTH + HEAD_SIZE)
+                expo = jnp.exp2(dot_t(query, key) * (SCALE * LOG2_E) + bias)
+                d_score = (expo * (dot_t(grad_b, value) - inner)).astype(jnp.bfloat16)
+                d_key = dot_rows(d_score, query)
+                d_value = dot_rows(expo.astype(jnp.bfloat16), grad_b)
+                kacc_ref[h, 0, at, :] += d_key[:BLK]
+                kacc_ref[h, 1, at, :] += d_key[BLK:]
+                vacc_ref[h, 0, at, :] += d_value[:BLK]
+                vacc_ref[h, 1, at, :] += d_value[BLK:]
+                out.append(carry[h] + matrix_product(d_score, key))
+            return tuple(out)
+
+        empty = jnp.zeros((2 * BLK, HEAD_SIZE), jnp.float32)
+        carry = step(j, last_bias(first_key, j, parity), (empty,) * TOGETHER)
+        carry = lax.fori_loop(
             lax.div(first_key, 2),
             j,
             lambda m, c: step(m, key_bias(first_key, m, parity), c),
-            dq,
+            carry,
         )
-        dq = (dq * SCALE).astype(jnp.bfloat16)
-        dq_ref[rows, :HEAD_SIZE] = dq[:BLK]
-        dq_ref[rows, HEAD_SIZE:] = dq[BLK:]
+        for h, dq in enumerate(carry):
+            dq = (dq * SCALE).astype(jnp.bfloat16)
+            dq_ref[rows, head_lanes(h)] = jnp.concatenate([dq[:BLK], dq[BLK:]], axis=1)
         return 0
 
     lax.fori_loop(0, blocks, one_block, 0)
-    for half, ref in enumerate((down_ref, dfar_ref)):
-        ref[:, :HEAD_SIZE] = (kacc_ref[half] * SCALE).astype(jnp.bfloat16)
-        ref[:, HEAD_SIZE:] = vacc_ref[half].astype(jnp.bfloat16)
+    for h in range(TOGETHER):
+        for half, ref in enumerate((down_ref, dfar_ref)):
+            first = h * GROUP_WIDTH
+            ref[:, first : first + HEAD_SIZE] = (kacc_ref[h, half] * SCALE).astype(jnp.bfloat16)
+            ref[:, first + HEAD_SIZE : first + GROUP_WIDTH] = vacc_ref[h, half].astype(
+                jnp.bfloat16
+            )
 
 
 def attend_back(group, info, query, d_attn, attn, total, own, far, after=()):
-    rows = query.shape[0] // 2
-    count = query.shape[1] // (2 * HEAD_SIZE)
-    wide = pl.BlockSpec((rows, 2 * HEAD_SIZE), lambda r, s: (group, r))
-    here = pl.BlockSpec((rows, 2 * HEAD_SIZE), lambda r, s: (0, r))
-    shape = jax.ShapeDtypeStruct((rows, query.shape[1]), jnp.bfloat16)
+    rows, width = query.shape
+    span = TOGETHER * GROUP_WIDTH
+    here = pl.BlockSpec((rows, span), lambda r, s: (0, r))
+    there = pl.BlockSpec((rows, span), lambda r, s: (0, (r + 1) % 2))
+    shape = jax.ShapeDtypeStruct((rows, width), jnp.bfloat16)
     return call(
         functools.partial(attend_back_kernel, group),
         [query, d_attn, attn, total, own, far],
-        [
-            wide,
-            here,
-            here,
-            pl.BlockSpec((rows, HEAD_SIZE), lambda r, s: (0, r)),
-            here,
-            pl.BlockSpec((rows, 2 * HEAD_SIZE), lambda r, s: (0, (r + 2) % 4)),
-        ],
+        [here, here, here, pl.BlockSpec((rows, span // 2), lambda r, s: (0, r)), here, there],
         [here] * 3,
         [shape] * 3,
-        (count,),
+        (width // span,),
         after,
         info,
         scratch_shapes=[
-            pltpu.VMEM((2, rows, HEAD_SIZE), jnp.float32),
-            pltpu.VMEM((2, rows, HEAD_SIZE), jnp.float32),
+            pltpu.VMEM((TOGETHER, 2, rows, HEAD_SIZE), jnp.float32),
+            pltpu.VMEM((TOGETHER, 2, rows, HEAD_SIZE), jnp.float32),
         ],
         name="attend_back",
     )
@@ -828,111 +847,169 @@
 ROW_STEP = 512
 
 
-def ffn_up_kernel(x_ref, g0, g1, g2, g3, u0, u1, u2, u3, act_ref, dgate_ref, silu_ref):
-    gate_w = jnp.concatenate([g0[...], g1[...], g2[...], g3[...]], axis=1).T
-    up_w = jnp.concatenate([u0[...], u1[...], u2[...], u3[...]], axis=1).T
-    for first in range(0, x_ref.shape[0], ROW_STEP):
-        rows = slice(first, first + ROW_STEP)
-        gate = matrix_product(x_ref[rows, :], gate_w)
-        upper = matrix_product(x_ref[rows, :], up_w)
+def row_steps(*refs):
+    for first_ref in range(len(refs)):
+        for first in range(0, refs[first_ref].shape[0], ROW_STEP):
+            begin = first_ref * refs[first_ref].shape[0] + first
+            yield refs[first_ref][first : first + ROW_STEP, :], slice(begin, begin + ROW_STEP)
+
+
+def joined(refs):
+    return jnp.concatenate([ref[...] for ref in refs], axis=1)
+
+
+def ffn_kernel(pieces, xa_ref, xb_ref, *refs):
+    gate_w = joined(refs[:pieces]).T
+    up_w, d_act_ref = refs[pieces][...].T, refs[pieces + 1]
+    act_ref, gate_ref, up_ref = refs[pieces + 2 :]
+    for x, rows in row_steps(xa_ref, xb_ref):
+        gate = matrix_product(x, gate_w)
+        upper = matrix_product(x, up_w)
+        d_act = d_act_ref[rows, :].astype(jnp.float32)
         sig = 0.5 * jnp.tanh(0.5 * gate) + 0.5
         silu = gate * sig
         act_ref[rows, :] = (silu * upper).astype(jnp.bfloat16)
-        silu_ref[rows, :] = silu.astype(jnp.bfloat16)
-        dgate_ref[rows, :] = (upper * (sig + silu * (1.0 - sig))).astype(jnp.bfloat16)
-
-
-def ffn_up(x, gates, ups, after=()):
-    rows, width = x.shape
-    hidden, depth = gates[0].shape
-    weight = pl.BlockSpec((HIDDEN_TILE, depth), lambda j: (j, 0))
-    out = pl.BlockSpec((rows, HIDDEN_TILE), lambda j: (0, j))
-    shape = jax.ShapeDtypeStruct((rows, hidden), jnp.bfloat16)
+        gate_ref[rows, :] = (d_act * upper * (sig + silu * (1.0 - sig))).astype(jnp.bfloat16)
+        up_ref[rows, :] = (d_act * silu).astype(jnp.bfloat16)
+
+
+def ffn(xs, gates, up, d_act, after=()):
+    rows, width = xs[0].shape
+    hidden = up.shape[0]
+    out = pl.BlockSpec((2 * rows, HIDDEN_TILE), lambda j: (0, j))
+    shape = jax.ShapeDtypeStruct((2 * rows, hidden), jnp.bfloat16)
     return call(
-        ffn_up_kernel,
-        [x, *gates, *ups],
-        [pl.BlockSpec((rows, width), lambda j: (0, 0))] + [weight] * 8,
+        functools.partial(ffn_kernel, len(gates)),
+        [*xs, *gates, up, d_act],
+        [pl.BlockSpec((rows, width), lambda j: (0, 0))] * 2
+        + [pl.BlockSpec((HIDDEN_TILE, w.shape[1]), lambda j: (j, 0)) for w in (*gates, up)]
+        + [out],
         [out] * 3,
         [shape] * 3,
         (hidden // HIDDEN_TILE,),
         after,
-        name="ffn_up",
-    )
-
-
-def ffn_back_kernel(dy_ref, wa_ref, wb_ref, dgate_ref, silu_ref, gate_ref, up_ref):
-    weight = jnp.concatenate([wa_ref[...], wb_ref[...]], axis=1).T
-    for first in range(0, dy_ref.shape[0], ROW_STEP):
-        rows = slice(first, first + ROW_STEP)
-        d_act = matrix_product(dy_ref[rows, :], weight)
-        gate_ref[rows, :] = (d_act * dgate_ref[rows, :].astype(jnp.float32)).astype(jnp.bfloat16)
-        up_ref[rows, :] = (d_act * silu_ref[rows, :].astype(jnp.float32)).astype(jnp.bfloat16)
-
-
-def ffn_back(dy, downs, dgate, silu, after=()):
-    rows, width = dy.shape
-    hidden = downs[0].shape[0]
-    out = pl.BlockSpec((rows, HIDDEN_TILE), lambda j: (0, j))
-    shape = jax.ShapeDtypeStruct((rows, hidden), jnp.bfloat16)
+        name="ffn",
+    )
+
+
+def to_hidden_kernel(xs, *refs):
+    weight = joined(refs[xs:-1]).T
+    for x, rows in row_steps(*refs[:xs]):
+        refs[-1][rows, :] = matrix_product(x, weight).astype(refs[-1].dtype)
+
+
+def to_hidden(xs, weights, dtype=jnp.bfloat16, after=()):
+    rows, width = xs[0].shape
+    hidden = weights[0].shape[0]
     return call(
-        ffn_back_kernel,
-        [dy, *downs, dgate, silu],
-        [
-            pl.BlockSpec((rows, width), lambda j: (0, 0)),
-            pl.BlockSpec((HIDDEN_TILE, width // 2), lambda j: (j, 0)),
-            pl.BlockSpec((HIDDEN_TILE, width // 2), lambda j: (j, 0)),
-            out,
-            out,
-        ],
-        [out] * 2,
-        [shape] * 2,
+        functools.partial(to_hidden_kernel, len(xs)),
+        [*xs, *weights],
+        [pl.BlockSpec((rows, width), lambda j: (0, 0))] * len(xs)
+        + [pl.BlockSpec((HIDDEN_TILE, w.shape[1]), lambda j: (j, 0)) for w in weights],
+        pl.BlockSpec((len(xs) * rows, HIDDEN_TILE), lambda j: (0, j)),
+        jax.ShapeDtypeStruct((len(xs) * rows, hidden), dtype),
         (hidden // HIDDEN_TILE,),
         after,
-        name="ffn_back",
-    )
-
-
-def weight_grad_kernel(left_ref, right_ref, *out_refs):
-    left = left_ref[...].T
-    span = out_refs[0].shape[1]
-    for i, out_ref in enumerate(out_refs):
-        right = right_ref[:, i * span : (i + 1) * span]
-        out_ref[...] = matrix_product(left, right).astype(jnp.bfloat16)
-
-
-def weight_grad(left, right, first, last, count, after=()):
-    rows, hidden = left.shape
-    width = last - first
-    shape = jax.ShapeDtypeStruct((hidden, width // count), jnp.bfloat16)
+        name="to_hidden",
+    )
+
+
+MODEL_STEP = 512
+
+
+def left_parts(left_refs, rights):
+    if len(left_refs) == rights:
+        return [ref[...].T for ref in left_refs]
+    rows = left_refs[0].shape[0] // rights
+    return [left_refs[0][k * rows : (k + 1) * rows, :].T for k in range(rights)]
+
+
+def weight_cols_kernel(lefts, rights, *refs):
+    left_refs, right_refs, out_refs = refs[:lefts], refs[lefts : lefts + rights], refs[lefts + rights :]
+    parts = left_parts(left_refs, rights)
+    for first in range(0, right_refs[0].shape[1], MODEL_STEP):
+        cols = slice(first, first + MODEL_STEP)
+        term = matrix_product(parts[0], right_refs[0][:, cols])
+        for part, ref in zip(parts[1:], right_refs[1:]):
+            term = term + matrix_product(part, ref[:, cols])
+        term = term.astype(jnp.bfloat16)
+        begin = 0
+        for out_ref in out_refs:
+            end = begin + out_ref.shape[1]
+            low, high = max(begin, first), min(end, first + MODEL_STEP)
+            if low < high:
+                out_ref[:, low - begin : high - begin] = term[:, low - first : high - first]
+            begin = end
+
+
+def weight_cols(lefts, rights, first, widths, after=()):
+    rows, hidden = lefts[0].shape
+    width = sum(widths)
     return call(
-        weight_grad_kernel,
-        [left, right],
-        [
-            pl.BlockSpec((rows, HIDDEN_TILE), lambda j: (0, j)),
-            pl.BlockSpec((rows, width), lambda j: (0, first // width)),
-        ],
-        [pl.BlockSpec((HIDDEN_TILE, width // count), lambda j: (j, 0))] * count,
+        functools.partial(weight_cols_kernel, len(lefts), len(rights)),
+        [*lefts, *rights],
+        [pl.BlockSpec((rows, HIDDEN_TILE), lambda j: (0, j))] * len(lefts)
+        + [pl.BlockSpec((rights[0].shape[0], width), lambda j: (0, first // width))] * len(rights),
+        [pl.BlockSpec((HIDDEN_TILE, w), lambda j: (j, 0)) for w in widths],
+        [jax.ShapeDtypeStruct((hidden, w), jnp.bfloat16) for w in widths],
+        (hidden // HIDDEN_TILE,),
+        after,
+        name="weight_cols",
+    )
+
+
+def weight_rows_kernel(lefts, rights, *refs):
+    left_refs, right_refs, out_refs = refs[:lefts], refs[lefts : lefts + rights], refs[lefts + rights :]
+    parts = left_parts(left_refs, rights)
+    span = out_refs[0].shape[0]
+    inside = HIDDEN_TILE // span
+    for first in range(0, right_refs[0].shape[1], MODEL_STEP):
+        cols = slice(first, first + MODEL_STEP)
+        term = matrix_product(parts[0], right_refs[0][:, cols])
+        for part, ref in zip(parts[1:], right_refs[1:]):
+            term = term + matrix_product(part, ref[:, cols])
+        term = term.astype(jnp.bfloat16)
+        for i, out_ref in enumerate(out_refs):
+
+            @pl.when(pl.program_id(0) == i // inside)
+            def _():
+                out_ref[:, cols] = term[(i % inside) * span : (i % inside + 1) * span]
+
+
+def weight_rows(lefts, rights, count, after=()):
+    rows, hidden = lefts[0].shape
+    width = rights[0].shape[1]
+    shape = jax.ShapeDtypeStruct((hidden // count, width), jnp.bfloat16)
+    return call(
+        functools.partial(weight_rows_kernel, len(lefts), len(rights)),
+        [*lefts, *rights],
+        [pl.BlockSpec((rows, HIDDEN_TILE), lambda j: (0, j))] * len(lefts)
+        + [pl.BlockSpec((rights[0].shape[0], width), lambda j: (0, 0))] * len(rights),
+        [pl.BlockSpec((hidden // count, width), lambda j: (0, 0))] * count,
         [shape] * count,
         (hidden // HIDDEN_TILE,),
         after,
-        name="weight_grad",
-    )
-
-
-def to_model_kernel(terms, order_ref, *refs):
-    left_refs, weight_refs = refs[:terms], refs[terms:-2]
+        name="weight_rows",
+    )
+
+
+def to_model_kernel(counts, order_ref, *refs):
+    left_refs, weight_refs = refs[: len(counts)], refs[len(counts) : -2]
     out_ref, acc_ref = refs[-2:]
-    pieces = len(weight_refs) // terms
-    span = weight_refs[0].shape[1]
 
     @pl.when(pl.program_id(0) == 0)
     def _():
         acc_ref[...] = jnp.zeros_like(acc_ref)
 
-    left = jnp.concatenate([ref[...] for ref in left_refs], axis=1)
-    for i in range(pieces):
-        weight = jnp.concatenate([weight_refs[t * pieces + i][...] for t in range(terms)], axis=0)
-        acc_ref[:, i * span : (i + 1) * span] += matrix_product(left, weight)
+    left = joined(left_refs)
+    terms, begin = [], 0
+    for count in counts:
+        terms.append(joined(weight_refs[begin : begin + count]))
+        begin += count
+    weight = jnp.concatenate(terms, axis=0)
+    for first in range(0, weight.shape[1], MODEL_STEP):
+        cols = slice(first, first + MODEL_STEP)
+        acc_ref[:, cols] += matrix_product(left, weight[:, cols])
 
     @pl.when(pl.program_id(0) == pl.num_programs(0) - 1)
     def _():
@@ -944,41 +1021,21 @@
 
 def to_model(lefts, weights, order, half, rows, after=()):
     hidden = lefts[0].shape[1]
-    span, pieces = weights[0][0].shape[1], len(weights[0])
+    flat = [w for pieces in weights for w in pieces]
+    width = sum(w.shape[1] for w in weights[0])
+    tile = HIDDEN_TILE if len(lefts) <= 2 else HIDDEN_TILE // 2
     return call(
-        functools.partial(to_model_kernel, len(lefts)),
-        [*lefts, *(w for group in weights for w in group)],
-        [pl.BlockSpec((rows, HIDDEN_TILE), lambda j, o: (half, j))] * len(lefts)
-        + [pl.BlockSpec((HIDDEN_TILE, span), lambda j, o: (j, 0))] * (len(lefts) * pieces),
-        pl.BlockSpec((rows, span * pieces), lambda j, o: (0, 0)),
-        jax.ShapeDtypeStruct((rows, span * pieces), jnp.bfloat16),
-        (hidden // HIDDEN_TILE,),
+        functools.partial(to_model_kernel, tuple(len(pieces) for pieces in weights)),
+        [*lefts, *flat],
+        [pl.BlockSpec((rows, tile), lambda j, o: (half, j))] * len(lefts)
+        + [pl.BlockSpec((tile, w.shape[1]), lambda j, o: (j, 0)) for w in flat],
+        pl.BlockSpec((rows, width), lambda j, o: (0, 0)),
+        jax.ShapeDtypeStruct((rows, width), jnp.bfloat16),
+        (hidden // tile,),
         after,
         order,
-        scratch_shapes=[pltpu.VMEM((rows, span * pieces), jnp.float32)],
+        scratch_shapes=[pltpu.VMEM((rows, width), jnp.float32)],
         name="to_model",
-    )
-
-
-def to_hidden_kernel(x_ref, weight_ref, out_ref):
-    out_ref[...] = matrix_product(x_ref[...], weight_ref[...].T).astype(jnp.bfloat16)
-
-
-def to_hidden(x, weight, after=()):
-    rows, width = x.shape
-    hidden = weight.shape[0]
-    return call(
-        to_hidden_kernel,
-        [x, weight],
-        [
-            pl.BlockSpec((rows, width), lambda j: (0, 0)),
-            pl.BlockSpec((HIDDEN_TILE, width), lambda j: (j, 0)),
-        ],
-        pl.BlockSpec((rows, HIDDEN_TILE), lambda j: (0, j)),
-        jax.ShapeDtypeStruct((rows, hidden), jnp.bfloat16),
-        (hidden // HIDDEN_TILE,),
-        after,
-        name="to_hidden",
     )
 
 
@@ -1091,41 +1148,32 @@
     half, fourth = width // 2, width // 4
 
     q_in, k_in = w_query.shape[1], key_matrix.shape[1]
-    down_0 = to_core(w_down, core)
-    down_x, down_y = swap(down_0, "x"), swap(down_0, "y")
-    down_c = swap(down_x, "y")
-    qkv_0 = gather_z(jnp.concatenate([w_query.T, key_matrix.T, value_matrix.T], axis=0))
-    gate_0 = gather_z(to_core(after(w_gate, down_0).T, core))
+    fourth, eighth = width // 4, width // 8
+    kvw_0 = gather_z(jnp.concatenate([key_matrix.T, value_matrix.T], axis=0))
+    qw_0 = gather_z(w_query.T)
+    up_0 = to_core(w_up.T, core)
+    up_x, up_y = swap(up_0, "x"), swap(up_0, "y")
+    down_0 = to_core(after(w_down, up_0), core)
+    gate_0 = to_core(after(w_gate, up_0).T, core)
+    low = up_0.shape[0] // 2
     out_0 = gather_z(w_out)
-    up_0 = gather_z(to_core(after(w_up, down_0).T, core))
-    down_w = [
-        gather_z(jnp.concatenate([down_0, down_x], axis=1)),
-        gather_z(jnp.concatenate([down_y, down_c], axis=1)),
+    dlo_0 = gather_z(down_0[:low])
+    kvw_0, up_x, up_y = sync(kvw_0, up_x, up_y)
+    kvw_x, kvw_y = swap(kvw_0, "x"), swap(kvw_0, "y")
+    middle = kvw_0.shape[0] // 2
+    kvw_x, kvw_y, qw_0 = sync(kvw_x, kvw_y, qw_0)
+    kvw_ca, kvw_cb = swap(kvw_y[:middle], "x"), swap(kvw_x[middle:], "y")
+    qw_x, qw_y = swap(qw_0, "x"), swap(qw_0, "y")
+    kvw_ca, kvw_cb, qw_x, qw_y, out_0 = sync(kvw_ca, kvw_cb, qw_x, qw_y, out_0)
+    qw_ca, qw_cb = swap(qw_y[:middle], "x"), swap(qw_x[middle:], "y")
+    out_x, out_y = swap(out_0, "x"), swap(out_0, "y")
+    kvw = [
+        a.reshape(4, 2 * k_in, width)
+        for a in (kvw_0, kvw_x, kvw_y, jnp.concatenate([kvw_ca, kvw_cb], axis=0))
     ]
-    qkv_start = after(qkv_0, down_x, down_y, down_c)
-    qkv_x, qkv_y = swap(qkv_start, "x"), swap(qkv_start, "y")
-    middle = qkv_0.shape[0] // 2
-    qkv_y_top, qkv_x_low, _, _ = lax.optimization_barrier(
-        (qkv_y[:middle], qkv_x[middle:], qkv_x, qkv_y)
-    )
-    qkv_c = jnp.concatenate([swap(qkv_y_top, "x"), swap(qkv_x_low, "y")], axis=0)
-    qkv_p = [
-        a.reshape(4, q_in + 2 * k_in, width) for a in (qkv_0, qkv_x, qkv_y, qkv_c)
-    ]
-    q_w = jnp.concatenate([a[:, :q_in].reshape(-1, width) for a in qkv_p], axis=0)
     kv_w = jnp.concatenate(
-        [
-            part.reshape(-1, width)
-            for a in qkv_p
-            for part in (a[:, q_in : q_in + k_in], a[:, q_in + k_in :])
-        ],
-        axis=0,
-    )
-    split = gate_0.shape[0] // 2
-    gate_send = after(gate_0, qkv_c)
-    gate_x, gate_y = swap(gate_send, "x"), swap(gate_send, "y")
-    out_send = after(out_0, qkv_c)
-    out_x, out_y = swap(out_send, "x"), swap(out_send, "y")
+        [part.reshape(-1, width) for a in kvw for part in (a[:, :k_in], a[:, k_in:])], axis=0
+    )
 
     lengths_here = jnp.concatenate([seq_lens[0], block_pos[0]]).astype(f32)
     lengths_there = swap(lengths_here[None, :], "c")[0].astype(jnp.int32)
@@ -1155,159 +1203,218 @@
     nx, nc, ny = blocks // 4, (blocks // 2) % 2, blocks % 2
     order_back = ((ny ^ yi) * 4 + (nx ^ xi) * 2 + nc).astype(jnp.int32)
 
-    def both(own):
-        return jnp.concatenate([own, swap(own, "c")], axis=0)
+    def stacked(first, second):
+        return jnp.concatenate([first, second], axis=0)
 
     inputs = tokens.astype(f32)
-    first_normed, scale1 = rms_parts(inputs, norm1_gain)
-    normed1 = both(first_normed.astype(bf16))
+    normed1 = rms_parts(inputs, norm1_gain)[0].astype(bf16)
+    normed1 = [normed1, swap(normed1, "c")]
     dy_own = (valid * cotangent.astype(f32)).astype(bf16)
-    dy = both(reorder(dy_own, order))
-
-    q_raw = dot_t(normed1, q_w)
-    query = make_heads(q_raw, cos_tab, sin_tab, query_gain, 1, 0, 2 * rows)
-    kv_raw = dot_t(after(normed1, query), kv_w)
-    kv0 = make_heads(kv_raw, cos_tab, sin_tab, key_gain, 2, 0, rows)
-    kv1 = make_heads(kv_raw, cos_tab, sin_tab, key_gain, 2, rows, rows, [kv0])
-    kv0, kv1, gate_x, gate_y, out_x, out_y, up_0 = sync(
-        kv0, kv1, gate_x, gate_y, out_x, out_y, up_0
-    )
-    kv_far0 = swap(kv0, "y")
-    kv_far1 = swap(after(kv1, kv_far0), "y")
-    out_c = swap(out_y, "x")
-    up_x = swap(up_0, "x")
-    attn0, totals0 = attend(0, info, query, kv0, kv_far0, [dy])
-    kv_far1, attn0, up_0, up_x, gate_y, out_c = sync(kv_far1, attn0, up_0, up_x, gate_y, out_c)
+
+    normed1[0], kv_w = sync(normed1[0], kv_w)
+    kv_raw = [to_hidden([normed1[0]], [kv_w], f32)]
+    kv_raw.append(to_hidden([normed1[1]], [kv_w], f32, [kv_raw[0]]))
+    kv = [make_heads(g, kv_raw[g], cos_tab, sin_tab, key_gain, 2, [kv_raw[1]]) for g in range(2)]
+    kv[0], kv[1], qw_ca, qw_cb, out_x, out_y, up_y, dy_own, normed1[0], gate_0, glo_in = sync(
+        *kv, qw_ca, qw_cb, out_x, out_y, up_y, dy_own, normed1[0], gate_0, gate_0[:low]
+    )
+    kv_far0, out_c, up_c = swap(kv[0], "y"), swap(out_y, "x"), swap(up_y, "x")
+    glo_0 = gather_z(glo_in)
+    dhi_0, ghi_0 = gather_z(down_0[low:]), gather_z(gate_0[low:])
+    q_w = jnp.concatenate([qw_0, qw_x, qw_y, qw_ca, qw_cb], axis=0)
+    q_raw = [to_hidden([normed1[0]], [q_w], f32)]
+    q_raw.append(to_hidden([normed1[1]], [q_w], f32, [q_raw[0]]))
+    query = [
+        make_heads(g, q_raw[g], cos_tab, sin_tab, query_gain, 1, [q_raw[1]]) for g in range(2)
+    ]
+    dy = [reorder(dy_own, order, query)]
+    kv_far0, out_c, up_c, dlo_0, dy[0] = sync(kv_far0, out_c, up_c, dlo_0, dy[0])
+    dlo_x, dlo_y = swap(dlo_0, "x"), swap(dlo_0, "y")
+    dy.append(swap(dy[0], "c"))
+    up_in = jnp.concatenate([up_0, up_x, up_y, up_c], axis=1)
+    ulo, uhi = gather_z(up_in[:low]), gather_z(up_in[low:])
+    attn0, totals0 = attend(0, info, query[0], kv[0], kv_far0)
     out_w = jnp.concatenate([out_0, out_x, out_y, out_c], axis=0)
-    up_y, gate_c = swap(up_0, "y"), swap(gate_y, "x")
-    attn1, totals1 = attend(1, info, query, kv1, kv_far1)
+    attn0, out_w, dlo_x, dlo_y, kv_1 = sync(attn0, out_w, dlo_x, dlo_y, kv[1])
+    kv_far1, dlo_c = swap(kv_1, "y"), swap(dlo_y, "x")
+    kv_far1, dlo_c, glo_0 = sync(kv_far1, dlo_c, glo_0)
+    glo_x, glo_y = swap(glo_0, "x"), swap(glo_0, "y")
+    attn1, totals1 = attend(1, info, query[1], kv[1], kv_far1)
+    attn1, glo_x, glo_y, glo_0 = sync(attn1, glo_x, glo_y, glo_0)
+    glo_ca, glo_cb = swap(glo_y[:, :eighth], "x"), swap(glo_x[:, eighth:], "y")
     same = jnp.arange(8, dtype=jnp.int32)
     out_term = to_model([attn1], [[out_w]], same, 0, rows)
     out_there = swap(out_term, "c")
     out_here = to_model([attn0], [[out_w]], same, 0, rows, [out_term])
-    resid, normed2_own = resid_norm(
-        tokens, out_here, out_there, norm2_gain, order_back, [down_w[0]]
-    )
-    normed2_b = both(normed2_own)
-    up_y_top, up_x_low, *_ = sync(up_y[:split], up_x[split:], up_y, gate_c, normed2_own)
-    up_c = jnp.concatenate([swap(up_y_top, "x"), swap(up_x_low, "y")], axis=0)
-    gate_w, up_w = [gate_0, gate_x, gate_y, gate_c], [up_0, up_x, up_y, up_c]
-    act, dgate, silu = ffn_up(normed2_b, gate_w, up_w, [dy])
-
-    def stacked(first, second):
-        return jnp.concatenate([first, second], axis=0)
-
-    def corner_start(corner):
-        span = corner.shape[0] // 2
-        return swap(corner[:span], "x"), swap(corner[span:], "y")
-
-    def corner_add(along_x, along_y, from_x, from_y):
-        span = from_x.shape[0]
+    dlo = [dlo_0, dlo_x, dlo_y, dlo_c]
+    d_act_lo = to_hidden(dy, dlo, bf16, [out_here])
+    out_here, d_act_lo, glo_ca, glo_cb, dhi_0, ghi_0 = sync(
+        out_here, d_act_lo, glo_ca, glo_cb, dhi_0, ghi_0
+    )
+    dhi_x, dhi_y = swap(dhi_0, "x"), swap(dhi_0, "y")
+    ghi_x, ghi_y = swap(ghi_0, "x"), swap(ghi_0, "y")
+    resid, normed2_own = resid_norm(tokens, out_here, out_there, norm2_gain, order_back)
+    normed2 = [normed2_own, swap(normed2_own, "c")]
+    glo = [glo_0, glo_x, glo_y, glo_ca, glo_cb]
+    act_lo, gg_lo, ug_lo = ffn(normed2, glo, ulo, d_act_lo)
+    act_lo, dhi_x, dhi_y, ghi_x, ghi_y = sync(act_lo, dhi_x, dhi_y, ghi_x, ghi_y)
+    dhi_c, ghi_c = swap(dhi_y, "x"), swap(ghi_x, "y")
+    dhi = [dhi_0, dhi_x, dhi_y, dhi_c]
+
+    widths = [fourth, fourth, fourth, eighth, eighth]
+
+    def corner_add(along_x, along_y, from_a, from_b):
         return (
-            stacked(along_x[:span], along_x[span:] + from_y),
-            stacked(along_y[:span] + from_x, along_y[span:]),
+            jnp.concatenate([along_x[:, :eighth], along_x[:, eighth:] + from_b], axis=1),
+            jnp.concatenate([along_y[:, :eighth] + from_a, along_y[:, eighth:]], axis=1),
         )
 
-    (down_first,) = weight_grad(act, dy, 0, half, 1)
-    (down_second,) = weight_grad(act, dy, half, width, 1, [down_first])
-    down_a, down_b = scatter_z(down_first), scatter_z(down_second)
-    gate_grad, up_grad = ffn_back(dy, down_w, dgate, silu, [down_second])
-    g_own, g_x, g_y, g_c = weight_grad(gate_grad, normed2_b, 0, width, 4)
-    g_from = corner_start(g_c)
-    u_own, u_x, u_y, u_c = weight_grad(up_grad, normed2_b, 0, width, 4, [g_own])
-    g_x, g_y, _ = sync(*corner_add(g_x, g_y, *g_from), u_own)
-    got_gx, got_gy = swap(g_x, "x"), swap(g_y, "y")
-    there = to_model([gate_grad, up_grad], [gate_w, up_w], order, 1, rows, [g_x, g_y, down_a])
+    (dlo_grad,) = weight_cols([act_lo], dy, 0, [width])
+    dlo_sum = scatter_z(dlo_grad)
+    gl_0, gl_x, gl_y, gl_ca, gl_cb = weight_cols([gg_lo], normed2, 0, widths, [dlo_grad])
+    gl_ca, gl_cb, ghi_c, dhi_c = sync(gl_ca, gl_cb, ghi_c, dhi_c)
+    from_a, from_b = swap(gl_ca, "x"), swap(gl_cb, "y")
+    ul_0, ul_x, ul_y, ul_ca, ul_cb = weight_cols([ug_lo], normed2, 0, widths, [gl_0])
+    d_act_hi = to_hidden(dy, dhi, bf16, [ul_0])
+    ghi = [ghi_0, ghi_x, ghi_y, ghi_c]
+    gl_x, gl_y, from_a, from_b, ul_ca, ul_cb, d_act_hi = sync(
+        gl_x, gl_y, from_a, from_b, ul_ca, ul_cb, d_act_hi
+    )
+    gl_x, gl_y = corner_add(gl_x, gl_y, from_a, from_b)
+    got_x, got_y = swap(gl_x, "x"), swap(gl_y, "y")
+    from_a, from_b = swap(ul_ca, "x"), swap(ul_cb, "y")
+    act_hi, gg_hi, ug_hi = ffn(normed2, ghi, uhi, d_act_hi)
+    dh_0, dh_x, dh_y, dh_ca, dh_cb = weight_cols([act_hi], dy, 0, widths)
+    gl_0, got_x, got_y, ul_x, ul_y, from_a, from_b, dh_0, gg_hi = sync(
+        gl_0, got_x, got_y, ul_x, ul_y, from_a, from_b, dh_0, gg_hi
+    )
+    ul_x, ul_y = corner_add(ul_x, ul_y, from_a, from_b)
+    glo_near = gl_0 + got_x + got_y
+    got_x, got_y = swap(ul_x, "x"), swap(ul_y, "y")
+    glo_sum = scatter_z(glo_near)
+    gh_0, gh_x, gh_y, gh_ca, gh_cb = weight_cols([gg_hi], normed2, 0, widths, [ul_x, ul_y])
+    uh_0, uh_x, uh_y, uh_ca, uh_cb = weight_cols([ug_hi], normed2, 0, widths, [gh_0])
+    ul_0, got_x, got_y, dh_ca, dh_cb, gh_ca, gh_cb, uh_0, gg_hi = sync(
+        ul_0, got_x, got_y, dh_ca, dh_cb, gh_ca, gh_cb, uh_0, gg_hi
+    )
+    from_da, from_db = swap(dh_ca, "x"), swap(dh_cb, "y")
+    from_ga, from_gb = swap(gh_ca, "x"), swap(gh_cb, "y")
+    ulo_near = ul_0 + got_x + got_y
+    ulo_sum = scatter_z(ulo_near)
+    grads = [gg_lo, ug_lo, gg_hi, ug_hi]
+    both_w = [glo, [ulo], ghi, [uhi]]
+    there = to_model(grads, both_w, order, 1, rows, [ulo_near])
+    dh_x, dh_y, from_da, from_db, gh_x, gh_y, from_ga, from_gb, uh_ca, uh_cb, there = sync(
+        dh_x, dh_y, from_da, from_db, gh_x, gh_y, from_ga, from_gb, uh_ca, uh_cb, there
+    )
     normed2_there = swap(there, "c")
-    normed2_own = to_model([gate_grad, up_grad], [gate_w, up_w], order, 0, rows, [there])
-    g_own, got_gx, got_gy, normed2_own, u_c = sync(g_own, got_gx, got_gy, normed2_own, u_c)
-    gate_sum = scatter_z(g_own + got_gx + got_gy)
-    u_from = corner_start(u_c)
+    dh_x, dh_y = corner_add(dh_x, dh_y, from_da, from_db)
+    gh_x, gh_y = corner_add(gh_x, gh_y, from_ga, from_gb)
+    got_x, got_y = swap(dh_x, "x"), swap(dh_y, "y")
+    from_a, from_b = swap(uh_ca, "x"), swap(uh_cb, "y")
+    grad_own = to_model(grads, both_w, order, 0, rows, [dh_x, dh_y, gh_x, gh_y])
     resid_grad, resid_here, gain2_sum = norm_return(
-        resid, dy_own, normed2_own, normed2_there, norm2_gain, (f32, bf16)
+        resid, dy_own, grad_own, normed2_there, norm2_gain, (f32, bf16)
+    )
+    dh_0, got_x, got_y, uh_x, uh_y, from_a, from_b, resid_here, gh_x, gh_y = sync(
+        dh_0, got_x, got_y, uh_x, uh_y, from_a, from_b, resid_here, gh_x, gh_y
     )
     resid_there = swap(resid_here, "c")
-    mixed_term = to_model([act], [down_w], order, 1, rows, [resid_here])
-    mixed_there = swap(mixed_term, "c")
-    resid_here, mixed_term, down_b, *u_from = sync(resid_here, mixed_term, down_b, *u_from)
-    u_x, u_y = corner_add(u_x, u_y, *u_from)
-    d_own, d_x = down_a[:, :fourth], down_a[:, fourth:]
-    d_y, d_c = down_b[:, :fourth], down_b[:, fourth:]
-    resid_here, u_x, u_y, d_c = sync(resid_here, u_x, u_y, d_c)
-    got_ux, got_uy = swap(u_x, "x"), swap(u_y, "y")
-    got_dc = swap(d_c, "x")
-
-    d_attn0 = to_hidden(resid_here, out_w)
-    dq0, dkv0, dkv0_far = attend_back(0, info, query, d_attn0, attn0, totals0, kv0, kv_far0)
+    uh_x, uh_y = corner_add(uh_x, uh_y, from_a, from_b)
+    dhi_near = dh_0 + got_x + got_y
+    got_x, got_y = swap(gh_x, "x"), swap(gh_y, "y")
+    got_ux, got_uy = swap(uh_x, "x"), swap(uh_y, "y")
+    dhi_sum = scatter_z(dhi_near)
+
+    d_attn0 = to_hidden([resid_here], [out_w], bf16, [uh_x, uh_y, dhi_near])
+    dq0, dkv0, dkv0_far = attend_back(0, info, query[0], d_attn0, attn0, totals0, kv[0], kv_far0)
+    gh_0, got_x, got_y, uh_0, got_ux, got_uy, resid_there, dkv0_far, dlo_sum = sync(
+        gh_0, got_x, got_y, uh_0, got_ux, got_uy, resid_there, dkv0_far, dlo_sum
+    )
     dkv0_back = swap(dkv0_far, "y")
-    mixed_own = to_model([act], [down_w], order, 0, rows, [dkv0_far])
-    mixed_own, resid_there, u_own, got_ux, got_uy, got_dc = sync(
-        mixed_own, resid_there, u_own, got_ux, got_uy, got_dc
-    )
-    up_sum = scatter_z(u_own + got_ux + got_uy)
-    d_y = d_y + got_dc
-    d_x, d_y, resid_there = sync(d_x, d_y, resid_there)
-    got_dx, got_dy = swap(d_x, "x"), swap(d_y, "y")
-    d_attn1 = to_hidden(resid_there, out_w)
-    dq1, dkv1, dkv1_far = attend_back(1, info, query, d_attn1, attn1, totals1, kv1, kv_far1)
-    dkv1_far, dkv0_back, d_own, got_dx, got_dy, dq1 = sync(
-        dkv1_far, dkv0_back, d_own, got_dx, got_dy, dq1
+    dl_0, dl_x, dl_y, dl_c = (dlo_sum[:, i * fourth : (i + 1) * fourth] for i in range(4))
+    from_l = swap(dl_c, "x")
+    ghi_near, uhi_near = gh_0 + got_x + got_y, uh_0 + got_ux + got_uy
+    ghi_sum, uhi_sum = scatter_z(ghi_near), scatter_z(uhi_near)
+    o_0, o_x, o_y, o_c = weight_rows(
+        [attn0, attn1], [resid_here, resid_there], 4, [ghi_near, uhi_near]
+    )
+    d_attn1 = to_hidden([resid_there], [out_w], bf16, [o_0])
+    dq1, dkv1, dkv1_far = attend_back(1, info, query[1], d_attn1, attn1, totals1, kv[1], kv_far1)
+    dkv1_far, dkv0_back, o_c, dl_x, dl_y, from_l, dq1 = sync(
+        dkv1_far, dkv0_back, o_c, dl_x, dl_y, from_l, dq1
     )
     dkv1_back = swap(dkv1_far, "y")
-    q_grad, q_gains = heads_return(
-        q_raw, stacked(dq0, dq1), [], cos_tab, sin_tab, query_gain, 1
-    )
-    (o_grad,) = weight_grad(
-        stacked(attn0, attn1), stacked(after(resid_here, q_grad), resid_there), 0, width, 1
-    )
-    (w_grad,) = weight_grad(q_grad, normed1, 0, width, 1)
-    a_own, a_x, a_y, a_c = (
-        stacked(*pair) for pair in zip(jnp.split(w_grad, 4), jnp.split(o_grad, 4))
-    )
-    dkv1_back, a_own, a_x, a_y, a_c = sync(dkv1_back, a_own, a_x, a_y, a_c)
-    a_from = corner_start(a_c)
-    kv_grad, k_gains = heads_return(
-        kv_raw,
-        stacked(dkv0, dkv1),
-        [stacked(dkv0_back, dkv1_back)],
-        cos_tab,
-        sin_tab,
-        key_gain,
-        2,
-    )
-    (w_grad,) = weight_grad(kv_grad, normed1, 0, width, 1)
-    kv_own, kv_x, kv_y, kv_c, *a_from = sync(*jnp.split(w_grad, 4), *a_from)
-    kv_from = corner_start(kv_c)
-    a_x, a_y = corner_add(a_x, a_y, *a_from)
-    got_ax, got_ay = swap(a_x, "x"), swap(a_y, "y")
-    term_there = to_model([q_grad, kv_grad], [[q_w], [kv_w]], same, 1, rows, [a_x, a_y])
+    from_o = swap(o_c, "x")
+    got_lx = swap(dl_x, "x")
+    back = (cos_tab, sin_tab)
+    q_grad = [
+        heads_return(g, q_raw[g], d, [], *back, query_gain, 1, [dq1])
+        for g, d in enumerate((dq0, dq1))
+    ]
+    q_gains = q_grad[0][1] + q_grad[1][1]
+    q_grad = [q_grad[0][0], q_grad[1][0]]
+    w_0, w_x, w_y, w_c = weight_rows(q_grad, normed1, 4)
+    mixed_term = to_model([act_lo, act_hi], [dlo, dhi], order, 1, rows, [w_0])
+    dkv1_back, from_o, w_c, mixed_term, o_x, o_y, dl_y = sync(
+        dkv1_back, from_o, w_c, mixed_term, o_x, o_y, dl_y
+    )
+
+    def halves(array):
+        span = array.shape[0] // 2
+        return array[:span], array[span:]
+
+    def corner_rows(along_x, along_y, from_a, from_b):
+        (x_a, x_b), (y_a, y_b) = halves(along_x), halves(along_y)
+        return stacked(x_a, x_b + from_b), stacked(y_a + from_a, y_b)
+
+    w_a, w_b = halves(w_c)
+    from_wa, from_wb = swap(w_a, "x"), swap(w_b, "y")
+    got_ox, got_oy = swap(o_x, "x"), swap(o_y + from_o, "y")
+    kv_grad = [
+        heads_return(g, kv_raw[g], d, [e], *back, key_gain, 2)
+        for g, (d, e) in enumerate(((dkv0, dkv0_back), (dkv1, dkv1_back)))
+    ]
+    k_gains = kv_grad[0][1] + kv_grad[1][1]
+    kv_grad = [kv_grad[0][0], kv_grad[1][0]]
+    kv_0, kv_x, kv_y, kv_c = weight_rows(kv_grad, normed1, 4)
+    kv_c, from_wa, from_wb, got_ox, got_oy, w_x, w_y, kv_grad[1] = sync(
+        kv_c, from_wa, from_wb, got_ox, got_oy, w_x, w_y, kv_grad[1]
+    )
+    kv_a, kv_b = halves(kv_c)
+    from_a, from_b = swap(kv_a, "x"), swap(kv_b, "y")
+    w_x, w_y = corner_rows(w_x, w_y, from_wa, from_wb)
+    got_wx, got_wy = swap(w_x, "x"), swap(w_y, "y")
+    term_there = to_model([q_grad[1], kv_grad[1]], [[q_w], [kv_w]], same, 0, rows)
+    o_near = o_0 + got_ox + got_oy
+    kv_x, kv_y, from_a, from_b, term_there, o_near = sync(
+        kv_x, kv_y, from_a, from_b, term_there, o_near
+    )
+    o_sum = scatter_z(o_near)
     normed1_there = swap(term_there, "c")
-    q_grad, kv_x, kv_y, term_there, *kv_from = sync(q_grad, kv_x, kv_y, term_there, *kv_from)
-    kv_x, kv_y = corner_add(kv_x, kv_y, *kv_from)
-    got_kvx, got_kvy = swap(kv_x, "x"), swap(kv_y, "y")
-    term_own = to_model([q_grad, kv_grad], [[q_w], [kv_w]], same, 0, rows)
-    tokens_grad, gain1_sum = norm_return(
-        tokens, resid_grad, term_own, normed1_there, norm1_gain, (f32,), [kv_x, kv_y]
-    )
-    gain1_part, gain2_part = gain1_sum[0], gain2_sum[0]
-    a_near = after(a_own, term_own) + got_ax + got_ay
-    a_sum = scatter_z(
-        jnp.concatenate(
-            [a.reshape(4, q_in, width) for a in jnp.split(a_near, 2)], axis=1
-        ).reshape(8 * q_in, width)
-    )
-    kv_near = kv_own + got_kvx + got_kvy
+    kv_x, kv_y = corner_rows(kv_x, kv_y, from_a, from_b)
+    got_kx, got_ky = swap(kv_x, "x"), swap(kv_y, "y")
+    term_own = to_model([q_grad[0], kv_grad[0]], [[q_w], [kv_w]], same, 0, rows, [kv_x, kv_y])
+    w_0, got_wx, got_wy, kv_0, got_kx, got_ky, term_own, dl_y = sync(
+        w_0, got_wx, got_wy, kv_0, got_kx, got_ky, term_own, dl_y + from_l
+    )
+    kv_near = kv_0 + got_kx + got_ky
     kv_sum = scatter_z(
         kv_near.reshape(2, 4, k_in, width).swapaxes(0, 1).reshape(8 * k_in, width)
     )
+    w_near = w_0 + got_wx + got_wy
+    w_sum = scatter_z(w_near)
+    got_ly = swap(dl_y, "y")
+    tokens_grad, gain1_sum = norm_return(
+        tokens, resid_grad, term_own, normed1_there, norm1_gain, (f32,), [kv_near, w_near]
+    )
+    gain1_part, gain2_part = gain1_sum[0], gain2_sum[0]
+    mixed_own = to_model([act_lo, act_hi], [dlo, dhi], order, 0, rows, [gain1_sum])
+    mixed_there = swap(mixed_term, "c")
     output = (
         valid * (resid + mixed_own.astype(f32) + mixed_there.astype(f32))
     ).astype(bf16)
-
-    down_sum = after(d_own, term_own) + got_dx + got_dy
-    gate_sum, up_sum, down_sum = jnp.split(
-        from_core(jnp.concatenate([gate_sum, up_sum, down_sum], axis=0), core, 3), 3
-    )
+    dlo_sum = dl_0 + got_lx + got_ly
 
     gains = jnp.concatenate([gain1_part, gain2_part, q_gains[0], k_gains[0]])[None, :]
     for axis in ("c", "x", "y"):
@@ -1316,16 +1423,23 @@
         gains = gains + lax.ppermute(gains, "z", [(i, i ^ step) for i in range(4)])
     gains = gains[0]
 
+    gate_sum, up_sum, down_sum = (
+        jnp.concatenate(pair, axis=0)
+        for pair in ((glo_sum, ghi_sum), (ulo_sum, uhi_sum), (dlo_sum, dhi_sum))
+    )
+    gate_sum, up_sum, down_sum = from_core(
+        [(a[:, :eighth], a[:, eighth:]) for a in (gate_sum, up_sum, down_sum)], core
+    )
     return (
         output,
         tokens_grad,
         gains[:width],
-        a_sum[:q_in].astype(f32).T,
+        w_sum.astype(f32).T,
         kv_sum[:k_in].astype(f32).T,
         kv_sum[k_in:].astype(f32).T,
         gains[2 * width : 2 * width + HEAD_SIZE],
         gains[2 * width + HEAD_SIZE :],
-        a_sum[q_in:].astype(f32),
+        o_sum.astype(f32),
         gains[width : 2 * width],
         gate_sum.astype(f32).T,
         up_sum.astype(f32).T,

time: 1300 us -> 1190 us (0.915)
  waiting for transfers between devices: 277 us -> 182 us
  Pallas kernels: 686 us -> 739 us
  other arithmetic: 131 us -> 98.2 us
  matrix products: 32 us -> 0 us
    ppermute x56 -> x81, waiting for transfers between devices: 273 us -> 154 us  [swap(): return lax.ppermute(array, axis, SWAP)]
    pallas_call x32 -> x43, Pallas kernels: 686 us -> 739 us  [call(): pl.pallas_call(body, grid_spec=pltpu.PrefetchScalarGridSpec(num_scalar_pr...]
    dot_general x2 -> x0, matrix products: 32 us -> none  [dot_t(): lax.dot_general(left, right, (((1,), (1,)), ((), ())), preferred_element_...]
    concatenate x17 -> x4, other arithmetic: 32.6 us -> 2.33 us  [stacked(): return jnp.concatenate([first, second], axis=0)]
    ppermute x56 -> x81, starting transfers between devices: 58.9 us -> 77.3 us  [swap(): return lax.ppermute(array, axis, SWAP)]
    ppermute x2, starting transfers between devices: 19.9 us -> 4.15 us  [chip_layer(): gains = gains + lax.ppermute(gains, 'z', [(i, i ^ step) for i in range(4)])]
    reduce_scatter x6 -> x9, waiting for transfers between devices: 0.07 us -> 13.9 us  [scatter_z(): return lax.psum_scatter(array, 'z', scatter_dimension=0, tiled=True)]
    concatenate x8 -> x15, other arithmetic: 28.4 us -> 15.3 us  [the longest x1 3.64 us: chip_layer(): out_w = jnp.concatenate([out_0, out_x, out_y, out_c], axis=0)]
  transfers between devices with their start and end apart: 70 -> 101, of which waited for: 23 -> 20; matrix products, arithmetic and copies ran while one was open for 17% -> 12% of each run, Pallas kernels for 53% -> 63%
where the time goes in v3:
time: 1190 us; the launch traced here: 1180 us
  Pallas kernels  739 us (62%)
  waiting for transfers between devices  182 us (15%)
  other arithmetic  98.2 us (8%)
  starting transfers between devices  82.7 us (7%)
  local copies, waits for them, and re-layouts  63.3 us (5%)
  between operations  16 us (1%)
    pallas_call x43, Pallas kernels, call(): pl.pallas_call(body, grid_spec=pltpu.PrefetchScalarGridSpec(num_scalar_pr...  739 us
    ppermute x81, waiting for transfers between devices, swap(): return lax.ppermute(array, axis, SWAP)  154 us
    ppermute x81, starting transfers between devices, swap(): return lax.ppermute(array, axis, SWAP)  77.3 us
    unnamed x163, local copies, waits for them, and re-layouts  32.6 us
  transfers between devices with their start and end apart: 101, of which 20 were waited for; matrix products, arithmetic and copies ran while one was open for 12% of the time, Pallas kernels for 63%

profile of v3, /device:TPU:0, one launch (start us, length us, event | category | flops | bytes accessed | tf_op | source)
XLA Modules:
  0.0 1180.9 jit_solution(2053488654025881920)
XLA Ops:
  98.9 18.6 %collective-permute-done.6 = bf16[128,2048]{1,0:T(8,128)(2,1)} collective-permute-done((bf16[128,2048]{1,0:T(8,128)(2,1)}, bf16[128,2048]{1,0:T(8,128)(2,1)}, u32[]{:S(2)}, u32[]{:S(2)}) %collective-permute-start.6) | collective-permute-done | bytes 524320 | tf_op jit(solution)/shard_map/ppermute | solution.py:467
  216.4 29.4 %attend.2 = (bf16[1024,1024]{1,0:T(8,128)(2,1)}, f32[1024,512]{1,0:T(8,128)}) custom-call(s32[2,9]{1,0:T(2,128)} %pad_add_fusion.refs_0_, bf16[1024,1024]{1,0:T(8,128)(2,1)} %make_heads.6.refs_2_.refs_1_, bf16[1024,1024]{1,0:T(8,128)(2,1)} %make_heads.4.refs_2_.refs_5_, bf16[1024,1024]{1,0:T(8,128)(2,1)} %copy-done.11), custom_call_target="tpu_custom_call" | custom-call | flops 1000 | bytes 1000 | tf_op jit(solution)/shard_map/attend/pallas_call | solution.py:525
  250.6 28.3 %collective-permute-done.23.refs_5_.refs_6_ = bf16[1536,512]{1,0:T(8,128)(2,1)} collective-permute-done((bf16[1536,512]{1,0:T(8,128)(2,1)}, bf16[1536,512]{1,0:T(8,128)(2,1)}, u32[]{:S(2)}, u32[]{:S(2)}) %collective-permute-start.23) | collective-permute-done | bytes 1572896 | tf_op jit(solution)/shard_map/ppermute | solution.py:467
  278.9 16.1 %collective-permute-done.22.refs_3_.refs_6_ = bf16[1024,1024]{1,0:T(8,128)(2,1)} collective-permute-done((bf16[1024,1024]{1,0:T(8,128)(2,1)S(1)}, bf16[1024,1024]{1,0:T(8,128)(2,1)}, u32[]{:S(2)}, u32[]{:S(2)}) %collective-permute-start.22) | collective-permute-done | bytes 2097184 | tf_op jit(solution)/shard_map/ppermute | solution.py:467
  295.6 22.2 %attend.3 = (bf16[1024,1024]{1,0:T(8,128)(2,1)}, f32[1024,512]{1,0:T(8,128)}) custom-call(s32[2,9]{1,0:T(2,128)} %pad_add_fusion.refs_0_, bf16[1024,1024]{1,0:T(8,128)(2,1)} %make_heads.7.refs_3_.refs_1_, bf16[1024,1024]{1,0:T(8,128)(2,1)} %make_heads.5.refs_2_.refs_5_, bf16[1024,1024]{1,0:T(8,128)(2,1)} %collective-permute-done.22.refs_3_.refs_6_), custom_call_target="tpu_custom_call" | custom-call | flops 1000 | bytes 1000 | tf_op jit(solution)/shard_map/attend/pallas_call | solution.py:525
  352.0 19.2 %to_hidden.12.refs_8_ = bf16[2048,1536]{1,0:T(8,128)(2,1)} custom-call(bf16[1024,2048]{1,0:T(8,128)(2,1)} %reorder.1.refs_0_.refs_1_, bf16[1024,2048]{1,0:T(8,128)(2,1)} %copy-done, bf16[1536,512]{1,0:T(8,128)(2,1)} %all-gather.16.cloned.1.call-done.refs_2_.refs_3_, bf16[1536,512]{1,0:T(8,128)(2,1)} %copy-done.5, ...), custom_call_target="tpu_custom_call" | custom-call | flops 1000 | bytes 1000 | tf_op jit(solution)/shard_map/to_hidden/pallas_call | solution.py:525
  372.4 12.8 %resid_norm.1 = (f32[1024,2048]{1,0:T(8,128)}, bf16[1024,2048]{1,0:T(8,128)(2,1)}) custom-call(s32[8]{0:T(128)} %add_add_fusion.9.refs_0_, bf16[1024,2048]{1,0:T(8,128)(2,1)} %refs_0_.1, bf16[1024,2048]{1,0:T(8,128)(2,1)} %to_model.9.refs_6_.refs_2_, bf16[1024,2048]{1,0:T(8,128)(2,1)} %collective-permute-done.29.refs_3_, f32[1,2048]{1,0:T(1,128)} %bitcast.116), custom_call_target="tpu_custom_call" | custom-call | flops 1000 | bytes 1000 | tf_op jit(solution)/shard_map/resid_norm/pallas_call | solution.py:525
  392.7 39.9 %ffn.2 = (bf16[2048,1536]{1,0:T(8,128)(2,1)}, bf16[2048,1536]{1,0:T(8,128)(2,1)}, bf16[2048,1536]{1,0:T(8,128)(2,1)}) custom-call(bf16[1024,2048]{1,0:T(8,128)(2,1)} %get-tuple-element.273.refs_0_.refs_1_, bf16[1024,2048]{1,0:T(8,128)(2,1)} %collective-permute-done.30.refs_1_.refs_2_, bf16[1536,512]{1,0:T(8,128)(2,1)} %all-gather.18.cloned.1.call-done.refs_2_.refs_5_, ...), custom_call_target="tpu_custom_call" | custom-call | flops 1000 | bytes 1000 | tf_op jit(solution)/shard_map/ffn/pallas_call | solution.py:525
  432.6 23.5 %collective-permute-done.34.refs_4_.refs_13_ = bf16[1536,512]{1,0:T(8,128)(2,1)} collective-permute-done((bf16[1536,512]{1,0:T(8,128)(2,1)}, bf16[1536,512]{1,0:T(8,128)(2,1)}, u32[]{:S(2)}, u32[]{:S(2)}) %collective-permute-start.34) | collective-permute-done | bytes 1572896 | tf_op jit(solution)/shard_map/ppermute | solution.py:467
  457.8 19.0 %weight_cols.6.refs_3_ = bf16[1536,2048]{1,0:T(8,128)(2,1)} custom-call(bf16[2048,1536]{1,0:T(8,128)(2,1)} %get-tuple-element.283.refs_0_.refs_1_, bf16[1024,2048]{1,0:T(8,128)(2,1)} %reorder.1.refs_0_.refs_1_, bf16[1024,2048]{1,0:T(8,128)(2,1)} %copy-done), custom_call_target="tpu_custom_call" | custom-call | flops 1000 | bytes 1000 | tf_op jit(solution)/shard_map/weight_cols/pallas_call | solution.py:525
  478.9 18.7 %weight_cols.7 = (bf16[1536,512]{1,0:T(8,128)(2,1)}, bf16[1536,512]{1,0:T(8,128)(2,1)}, bf16[1536,512]{1,0:T(8,128)(2,1)}, bf16[1536,256]{1,0:T(8,128)(2,1)}, bf16[1536,256]{1,0:T(8,128)(2,1)}) custom-call(bf16[2048,1536]{1,0:T(8,128)(2,1)} %get-tuple-element.286.refs_0_.refs_1_, bf16[1024,2048]{1,0:T(8,128)(2,1)} %get-tuple-element.273.refs_0_.refs_1_, ...), custom_call_target="tpu_custom_call" | custom-call | flops 1000 | bytes 1000 | tf_op jit(solution)/shard_map/weight_cols/pallas_call | solution.py:525
  497.6 15.4 %collective-permute-done.35.refs_5_.refs_14_ = bf16[1536,512]{1,0:T(8,128)(2,1)S(1)} collective-permute-done((bf16[1536,512]{1,0:T(8,128)(2,1)}, bf16[1536,512]{1,0:T(8,128)(2,1)S(1)}, u32[]{:S(2)}, u32[]{:S(2)}) %collective-permute-start.35) | collective-permute-done | bytes 1572896 | tf_op jit(solution)/shard_map/ppermute | solution.py:467
  516.0 18.5 %weight_cols.8 = (bf16[1536,512]{1,0:T(8,128)(2,1)}, bf16[1536,512]{1,0:T(8,128)(2,1)}, bf16[1536,512]{1,0:T(8,128)(2,1)}, bf16[1536,256]{1,0:T(8,128)(2,1)}, bf16[1536,256]{1,0:T(8,128)(2,1)}) custom-call(bf16[2048,1536]{1,0:T(8,128)(2,1)} %get-tuple-element.295.refs_0_.refs_2_, bf16[1024,2048]{1,0:T(8,128)(2,1)} %get-tuple-element.273.refs_0_.refs_1_, ...), custom_call_target="tpu_custom_call" | custom-call | flops 1000 | bytes 1000 | tf_op jit(solution)/shard_map/weight_cols/pallas_call | solution.py:525
  534.6 19.4 %to_hidden.13.refs_7_ = bf16[2048,1536]{1,0:T(8,128)(2,1)} custom-call(bf16[1024,2048]{1,0:T(8,128)(2,1)} %reorder.1.refs_0_.refs_1_, bf16[1024,2048]{1,0:T(8,128)(2,1)} %copy-done, bf16[1536,512]{1,0:T(8,128)(2,1)} %all-gather.20.cloned.1.call-done.refs_2_.refs_7_, bf16[1536,512]{1,0:T(8,128)(2,1)} %collective-permute-done.31.refs_3_.refs_8_, ...), custom_call_target="tpu_custom_call" | custom-call | flops 1000 | bytes 1000 | tf_op jit(solution)/shard_map/to_hidden/pallas_call | solution.py:525
  558.8 38.3 %ffn.3 = (bf16[2048,1536]{1,0:T(8,128)(2,1)}, bf16[2048,1536]{1,0:T(8,128)(2,1)}, bf16[2048,1536]{1,0:T(8,128)(2,1)}) custom-call(bf16[1024,2048]{1,0:T(8,128)(2,1)} %get-tuple-element.273.refs_0_.refs_1_, bf16[1024,2048]{1,0:T(8,128)(2,1)} %collective-permute-done.30.refs_1_.refs_2_, bf16[1536,512]{1,0:T(8,128)(2,1)} %all-gather.22.cloned.1.call-done.refs_2_.refs_11_, ...), custom_call_target="tpu_custom_call" | custom-call | flops 1000 | bytes 1000 | tf_op jit(solution)/shard_map/ffn/pallas_call | solution.py:525
  597.0 18.6 %weight_cols.9 = (bf16[1536,512]{1,0:T(8,128)(2,1)}, bf16[1536,512]{1,0:T(8,128)(2,1)}, bf16[1536,512]{1,0:T(8,128)(2,1)}, bf16[1536,256]{1,0:T(8,128)(2,1)}, bf16[1536,256]{1,0:T(8,128)(2,1)}) custom-call(bf16[2048,1536]{1,0:T(8,128)(2,1)} %get-tuple-element.302.refs_0_.refs_2_, bf16[1024,2048]{1,0:T(8,128)(2,1)} %reorder.1.refs_0_.refs_1_, ...), custom_call_target="tpu_custom_call" | custom-call | flops 1000 | bytes 1000 | tf_op jit(solution)/shard_map/weight_cols/pallas_call | solution.py:525
  621.5 18.6 %weight_cols.10 = (bf16[1536,512]{1,0:T(8,128)(2,1)}, bf16[1536,512]{1,0:T(8,128)(2,1)}, bf16[1536,512]{1,0:T(8,128)(2,1)}, bf16[1536,256]{1,0:T(8,128)(2,1)}, bf16[1536,256]{1,0:T(8,128)(2,1)}) custom-call(bf16[2048,1536]{1,0:T(8,128)(2,1)} %get-tuple-element.325.refs_0_.refs_3_, bf16[1024,2048]{1,0:T(8,128)(2,1)} %get-tuple-element.273.refs_0_.refs_1_, ...), custom_call_target="tpu_custom_call" | custom-call | flops 1000 | bytes 1000 | tf_op jit(solution)/shard_map/weight_cols/pallas_call | solution.py:525
  640.1 18.6 %weight_cols.11 = (bf16[1536,512]{1,0:T(8,128)(2,1)}, bf16[1536,512]{1,0:T(8,128)(2,1)}, bf16[1536,512]{1,0:T(8,128)(2,1)}, bf16[1536,256]{1,0:T(8,128)(2,1)}, bf16[1536,256]{1,0:T(8,128)(2,1)}) custom-call(bf16[2048,1536]{1,0:T(8,128)(2,1)} %get-tuple-element.322.refs_0_.refs_4_, bf16[1024,2048]{1,0:T(8,128)(2,1)} %get-tuple-element.273.refs_0_.refs_1_, ...), custom_call_target="tpu_custom_call" | custom-call | flops 1000 | bytes 1000 | tf_op jit(solution)/shard_map/weight_cols/pallas_call | solution.py:525
  664.3 34.6 %to_model.10 = bf16[1024,2048]{1,0:T(8,128)(2,1)} custom-call(s32[8]{0:T(128)} %xor_add_fusion.refs_0_, bf16[2048,1536]{1,0:T(8,128)(2,1)} %get-tuple-element.286.refs_0_.refs_1_, bf16[2048,1536]{1,0:T(8,128)(2,1)} %get-tuple-element.295.refs_0_.refs_2_, bf16[2048,1536]{1,0:T(8,128)(2,1)} %get-tuple-element.325.refs_0_.refs_3_, ...), custom_call_target="tpu_custom_call" | custom-call | flops 1000 | bytes 1000 | tf_op jit(solution)/shard_map/to_model/pallas_call | solution.py:525
  716.5 34.8 %to_model.11.refs_2_ = bf16[1024,2048]{1,0:T(8,128)(2,1)} custom-call(s32[8]{0:T(128)} %xor_add_fusion.refs_0_, bf16[2048,1536]{1,0:T(8,128)(2,1)} %get-tuple-element.286.refs_0_.refs_1_, bf16[2048,1536]{1,0:T(8,128)(2,1)} %get-tuple-element.295.refs_0_.refs_2_, bf16[2048,1536]{1,0:T(8,128)(2,1)} %get-tuple-element.325.refs_0_.refs_3_, ...), custom_call_target="tpu_custom_call" | custom-call | flops 1000 | bytes 1000 | tf_op jit(solution)/shard_map/to_model/pallas_call | solution.py:525
  751.3 15.3 %norm_return.2 = (f32[1024,2048]{1,0:T(8,128)}, bf16[1024,2048]{1,0:T(8,128)(2,1)}, f32[8,2048]{1,0:T(8,128)}) custom-call(f32[1024,2048]{1,0:T(8,128)} %get-tuple-element.272.refs_0_, bf16[1024,2048]{1,0:T(8,128)(2,1)} %multiply_convert_fusion.1.refs_1_, bf16[1024,2048]{1,0:T(8,128)(2,1)} %to_model.11.refs_2_, ...), custom_call_target="tpu_custom_call" | custom-call | flops 1000 | bytes 1000 | tf_op jit(solution)/shard_map/norm_return/pallas_call | solution.py:525
  786.4 46.3 %attend_back.2 = (bf16[1024,1024]{1,0:T(8,128)(2,1)}, bf16[1024,1024]{1,0:T(8,128)(2,1)}, bf16[1024,1024]{1,0:T(8,128)(2,1)}) custom-call(s32[2,9]{1,0:T(2,128)} %pad_add_fusion.refs_0_, bf16[1024,1024]{1,0:T(8,128)(2,1)} %make_heads.6.refs_2_.refs_1_, bf16[1024,1024]{1,0:T(8,128)(2,1)} %to_hidden.14.refs_2_, ...), custom_call_target="tpu_custom_call" | custom-call | flops 1000 | bytes 1000 | tf_op jit(solution)/shard_map/attend_back/pallas_call | solution.py:525
  855.0 16.5 %weight_rows.3 = (bf16[256,2048]{1,0:T(8,128)(2,1)}, bf16[256,2048]{1,0:T(8,128)(2,1)}, bf16[256,2048]{1,0:T(8,128)(2,1)}, bf16[256,2048]{1,0:T(8,128)(2,1)}) custom-call(bf16[1024,1024]{1,0:T(8,128)(2,1)} %get-tuple-element.256.refs_1_.refs_3_.refs_0_, bf16[1024,1024]{1,0:T(8,128)(2,1)} %get-tuple-element.264.refs_1_.refs_3_, ...), custom_call_target="tpu_custom_call" | custom-call | flops 1000 | bytes 1000 | tf_op jit(solution)/shard_map/weight_rows/pallas_call | solution.py:525
  880.2 35.5 %attend_back.3 = (bf16[1024,1024]{1,0:T(8,128)(2,1)}, bf16[1024,1024]{1,0:T(8,128)(2,1)}, bf16[1024,1024]{1,0:T(8,128)(2,1)}) custom-call(s32[2,9]{1,0:T(2,128)} %pad_add_fusion.refs_0_, bf16[1024,1024]{1,0:T(8,128)(2,1)} %make_heads.7.refs_3_.refs_1_, bf16[1024,1024]{1,0:T(8,128)(2,1)} %to_hidden.15.refs_2_, ...), custom_call_target="tpu_custom_call" | custom-call | flops 1000 | bytes 1000 | tf_op jit(solution)/shard_map/attend_back/pallas_call | solution.py:525
  938.7 16.5 %weight_rows.4 = (bf16[256,2048]{1,0:T(8,128)(2,1)}, bf16[256,2048]{1,0:T(8,128)(2,1)}, bf16[256,2048]{1,0:T(8,128)(2,1)}, bf16[256,2048]{1,0:T(8,128)(2,1)}) custom-call(bf16[1024,1024]{1,0:T(8,128)(2,1)} %get-tuple-element.384.refs_0_.refs_1_, bf16[1024,1024]{1,0:T(8,128)(2,1)} %get-tuple-element.385.refs_1_, bf16[1024,2048]{1,0:T(8,128)(2,1)} %fusion.2.refs_0_.refs_2_, ...), custom_call_target="tpu_custom_call" | custom-call | flops 1000 | bytes 1000 | tf_op jit(solution)/shard_map/weight_rows/pallas_call | solution.py:525
  955.2 20.7 %to_model.12 = bf16[1024,2048]{1,0:T(8,128)(2,1)} custom-call(s32[8]{0:T(128)} %xor_add_fusion.refs_0_, bf16[2048,1536]{1,0:T(8,128)(2,1)} %get-tuple-element.283.refs_0_.refs_1_, bf16[2048,1536]{1,0:T(8,128)(2,1)} %get-tuple-element.302.refs_0_.refs_2_, bf16[1536,512]{1,0:T(8,128)(2,1)} %all-gather.16.cloned.1.call-done.refs_2_.refs_3_, ...), custom_call_target="tpu_custom_call" | custom-call | flops 1000 | bytes 1000 | tf_op jit(solution)/shard_map/to_model/pallas_call | solution.py:525
  995.9 16.8 %weight_rows.5 = (bf16[256,2048]{1,0:T(8,128)(2,1)}, bf16[256,2048]{1,0:T(8,128)(2,1)}, bf16[256,2048]{1,0:T(8,128)(2,1)}, bf16[256,2048]{1,0:T(8,128)(2,1)}) custom-call(bf16[1024,1024]{1,0:T(8,128)(2,1)} %get-tuple-element.389.refs_0_.refs_2_, bf16[1024,1024]{1,0:T(8,128)(2,1)} %get-tuple-element.414.refs_1_.refs_2_, ...), custom_call_target="tpu_custom_call" | custom-call | flops 1000 | bytes 1000 | tf_op jit(solution)/shard_map/weight_rows/pallas_call | solution.py:525
  1022.1 15.9 %to_model.13 = bf16[1024,2048]{1,0:T(8,128)(2,1)} custom-call(s32[8]{0:T(128)} %iota.44.refs_0_, bf16[1024,1024]{1,0:T(8,128)(2,1)} %get-tuple-element.385.refs_1_, bf16[1024,1024]{1,0:T(8,128)(2,1)} %get-tuple-element.414.refs_1_.refs_2_, bf16[1024,2048]{1,0:T(8,128)(2,1)} %constant_dynamic-update-slice_fusion.8.refs_1_.refs_3_, ...), custom_call_target="tpu_custom_call" | custom-call | flops 1000 | bytes 1000 | tf_op jit(solution)/shard_map/to_model/pallas_call | solution.py:525
  1059.0 16.2 %to_model.14.refs_2_ = bf16[1024,2048]{1,0:T(8,128)(2,1)} custom-call(s32[8]{0:T(128)} %iota.45.refs_0_, bf16[1024,1024]{1,0:T(8,128)(2,1)} %get-tuple-element.384.refs_0_.refs_1_, bf16[1024,1024]{1,0:T(8,128)(2,1)} %get-tuple-element.389.refs_0_.refs_2_, bf16[1024,2048]{1,0:T(8,128)(2,1)} %constant_dynamic-update-slice_fusion.8.refs_1_.refs_3_, ...), custom_call_target="tpu_custom_call" | custom-call | flops 1000 | bytes 1000 | tf_op jit(solution)/shard_map/to_model/pallas_call | solution.py:525
  1098.7 14.0 %norm_return.3 = (f32[1024,2048]{1,0:T(8,128)}, f32[8,2048]{1,0:T(8,128)}) custom-call(bf16[1024,2048]{1,0:T(8,128)(2,1)} %refs_0_.1, f32[1024,2048]{1,0:T(8,128)} %get-tuple-element.348.refs_1_, bf16[1024,2048]{1,0:T(8,128)(2,1)} %to_model.14.refs_2_, bf16[1024,2048]{1,0:T(8,128)(2,1)} %collective-permute-done.73.refs_3_, f32[1,2048]{1,0:T(1,128)} %bitcast.113, ...), custom_call_target="tpu_custom_call" | custom-call | flops 1000 | bytes 1000 | tf_op jit(solution)/shard_map/norm_return/pallas_call | solution.py:525
  1126.3 13.9 %reduce-scatter.14.cloned.1.call-done = bf16[64,2048]{1,0:T(8,128)(2,1)} async-done(((bf16[256,2048]{1,0:T(8,128)(2,1)}), bf16[64,2048]{1,0:T(8,128)(2,1)}) %reduce-scatter.14.cloned.1.call-update) | async-done | bytes 262160 | tf_op jit(solution)/shard_map/reduce_scatter | solution.py:487
  1141.9 20.8 %to_model.15 = bf16[1024,2048]{1,0:T(8,128)(2,1)} custom-call(s32[8]{0:T(128)} %xor_add_fusion.refs_0_, bf16[2048,1536]{1,0:T(8,128)(2,1)} %get-tuple-element.283.refs_0_.refs_1_, bf16[2048,1536]{1,0:T(8,128)(2,1)} %get-tuple-element.302.refs_0_.refs_2_, bf16[1536,512]{1,0:T(8,128)(2,1)} %all-gather.16.cloned.1.call-done.refs_2_.refs_3_, ...), custom_call_target="tpu_custom_call" | custom-call | flops 1000 | bytes 1000 | tf_op jit(solution)/shard_map/to_model/pallas_call | solution.py:525
  (533 shorter events, 452.0 us)
Async XLA Ops:
  8.9 60.9 %all-gather.12.cloned.1.call-start = ((), (), s32[]{:S(2)}) async-start(), calls=%async_computation.10 | async-start | bytes 1310720 | tf_op jit(solution)/shard_map/all_gather | solution.py:483
  9.7 89.2 %all-gather.14.cloned.1.call-start = ((), (), s32[]{:S(2)}) async-start(), calls=%async_computation.11 | async-start | bytes 1310720 | tf_op jit(solution)/shard_map/all_gather | solution.py:483
  18.9 118.4 %collective-permute-start.10 = (bf16[1024,2048]{1,0:T(8,128)(2,1)}, bf16[1024,2048]{1,0:T(8,128)(2,1)}, u32[]{:S(2)}, u32[]{:S(2)}) collective-permute-start(bf16[1024,2048]{1,0:T(8,128)(2,1)} %fusion.2.refs_0_.refs_2_), channel_id=1, source_target_pairs={{0,8},{8,0},{1,9},{9,1},{2,10},{10,2},{3,11},{11,3},{4,12},{12,4},... | collective-permute-start | bytes 12582920 | tf_op jit(solution)/shard_map/ppermute | solution.py:467
  19.5 188.2 %all-gather.16.cloned.1.call-start = ((), (), s32[]{:S(2)}) async-start(), calls=%async_computation.12 | async-start | bytes 1966080 | tf_op jit(solution)/shard_map/all_gather | solution.py:483
  60.4 190.1 %all-gather.18.cloned.1.call-start = ((), (), s32[]{:S(2)}) async-start(), calls=%async_computation.13 | async-start | bytes 1966080 | tf_op jit(solution)/shard_map/all_gather | solution.py:483
  157.6 213.6 %all-gather.20.cloned.1.call-start = ((), (), s32[]{:S(2)}) async-start(), calls=%async_computation.14 | async-start | bytes 1966080 | tf_op jit(solution)/shard_map/all_gather | solution.py:483
  158.6 212.7 %all-gather.22.cloned.1.call-start = ((), (), s32[]{:S(2)}) async-start(), calls=%async_computation.15 | async-start | bytes 1966080 | tf_op jit(solution)/shard_map/all_gather | solution.py:483
  161.4 228.0 %all-gather.24.cloned.1.call-start = ((), (), s32[]{:S(2)}) async-start(), calls=%async_computation.16 | async-start | bytes 7864320 | tf_op jit(solution)/shard_map/all_gather | solution.py:483
  212.3 346.4 %all-gather.26.cloned.1.call-start = ((), (), s32[]{:S(2)}) async-start(), calls=%async_computation.17 | async-start | bytes 7864320 | tf_op jit(solution)/shard_map/all_gather | solution.py:483
  295.5 548.1 %reduce-scatter.10.cloned.1.call-start = ((), (), s32[]{:S(2)}) async-start(), calls=%async_computation.18 | async-start | bytes 7864320 | tf_op jit(solution)/shard_map/reduce_scatter | solution.py:487
  389.3 66.8 %collective-permute-start.34 = (bf16[1536,512]{1,0:T(8,128)(2,1)}, bf16[1536,512]{1,0:T(8,128)(2,1)}, u32[]{:S(2)}, u32[]{:S(2)}) collective-permute-start(bf16[1536,512]{1,0:T(8,128)(2,1)} %all-gather.22.cloned.1.call-done.refs_2_.refs_11_), channel_id=1, source_target_pairs={{0,4},{4,0},{1,5},{5,1},{2,6},{6,2},{3,7},{7,3},{8,12},{12,8},{9,1... | collective-permute-start | bytes 4718600 | tf_op jit(solution)/shard_map/ppermute | solution.py:467
  389.3 68.4 %collective-permute-start.33 = (bf16[1536,512]{1,0:T(8,128)(2,1)}, bf16[1536,512]{1,0:T(8,128)(2,1)}, u32[]{:S(2)}, u32[]{:S(2)}) collective-permute-start(bf16[1536,512]{1,0:T(8,128)(2,1)} %all-gather.22.cloned.1.call-done.refs_2_.refs_11_), channel_id=1, source_target_pairs={{0,16},{16,0},{1,17},{17,1},{2,18},{18,2},{3,19},{19,3},{4,20},{20... | collective-permute-start | bytes 4718600 | tf_op jit(solution)/shard_map/ppermute | solution.py:467
  476.8 573.1 %reduce-scatter.18.cloned.1.call-start = ((), (), s32[]{:S(2)}) async-start(), calls=%async_computation.22 | async-start | bytes 1966080 | tf_op jit(solution)/shard_map/reduce_scatter | solution.py:487
  554.3 61.4 %collective-permute-start.40 = (bf16[1536,512]{1,0:T(8,128)(2,1)S(1)}, bf16[1536,512]{1,0:T(8,128)(2,1)}, u32[]{:S(2)}, u32[]{:S(2)}) collective-permute-start(bf16[1536,512]{1,0:T(8,128)(2,1)S(1)} %pad_maximum_fusion.3), channel_id=1, source_target_pairs={{0,4},{4,0},{1,5},{5,1},{2,6},{6,2},{3,7},{7,3},{8,12},{12,8},{9,1... | collective-permute-start | bytes 4718600 | tf_op jit(solution)/shard_map/ppermute | solution.py:467
  702.2 349.4 %reduce-scatter.22.cloned.1.call-start = ((), (), s32[]{:S(2)}) async-start(), calls=%async_computation.24 | async-start | bytes 1966080 | tf_op jit(solution)/shard_map/reduce_scatter | solution.py:487
  702.3 64.3 %collective-permute-start.52 = (bf16[1536,256]{1,0:T(8,128)(2,1)}, bf16[1536,256]{1,0:T(8,128)(2,1)}, u32[]{:S(2)}, u32[]{:S(2)}) collective-permute-start(bf16[1536,256]{1,0:T(8,128)(2,1)} %get-tuple-element.352), channel_id=1, source_target_pairs={{0,16},{16,0},{1,17},{17,1},{2,18},{18,2},{3,19},{19,3},{4,20},{20... | collective-permute-start | bytes 2359304 | tf_op jit(solution)/shard_map/ppermute | solution.py:467
  702.9 63.7 %collective-permute-start.53 = (bf16[1536,256]{1,0:T(8,128)(2,1)}, bf16[1536,256]{1,0:T(8,128)(2,1)}, u32[]{:S(2)}, u32[]{:S(2)}) collective-permute-start(bf16[1536,256]{1,0:T(8,128)(2,1)} %get-tuple-element.353), channel_id=1, source_target_pairs={{0,4},{4,0},{1,5},{5,1},{2,6},{6,2},{3,7},{7,3},{8,12},{12,8},{9,1... | collective-permute-start | bytes 2359304 | tf_op jit(solution)/shard_map/ppermute | solution.py:467
  705.5 61.2 %collective-permute-start.51 = (bf16[1536,512]{1,0:T(8,128)(2,1)S(1)}, bf16[1536,512]{1,0:T(8,128)(2,1)S(1)}, u32[]{:S(2)}, u32[]{:S(2)}) collective-permute-start(bf16[1536,512]{1,0:T(8,128)(2,1)S(1)} %pad_maximum_fusion.7.refs_17_), channel_id=1, source_target_pairs={{0,4},{4,0},{1,5},{5,1},{2,6},{6,2},{3,7},{7,3},{8,12},{12,8},{9,1... | collective-permute-start | bytes 4718600 | tf_op jit(solution)/shard_map/ppermute | solution.py:467
  767.8 75.8 %collective-permute-start.58 = (bf16[1024,2048]{1,0:T(8,128)(2,1)}, bf16[1024,2048]{1,0:T(8,128)(2,1)}, u32[]{:S(2)}, u32[]{:S(2)}) collective-permute-start(bf16[1024,2048]{1,0:T(8,128)(2,1)} %get-tuple-element.355.refs_0_.refs_2_), channel_id=1, source_target_pairs={{0,8},{8,0},{1,9},{9,1},{2,10},{10,2},{3,11},{11,3},{4,12},{12,4},... | collective-permute-start | bytes 12582920 | tf_op jit(solution)/shard_map/ppermute | solution.py:467
  767.9 284.9 %reduce-scatter.20.cloned.1.call-start = ((), (), s32[]{:S(2)}) async-start(), calls=%async_computation.23 | async-start | bytes 1966080 | tf_op jit(solution)/shard_map/reduce_scatter | solution.py:487
  770.0 62.7 %collective-permute-start.57 = (bf16[1536,512]{1,0:T(8,128)(2,1)S(1)}, bf16[1536,512]{1,0:T(8,128)(2,1)}, u32[]{:S(2)}, u32[]{:S(2)}) collective-permute-start(bf16[1536,512]{1,0:T(8,128)(2,1)S(1)} %pad_maximum_fusion.11.refs_3_), channel_id=1, source_target_pairs={{0,4},{4,0},{1,5},{5,1},{2,6},{6,2},{3,7},{7,3},{8,12},{12,8},{9,1... | collective-permute-start | bytes 4718600 | tf_op jit(solution)/shard_map/ppermute | solution.py:467
  774.5 69.2 %collective-permute-start.54 = (bf16[1536,512]{1,0:T(8,128)(2,1)}, bf16[1536,512]{1,0:T(8,128)(2,1)}, u32[]{:S(2)}, u32[]{:S(2)}) collective-permute-start(bf16[1536,512]{1,0:T(8,128)(2,1)} %pad_maximum_fusion.8.refs_18_), channel_id=1, source_target_pairs={{0,16},{16,0},{1,17},{17,1},{2,18},{18,2},{3,19},{19,3},{4,20},{20... | collective-permute-start | bytes 4718600 | tf_op jit(solution)/shard_map/ppermute | solution.py:467
  775.5 68.1 %collective-permute-start.55 = (bf16[1536,512]{1,0:T(8,128)(2,1)}, bf16[1536,512]{1,0:T(8,128)(2,1)}, u32[]{:S(2)}, u32[]{:S(2)}) collective-permute-start(bf16[1536,512]{1,0:T(8,128)(2,1)} %pad_maximum_fusion.9.refs_19_), channel_id=1, source_target_pairs={{0,4},{4,0},{1,5},{5,1},{2,6},{6,2},{3,7},{7,3},{8,12},{12,8},{9,1... | collective-permute-start | bytes 4718600 | tf_op jit(solution)/shard_map/ppermute | solution.py:467
  847.4 207.1 %reduce-scatter.24.cloned.1.call-start = ((), (), s32[]{:S(2)}) async-start(), calls=%async_computation.25 | async-start | bytes 1966080 | tf_op jit(solution)/shard_map/reduce_scatter | solution.py:487
  847.4 68.3 %collective-permute-start.59 = (bf16[1024,1024]{1,0:T(8,128)(2,1)}, bf16[1024,1024]{1,0:T(8,128)(2,1)S(1)}, u32[]{:S(2)}, u32[]{:S(2)}) collective-permute-start(bf16[1024,1024]{1,0:T(8,128)(2,1)} %get-tuple-element.379), channel_id=1, source_target_pairs={{0,4},{4,0},{1,5},{5,1},{2,6},{6,2},{3,7},{7,3},{8,12},{12,8},{9,1... | collective-permute-start | bytes 6291464 | tf_op jit(solution)/shard_map/ppermute | solution.py:467
  850.8 64.9 %collective-permute-start.60 = (bf16[384,512]{1,0:T(8,128)(2,1)S(1)}, bf16[384,512]{1,0:T(8,128)(2,1)S(1)}, u32[]{:S(2)}, u32[]{:S(2)}) collective-permute-start(bf16[384,512]{1,0:T(8,128)(2,1)S(1)} %get-tuple-element.473), channel_id=1, source_target_pairs={{0,16},{16,0},{1,17},{17,1},{2,18},{18,2},{3,19},{19,3},{4,20},{20... | collective-permute-start | bytes 1179656 | tf_op jit(solution)/shard_map/ppermute | solution.py:467
  880.1 208.6 %reduce-scatter.26.cloned.1.call-start = ((), (), s32[]{:S(2)}) async-start(), calls=%async_computation.26 | async-start | bytes 1966080 | tf_op jit(solution)/shard_map/reduce_scatter | solution.py:487
  915.7 60.2 %collective-permute-start.61 = (bf16[1024,1024]{1,0:T(8,128)(2,1)}, bf16[1024,1024]{1,0:T(8,128)(2,1)S(1)}, u32[]{:S(2)}, u32[]{:S(2)}) collective-permute-start(bf16[1024,1024]{1,0:T(8,128)(2,1)} %get-tuple-element.391), channel_id=1, source_target_pairs={{0,4},{4,0},{1,5},{5,1},{2,6},{6,2},{3,7},{7,3},{8,12},{12,8},{9,1... | collective-permute-start | bytes 6291464 | tf_op jit(solution)/shard_map/ppermute | solution.py:467
  981.4 114.1 %reduce-scatter.16.cloned.1.call-start = ((), (), s32[]{:S(2)}) async-start(), calls=%async_computation.21 | async-start | bytes 1310720 | tf_op jit(solution)/shard_map/reduce_scatter | solution.py:487
  1043.1 78.1 %reduce-scatter.12.cloned.1.call-start = ((), (), s32[]{:S(2)}) async-start(), calls=%async_computation.19 | async-start | bytes 1310720 | tf_op jit(solution)/shard_map/reduce_scatter | solution.py:487
  1080.1 60.0 %reduce-scatter.14.cloned.1.call-start = ((), (), s32[]{:S(2)}) async-start(), calls=%async_computation.20 | async-start | bytes 1310720 | tf_op jit(solution)/shard_map/reduce_scatter | solution.py:487
  1092.0 71.8 %collective-permute-start.74 = (bf16[1024,2048]{1,0:T(8,128)(2,1)}, bf16[1024,2048]{1,0:T(8,128)(2,1)}, u32[]{:S(2)}, u32[]{:S(2)}) collective-permute-start(bf16[1024,2048]{1,0:T(8,128)(2,1)} %to_model.12), channel_id=1, source_target_pairs={{0,8},{8,0},{1,9},{9,1},{2,10},{10,2},{3,11},{11,3},{4,12},{12,4},... | collective-permute-start | bytes 12582920 | tf_op jit(solution)/shard_map/ppermute | solution.py:467
  (143 other events, 2930.3 us)
Sparse Core Ops, SparseCore 0:
  10.2 30.6 all-gather.9
  42.4 27.4 all-gather.11
  71.4 27.4 all-gather.13
  100.9 36.5 all-gather.15
  157.8 37.4 all-gather.17
  196.7 35.9 all-gather.19
  234.3 35.9 all-gather.21
  271.8 114.2 all-gather.23
  388.2 113.5 all-gather.25
  504.6 108.9 reduce-scatter.9
  702.4 36.4 reduce-scatter.17
  768.0 36.7 reduce-scatter.21
  847.5 36.6 reduce-scatter.19
  886.9 34.2 reduce-scatter.23
  981.5 45.8 reduce-scatter.25
  1043.2 36.5 reduce-scatter.15
  1082.1 29.6 reduce-scatter.11
  1114.0 26.1 reduce-scatter.13

commit v4 on v3

--- a/solution.py
+++ b/solution.py
@@ -559,10 +559,10 @@
 
 
 def lane_mean(value):
-    ones = jnp.full((HEAD_SIZE, HEAD_SIZE), 1.0 / HEAD_SIZE, jnp.bfloat16)
+    ones = jnp.full((2 * HEAD_SIZE, HEAD_SIZE), 1.0 / HEAD_SIZE, jnp.bfloat16)
     high = value.astype(jnp.bfloat16)
     low = (value - high.astype(jnp.float32)).astype(jnp.bfloat16)
-    return matrix_product(high, ones) + matrix_product(low, ones)
+    return matrix_product(jnp.concatenate([high, low], axis=1), ones)
 
 
 def heads_kernel(count, raw_ref, cos_ref, sin_ref, gain_ref, out_ref):
@@ -653,15 +653,16 @@
     return jnp.concatenate([block[:, :HEAD_SIZE], block[:, HEAD_SIZE:]], axis=0)
 
 
-def key_bias(first_key, pair, parity):
-    cols = lax.broadcasted_iota(jnp.int32, (1, 2 * BLK), 1)
+def key_bias(first_key, pair, parity, queries=0):
+    shape = (1, 2 * BLK) if queries == 0 else (2 * BLK, 1)
+    cols = lax.broadcasted_iota(jnp.int32, shape, 1 - queries)
     block = 2 * pair + jnp.where(cols < BLK, parity, 1 - parity)
     return jnp.where(block >= first_key, 0.0, NEG_FILL)
 
 
-def last_bias(first_key, pair, parity):
-    rows = lax.broadcasted_iota(jnp.int32, (2 * BLK, 2 * BLK), 0)
-    cols = lax.broadcasted_iota(jnp.int32, (2 * BLK, 2 * BLK), 1)
+def last_bias(first_key, pair, parity, queries=0):
+    rows = lax.broadcasted_iota(jnp.int32, (2 * BLK, 2 * BLK), queries)
+    cols = lax.broadcasted_iota(jnp.int32, (2 * BLK, 2 * BLK), 1 - queries)
     far = (parity == 1) & (2 * pair >= first_key)
     own = lax.rem(cols, BLK) <= lax.rem(rows, BLK)
     far_bias = jnp.where(far, 0.0, NEG_FILL)
@@ -743,6 +744,13 @@
     )
 
 
+def row_sums(value):
+    ones = jnp.ones((8, 2 * HEAD_SIZE), jnp.bfloat16)
+    high = value.astype(jnp.bfloat16)
+    low = (value - high.astype(jnp.float32)).astype(jnp.bfloat16)
+    return dot_t(ones, jnp.concatenate([high, low], axis=1))[:1]
+
+
 def attend_back_kernel(
     group,
     info_ref,
@@ -776,7 +784,7 @@
                 [l_ref[rows, at : at + 1], l_ref[rows, at + 1 : at + 2]], axis=0
             )
             grad_b = (grad / total).astype(jnp.bfloat16)
-            inner = jnp.sum(grad_b.astype(jnp.float32) * attn, axis=1, keepdims=True)
+            inner = row_sums(grad_b.astype(jnp.float32) * attn)
             held.append((query, grad_b, inner))
 
         def step(m, bias, carry):
@@ -786,23 +794,23 @@
                 query, grad_b, inner = held[h]
                 key = pair_of(own_ref, far_ref, m, h * GROUP_WIDTH)
                 value = pair_of(own_ref, far_ref, m, h * GROUP_WIDTH + HEAD_SIZE)
-                expo = jnp.exp2(dot_t(query, key) * (SCALE * LOG2_E) + bias)
-                d_score = (expo * (dot_t(grad_b, value) - inner)).astype(jnp.bfloat16)
-                d_key = dot_rows(d_score, query)
-                d_value = dot_rows(expo.astype(jnp.bfloat16), grad_b)
+                expo = jnp.exp2(dot_t(key, query) * (SCALE * LOG2_E) + bias)
+                d_score = (expo * (dot_t(value, grad_b) - inner)).astype(jnp.bfloat16)
+                d_key = matrix_product(d_score, query)
+                d_value = matrix_product(expo.astype(jnp.bfloat16), grad_b)
                 kacc_ref[h, 0, at, :] += d_key[:BLK]
                 kacc_ref[h, 1, at, :] += d_key[BLK:]
                 vacc_ref[h, 0, at, :] += d_value[:BLK]
                 vacc_ref[h, 1, at, :] += d_value[BLK:]
-                out.append(carry[h] + matrix_product(d_score, key))
+                out.append(carry[h] + dot_rows(d_score, key))
             return tuple(out)
 
         empty = jnp.zeros((2 * BLK, HEAD_SIZE), jnp.float32)
-        carry = step(j, last_bias(first_key, j, parity), (empty,) * TOGETHER)
+        carry = step(j, last_bias(first_key, j, parity, 1), (empty,) * TOGETHER)
         carry = lax.fori_loop(
             lax.div(first_key, 2),
             j,
-            lambda m, c: step(m, key_bias(first_key, m, parity), c),
+            lambda m, c: step(m, key_bias(first_key, m, parity, 1), c),
             carry,
         )
         for h, dq in enumerate(carry):
@@ -844,7 +852,7 @@
 
 
 HIDDEN_TILE = 512
-ROW_STEP = 512
+ROW_STEP = 1024
 
 
 def row_steps(*refs):
@@ -915,6 +923,7 @@
 
 
 MODEL_STEP = 512
+ROWS_STEP = 512
 
 
 def left_parts(left_refs, rights):
@@ -924,9 +933,8 @@
     return [left_refs[0][k * rows : (k + 1) * rows, :].T for k in range(rights)]
 
 
-def weight_cols_kernel(lefts, rights, *refs):
-    left_refs, right_refs, out_refs = refs[:lefts], refs[lefts : lefts + rights], refs[lefts + rights :]
-    parts = left_parts(left_refs, rights)
+def weight_cols_step(left_ref, right_refs, out_refs):
+    parts = left_parts([left_ref], len(right_refs))
     for first in range(0, right_refs[0].shape[1], MODEL_STEP):
         cols = slice(first, first + MODEL_STEP)
         term = matrix_product(parts[0], right_refs[0][:, cols])
@@ -942,38 +950,87 @@
             begin = end
 
 
-def weight_cols(lefts, rights, first, widths, after=()):
-    rows, hidden = lefts[0].shape
-    width = sum(widths)
+def weight_cols_kernel(steps, counts, *refs):
+    ins, outs = refs[: 3 * len(counts)], refs[3 * len(counts) :]
+    begin = 0
+    for i, count in enumerate(counts):
+        out_refs = outs[begin : begin + count]
+        begin += count
+
+        @pl.when(pl.program_id(0) // steps == i)
+        def _():
+            weight_cols_step(ins[3 * i], ins[3 * i + 1 : 3 * i + 3], out_refs)
+
+
+def weight_cols(*jobs, after=()):
+    rows, hidden = jobs[0][0].shape
+    steps = hidden // HIDDEN_TILE
+    inputs, in_specs, out_specs, out_shape = [], [], [], []
+    for i, (left, rights, widths) in enumerate(jobs):
+
+        def at(j, i=i):
+            return jnp.clip(j - i * steps, 0, steps - 1)
+
+        inputs += [left, *rights]
+        in_specs += [pl.BlockSpec((rows, HIDDEN_TILE), lambda j, at=at: (0, at(j)))]
+        in_specs += [
+            pl.BlockSpec(r.shape, lambda j: (0, 0), pipeline_mode=pl.Buffered(1)) for r in rights
+        ]
+        out_specs += [pl.BlockSpec((HIDDEN_TILE, w), lambda j, at=at: (at(j), 0)) for w in widths]
+        out_shape += [jax.ShapeDtypeStruct((hidden, w), jnp.bfloat16) for w in widths]
     return call(
-        functools.partial(weight_cols_kernel, len(lefts), len(rights)),
-        [*lefts, *rights],
-        [pl.BlockSpec((rows, HIDDEN_TILE), lambda j: (0, j))] * len(lefts)
-        + [pl.BlockSpec((rights[0].shape[0], width), lambda j: (0, first // width))] * len(rights),
-        [pl.BlockSpec((HIDDEN_TILE, w), lambda j: (j, 0)) for w in widths],
-        [jax.ShapeDtypeStruct((hidden, w), jnp.bfloat16) for w in widths],
-        (hidden // HIDDEN_TILE,),
+        functools.partial(weight_cols_kernel, steps, tuple(len(job[2]) for job in jobs)),
+        inputs,
+        in_specs,
+        out_specs,
+        out_shape,
+        (steps * len(jobs),),
         after,
         name="weight_cols",
     )
 
 
+def add_halves_kernel(x_ref, y_ref, a_ref, b_ref, x_out, y_out):
+    x_out[...] = x_ref[...] + b_ref[...]
+    y_out[...] = y_ref[...] + a_ref[...]
+
+
+def add_halves(along_x, along_y, from_a, from_b):
+    rows, width = along_x.shape
+    tile = rows // 2
+    half = width // 2
+    left = pl.BlockSpec((tile, half), lambda i: (i, 0))
+    right = pl.BlockSpec((tile, half), lambda i: (i, 1))
+    shape = jax.ShapeDtypeStruct((rows, width), along_x.dtype)
+    return call(
+        add_halves_kernel,
+        [along_x, along_y, from_a, from_b],
+        [right, left, left, left],
+        [right, left],
+        [shape, shape],
+        (rows // tile,),
+        input_output_aliases={0: 0, 1: 1},
+        name="add_halves",
+    )
+
+
 def weight_rows_kernel(lefts, rights, *refs):
-    left_refs, right_refs, out_refs = refs[:lefts], refs[lefts : lefts + rights], refs[lefts + rights :]
-    parts = left_parts(left_refs, rights)
+    left_refs, right_refs = refs[:lefts], refs[lefts : lefts + rights]
+    out_refs, turned_ref = refs[lefts + rights : -1], refs[-1]
+    rows = right_refs[0].shape[0]
+
+    @pl.when(pl.program_id(0) == 0)
+    def _():
+        for k, ref in enumerate(left_refs):
+            turned_ref[:, k * rows : (k + 1) * rows] = ref[...].T
+
     span = out_refs[0].shape[0]
-    inside = HIDDEN_TILE // span
-    for first in range(0, right_refs[0].shape[1], MODEL_STEP):
-        cols = slice(first, first + MODEL_STEP)
-        term = matrix_product(parts[0], right_refs[0][:, cols])
-        for part, ref in zip(parts[1:], right_refs[1:]):
-            term = term + matrix_product(part, ref[:, cols])
-        term = term.astype(jnp.bfloat16)
-        for i, out_ref in enumerate(out_refs):
-
-            @pl.when(pl.program_id(0) == i // inside)
-            def _():
-                out_ref[:, cols] = term[(i % inside) * span : (i % inside + 1) * span]
+    term = matrix_product(turned_ref[:, :rows], right_refs[0][...])
+    for k in range(1, rights):
+        term = term + matrix_product(turned_ref[:, k * rows : (k + 1) * rows], right_refs[k][...])
+    term = term.astype(jnp.bfloat16)
+    for i, out_ref in enumerate(out_refs):
+        out_ref[...] = term[i * span : (i + 1) * span]
 
 
 def weight_rows(lefts, rights, count, after=()):
@@ -983,12 +1040,15 @@
     return call(
         functools.partial(weight_rows_kernel, len(lefts), len(rights)),
         [*lefts, *rights],
-        [pl.BlockSpec((rows, HIDDEN_TILE), lambda j: (0, j))] * len(lefts)
-        + [pl.BlockSpec((rights[0].shape[0], width), lambda j: (0, 0))] * len(rights),
-        [pl.BlockSpec((hidden // count, width), lambda j: (0, 0))] * count,
+        [
+            pl.BlockSpec((rows, hidden), lambda j: (0, 0), pipeline_mode=pl.Buffered(1))
+        ] * len(lefts)
+        + [pl.BlockSpec((rows, ROWS_STEP), lambda j: (0, j))] * len(rights),
+        [pl.BlockSpec((hidden // count, ROWS_STEP), lambda j: (0, j))] * count,
         [shape] * count,
-        (hidden // HIDDEN_TILE,),
+        (width // ROWS_STEP,),
         after,
+        scratch_shapes=[pltpu.VMEM((hidden, len(lefts) * rows), jnp.bfloat16)],
         name="weight_rows",
     )
 
@@ -1023,7 +1083,7 @@
     hidden = lefts[0].shape[1]
     flat = [w for pieces in weights for w in pieces]
     width = sum(w.shape[1] for w in weights[0])
-    tile = HIDDEN_TILE if len(lefts) <= 2 else HIDDEN_TILE // 2
+    tile = HIDDEN_TILE // 2
     return call(
         functools.partial(to_model_kernel, tuple(len(pieces) for pieces in weights)),
         [*lefts, *flat],
@@ -1048,7 +1108,7 @@
         + own_ref[...].astype(jnp.float32)
         + there_ref[...].astype(jnp.float32)
     )
-    resid_ref[...] = resid
+    resid_ref[...] = resid.astype(jnp.bfloat16)
     scale = lax.rsqrt(jnp.mean(resid * resid, axis=-1, keepdims=True) + EPS_NORM)
     normed = (resid * scale * gain_ref[...]).astype(jnp.bfloat16)
     block = normed.shape[1] // order_ref.shape[0]
@@ -1066,7 +1126,7 @@
         [tile, tile, tile, pl.BlockSpec((1, width), lambda i, o: (0, 0))],
         [tile, tile],
         [
-            jax.ShapeDtypeStruct((rows, width), jnp.float32),
+            jax.ShapeDtypeStruct((rows, width), jnp.bfloat16),
             jax.ShapeDtypeStruct((rows, width), jnp.bfloat16),
         ],
         (rows // NORM_TILE,),
@@ -1158,10 +1218,9 @@
     low = up_0.shape[0] // 2
     out_0 = gather_z(w_out)
     dlo_0 = gather_z(down_0[:low])
-    kvw_0, up_x, up_y = sync(kvw_0, up_x, up_y)
     kvw_x, kvw_y = swap(kvw_0, "x"), swap(kvw_0, "y")
     middle = kvw_0.shape[0] // 2
-    kvw_x, kvw_y, qw_0 = sync(kvw_x, kvw_y, qw_0)
+    kvw_x, kvw_y, qw_0, up_x, up_y = sync(kvw_x, kvw_y, qw_0, up_x, up_y)
     kvw_ca, kvw_cb = swap(kvw_y[:middle], "x"), swap(kvw_x[middle:], "y")
     qw_x, qw_y = swap(qw_0, "x"), swap(qw_0, "y")
     kvw_ca, kvw_cb, qw_x, qw_y, out_0 = sync(kvw_ca, kvw_cb, qw_x, qw_y, out_0)
@@ -1206,127 +1265,137 @@
     def stacked(first, second):
         return jnp.concatenate([first, second], axis=0)
 
-    inputs = tokens.astype(f32)
+    inputs = after(tokens, up_0).astype(f32)
     normed1 = rms_parts(inputs, norm1_gain)[0].astype(bf16)
     normed1 = [normed1, swap(normed1, "c")]
     dy_own = (valid * cotangent.astype(f32)).astype(bf16)
 
+    def project(group, rows_in, weight, gain, count, wait=()):
+        raw = to_hidden([rows_in], [weight], f32, wait)
+        return raw, make_heads(group, raw, cos_tab, sin_tab, gain, count)
+
     normed1[0], kv_w = sync(normed1[0], kv_w)
-    kv_raw = [to_hidden([normed1[0]], [kv_w], f32)]
-    kv_raw.append(to_hidden([normed1[1]], [kv_w], f32, [kv_raw[0]]))
-    kv = [make_heads(g, kv_raw[g], cos_tab, sin_tab, key_gain, 2, [kv_raw[1]]) for g in range(2)]
-    kv[0], kv[1], qw_ca, qw_cb, out_x, out_y, up_y, dy_own, normed1[0], gate_0, glo_in = sync(
-        *kv, qw_ca, qw_cb, out_x, out_y, up_y, dy_own, normed1[0], gate_0, gate_0[:low]
-    )
-    kv_far0, out_c, up_c = swap(kv[0], "y"), swap(out_y, "x"), swap(up_y, "x")
+    kv_raw0, kv0 = project(0, normed1[0], kv_w, key_gain, 2)
+    kv0, qw_ca, qw_cb, out_x, out_y, up_y, normed1[0], gate_0, glo_in = sync(
+        kv0, qw_ca, qw_cb, out_x, out_y, up_y, normed1[0], gate_0, gate_0[:low]
+    )
+    kv_far0, out_c, up_c = swap(kv0, "y"), swap(out_y, "x"), swap(up_y, "x")
     glo_0 = gather_z(glo_in)
     dhi_0, ghi_0 = gather_z(down_0[low:]), gather_z(gate_0[low:])
     q_w = jnp.concatenate([qw_0, qw_x, qw_y, qw_ca, qw_cb], axis=0)
-    q_raw = [to_hidden([normed1[0]], [q_w], f32)]
-    q_raw.append(to_hidden([normed1[1]], [q_w], f32, [q_raw[0]]))
-    query = [
-        make_heads(g, q_raw[g], cos_tab, sin_tab, query_gain, 1, [q_raw[1]]) for g in range(2)
-    ]
-    dy = [reorder(dy_own, order, query)]
-    kv_far0, out_c, up_c, dlo_0, dy[0] = sync(kv_far0, out_c, up_c, dlo_0, dy[0])
+    q_raw0, query0 = project(0, normed1[0], q_w, query_gain, 1)
+    kv_raw1, kv1 = project(1, normed1[1], kv_w, key_gain, 2, [query0])
+    kv_far0, out_c, up_c, dlo_0, kv1, normed1[1], dy_own = sync(
+        kv_far0, out_c, up_c, dlo_0, kv1, normed1[1], dy_own
+    )
     dlo_x, dlo_y = swap(dlo_0, "x"), swap(dlo_0, "y")
-    dy.append(swap(dy[0], "c"))
     up_in = jnp.concatenate([up_0, up_x, up_y, up_c], axis=1)
     ulo, uhi = gather_z(up_in[:low]), gather_z(up_in[low:])
-    attn0, totals0 = attend(0, info, query[0], kv[0], kv_far0)
+    attn0, totals0 = attend(0, info, query0, kv0, kv_far0)
     out_w = jnp.concatenate([out_0, out_x, out_y, out_c], axis=0)
-    attn0, out_w, dlo_x, dlo_y, kv_1 = sync(attn0, out_w, dlo_x, dlo_y, kv[1])
+    attn0, out_w, dlo_x, dlo_y, kv_1, normed1[1] = sync(
+        attn0, out_w, dlo_x, dlo_y, kv1, normed1[1]
+    )
+    q_raw1, query1 = project(1, normed1[1], q_w, query_gain, 1)
+    dy = [reorder(dy_own, order, [query1])]
+    dy.append(swap(dy[0], "c"))
+    query, q_raw = [query0, query1], [q_raw0, q_raw1]
+    kv, kv_raw = [kv0, kv1], [kv_raw0, kv_raw1]
     kv_far1, dlo_c = swap(kv_1, "y"), swap(dlo_y, "x")
-    kv_far1, dlo_c, glo_0 = sync(kv_far1, dlo_c, glo_0)
+    kv_far1, dlo_c, glo_0, query[1], dy[0] = sync(kv_far1, dlo_c, glo_0, query[1], dy[0])
     glo_x, glo_y = swap(glo_0, "x"), swap(glo_0, "y")
     attn1, totals1 = attend(1, info, query[1], kv[1], kv_far1)
-    attn1, glo_x, glo_y, glo_0 = sync(attn1, glo_x, glo_y, glo_0)
+    attn1, glo_x, glo_y, glo_0, dhi_0 = sync(attn1, glo_x, glo_y, glo_0, dhi_0)
     glo_ca, glo_cb = swap(glo_y[:, :eighth], "x"), swap(glo_x[:, eighth:], "y")
+    dhi_x, dhi_y = swap(dhi_0, "x"), swap(dhi_0, "y")
     same = jnp.arange(8, dtype=jnp.int32)
     out_term = to_model([attn1], [[out_w]], same, 0, rows)
     out_there = swap(out_term, "c")
     out_here = to_model([attn0], [[out_w]], same, 0, rows, [out_term])
     dlo = [dlo_0, dlo_x, dlo_y, dlo_c]
     d_act_lo = to_hidden(dy, dlo, bf16, [out_here])
-    out_here, d_act_lo, glo_ca, glo_cb, dhi_0, ghi_0 = sync(
-        out_here, d_act_lo, glo_ca, glo_cb, dhi_0, ghi_0
-    )
-    dhi_x, dhi_y = swap(dhi_0, "x"), swap(dhi_0, "y")
+    resid, normed2_own = resid_norm(
+        tokens, out_here, out_there, norm2_gain, order_back, [d_act_lo]
+    )
+    normed2_own, glo_ca, glo_cb, dhi_x, dhi_y, ghi_0 = sync(
+        normed2_own, glo_ca, glo_cb, dhi_x, dhi_y, ghi_0
+    )
+    normed2 = [normed2_own, swap(normed2_own, "c")]
     ghi_x, ghi_y = swap(ghi_0, "x"), swap(ghi_0, "y")
-    resid, normed2_own = resid_norm(tokens, out_here, out_there, norm2_gain, order_back)
-    normed2 = [normed2_own, swap(normed2_own, "c")]
     glo = [glo_0, glo_x, glo_y, glo_ca, glo_cb]
     act_lo, gg_lo, ug_lo = ffn(normed2, glo, ulo, d_act_lo)
-    act_lo, dhi_x, dhi_y, ghi_x, ghi_y = sync(act_lo, dhi_x, dhi_y, ghi_x, ghi_y)
+    act_lo, dhi_y, ghi_x, ghi_y = sync(act_lo, dhi_y, ghi_x, ghi_y)
     dhi_c, ghi_c = swap(dhi_y, "x"), swap(ghi_x, "y")
-    dhi = [dhi_0, dhi_x, dhi_y, dhi_c]
 
     widths = [fourth, fourth, fourth, eighth, eighth]
-
-    def corner_add(along_x, along_y, from_a, from_b):
-        return (
-            jnp.concatenate([along_x[:, :eighth], along_x[:, eighth:] + from_b], axis=1),
-            jnp.concatenate([along_y[:, :eighth] + from_a, along_y[:, eighth:]], axis=1),
-        )
-
-    (dlo_grad,) = weight_cols([act_lo], dy, 0, [width])
+    dlo_grad, gl_0, gl_x, gl_y, gl_ca, gl_cb = weight_cols(
+        (act_lo, dy, [width]), (gg_lo, normed2, widths)
+    )
+    dlo_grad, gl_ca, gl_cb, dhi_c, ghi_c, ug_lo = sync(
+        dlo_grad, gl_ca, gl_cb, dhi_c, ghi_c, ug_lo
+    )
     dlo_sum = scatter_z(dlo_grad)
-    gl_0, gl_x, gl_y, gl_ca, gl_cb = weight_cols([gg_lo], normed2, 0, widths, [dlo_grad])
-    gl_ca, gl_cb, ghi_c, dhi_c = sync(gl_ca, gl_cb, ghi_c, dhi_c)
     from_a, from_b = swap(gl_ca, "x"), swap(gl_cb, "y")
-    ul_0, ul_x, ul_y, ul_ca, ul_cb = weight_cols([ug_lo], normed2, 0, widths, [gl_0])
-    d_act_hi = to_hidden(dy, dhi, bf16, [ul_0])
-    ghi = [ghi_0, ghi_x, ghi_y, ghi_c]
-    gl_x, gl_y, from_a, from_b, ul_ca, ul_cb, d_act_hi = sync(
-        gl_x, gl_y, from_a, from_b, ul_ca, ul_cb, d_act_hi
-    )
-    gl_x, gl_y = corner_add(gl_x, gl_y, from_a, from_b)
+    ul_0, ul_x, ul_y, ul_ca, ul_cb = weight_cols((ug_lo, normed2, widths))
+    dhi, ghi = [dhi_0, dhi_x, dhi_y, dhi_c], [ghi_0, ghi_x, ghi_y, ghi_c]
+    gl_x, gl_y, from_a, from_b, ul_ca, ul_cb, dhi[3] = sync(
+        gl_x, gl_y, from_a, from_b, ul_ca, ul_cb, dhi[3]
+    )
+    from_ua, from_ub = swap(ul_ca, "x"), swap(ul_cb, "y")
+    gl_x, gl_y = add_halves(gl_x, gl_y, from_a, from_b)
+    d_act_hi = to_hidden(dy, dhi)
+    gl_x, gl_y, ul_x, ul_y, from_ua, from_ub, d_act_hi = sync(
+        gl_x, gl_y, ul_x, ul_y, from_ua, from_ub, d_act_hi
+    )
     got_x, got_y = swap(gl_x, "x"), swap(gl_y, "y")
-    from_a, from_b = swap(ul_ca, "x"), swap(ul_cb, "y")
+    ul_x, ul_y = add_halves(ul_x, ul_y, from_ua, from_ub)
     act_hi, gg_hi, ug_hi = ffn(normed2, ghi, uhi, d_act_hi)
-    dh_0, dh_x, dh_y, dh_ca, dh_cb = weight_cols([act_hi], dy, 0, widths)
-    gl_0, got_x, got_y, ul_x, ul_y, from_a, from_b, dh_0, gg_hi = sync(
-        gl_0, got_x, got_y, ul_x, ul_y, from_a, from_b, dh_0, gg_hi
-    )
-    ul_x, ul_y = corner_add(ul_x, ul_y, from_a, from_b)
+    gl_0, got_x, got_y, ul_x, ul_y, act_hi, gg_hi, ug_hi = sync(
+        gl_0, got_x, got_y, ul_x, ul_y, act_hi, gg_hi, ug_hi
+    )
+    got_ux, got_uy = swap(ul_x, "x"), swap(ul_y, "y")
     glo_near = gl_0 + got_x + got_y
-    got_x, got_y = swap(ul_x, "x"), swap(ul_y, "y")
     glo_sum = scatter_z(glo_near)
-    gh_0, gh_x, gh_y, gh_ca, gh_cb = weight_cols([gg_hi], normed2, 0, widths, [ul_x, ul_y])
-    uh_0, uh_x, uh_y, uh_ca, uh_cb = weight_cols([ug_hi], normed2, 0, widths, [gh_0])
-    ul_0, got_x, got_y, dh_ca, dh_cb, gh_ca, gh_cb, uh_0, gg_hi = sync(
-        ul_0, got_x, got_y, dh_ca, dh_cb, gh_ca, gh_cb, uh_0, gg_hi
-    )
-    from_da, from_db = swap(dh_ca, "x"), swap(dh_cb, "y")
-    from_ga, from_gb = swap(gh_ca, "x"), swap(gh_cb, "y")
-    ulo_near = ul_0 + got_x + got_y
+    dh_0, dh_x, dh_y, dh_ca, dh_cb, gh_0, gh_x, gh_y, gh_ca, gh_cb = weight_cols(
+        (act_hi, dy, widths), (gg_hi, normed2, widths), after=[glo_near]
+    )
+    ul_0, got_ux, got_uy, dh_ca, dh_cb, ug_hi = sync(ul_0, got_ux, got_uy, dh_ca, dh_cb, ug_hi)
+    from_a, from_b = swap(dh_ca, "x"), swap(dh_cb, "y")
+    ulo_near = ul_0 + got_ux + got_uy
     ulo_sum = scatter_z(ulo_near)
+    uh_0, uh_x, uh_y, uh_ca, uh_cb = weight_cols((ug_hi, normed2, widths), after=[ulo_near])
+    dh_x, dh_y, from_a, from_b, gg_hi, uh_0 = sync(dh_x, dh_y, from_a, from_b, gg_hi, uh_0)
+    dh_x, dh_y = add_halves(dh_x, dh_y, from_a, from_b)
+    dh_x, dh_y, gg_hi = sync(dh_x, dh_y, gg_hi)
+    got_x, got_y = swap(dh_x, "x"), swap(dh_y, "y")
     grads = [gg_lo, ug_lo, gg_hi, ug_hi]
     both_w = [glo, [ulo], ghi, [uhi]]
-    there = to_model(grads, both_w, order, 1, rows, [ulo_near])
-    dh_x, dh_y, from_da, from_db, gh_x, gh_y, from_ga, from_gb, uh_ca, uh_cb, there = sync(
-        dh_x, dh_y, from_da, from_db, gh_x, gh_y, from_ga, from_gb, uh_ca, uh_cb, there
+    there = to_model(grads, both_w, order, 1, rows)
+    dh_0, got_x, got_y, gh_ca, gh_cb, uh_ca, uh_cb, there, gg_hi = sync(
+        dh_0, got_x, got_y, gh_ca, gh_cb, uh_ca, uh_cb, there, gg_hi
     )
     normed2_there = swap(there, "c")
-    dh_x, dh_y = corner_add(dh_x, dh_y, from_da, from_db)
-    gh_x, gh_y = corner_add(gh_x, gh_y, from_ga, from_gb)
-    got_x, got_y = swap(dh_x, "x"), swap(dh_y, "y")
-    from_a, from_b = swap(uh_ca, "x"), swap(uh_cb, "y")
-    grad_own = to_model(grads, both_w, order, 0, rows, [dh_x, dh_y, gh_x, gh_y])
-    resid_grad, resid_here, gain2_sum = norm_return(
-        resid, dy_own, grad_own, normed2_there, norm2_gain, (f32, bf16)
-    )
-    dh_0, got_x, got_y, uh_x, uh_y, from_a, from_b, resid_here, gh_x, gh_y = sync(
-        dh_0, got_x, got_y, uh_x, uh_y, from_a, from_b, resid_here, gh_x, gh_y
-    )
-    resid_there = swap(resid_here, "c")
-    uh_x, uh_y = corner_add(uh_x, uh_y, from_a, from_b)
+    from_ga, from_gb = swap(gh_ca, "x"), swap(gh_cb, "y")
+    from_ua, from_ub = swap(uh_ca, "x"), swap(uh_cb, "y")
     dhi_near = dh_0 + got_x + got_y
+    dhi_sum = scatter_z(dhi_near)
+    grads = [gg_lo, ug_lo, gg_hi, ug_hi]
+    grad_own = to_model(grads, both_w, order, 0, rows, [dhi_near])
+    gh_x, gh_y, from_ga, from_gb, uh_x, uh_y, from_ua, from_ub, grad_own = sync(
+        gh_x, gh_y, from_ga, from_gb, uh_x, uh_y, from_ua, from_ub, grad_own
+    )
+    gh_x, gh_y = add_halves(gh_x, gh_y, from_ga, from_gb)
+    uh_x, uh_y = add_halves(uh_x, uh_y, from_ua, from_ub)
+    gh_x, gh_y, uh_x, uh_y, grad_own = sync(gh_x, gh_y, uh_x, uh_y, grad_own)
     got_x, got_y = swap(gh_x, "x"), swap(gh_y, "y")
     got_ux, got_uy = swap(uh_x, "x"), swap(uh_y, "y")
-    dhi_sum = scatter_z(dhi_near)
-
-    d_attn0 = to_hidden([resid_here], [out_w], bf16, [uh_x, uh_y, dhi_near])
+    resid_here, gain2_sum = norm_return(
+        resid, dy_own, grad_own, normed2_there, norm2_gain, (bf16,)
+    )
+    resid_first = resid_here
+    resid_there = swap(resid_here, "c")
+
+    d_attn0 = to_hidden([resid_here], [out_w])
     dq0, dkv0, dkv0_far = attend_back(0, info, query[0], d_attn0, attn0, totals0, kv[0], kv_far0)
     gh_0, got_x, got_y, uh_0, got_ux, got_uy, resid_there, dkv0_far, dlo_sum = sync(
         gh_0, got_x, got_y, uh_0, got_ux, got_uy, resid_there, dkv0_far, dlo_sum
@@ -1356,9 +1425,11 @@
     q_grad = [q_grad[0][0], q_grad[1][0]]
     w_0, w_x, w_y, w_c = weight_rows(q_grad, normed1, 4)
     mixed_term = to_model([act_lo, act_hi], [dlo, dhi], order, 1, rows, [w_0])
-    dkv1_back, from_o, w_c, mixed_term, o_x, o_y, dl_y = sync(
-        dkv1_back, from_o, w_c, mixed_term, o_x, o_y, dl_y
-    )
+    dkv1_back, from_o, w_c, mixed_term, o_x, o_y, dl_y, got_lx, gate_sum, up_sum = sync(
+        dkv1_back, from_o, w_c, mixed_term, o_x, o_y, dl_y, got_lx, glo_sum, ulo_sum
+    )
+    glo_sum, ulo_sum = gate_sum, up_sum
+    got_ly = swap(dl_y + from_l, "y")
 
     def halves(array):
         span = array.shape[0] // 2
@@ -1378,25 +1449,23 @@
     k_gains = kv_grad[0][1] + kv_grad[1][1]
     kv_grad = [kv_grad[0][0], kv_grad[1][0]]
     kv_0, kv_x, kv_y, kv_c = weight_rows(kv_grad, normed1, 4)
-    kv_c, from_wa, from_wb, got_ox, got_oy, w_x, w_y, kv_grad[1] = sync(
-        kv_c, from_wa, from_wb, got_ox, got_oy, w_x, w_y, kv_grad[1]
+    kv_c, from_wa, from_wb, got_ox, got_oy, w_x, w_y, kv_grad[1], got_ly = sync(
+        kv_c, from_wa, from_wb, got_ox, got_oy, w_x, w_y, kv_grad[1], got_ly
     )
     kv_a, kv_b = halves(kv_c)
     from_a, from_b = swap(kv_a, "x"), swap(kv_b, "y")
     w_x, w_y = corner_rows(w_x, w_y, from_wa, from_wb)
     got_wx, got_wy = swap(w_x, "x"), swap(w_y, "y")
-    term_there = to_model([q_grad[1], kv_grad[1]], [[q_w], [kv_w]], same, 0, rows)
     o_near = o_0 + got_ox + got_oy
-    kv_x, kv_y, from_a, from_b, term_there, o_near = sync(
-        kv_x, kv_y, from_a, from_b, term_there, o_near
-    )
     o_sum = scatter_z(o_near)
+    term_there = to_model([q_grad[1], kv_grad[1]], [[q_w], [kv_w]], same, 0, rows, [o_near])
+    kv_x, kv_y, from_a, from_b, term_there = sync(kv_x, kv_y, from_a, from_b, term_there)
     normed1_there = swap(term_there, "c")
     kv_x, kv_y = corner_rows(kv_x, kv_y, from_a, from_b)
     got_kx, got_ky = swap(kv_x, "x"), swap(kv_y, "y")
     term_own = to_model([q_grad[0], kv_grad[0]], [[q_w], [kv_w]], same, 0, rows, [kv_x, kv_y])
-    w_0, got_wx, got_wy, kv_0, got_kx, got_ky, term_own, dl_y = sync(
-        w_0, got_wx, got_wy, kv_0, got_kx, got_ky, term_own, dl_y + from_l
+    w_0, got_wx, got_wy, kv_0, got_kx, got_ky, term_own = sync(
+        w_0, got_wx, got_wy, kv_0, got_kx, got_ky, term_own
     )
     kv_near = kv_0 + got_kx + got_ky
     kv_sum = scatter_z(
@@ -1404,24 +1473,28 @@
     )
     w_near = w_0 + got_wx + got_wy
     w_sum = scatter_z(w_near)
-    got_ly = swap(dl_y, "y")
     tokens_grad, gain1_sum = norm_return(
-        tokens, resid_grad, term_own, normed1_there, norm1_gain, (f32,), [kv_near, w_near]
+        tokens, resid_first, term_own, normed1_there, norm1_gain, (f32,), [kv_near, w_near]
     )
     gain1_part, gain2_part = gain1_sum[0], gain2_sum[0]
+    gains = jnp.concatenate([gain1_part, gain2_part, q_gains[0], k_gains[0]])[None, :]
+    gains = gains + swap(gains, "c")
+    gains, act_hi = sync(gains, act_hi)
+    gains_x = swap(gains, "x")
     mixed_own = to_model([act_lo, act_hi], [dlo, dhi], order, 0, rows, [gain1_sum])
     mixed_there = swap(mixed_term, "c")
+    gains, gains_x, mixed_own = sync(gains, gains_x, mixed_own)
+    gains = gains + gains_x
+    gains = gains + swap(gains, "y")
+    gains, mixed_own, kv_sum, w_sum, o_sum = sync(gains, mixed_own, kv_sum, w_sum, o_sum)
+    gains_z = lax.ppermute(gains, "z", [(i, i ^ 1) for i in range(4)])
     output = (
-        valid * (resid + mixed_own.astype(f32) + mixed_there.astype(f32))
+        valid * (resid.astype(f32) + mixed_own.astype(f32) + mixed_there.astype(f32))
     ).astype(bf16)
+    gains, gains_z, output = sync(gains, gains_z, output)
+    gains = gains + gains_z
+    gains = (gains + lax.ppermute(gains, "z", [(i, i ^ 2) for i in range(4)]))[0]
     dlo_sum = dl_0 + got_lx + got_ly
-
-    gains = jnp.concatenate([gain1_part, gain2_part, q_gains[0], k_gains[0]])[None, :]
-    for axis in ("c", "x", "y"):
-        gains = gains + swap(gains, axis)
-    for step in (1, 2):
-        gains = gains + lax.ppermute(gains, "z", [(i, i ^ step) for i in range(4)])
-    gains = gains[0]
 
     gate_sum, up_sum, down_sum = (
         jnp.concatenate(pair, axis=0)

time: 1190 us -> 1120 us (0.941)
  Pallas kernels: 739 us -> 713 us
  other arithmetic: 98.2 us -> 77.3 us
    ppermute x81, waiting for transfers between devices: 154 us -> 108 us  [swap(): return lax.ppermute(array, axis, SWAP)]
    all_gather x9, waiting for transfers between devices: 12.8 us -> 46.2 us  [gather_z(): return lax.all_gather(array, 'z', axis=0, tiled=True)]
    pallas_call x43 -> x46, Pallas kernels: 739 us -> 713 us  [call(): pl.pallas_call(body, grid_spec=pltpu.PrefetchScalarGridSpec(num_scalar_pr...]
    unnamed x163 -> x147, local copies, waits for them, and re-layouts: 32.6 us -> 27.7 us
  transfers between devices with their start and end apart: 101 -> 101, of which waited for: 20 -> 25; matrix products, arithmetic and copies ran while one was open for 12% -> 11% of each run, Pallas kernels for 63% -> 64%
where the time goes in v4:
time: 1120 us; the launch traced here: 1110 us
  Pallas kernels  713 us (64%)
  waiting for transfers between devices  171 us (15%)
  starting transfers between devices  78.7 us (7%)
  other arithmetic  77.3 us (7%)
  local copies, waits for them, and re-layouts  54.6 us (5%)
  between operations  15.7 us (1%)
    pallas_call x46, Pallas kernels, call(): pl.pallas_call(body, grid_spec=pltpu.PrefetchScalarGridSpec(num_scalar_pr...  713 us
    ppermute x81, waiting for transfers between devices, swap(): return lax.ppermute(array, axis, SWAP)  108 us
    ppermute x81, starting transfers between devices, swap(): return lax.ppermute(array, axis, SWAP)  75.4 us
    all_gather x9, waiting for transfers between devices, gather_z(): return lax.all_gather(array, 'z', axis=0, tiled=True)  46.2 us
    unnamed x147, local copies, waits for them, and re-layouts  27.7 us
  transfers between devices with their start and end apart: 101, of which 25 were waited for; matrix products, arithmetic and copies ran while one was open for 11% of the time, Pallas kernels for 64%

profile of v4, /device:TPU:0, one launch (start us, length us, event | category | flops | bytes accessed | tf_op | source)
XLA Modules:
  0.0 1110.4 jit_solution(10895069619133366649)
XLA Ops:
  50.0 19.8 %all-gather.12.cloned.1.call-done = bf16[256,2048]{1,0:T(8,128)(2,1)} async-done(((bf16[64,2048]{1,0:T(8,128)(2,1)}), bf16[256,2048]{1,0:T(8,128)(2,1)}) %all-gather.12.cloned.1.call-update) | async-done | bytes 1048592 | tf_op jit(solution)/shard_map/all_gather | solution.py:483
  79.4 19.5 %all-gather.14.cloned.1.call-done = bf16[256,2048]{1,0:T(8,128)(2,1)} async-done(((bf16[64,2048]{1,0:T(8,128)(2,1)}), bf16[256,2048]{1,0:T(8,128)(2,1)}) %all-gather.14.cloned.1.call-update) | async-done | bytes 1048592 | tf_op jit(solution)/shard_map/all_gather | solution.py:483
  200.2 22.3 %attend.2 = (bf16[1024,1024]{1,0:T(8,128)(2,1)}, f32[1024,512]{1,0:T(8,128)}) custom-call(s32[2,9]{1,0:T(2,128)} %pad_add_fusion.refs_0_, bf16[1024,1024]{1,0:T(8,128)(2,1)} %make_heads.5.refs_2_.refs_1_, bf16[1024,1024]{1,0:T(8,128)(2,1)} %make_heads.4.refs_2_.refs_5_, bf16[1024,1024]{1,0:T(8,128)(2,1)} %copy-done.10), custom_call_target="tpu_custom_call" | custom-call | flops 1000 | bytes 1000 | tf_op jit(solution)/shard_map/attend/pallas_call | solution.py:525
  269.2 9.9 collective-permute-done.22.refs_3_.refs_6_
  281.2 22.2 %attend.3 = (bf16[1024,1024]{1,0:T(8,128)(2,1)}, f32[1024,512]{1,0:T(8,128)}) custom-call(s32[2,9]{1,0:T(2,128)} %pad_add_fusion.refs_0_, bf16[1024,1024]{1,0:T(8,128)(2,1)} %make_heads.7.refs_2_.refs_1_, bf16[1024,1024]{1,0:T(8,128)(2,1)} %make_heads.6.refs_2_.refs_5_, bf16[1024,1024]{1,0:T(8,128)(2,1)} %collective-permute-done.22.refs_3_.refs_6_), custom_call_target="tpu_custom_call" | custom-call | flops 1000 | bytes 1000 | tf_op jit(solution)/shard_map/attend/pallas_call | solution.py:525
  303.4 9.4 collective-permute-done.25.refs_4_.refs_7_
  313.8 10.5 to_model.8.refs_3_
  331.9 10.4 to_model.9.refs_6_.refs_2_
  342.3 19.2 %to_hidden.12.refs_5_.refs_8_ = bf16[2048,1536]{1,0:T(8,128)(2,1)} custom-call(bf16[1024,2048]{1,0:T(8,128)(2,1)} %reorder.1.refs_0_.refs_1_, bf16[1024,2048]{1,0:T(8,128)(2,1)} %collective-permute-done.27.refs_1_.refs_2_, bf16[1536,512]{1,0:T(8,128)(2,1)} %all-gather.16.cloned.1.call-done.refs_2_.refs_3_, bf16[1536,512]{1,0:T(8,128)(2,1)} %copy-done.7, ...), custom_call_target="tpu_custom_call" | custom-call | flops 1000 | bytes 1000 | tf_op jit(solution)/shard_map/to_hidden/pallas_call | solution.py:525
  361.5 11.2 %resid_norm.1 = (bf16[1024,2048]{1,0:T(8,128)(2,1)}, bf16[1024,2048]{1,0:T(8,128)(2,1)}) custom-call(s32[8]{0:T(128)} %add_add_fusion.9.refs_0_, bf16[1024,2048]{1,0:T(8,128)(2,1)} %refs_0_.1, bf16[1024,2048]{1,0:T(8,128)(2,1)} %to_model.9.refs_6_.refs_2_, bf16[1024,2048]{1,0:T(8,128)(2,1)} %collective-permute-done.26.refs_3_, f32[1,2048]{1,0:T(1,128)} %bitcast.113, ...), custom_call_target="tpu_custom_call" | custom-call | flops 1000 | bytes 1000 | tf_op jit(solution)/shard_map/resid_norm/pallas_call | solution.py:525
  388.2 37.4 %ffn.2 = (bf16[2048,1536]{1,0:T(8,128)(2,1)}, bf16[2048,1536]{1,0:T(8,128)(2,1)}, bf16[2048,1536]{1,0:T(8,128)(2,1)}) custom-call(bf16[1024,2048]{1,0:T(8,128)(2,1)} %get-tuple-element.322.refs_0_.refs_4_.refs_1_, bf16[1024,2048]{1,0:T(8,128)(2,1)} %collective-permute-done.32.refs_1_.refs_5_.refs_2_, ...), custom_call_target="tpu_custom_call" | custom-call | flops 1000 | bytes 1000 | tf_op jit(solution)/shard_map/ffn/pallas_call | solution.py:525
  427.9 37.0 %weight_cols.4 = (bf16[1536,2048]{1,0:T(8,128)(2,1)}, bf16[1536,512]{1,0:T(8,128)(2,1)}, bf16[1536,512]{1,0:T(8,128)(2,1)}, bf16[1536,512]{1,0:T(8,128)(2,1)}, b...) custom-call(bf16[2048,1536]{1,0:T(8,128)(2,1)} %get-tuple-element.331.refs_0_.refs_1_, ...), custom_call_target="tpu_custom_call" | custom-call | flops 1000 | bytes 1000 | tf_op jit(solution)/shard_map/weight_cols/pallas_call | solution.py:525
  469.5 19.1 %weight_cols.5 = (bf16[1536,512]{1,0:T(8,128)(2,1)}, bf16[1536,512]{1,0:T(8,128)(2,1)}, bf16[1536,512]{1,0:T(8,128)(2,1)}, bf16[1536,256]{1,0:T(8,128)(2,1)}, bf16[1536,256]{1,0:T(8,128)(2,1)}) custom-call(bf16[2048,1536]{1,0:T(8,128)(2,1)} %get-tuple-element.344.refs_0_.refs_2_, bf16[1024,2048]{1,0:T(8,128)(2,1)} %get-tuple-element.322.refs_0_.refs_4_.refs_1_, ...), custom_call_target="tpu_custom_call" | custom-call | flops 1000 | bytes 1000 | tf_op jit(solution)/shard_map/weight_cols/pallas_call | solution.py:525
  493.8 19.8 %to_hidden.13.refs_7_ = bf16[2048,1536]{1,0:T(8,128)(2,1)} custom-call(bf16[1024,2048]{1,0:T(8,128)(2,1)} %reorder.1.refs_0_.refs_1_, bf16[1024,2048]{1,0:T(8,128)(2,1)} %collective-permute-done.27.refs_1_.refs_2_, bf16[1536,512]{1,0:T(8,128)(2,1)} %all-gather.20.cloned.1.call-done.refs_2_.refs_7_, ...), custom_call_target="tpu_custom_call" | custom-call | flops 1000 | bytes 1000 | tf_op jit(solution)/shard_map/to_hidden/pallas_call | solution.py:525
  519.0 37.0 %ffn.3 = (bf16[2048,1536]{1,0:T(8,128)(2,1)}, bf16[2048,1536]{1,0:T(8,128)(2,1)}, bf16[2048,1536]{1,0:T(8,128)(2,1)}) custom-call(bf16[1024,2048]{1,0:T(8,128)(2,1)} %get-tuple-element.322.refs_0_.refs_4_.refs_1_, bf16[1024,2048]{1,0:T(8,128)(2,1)} %collective-permute-done.32.refs_1_.refs_5_.refs_2_, ...), custom_call_target="tpu_custom_call" | custom-call | flops 1000 | bytes 1000 | tf_op jit(solution)/shard_map/ffn/pallas_call | solution.py:525
  560.9 37.3 %weight_cols.6 = (bf16[1536,512]{1,0:T(8,128)(2,1)}, bf16[1536,512]{1,0:T(8,128)(2,1)}, bf16[1536,512]{1,0:T(8,128)(2,1)}, bf16[1536,256]{1,0:T(8,128)(2,1)}, bf...) custom-call(bf16[2048,1536]{1,0:T(8,128)(2,1)} %get-tuple-element.51, ...), custom_call_target="tpu_custom_call" | custom-call | flops 1000 | bytes 1000 | tf_op jit(solution)/shard_map/weight_cols/pallas_call | solution.py:525
  603.6 19.0 %weight_cols.7 = (bf16[1536,512]{1,0:T(8,128)(2,1)}, bf16[1536,512]{1,0:T(8,128)(2,1)}, bf16[1536,512]{1,0:T(8,128)(2,1)}, bf16[1536,256]{1,0:T(8,128)(2,1)}, bf16[1536,256]{1,0:T(8,128)(2,1)}) custom-call(bf16[2048,1536]{1,0:T(8,128)(2,1)} %get-tuple-element.392.refs_0_.refs_4_, bf16[1024,2048]{1,0:T(8,128)(2,1)} %get-tuple-element.322.refs_0_.refs_4_.refs_1_, ...), custom_call_target="tpu_custom_call" | custom-call | flops 1000 | bytes 1000 | tf_op jit(solution)/shard_map/weight_cols/pallas_call | solution.py:525
  628.2 34.6 %to_model.10 = bf16[1024,2048]{1,0:T(8,128)(2,1)} custom-call(s32[8]{0:T(128)} %xor_add_fusion.refs_0_, bf16[2048,1536]{1,0:T(8,128)(2,1)} %get-tuple-element.332.refs_3_.refs_1_, bf16[2048,1536]{1,0:T(8,128)(2,1)} %get-tuple-element.344.refs_0_.refs_2_, bf16[2048,1536]{1,0:T(8,128)(2,1)} %get-tuple-element.417.refs_3_, ...), custom_call_target="tpu_custom_call" | custom-call | flops 1000 | bytes 1000 | tf_op jit(solution)/shard_map/to_model/pallas_call | solution.py:525
  669.9 34.4 %to_model.11.refs_2_ = bf16[1024,2048]{1,0:T(8,128)(2,1)} custom-call(s32[8]{0:T(128)} %xor_add_fusion.refs_0_, bf16[2048,1536]{1,0:T(8,128)(2,1)} %get-tuple-element.332.refs_3_.refs_1_, bf16[2048,1536]{1,0:T(8,128)(2,1)} %get-tuple-element.344.refs_0_.refs_2_, bf16[2048,1536]{1,0:T(8,128)(2,1)} %get-tuple-element.417.refs_3_, ...), custom_call_target="tpu_custom_call" | custom-call | flops 1000 | bytes 1000 | tf_op jit(solution)/shard_map/to_model/pallas_call | solution.py:525
  710.1 12.0 %norm_return.2 = (bf16[1024,2048]{1,0:T(8,128)(2,1)}, f32[8,2048]{1,0:T(8,128)}) custom-call(bf16[1024,2048]{1,0:T(8,128)(2,1)} %get-tuple-element.316.refs_0_, bf16[1024,2048]{1,0:T(8,128)(2,1)} %multiply_convert_fusion.1.refs_1_, bf16[1024,2048]{1,0:T(8,128)(2,1)} %to_model.11.refs_2_, bf16[1024,2048]{1,0:T(8,128)(2,1)} %collective-permute-done.53.refs_3_, ...), custom_call_target="tpu_custom_call" | custom-call | flops 1000 | bytes 1000 | tf_op jit(solution)/shard_map/norm_return/pallas_call | solution.py:525
  735.1 33.7 %attend_back.2 = (bf16[1024,1024]{1,0:T(8,128)(2,1)}, bf16[1024,1024]{1,0:T(8,128)(2,1)}, bf16[1024,1024]{1,0:T(8,128)(2,1)}) custom-call(s32[2,9]{1,0:T(2,128)} %pad_add_fusion.refs_0_, bf16[1024,1024]{1,0:T(8,128)(2,1)} %make_heads.5.refs_2_.refs_1_, bf16[1024,1024]{1,0:T(8,128)(2,1)} %to_hidden.14.refs_2_, ...), custom_call_target="tpu_custom_call" | custom-call | flops 1000 | bytes 1000 | tf_op jit(solution)/shard_map/attend_back/pallas_call | solution.py:525
  771.1 21.8 %collective-permute-done.56 = bf16[1536,512]{1,0:T(8,128)(2,1)} collective-permute-done((bf16[1536,512]{1,0:T(8,128)(2,1)}, bf16[1536,512]{1,0:T(8,128)(2,1)}, u32[]{:S(2)}, u32[]{:S(2)}) %collective-permute-start.56) | collective-permute-done | bytes 1572896 | tf_op jit(solution)/shard_map/ppermute | solution.py:467
  805.8 14.6 %weight_rows.3 = (bf16[256,2048]{1,0:T(8,128)(2,1)}, bf16[256,2048]{1,0:T(8,128)(2,1)}, bf16[256,2048]{1,0:T(8,128)(2,1)}, bf16[256,2048]{1,0:T(8,128)(2,1)}) custom-call(bf16[1024,1024]{1,0:T(8,128)(2,1)} %get-tuple-element.301.refs_1_.refs_3_.refs_0_, bf16[1024,1024]{1,0:T(8,128)(2,1)} %get-tuple-element.312.refs_1_.refs_3_, ...), custom_call_target="tpu_custom_call" | custom-call | flops 1000 | bytes 1000 | tf_op jit(solution)/shard_map/weight_rows/pallas_call | solution.py:525
  828.9 33.6 %attend_back.3 = (bf16[1024,1024]{1,0:T(8,128)(2,1)}, bf16[1024,1024]{1,0:T(8,128)(2,1)}, bf16[1024,1024]{1,0:T(8,128)(2,1)}) custom-call(s32[2,9]{1,0:T(2,128)} %pad_add_fusion.refs_0_, bf16[1024,1024]{1,0:T(8,128)(2,1)} %make_heads.7.refs_2_.refs_1_, bf16[1024,1024]{1,0:T(8,128)(2,1)} %to_hidden.15.refs_2_, ...), custom_call_target="tpu_custom_call" | custom-call | flops 1000 | bytes 1000 | tf_op jit(solution)/shard_map/attend_back/pallas_call | solution.py:525
  884.8 14.4 %weight_rows.4 = (bf16[256,2048]{1,0:T(8,128)(2,1)}, bf16[256,2048]{1,0:T(8,128)(2,1)}, bf16[256,2048]{1,0:T(8,128)(2,1)}, bf16[256,2048]{1,0:T(8,128)(2,1)}) custom-call(bf16[1024,1024]{1,0:T(8,128)(2,1)} %get-tuple-element.462.refs_0_.refs_1_, bf16[1024,1024]{1,0:T(8,128)(2,1)} %get-tuple-element.463.refs_1_, bf16[1024,2048]{1,0:T(8,128)(2,1)} %fusion.2.refs_0_.refs_2_, ...), custom_call_target="tpu_custom_call" | custom-call | flops 1000 | bytes 1000 | tf_op jit(solution)/shard_map/weight_rows/pallas_call | solution.py:525
  899.3 20.9 %to_model.12 = bf16[1024,2048]{1,0:T(8,128)(2,1)} custom-call(s32[8]{0:T(128)} %xor_add_fusion.refs_0_, bf16[2048,1536]{1,0:T(8,128)(2,1)} %get-tuple-element.331.refs_0_.refs_1_, bf16[2048,1536]{1,0:T(8,128)(2,1)} %get-tuple-element.517.refs_0_.refs_2_, bf16[1536,512]{1,0:T(8,128)(2,1)} %all-gather.16.cloned.1.call-done.refs_2_.refs_3_, ...), custom_call_target="tpu_custom_call" | custom-call | flops 1000 | bytes 1000 | tf_op jit(solution)/shard_map/to_model/pallas_call | solution.py:525
  939.1 14.3 %weight_rows.5 = (bf16[256,2048]{1,0:T(8,128)(2,1)}, bf16[256,2048]{1,0:T(8,128)(2,1)}, bf16[256,2048]{1,0:T(8,128)(2,1)}, bf16[256,2048]{1,0:T(8,128)(2,1)}) custom-call(bf16[1024,1024]{1,0:T(8,128)(2,1)} %get-tuple-element.467.refs_0_.refs_2_, bf16[1024,1024]{1,0:T(8,128)(2,1)} %get-tuple-element.495.refs_1_.refs_2_, ...), custom_call_target="tpu_custom_call" | custom-call | flops 1000 | bytes 1000 | tf_op jit(solution)/shard_map/weight_rows/pallas_call | solution.py:525
  972.8 15.5 %to_model.13 = bf16[1024,2048]{1,0:T(8,128)(2,1)} custom-call(s32[8]{0:T(128)} %iota.44.refs_0_, bf16[1024,1024]{1,0:T(8,128)(2,1)} %get-tuple-element.463.refs_1_, bf16[1024,1024]{1,0:T(8,128)(2,1)} %get-tuple-element.495.refs_1_.refs_2_, bf16[1024,2048]{1,0:T(8,128)(2,1)} %constant_dynamic-update-slice_fusion.8.refs_1_.refs_3_, ...), custom_call_target="tpu_custom_call" | custom-call | flops 1000 | bytes 1000 | tf_op jit(solution)/shard_map/to_model/pallas_call | solution.py:525
  996.9 15.4 %to_model.14.refs_2_ = bf16[1024,2048]{1,0:T(8,128)(2,1)} custom-call(s32[8]{0:T(128)} %iota.45.refs_0_, bf16[1024,1024]{1,0:T(8,128)(2,1)} %get-tuple-element.462.refs_0_.refs_1_, bf16[1024,1024]{1,0:T(8,128)(2,1)} %get-tuple-element.467.refs_0_.refs_2_, bf16[1024,2048]{1,0:T(8,128)(2,1)} %constant_dynamic-update-slice_fusion.8.refs_1_.refs_3_, ...), custom_call_target="tpu_custom_call" | custom-call | flops 1000 | bytes 1000 | tf_op jit(solution)/shard_map/to_model/pallas_call | solution.py:525
  1032.0 13.2 %norm_return.3 = (f32[1024,2048]{1,0:T(8,128)}, f32[8,2048]{1,0:T(8,128)}) custom-call(bf16[1024,2048]{1,0:T(8,128)(2,1)} %refs_0_.1, bf16[1024,2048]{1,0:T(8,128)(2,1)} %get-tuple-element.436.refs_0_.refs_2_.refs_1_, bf16[1024,2048]{1,0:T(8,128)(2,1)} %to_model.14.refs_2_, bf16[1024,2048]{1,0:T(8,128)(2,1)} %collective-permute-done.75.refs_3_, ...), custom_call_target="tpu_custom_call" | custom-call | flops 1000 | bytes 1000 | tf_op jit(solution)/shard_map/norm_return/pallas_call | solution.py:525
  1048.7 20.4 %to_model.15 = bf16[1024,2048]{1,0:T(8,128)(2,1)} custom-call(s32[8]{0:T(128)} %xor_add_fusion.refs_0_, bf16[2048,1536]{1,0:T(8,128)(2,1)} %get-tuple-element.331.refs_0_.refs_1_, bf16[2048,1536]{1,0:T(8,128)(2,1)} %get-tuple-element.517.refs_0_.refs_2_, bf16[1536,512]{1,0:T(8,128)(2,1)} %all-gather.16.cloned.1.call-done.refs_2_.refs_3_, ...), custom_call_target="tpu_custom_call" | custom-call | flops 1000 | bytes 1000 | tf_op jit(solution)/shard_map/to_model/pallas_call | solution.py:525
  1074.6 13.8 %reduce-scatter.16.cloned.1.call-done = bf16[64,2048]{1,0:T(8,128)(2,1)} async-done(((bf16[256,2048]{1,0:T(8,128)(2,1)}), bf16[64,2048]{1,0:T(8,128)(2,1)}) %reduce-scatter.16.cloned.1.call-update) | async-done | bytes 262160 | tf_op jit(solution)/shard_map/reduce_scatter | solution.py:487
  (500 shorter events, 421.3 us)
Async XLA Ops:
  8.9 60.9 %all-gather.12.cloned.1.call-start = ((), (), s32[]{:S(2)}) async-start(), calls=%async_computation.10 | async-start | bytes 1310720 | tf_op jit(solution)/shard_map/all_gather | solution.py:483
  9.7 89.2 %all-gather.14.cloned.1.call-start = ((), (), s32[]{:S(2)}) async-start(), calls=%async_computation.11 | async-start | bytes 1310720 | tf_op jit(solution)/shard_map/all_gather | solution.py:483
  12.6 173.4 %all-gather.16.cloned.1.call-start = ((), (), s32[]{:S(2)}) async-start(), calls=%async_computation.12 | async-start | bytes 1966080 | tf_op jit(solution)/shard_map/all_gather | solution.py:483
  46.7 213.8 %all-gather.18.cloned.1.call-start = ((), (), s32[]{:S(2)}) async-start(), calls=%async_computation.13 | async-start | bytes 1966080 | tf_op jit(solution)/shard_map/all_gather | solution.py:483
  142.9 160.5 %all-gather.20.cloned.1.call-start = ((), (), s32[]{:S(2)}) async-start(), calls=%async_computation.14 | async-start | bytes 1966080 | tf_op jit(solution)/shard_map/all_gather | solution.py:483
  143.4 229.3 %all-gather.22.cloned.1.call-start = ((), (), s32[]{:S(2)}) async-start(), calls=%async_computation.15 | async-start | bytes 1966080 | tf_op jit(solution)/shard_map/all_gather | solution.py:483
  143.5 47.9 %collective-permute-start.15 = (bf16[1024,1024]{1,0:T(8,128)(2,1)}, bf16[1024,1024]{1,0:T(8,128)(2,1)S(1)}, u32[]{:S(2)}, u32[]{:S(2)}) collective-permute-start(bf16[1024,1024]{1,0:T(8,128)(2,1)} %make_heads.4.refs_2_.refs_5_), channel_id=1, source_target_pairs={{0,4},{4,0},{1,5},{5,1},{2,6},{6,2},{3,7},{7,3},{8,12},{12,8},{9,1... | collective-permute-start | bytes 6291464 | tf_op jit(solution)/shard_map/ppermute | solution.py:467
  146.9 236.0 %all-gather.24.cloned.1.call-start = ((), (), s32[]{:S(2)}) async-start(), calls=%async_computation.16 | async-start | bytes 7864320 | tf_op jit(solution)/shard_map/all_gather | solution.py:483
  196.0 323.0 %all-gather.26.cloned.1.call-start = ((), (), s32[]{:S(2)}) async-start(), calls=%async_computation.17 | async-start | bytes 7864320 | tf_op jit(solution)/shard_map/all_gather | solution.py:483
  281.2 49.2 %collective-permute-start.27 = (bf16[1024,2048]{1,0:T(8,128)(2,1)}, bf16[1024,2048]{1,0:T(8,128)(2,1)}, u32[]{:S(2)}, u32[]{:S(2)}) collective-permute-start(bf16[1024,2048]{1,0:T(8,128)(2,1)} %reorder.1.refs_0_.refs_1_), channel_id=1, source_target_pairs={{0,8},{8,0},{1,9},{9,1},{2,10},{10,2},{3,11},{11,3},{4,12},{12,4},... | collective-permute-start | bytes 12582920 | tf_op jit(solution)/shard_map/ppermute | solution.py:467
  324.3 468.8 %reduce-scatter.10.cloned.1.call-start = ((), (), s32[]{:S(2)}) async-start(), calls=%async_computation.18 | async-start | bytes 7864320 | tf_op jit(solution)/shard_map/reduce_scatter | solution.py:487
  324.8 54.9 %collective-permute-start.31 = (bf16[1536,512]{1,0:T(8,128)(2,1)}, bf16[1536,512]{1,0:T(8,128)(2,1)}, u32[]{:S(2)}, u32[]{:S(2)}) collective-permute-start(bf16[1536,512]{1,0:T(8,128)(2,1)} %all-gather.20.cloned.1.call-done.refs_2_.refs_7_), channel_id=1, source_target_pairs={{0,4},{4,0},{1,5},{5,1},{2,6},{6,2},{3,7},{7,3},{8,12},{12,8},{9,1... | collective-permute-start | bytes 4718600 | tf_op jit(solution)/shard_map/ppermute | solution.py:467
  326.2 53.6 %collective-permute-start.30 = (bf16[1536,512]{1,0:T(8,128)(2,1)}, bf16[1536,512]{1,0:T(8,128)(2,1)}, u32[]{:S(2)}, u32[]{:S(2)}) collective-permute-start(bf16[1536,512]{1,0:T(8,128)(2,1)} %all-gather.20.cloned.1.call-done.refs_2_.refs_7_), channel_id=1, source_target_pairs={{0,16},{16,0},{1,17},{17,1},{2,18},{18,2},{3,19},{19,3},{4,20},{20... | collective-permute-start | bytes 4718600 | tf_op jit(solution)/shard_map/ppermute | solution.py:467
  329.5 49.2 %collective-permute-start.29 = (bf16[1536,256]{1,0:T(8,128)(2,1)}, bf16[1536,256]{1,0:T(8,128)(2,1)S(1)}, u32[]{:S(2)}, u32[]{:S(2)}) collective-permute-start(bf16[1536,256]{1,0:T(8,128)(2,1)} %slice.234), channel_id=1, source_target_pairs={{0,4},{4,0},{1,5},{5,1},{2,6},{6,2},{3,7},{7,3},{8,12},{12,8},{9,1... | collective-permute-start | bytes 2359304 | tf_op jit(solution)/shard_map/ppermute | solution.py:467
  330.3 49.4 %collective-permute-start.28 = (bf16[1536,256]{1,0:T(8,128)(2,1)}, bf16[1536,256]{1,0:T(8,128)(2,1)S(1)}, u32[]{:S(2)}, u32[]{:S(2)}) collective-permute-start(bf16[1536,256]{1,0:T(8,128)(2,1)} %slice.233), channel_id=1, source_target_pairs={{0,16},{16,0},{1,17},{17,1},{2,18},{18,2},{3,19},{19,3},{4,20},{20... | collective-permute-start | bytes 2359304 | tf_op jit(solution)/shard_map/ppermute | solution.py:467
  466.6 453.5 %reduce-scatter.12.cloned.1.call-start = ((), (), s32[]{:S(2)}) async-start(), calls=%async_computation.19 | async-start | bytes 1966080 | tf_op jit(solution)/shard_map/reduce_scatter | solution.py:487
  662.9 257.2 %reduce-scatter.14.cloned.1.call-start = ((), (), s32[]{:S(2)}) async-start(), calls=%async_computation.20 | async-start | bytes 1966080 | tf_op jit(solution)/shard_map/reduce_scatter | solution.py:487
  722.1 71.1 %collective-permute-start.58 = (bf16[1024,2048]{1,0:T(8,128)(2,1)}, bf16[1024,2048]{1,0:T(8,128)(2,1)}, u32[]{:S(2)}, u32[]{:S(2)}) collective-permute-start(bf16[1024,2048]{1,0:T(8,128)(2,1)} %get-tuple-element.436.refs_0_.refs_2_.refs_1_), channel_id=1, source_target_pairs={{0,8},{8,0},{1,9},{9,1},{2,10},{10,2},{3,11},{11,3},{4,12},{12,4},... | collective-permute-start | bytes 12582920 | tf_op jit(solution)/shard_map/ppermute | solution.py:467
  722.1 269.5 %reduce-scatter.22.cloned.1.call-start = ((), (), s32[]{:S(2)}) async-start(), calls=%async_computation.24 | async-start | bytes 1966080 | tf_op jit(solution)/shard_map/reduce_scatter | solution.py:487
  724.0 68.9 %collective-permute-start.56 = (bf16[1536,512]{1,0:T(8,128)(2,1)}, bf16[1536,512]{1,0:T(8,128)(2,1)}, u32[]{:S(2)}, u32[]{:S(2)}) collective-permute-start(bf16[1536,512]{1,0:T(8,128)(2,1)} %get-tuple-element.443), channel_id=1, source_target_pairs={{0,16},{16,0},{1,17},{17,1},{2,18},{18,2},{3,19},{19,3},{4,20},{20... | collective-permute-start | bytes 4718600 | tf_op jit(solution)/shard_map/ppermute | solution.py:467
  725.9 67.2 %collective-permute-start.57 = (bf16[1536,512]{1,0:T(8,128)(2,1)}, bf16[1536,512]{1,0:T(8,128)(2,1)}, u32[]{:S(2)}, u32[]{:S(2)}) collective-permute-start(bf16[1536,512]{1,0:T(8,128)(2,1)} %get-tuple-element.444), channel_id=1, source_target_pairs={{0,4},{4,0},{1,5},{5,1},{2,6},{6,2},{3,7},{7,3},{8,12},{12,8},{9,1... | collective-permute-start | bytes 4718600 | tf_op jit(solution)/shard_map/ppermute | solution.py:467
  796.4 196.9 %reduce-scatter.24.cloned.1.call-start = ((), (), s32[]{:S(2)}) async-start(), calls=%async_computation.25 | async-start | bytes 1966080 | tf_op jit(solution)/shard_map/reduce_scatter | solution.py:487
  796.5 66.1 %collective-permute-start.59 = (bf16[1024,1024]{1,0:T(8,128)(2,1)}, bf16[1024,1024]{1,0:T(8,128)(2,1)S(1)}, u32[]{:S(2)}, u32[]{:S(2)}) collective-permute-start(bf16[1024,1024]{1,0:T(8,128)(2,1)} %get-tuple-element.457), channel_id=1, source_target_pairs={{0,4},{4,0},{1,5},{5,1},{2,6},{6,2},{3,7},{7,3},{8,12},{12,8},{9,1... | collective-permute-start | bytes 6291464 | tf_op jit(solution)/shard_map/ppermute | solution.py:467
  802.0 223.6 %reduce-scatter.26.cloned.1.call-start = ((), (), s32[]{:S(2)}) async-start(), calls=%async_computation.26 | async-start | bytes 1966080 | tf_op jit(solution)/shard_map/reduce_scatter | solution.py:487
  804.1 58.4 %collective-permute-start.60 = (bf16[384,512]{1,0:T(8,128)(2,1)S(1)}, bf16[384,512]{1,0:T(8,128)(2,1)S(1)}, u32[]{:S(2)}, u32[]{:S(2)}) collective-permute-start(bf16[384,512]{1,0:T(8,128)(2,1)S(1)} %get-tuple-element.563), channel_id=1, source_target_pairs={{0,16},{16,0},{1,17},{17,1},{2,18},{18,2},{3,19},{19,3},{4,20},{20... | collective-permute-start | bytes 1179656 | tf_op jit(solution)/shard_map/ppermute | solution.py:467
  862.6 57.6 %collective-permute-start.61 = (bf16[1024,1024]{1,0:T(8,128)(2,1)}, bf16[1024,1024]{1,0:T(8,128)(2,1)}, u32[]{:S(2)}, u32[]{:S(2)}) collective-permute-start(bf16[1024,1024]{1,0:T(8,128)(2,1)} %get-tuple-element.469), channel_id=1, source_target_pairs={{0,4},{4,0},{1,5},{5,1},{2,6},{6,2},{3,7},{7,3},{8,12},{12,8},{9,1... | collective-permute-start | bytes 6291464 | tf_op jit(solution)/shard_map/ppermute | solution.py:467
  864.6 55.5 %collective-permute-start.62 = (bf16[256,2048]{1,0:T(8,128)(2,1)}, bf16[256,2048]{1,0:T(8,128)(2,1)S(1)}, u32[]{:S(2)}, u32[]{:S(2)}) collective-permute-start(bf16[256,2048]{1,0:T(8,128)(2,1)} %get-tuple-element.470), channel_id=1, source_target_pairs={{0,16},{16,0},{1,17},{17,1},{2,18},{18,2},{3,19},{19,3},{4,20},{20... | collective-permute-start | bytes 3145736 | tf_op jit(solution)/shard_map/ppermute | solution.py:467
  864.6 55.5 %collective-permute-start.63 = (bf16[384,512]{1,0:T(8,128)(2,1)}, bf16[384,512]{1,0:T(8,128)(2,1)}, u32[]{:S(2)}, u32[]{:S(2)}) collective-permute-start(bf16[384,512]{1,0:T(8,128)(2,1)} %get-tuple-element.475), channel_id=1, source_target_pairs={{0,16},{16,0},{1,17},{17,1},{2,18},{18,2},{3,19},{19,3},{4,20},{20... | collective-permute-start | bytes 1179656 | tf_op jit(solution)/shard_map/ppermute | solution.py:467
  920.8 153.8 %reduce-scatter.20.cloned.1.call-start = ((), (), s32[]{:S(2)}) async-start(), calls=%async_computation.23 | async-start | bytes 1310720 | tf_op jit(solution)/shard_map/reduce_scatter | solution.py:487
  972.2 102.4 %reduce-scatter.18.cloned.1.call-start = ((), (), s32[]{:S(2)}) async-start(), calls=%async_computation.22 | async-start | bytes 1310720 | tf_op jit(solution)/shard_map/reduce_scatter | solution.py:487
  1012.2 76.6 %collective-permute-start.80 = (bf16[1024,2048]{1,0:T(8,128)(2,1)}, bf16[1024,2048]{1,0:T(8,128)(2,1)}, u32[]{:S(2)}, u32[]{:S(2)}) collective-permute-start(bf16[1024,2048]{1,0:T(8,128)(2,1)} %to_model.12), channel_id=1, source_target_pairs={{0,8},{8,0},{1,9},{9,1},{2,10},{10,2},{3,11},{11,3},{4,12},{12,4},... | collective-permute-start | bytes 12582920 | tf_op jit(solution)/shard_map/ppermute | solution.py:467
  1023.3 65.1 %reduce-scatter.16.cloned.1.call-start = ((), (), s32[]{:S(2)}) async-start(), calls=%async_computation.21 | async-start | bytes 1310720 | tf_op jit(solution)/shard_map/reduce_scatter | solution.py:487
  (135 other events, 2771.7 us)
Sparse Core Ops, SparseCore 0:
  10.2 30.6 all-gather.9
  42.4 27.4 all-gather.11
  71.4 27.4 all-gather.13
  100.9 36.5 all-gather.15
  143.0 37.1 all-gather.17
  182.2 35.9 all-gather.19
  220.3 35.9 all-gather.21
  257.9 114.2 all-gather.23
  373.8 113.5 all-gather.25
  489.5 108.9 reduce-scatter.9
  663.0 35.0 reduce-scatter.11
  722.2 35.1 reduce-scatter.13
  796.6 36.0 reduce-scatter.21
  835.4 34.2 reduce-scatter.23
  920.9 41.0 reduce-scatter.25
  972.3 34.8 reduce-scatter.19
  1023.4 36.9 reduce-scatter.17
  1062.6 25.8 reduce-scatter.15

commit v5 on v4

--- a/solution.py
+++ b/solution.py
@@ -565,32 +565,34 @@
     return matrix_product(jnp.concatenate([high, low], axis=1), ones)
 
 
+HEADS_STEP = 4
+
+
 def heads_kernel(count, raw_ref, cos_ref, sin_ref, gain_ref, out_ref):
-    raw = raw_ref[:, :HEAD_SIZE]
-    value = raw * lax.rsqrt(lane_mean(raw * raw) + EPS_NORM) * gain_ref[...]
-    out_ref[:, :HEAD_SIZE] = (
-        value * cos_ref[...] + pltpu.roll(value, HEAD_SIZE // 2, 1) * sin_ref[...]
-    ).astype(jnp.bfloat16)
-    if count == 2:
-        out_ref[:, HEAD_SIZE:] = raw_ref[:, HEAD_SIZE:].astype(jnp.bfloat16)
+    for first in range(0, raw_ref.shape[1], count * HEAD_SIZE):
+        lanes = slice(first, first + HEAD_SIZE)
+        raw = raw_ref[:, lanes]
+        value = raw * lax.rsqrt(lane_mean(raw * raw) + EPS_NORM) * gain_ref[...]
+        out_ref[:, lanes] = (
+            value * cos_ref[...] + pltpu.roll(value, HEAD_SIZE // 2, 1) * sin_ref[...]
+        ).astype(jnp.bfloat16)
+        if count == 2:
+            lanes = slice(first + HEAD_SIZE, first + 2 * HEAD_SIZE)
+            out_ref[:, lanes] = raw_ref[:, lanes].astype(jnp.bfloat16)
 
 
 def make_heads(group, raw, cos_tab, sin_tab, gain, count, after=()):
     rows, width = raw.shape
     skip = group * (rows // ROW_TILE)
     table = pl.BlockSpec((ROW_TILE, HEAD_SIZE), lambda i, r: (i + skip, 0))
+    one = pl.BlockSpec((ROW_TILE, HEADS_STEP * HEAD_SIZE), lambda i, r: (i, r))
     return call(
         functools.partial(heads_kernel, count),
         [raw, cos_tab, sin_tab, gain[None, :]],
-        [
-            pl.BlockSpec((ROW_TILE, count * HEAD_SIZE), lambda i, r: (i, r)),
-            table,
-            table,
-            pl.BlockSpec((1, HEAD_SIZE), lambda i, r: (0, 0)),
-        ],
-        pl.BlockSpec((ROW_TILE, count * HEAD_SIZE), lambda i, r: (i, r)),
+        [one, table, table, pl.BlockSpec((1, HEAD_SIZE), lambda i, r: (0, 0))],
+        one,
         jax.ShapeDtypeStruct((rows, width), jnp.bfloat16),
-        (rows // ROW_TILE, width // (count * HEAD_SIZE)),
+        (rows // ROW_TILE, width // (HEADS_STEP * HEAD_SIZE)),
         after,
         name="make_heads",
     )
@@ -603,32 +605,37 @@
     def _():
         sum_ref[...] = jnp.zeros_like(sum_ref)
 
-    raw = raw_ref[:, :HEAD_SIZE]
-    upstream = up_refs[0][...].astype(jnp.float32)
-    for ref in up_refs[1:]:
-        upstream = upstream + ref[...].astype(jnp.float32)
-    if count == 2:
-        out_ref[:, HEAD_SIZE:] = upstream[:, HEAD_SIZE:].astype(jnp.bfloat16)
-        upstream = upstream[:, :HEAD_SIZE]
-    turned = upstream * cos_ref[...] - pltpu.roll(upstream, HEAD_SIZE // 2, 1) * sin_ref[...]
-    scale = lax.rsqrt(lane_mean(raw * raw) + EPS_NORM)
-    hat = raw * scale
-    weighted = turned * gain_ref[...]
-    out_ref[:, :HEAD_SIZE] = (scale * (weighted - hat * lane_mean(hat * weighted))).astype(
-        jnp.bfloat16
-    )
-    sum_ref[0:1, :] += jnp.sum(turned * hat, axis=0, keepdims=True)
+    total = jnp.zeros((1, HEAD_SIZE), jnp.float32)
+    for first in range(0, raw_ref.shape[1], count * HEAD_SIZE):
+        lanes = slice(first, first + HEAD_SIZE)
+        raw = raw_ref[:, lanes]
+        upstream = up_refs[0][:, lanes].astype(jnp.float32)
+        for ref in up_refs[1:]:
+            upstream = upstream + ref[:, lanes].astype(jnp.float32)
+        turned = upstream * cos_ref[...] - pltpu.roll(upstream, HEAD_SIZE // 2, 1) * sin_ref[...]
+        scale = lax.rsqrt(lane_mean(raw * raw) + EPS_NORM)
+        hat = raw * scale
+        weighted = turned * gain_ref[...]
+        out_ref[:, lanes] = (scale * (weighted - hat * lane_mean(hat * weighted))).astype(
+            jnp.bfloat16
+        )
+        total = total + jnp.sum(turned * hat, axis=0, keepdims=True)
+        if count == 2:
+            lanes = slice(first + HEAD_SIZE, first + 2 * HEAD_SIZE)
+            value_up = up_refs[0][:, lanes].astype(jnp.float32)
+            for ref in up_refs[1:]:
+                value_up = value_up + ref[:, lanes].astype(jnp.float32)
+            out_ref[:, lanes] = value_up.astype(jnp.bfloat16)
+    sum_ref[0:1, :] += total
 
 
 def heads_return(group, raw, upstream, far, cos_tab, sin_tab, gain, count, after=()):
     rows, width = raw.shape
-    heads = width // (count * HEAD_SIZE)
     skip = group * (rows // ROW_TILE)
+    span = HEADS_STEP * HEAD_SIZE
     table = pl.BlockSpec((ROW_TILE, HEAD_SIZE), lambda i, r: (i + skip, 0))
-    one = pl.BlockSpec((ROW_TILE, count * HEAD_SIZE), lambda i, r: (i, r))
-    across = pl.BlockSpec(
-        (ROW_TILE, count * HEAD_SIZE), lambda i, r: (i, (r + heads // 2) % heads)
-    )
+    one = pl.BlockSpec((ROW_TILE, span), lambda i, r: (i, r))
+    across = pl.BlockSpec((ROW_TILE, span), lambda i, r: (i, (r + 1) % 2))
     return call(
         functools.partial(heads_back_kernel, count),
         [raw, cos_tab, sin_tab, gain[None, :], upstream] + far,
@@ -639,7 +646,7 @@
             jax.ShapeDtypeStruct((rows, width), jnp.bfloat16),
             jax.ShapeDtypeStruct((8, HEAD_SIZE), jnp.float32),
         ],
-        (rows // ROW_TILE, heads),
+        (rows // ROW_TILE, width // span),
         after,
         name="heads_return",
     )
@@ -1099,7 +1106,7 @@
     )
 
 
-NORM_TILE = 128
+NORM_TILE = 256
 
 
 def resid_kernel(order_ref, tokens_ref, own_ref, there_ref, gain_ref, resid_ref, normed_ref):
@@ -1305,9 +1312,8 @@
     kv_far1, dlo_c, glo_0, query[1], dy[0] = sync(kv_far1, dlo_c, glo_0, query[1], dy[0])
     glo_x, glo_y = swap(glo_0, "x"), swap(glo_0, "y")
     attn1, totals1 = attend(1, info, query[1], kv[1], kv_far1)
-    attn1, glo_x, glo_y, glo_0, dhi_0 = sync(attn1, glo_x, glo_y, glo_0, dhi_0)
+    attn1, glo_x, glo_y, glo_0 = sync(attn1, glo_x, glo_y, glo_0)
     glo_ca, glo_cb = swap(glo_y[:, :eighth], "x"), swap(glo_x[:, eighth:], "y")
-    dhi_x, dhi_y = swap(dhi_0, "x"), swap(dhi_0, "y")
     same = jnp.arange(8, dtype=jnp.int32)
     out_term = to_model([attn1], [[out_w]], same, 0, rows)
     out_there = swap(out_term, "c")
@@ -1317,119 +1323,119 @@
     resid, normed2_own = resid_norm(
         tokens, out_here, out_there, norm2_gain, order_back, [d_act_lo]
     )
-    normed2_own, glo_ca, glo_cb, dhi_x, dhi_y, ghi_0 = sync(
-        normed2_own, glo_ca, glo_cb, dhi_x, dhi_y, ghi_0
-    )
+    normed2_own, glo_ca, glo_cb, dhi_0 = sync(normed2_own, glo_ca, glo_cb, dhi_0)
     normed2 = [normed2_own, swap(normed2_own, "c")]
-    ghi_x, ghi_y = swap(ghi_0, "x"), swap(ghi_0, "y")
+    dhi_x, dhi_y = swap(dhi_0, "x"), swap(dhi_0, "y")
     glo = [glo_0, glo_x, glo_y, glo_ca, glo_cb]
     act_lo, gg_lo, ug_lo = ffn(normed2, glo, ulo, d_act_lo)
-    act_lo, dhi_y, ghi_x, ghi_y = sync(act_lo, dhi_y, ghi_x, ghi_y)
-    dhi_c, ghi_c = swap(dhi_y, "x"), swap(ghi_x, "y")
+    act_lo, gg_lo, dhi_x, dhi_y, ghi_0 = sync(act_lo, gg_lo, dhi_x, dhi_y, ghi_0)
+    ghi_x, ghi_y = swap(ghi_0, "x"), swap(ghi_0, "y")
 
     widths = [fourth, fourth, fourth, eighth, eighth]
     dlo_grad, gl_0, gl_x, gl_y, gl_ca, gl_cb = weight_cols(
         (act_lo, dy, [width]), (gg_lo, normed2, widths)
     )
-    dlo_grad, gl_ca, gl_cb, dhi_c, ghi_c, ug_lo = sync(
-        dlo_grad, gl_ca, gl_cb, dhi_c, ghi_c, ug_lo
+    dlo_grad, gl_ca, gl_cb, ghi_x, ghi_y, ug_lo, dhi_x, dhi_y = sync(
+        dlo_grad, gl_ca, gl_cb, ghi_x, ghi_y, ug_lo, dhi_x, dhi_y
     )
     dlo_sum = scatter_z(dlo_grad)
+    dhi_ca, dhi_cb = swap(dhi_y[:, :eighth], "x"), swap(dhi_x[:, eighth:], "y")
+    ul_0, ul_x, ul_y, ul_ca, ul_cb = weight_cols((ug_lo, normed2, widths))
+    dhi_ca, dhi_cb, ul_ca, ul_cb, ghi_x, ghi_y = sync(dhi_ca, dhi_cb, ul_ca, ul_cb, ghi_x, ghi_y)
+    dhi = [dhi_0, dhi_x, dhi_y, dhi_ca, dhi_cb]
+    ghi_ca, ghi_cb = swap(ghi_y[:, :eighth], "x"), swap(ghi_x[:, eighth:], "y")
+    d_act_hi = to_hidden(dy, dhi)
+    ghi_ca, ghi_cb, gl_ca, gl_cb, d_act_hi = sync(ghi_ca, ghi_cb, gl_ca, gl_cb, d_act_hi)
+    ghi = [ghi_0, ghi_x, ghi_y, ghi_ca, ghi_cb]
     from_a, from_b = swap(gl_ca, "x"), swap(gl_cb, "y")
-    ul_0, ul_x, ul_y, ul_ca, ul_cb = weight_cols((ug_lo, normed2, widths))
-    dhi, ghi = [dhi_0, dhi_x, dhi_y, dhi_c], [ghi_0, ghi_x, ghi_y, ghi_c]
-    gl_x, gl_y, from_a, from_b, ul_ca, ul_cb, dhi[3] = sync(
-        gl_x, gl_y, from_a, from_b, ul_ca, ul_cb, dhi[3]
-    )
     from_ua, from_ub = swap(ul_ca, "x"), swap(ul_cb, "y")
+    act_hi, gg_hi, ug_hi = ffn(normed2, ghi, uhi, d_act_hi)
+    gl_x, gl_y, from_a, from_b, ul_x, ul_y, from_ua, from_ub, act_hi, gg_hi, ug_hi = sync(
+        gl_x, gl_y, from_a, from_b, ul_x, ul_y, from_ua, from_ub, act_hi, gg_hi, ug_hi
+    )
     gl_x, gl_y = add_halves(gl_x, gl_y, from_a, from_b)
-    d_act_hi = to_hidden(dy, dhi)
-    gl_x, gl_y, ul_x, ul_y, from_ua, from_ub, d_act_hi = sync(
-        gl_x, gl_y, ul_x, ul_y, from_ua, from_ub, d_act_hi
-    )
+    gl_x, gl_y, gg_hi = sync(gl_x, gl_y, gg_hi)
     got_x, got_y = swap(gl_x, "x"), swap(gl_y, "y")
-    ul_x, ul_y = add_halves(ul_x, ul_y, from_ua, from_ub)
-    act_hi, gg_hi, ug_hi = ffn(normed2, ghi, uhi, d_act_hi)
-    gl_0, got_x, got_y, ul_x, ul_y, act_hi, gg_hi, ug_hi = sync(
-        gl_0, got_x, got_y, ul_x, ul_y, act_hi, gg_hi, ug_hi
-    )
-    got_ux, got_uy = swap(ul_x, "x"), swap(ul_y, "y")
+    pieces = [fourth] * 4
+    dh_0, dh_x, dh_y, dh_ca, dh_cb, gh_0, gh_x, gh_y, gh_c = weight_cols(
+        (act_hi, dy, widths), (gg_hi, normed2, pieces)
+    )
+    gl_0, got_x, got_y, dh_ca, dh_cb, ug_hi, ul_x, ul_y = sync(
+        gl_0, got_x, got_y, dh_ca, dh_cb, ug_hi, ul_x, ul_y
+    )
+    from_a, from_b = swap(dh_ca, "x"), swap(dh_cb, "y")
     glo_near = gl_0 + got_x + got_y
     glo_sum = scatter_z(glo_near)
-    dh_0, dh_x, dh_y, dh_ca, dh_cb, gh_0, gh_x, gh_y, gh_ca, gh_cb = weight_cols(
-        (act_hi, dy, widths), (gg_hi, normed2, widths), after=[glo_near]
-    )
-    ul_0, got_ux, got_uy, dh_ca, dh_cb, ug_hi = sync(ul_0, got_ux, got_uy, dh_ca, dh_cb, ug_hi)
-    from_a, from_b = swap(dh_ca, "x"), swap(dh_cb, "y")
+    ul_x, ul_y = add_halves(ul_x, ul_y, from_ua, from_ub)
+    uh_0, uh_x, uh_y, uh_c = weight_cols(
+        (ug_hi, normed2, pieces), after=[glo_near, ul_x]
+    )
+    dh_x, dh_y, from_a, from_b, ul_x, ul_y, gg_hi, uh_0 = sync(
+        dh_x, dh_y, from_a, from_b, ul_x, ul_y, gg_hi, uh_0
+    )
+    got_ux, got_uy = swap(ul_x, "x"), swap(ul_y, "y")
+    dh_x, dh_y = add_halves(dh_x, dh_y, from_a, from_b)
+    grads = [gg_lo, ug_lo, gg_hi, ug_hi]
+    both_w = [glo, [ulo], ghi, [uhi]]
+    there = to_model(grads, both_w, order, 1, rows, [dh_x, dh_y])
+    ul_0, got_ux, got_uy, dh_x, dh_y, there, gg_hi = sync(
+        ul_0, got_ux, got_uy, dh_x, dh_y, there, gg_hi
+    )
+    normed2_there = swap(there, "c")
+    got_x, got_y = swap(dh_x, "x"), swap(dh_y, "y")
     ulo_near = ul_0 + got_ux + got_uy
     ulo_sum = scatter_z(ulo_near)
-    uh_0, uh_x, uh_y, uh_ca, uh_cb = weight_cols((ug_hi, normed2, widths), after=[ulo_near])
-    dh_x, dh_y, from_a, from_b, gg_hi, uh_0 = sync(dh_x, dh_y, from_a, from_b, gg_hi, uh_0)
-    dh_x, dh_y = add_halves(dh_x, dh_y, from_a, from_b)
-    dh_x, dh_y, gg_hi = sync(dh_x, dh_y, gg_hi)
-    got_x, got_y = swap(dh_x, "x"), swap(dh_y, "y")
     grads = [gg_lo, ug_lo, gg_hi, ug_hi]
-    both_w = [glo, [ulo], ghi, [uhi]]
-    there = to_model(grads, both_w, order, 1, rows)
-    dh_0, got_x, got_y, gh_ca, gh_cb, uh_ca, uh_cb, there, gg_hi = sync(
-        dh_0, got_x, got_y, gh_ca, gh_cb, uh_ca, uh_cb, there, gg_hi
-    )
-    normed2_there = swap(there, "c")
-    from_ga, from_gb = swap(gh_ca, "x"), swap(gh_cb, "y")
-    from_ua, from_ub = swap(uh_ca, "x"), swap(uh_cb, "y")
+    grad_own = to_model(grads, both_w, order, 0, rows, [ulo_near])
+    dh_0, got_x, got_y, gh_c, uh_c, grad_own = sync(dh_0, got_x, got_y, gh_c, uh_c, grad_own)
+    from_g, from_u = swap(gh_c, "x"), swap(uh_c, "y")
     dhi_near = dh_0 + got_x + got_y
     dhi_sum = scatter_z(dhi_near)
-    grads = [gg_lo, ug_lo, gg_hi, ug_hi]
-    grad_own = to_model(grads, both_w, order, 0, rows, [dhi_near])
-    gh_x, gh_y, from_ga, from_gb, uh_x, uh_y, from_ua, from_ub, grad_own = sync(
-        gh_x, gh_y, from_ga, from_gb, uh_x, uh_y, from_ua, from_ub, grad_own
-    )
-    gh_x, gh_y = add_halves(gh_x, gh_y, from_ga, from_gb)
-    uh_x, uh_y = add_halves(uh_x, uh_y, from_ua, from_ub)
-    gh_x, gh_y, uh_x, uh_y, grad_own = sync(gh_x, gh_y, uh_x, uh_y, grad_own)
+    resid_here, gain2_sum = norm_return(
+        resid, dy_own, grad_own, normed2_there, norm2_gain, (bf16,), [dhi_near]
+    )
+    resid_first = resid_here
+    resid_there = swap(resid_here, "c")
+    mixed_term = to_model([act_lo, act_hi], [dlo, dhi], order, 1, rows, [resid_here])
+    d_attn0 = to_hidden([resid_here], [out_w], bf16, [mixed_term])
+    gh_x, gh_y, from_g, uh_x, uh_y, from_u, mixed_term, d_attn0 = sync(
+        gh_x, gh_y, from_g, uh_x, uh_y, from_u, mixed_term, d_attn0
+    )
+    gh_y, uh_x = gh_y + from_g, uh_x + from_u
+    gh_x, gh_y, uh_x, uh_y, d_attn0 = sync(gh_x, gh_y, uh_x, uh_y, d_attn0)
     got_x, got_y = swap(gh_x, "x"), swap(gh_y, "y")
     got_ux, got_uy = swap(uh_x, "x"), swap(uh_y, "y")
-    resid_here, gain2_sum = norm_return(
-        resid, dy_own, grad_own, normed2_there, norm2_gain, (bf16,)
-    )
-    resid_first = resid_here
-    resid_there = swap(resid_here, "c")
-
-    d_attn0 = to_hidden([resid_here], [out_w])
+    mixed_there = swap(mixed_term, "c")
+
     dq0, dkv0, dkv0_far = attend_back(0, info, query[0], d_attn0, attn0, totals0, kv[0], kv_far0)
-    gh_0, got_x, got_y, uh_0, got_ux, got_uy, resid_there, dkv0_far, dlo_sum = sync(
-        gh_0, got_x, got_y, uh_0, got_ux, got_uy, resid_there, dkv0_far, dlo_sum
-    )
-    dkv0_back = swap(dkv0_far, "y")
+    o_0, o_x, o_y, o_c = weight_rows([attn0, attn1], [resid_here, resid_there], 4, [dq0])
+    gh_0, got_x, got_y, uh_0, got_ux, got_uy, resid_there, dkv0_far, dlo_sum, o_c = sync(
+        gh_0, got_x, got_y, uh_0, got_ux, got_uy, resid_there, dkv0_far, dlo_sum, o_c
+    )
+    dkv0_back, from_o = swap(dkv0_far, "y"), swap(o_c, "x")
     dl_0, dl_x, dl_y, dl_c = (dlo_sum[:, i * fourth : (i + 1) * fourth] for i in range(4))
-    from_l = swap(dl_c, "x")
+    from_l, got_lx = swap(dl_c, "x"), swap(dl_x, "x")
     ghi_near, uhi_near = gh_0 + got_x + got_y, uh_0 + got_ux + got_uy
     ghi_sum, uhi_sum = scatter_z(ghi_near), scatter_z(uhi_near)
-    o_0, o_x, o_y, o_c = weight_rows(
-        [attn0, attn1], [resid_here, resid_there], 4, [ghi_near, uhi_near]
-    )
-    d_attn1 = to_hidden([resid_there], [out_w], bf16, [o_0])
+    back = (cos_tab, sin_tab)
+    d_attn1 = to_hidden([resid_there], [out_w], bf16, [ghi_near, uhi_near])
     dq1, dkv1, dkv1_far = attend_back(1, info, query[1], d_attn1, attn1, totals1, kv[1], kv_far1)
-    dkv1_far, dkv0_back, o_c, dl_x, dl_y, from_l, dq1 = sync(
-        dkv1_far, dkv0_back, o_c, dl_x, dl_y, from_l, dq1
-    )
-    dkv1_back = swap(dkv1_far, "y")
-    from_o = swap(o_c, "x")
-    got_lx = swap(dl_x, "x")
-    back = (cos_tab, sin_tab)
-    q_grad = [
-        heads_return(g, q_raw[g], d, [], *back, query_gain, 1, [dq1])
-        for g, d in enumerate((dq0, dq1))
-    ]
-    q_gains = q_grad[0][1] + q_grad[1][1]
-    q_grad = [q_grad[0][0], q_grad[1][0]]
+    q_grad0, q_gain0 = heads_return(0, q_raw[0], dq0, [], *back, query_gain, 1, [dq1])
+    dkv1_far, dkv0_back, o_x, o_y, from_o, got_lx, dl_y, from_l, q_grad0 = sync(
+        dkv1_far, dkv0_back, o_x, o_y, from_o, got_lx, dl_y, from_l, q_grad0
+    )
+    dkv1_back, got_ox = swap(dkv1_far, "y"), swap(o_x, "x")
+    q_grad1, q_gain1 = heads_return(1, q_raw[1], dq1, [], *back, query_gain, 1, [q_grad0])
+    q_grad, q_gains = [q_grad0, q_grad1], q_gain0 + q_gain1
     w_0, w_x, w_y, w_c = weight_rows(q_grad, normed1, 4)
-    mixed_term = to_model([act_lo, act_hi], [dlo, dhi], order, 1, rows, [w_0])
-    dkv1_back, from_o, w_c, mixed_term, o_x, o_y, dl_y, got_lx, gate_sum, up_sum = sync(
-        dkv1_back, from_o, w_c, mixed_term, o_x, o_y, dl_y, got_lx, glo_sum, ulo_sum
-    )
-    glo_sum, ulo_sum = gate_sum, up_sum
-    got_ly = swap(dl_y + from_l, "y")
+    w_c, act_hi = sync(w_c, act_hi)
+    from_w = swap(w_c, "x")
+    mixed_own = to_model([act_lo, act_hi], [dlo, dhi], order, 0, rows)
+    dkv1_back, got_ox, from_w, mixed_own, o_y, dl_y, w_x, w_y = sync(
+        dkv1_back, got_ox, from_w, mixed_own, o_y + from_o, dl_y + from_l, w_x, w_y
+    )
+    got_oy, got_wx = swap(o_y, "y"), swap(w_x, "x")
+    got_wy = swap(w_y + from_w, "y")
 
     def halves(array):
         span = array.shape[0] // 2
@@ -1439,61 +1445,54 @@
         (x_a, x_b), (y_a, y_b) = halves(along_x), halves(along_y)
         return stacked(x_a, x_b + from_b), stacked(y_a + from_a, y_b)
 
-    w_a, w_b = halves(w_c)
-    from_wa, from_wb = swap(w_a, "x"), swap(w_b, "y")
-    got_ox, got_oy = swap(o_x, "x"), swap(o_y + from_o, "y")
     kv_grad = [
-        heads_return(g, kv_raw[g], d, [e], *back, key_gain, 2)
+        heads_return(g, kv_raw[g], d, [e], *back, key_gain, 2, [mixed_own, w_y])
         for g, (d, e) in enumerate(((dkv0, dkv0_back), (dkv1, dkv1_back)))
     ]
     k_gains = kv_grad[0][1] + kv_grad[1][1]
     kv_grad = [kv_grad[0][0], kv_grad[1][0]]
     kv_0, kv_x, kv_y, kv_c = weight_rows(kv_grad, normed1, 4)
-    kv_c, from_wa, from_wb, got_ox, got_oy, w_x, w_y, kv_grad[1], got_ly = sync(
-        kv_c, from_wa, from_wb, got_ox, got_oy, w_x, w_y, kv_grad[1], got_ly
-    )
+    kv_c, kv_grad[1], got_oy, got_wx = sync(kv_c, kv_grad[1], got_oy, got_wx)
     kv_a, kv_b = halves(kv_c)
     from_a, from_b = swap(kv_a, "x"), swap(kv_b, "y")
-    w_x, w_y = corner_rows(w_x, w_y, from_wa, from_wb)
-    got_wx, got_wy = swap(w_x, "x"), swap(w_y, "y")
-    o_near = o_0 + got_ox + got_oy
-    o_sum = scatter_z(o_near)
-    term_there = to_model([q_grad[1], kv_grad[1]], [[q_w], [kv_w]], same, 0, rows, [o_near])
-    kv_x, kv_y, from_a, from_b, term_there = sync(kv_x, kv_y, from_a, from_b, term_there)
+    term_there = to_model([q_grad[1], kv_grad[1]], [[q_w], [kv_w]], same, 0, rows)
+    o_0, got_oy, w_0, got_wx, got_wy, kv_x, kv_y, from_a, from_b, term_there, dl_y = sync(
+        o_0, got_oy, w_0, got_wx, got_wy, kv_x, kv_y, from_a, from_b, term_there, dl_y
+    )
     normed1_there = swap(term_there, "c")
     kv_x, kv_y = corner_rows(kv_x, kv_y, from_a, from_b)
-    got_kx, got_ky = swap(kv_x, "x"), swap(kv_y, "y")
-    term_own = to_model([q_grad[0], kv_grad[0]], [[q_w], [kv_w]], same, 0, rows, [kv_x, kv_y])
-    w_0, got_wx, got_wy, kv_0, got_kx, got_ky, term_own = sync(
-        w_0, got_wx, got_wy, kv_0, got_kx, got_ky, term_own
-    )
+    got_kx, got_ky, got_ly = swap(kv_x, "x"), swap(kv_y, "y"), swap(dl_y, "y")
+    o_near, w_near = o_0 + got_ox + got_oy, w_0 + got_wx + got_wy
+    ow_near = jnp.concatenate(
+        [o_near.reshape(4, q_in, width), w_near.reshape(4, q_in, width)], axis=1
+    ).reshape(8 * q_in, width)
+    ow_sum = scatter_z(ow_near)
+    term_own = to_model(
+        [q_grad[0], kv_grad[0]], [[q_w], [kv_w]], same, 0, rows, [kv_x, kv_y, ow_near]
+    )
+    kv_0, got_kx, got_ky, got_ly, term_own = sync(kv_0, got_kx, got_ky, got_ly, term_own)
     kv_near = kv_0 + got_kx + got_ky
     kv_sum = scatter_z(
         kv_near.reshape(2, 4, k_in, width).swapaxes(0, 1).reshape(8 * k_in, width)
     )
-    w_near = w_0 + got_wx + got_wy
-    w_sum = scatter_z(w_near)
     tokens_grad, gain1_sum = norm_return(
-        tokens, resid_first, term_own, normed1_there, norm1_gain, (f32,), [kv_near, w_near]
-    )
-    gain1_part, gain2_part = gain1_sum[0], gain2_sum[0]
+        tokens, resid_first, term_own, normed1_there, norm1_gain, (f32,), [kv_near]
+    )
+    gain1_part = gain1_sum[0]
+    gain2_part = gain2_sum[0]
     gains = jnp.concatenate([gain1_part, gain2_part, q_gains[0], k_gains[0]])[None, :]
     gains = gains + swap(gains, "c")
-    gains, act_hi = sync(gains, act_hi)
-    gains_x = swap(gains, "x")
-    mixed_own = to_model([act_lo, act_hi], [dlo, dhi], order, 0, rows, [gain1_sum])
-    mixed_there = swap(mixed_term, "c")
-    gains, gains_x, mixed_own = sync(gains, gains_x, mixed_own)
-    gains = gains + gains_x
-    gains = gains + swap(gains, "y")
-    gains, mixed_own, kv_sum, w_sum, o_sum = sync(gains, mixed_own, kv_sum, w_sum, o_sum)
-    gains_z = lax.ppermute(gains, "z", [(i, i ^ 1) for i in range(4)])
+    gains_xy = lax.ppermute(gains, ("x", "y"), [(i, i ^ 3) for i in range(4)])
+    gains_x, gains_y = swap(gains, "x"), swap(gains, "y")
+    gains = (gains + gains_x) + (gains_y + gains_xy)
+    gains, mixed_own, ow_sum = sync(gains, mixed_own, ow_sum)
+    gains_z = [lax.ppermute(gains, "z", [(i, i ^ k) for i in range(4)]) for k in (1, 2, 3)]
     output = (
         valid * (resid.astype(f32) + mixed_own.astype(f32) + mixed_there.astype(f32))
     ).astype(bf16)
-    gains, gains_z, output = sync(gains, gains_z, output)
-    gains = gains + gains_z
-    gains = (gains + lax.ppermute(gains, "z", [(i, i ^ 2) for i in range(4)]))[0]
+    gains, output, kv_sum, *gains_z = sync(gains, output, kv_sum, *gains_z)
+    o_sum, w_sum = ow_sum[:q_in], ow_sum[q_in:]
+    gains = ((gains + gains_z[0]) + (gains_z[1] + gains_z[2]))[0]
     dlo_sum = dl_0 + got_lx + got_ly
 
     gate_sum, up_sum, down_sum = (

time: 1120 us -> 1090 us (0.973)
  waiting for transfers between devices: 171 us -> 146 us
  starting transfers between devices: 78.7 us -> 100 us
  Pallas kernels: 713 us -> 692 us
    pallas_call x46 -> x44, Pallas kernels: 713 us -> 692 us  [call(): pl.pallas_call(body, grid_spec=pltpu.PrefetchScalarGridSpec(num_scalar_pr...]
    ppermute x2 -> x4, starting transfers between devices: 1.64 us -> 22.6 us  [the longest x3 21.6 us: chip_layer(): lax.ppermute(gains, 'z', [(i, i ^ k) for i in range(4)])]
    reduce_scatter x9 -> x8, waiting for transfers between devices: 13.9 us -> 0.07 us  [scatter_z(): return lax.psum_scatter(array, 'z', scatter_dimension=0, tiled=True)]
    ppermute x81 -> x80, waiting for transfers between devices: 108 us -> 101 us  [swap(): return lax.ppermute(array, axis, SWAP)]
    ppermute x81 -> x80, starting transfers between devices: 75.4 us -> 76 us  [swap(): return lax.ppermute(array, axis, SWAP)]
    unnamed x147 -> x151, local copies, waits for them, and re-layouts: 27.7 us -> 27.2 us
  transfers between devices with their start and end apart: 101 -> 101, of which waited for: 25 -> 21; matrix products, arithmetic and copies ran while one was open for 11% -> 11% of each run, Pallas kernels for 64% -> 64%
where the time goes in v5:
time: 1090 us; the launch traced here: 1080 us
  Pallas kernels  692 us (63%)
  waiting for transfers between devices  146 us (13%)
  starting transfers between devices  100 us (9%)
  other arithmetic  76.3 us (7%)
  local copies, waits for them, and re-layouts  55.2 us (5%)
  between operations  15.4 us (1%)
    pallas_call x44, Pallas kernels, call(): pl.pallas_call(body, grid_spec=pltpu.PrefetchScalarGridSpec(num_scalar_pr...  692 us
    ppermute x80, waiting for transfers between devices, swap(): return lax.ppermute(array, axis, SWAP)  101 us
    ppermute x80, starting transfers between devices, swap(): return lax.ppermute(array, axis, SWAP)  76 us
    all_gather x9, waiting for transfers between devices, gather_z(): return lax.all_gather(array, 'z', axis=0, tiled=True)  43.9 us
    unnamed x151, local copies, waits for them, and re-layouts  27.2 us
  transfers between devices with their start and end apart: 101, of which 21 were waited for; matrix products, arithmetic and copies ran while one was open for 11% of the time, Pallas kernels for 64%

profile of v5, /device:TPU:0, one launch (start us, length us, event | category | flops | bytes accessed | tf_op | source)
XLA Modules:
  0.0 1084.7 jit_solution(14125247160757323714)
XLA Ops:
  50.0 19.9 %all-gather.12.cloned.1.call-done = bf16[256,2048]{1,0:T(8,128)(2,1)} async-done(((bf16[64,2048]{1,0:T(8,128)(2,1)}), bf16[256,2048]{1,0:T(8,128)(2,1)}) %all-gather.12.cloned.1.call-update) | async-done | bytes 1048592 | tf_op jit(solution)/shard_map/all_gather | solution.py:483
  81.4 17.5 %all-gather.14.cloned.1.call-done = bf16[256,2048]{1,0:T(8,128)(2,1)} async-done(((bf16[64,2048]{1,0:T(8,128)(2,1)}), bf16[256,2048]{1,0:T(8,128)(2,1)}) %all-gather.14.cloned.1.call-update) | async-done | bytes 1048592 | tf_op jit(solution)/shard_map/all_gather | solution.py:483
  132.5 11.0 %collective-permute-done.11 = bf16[128,2048]{1,0:T(8,128)(2,1)S(1)} collective-permute-done((bf16[128,2048]{1,0:T(8,128)(2,1)S(1)}, bf16[128,2048]{1,0:T(8,128)(2,1)S(1)}, u32[]{:S(2)}, u32[]{:S(2)}) %collective-permute-start.11) | collective-permute-done | bytes 524320 | tf_op jit(solution)/shard_map/ppermute | solution.py:467
  198.0 22.3 %attend.2 = (bf16[1024,1024]{1,0:T(8,128)(2,1)}, f32[1024,512]{1,0:T(8,128)}) custom-call(s32[2,9]{1,0:T(2,128)} %pad_add_fusion.refs_0_, bf16[1024,1024]{1,0:T(8,128)(2,1)} %make_heads.5.refs_2_.refs_1_, bf16[1024,1024]{1,0:T(8,128)(2,1)} %make_heads.4.refs_2_.refs_5_, bf16[1024,1024]{1,0:T(8,128)(2,1)} %copy-done.9), custom_call_target="tpu_custom_call" | custom-call | flops 1000 | bytes 1000 | tf_op jit(solution)/shard_map/attend/pallas_call | solution.py:525
  261.9 12.6 %collective-permute-done.22.refs_3_.refs_6_ = bf16[1024,1024]{1,0:T(8,128)(2,1)} collective-permute-done((bf16[1024,1024]{1,0:T(8,128)(2,1)S(1)}, bf16[1024,1024]{1,0:T(8,128)(2,1)}, u32[]{:S(2)}, u32[]{:S(2)}) %collective-permute-start.22) | collective-permute-done | bytes 2097184 | tf_op jit(solution)/shard_map/ppermute | solution.py:467
  277.4 22.2 %attend.3 = (bf16[1024,1024]{1,0:T(8,128)(2,1)}, f32[1024,512]{1,0:T(8,128)}) custom-call(s32[2,9]{1,0:T(2,128)} %pad_add_fusion.refs_0_, bf16[1024,1024]{1,0:T(8,128)(2,1)} %make_heads.7.refs_2_.refs_1_, bf16[1024,1024]{1,0:T(8,128)(2,1)} %make_heads.6.refs_2_.refs_5_, bf16[1024,1024]{1,0:T(8,128)(2,1)} %collective-permute-done.22.refs_3_.refs_6_), custom_call_target="tpu_custom_call" | custom-call | flops 1000 | bytes 1000 | tf_op jit(solution)/shard_map/attend/pallas_call | solution.py:525
  306.1 10.5 to_model.8.refs_3_
  322.7 10.5 to_model.9.refs_6_.refs_2_
  333.2 19.2 %to_hidden.12.refs_5_.refs_8_ = bf16[2048,1536]{1,0:T(8,128)(2,1)} custom-call(bf16[1024,2048]{1,0:T(8,128)(2,1)} %reorder.1.refs_0_.refs_1_, bf16[1024,2048]{1,0:T(8,128)(2,1)} %collective-permute-done.27.refs_1_.refs_2_, bf16[1536,512]{1,0:T(8,128)(2,1)} %all-gather.16.cloned.1.call-done.refs_2_.refs_3_, bf16[1536,512]{1,0:T(8,128)(2,1)} %copy-done.6, ...), custom_call_target="tpu_custom_call" | custom-call | flops 1000 | bytes 1000 | tf_op jit(solution)/shard_map/to_hidden/pallas_call | solution.py:525
  371.2 37.6 %ffn.2 = (bf16[2048,1536]{1,0:T(8,128)(2,1)}, bf16[2048,1536]{1,0:T(8,128)(2,1)}, bf16[2048,1536]{1,0:T(8,128)(2,1)}) custom-call(bf16[1024,2048]{1,0:T(8,128)(2,1)} %get-tuple-element.319.refs_0_.refs_4_.refs_1_, bf16[1024,2048]{1,0:T(8,128)(2,1)} %collective-permute-done.30.refs_1_.refs_5_.refs_2_, ...), custom_call_target="tpu_custom_call" | custom-call | flops 1000 | bytes 1000 | tf_op jit(solution)/shard_map/ffn/pallas_call | solution.py:525
  410.1 37.0 %weight_cols.4 = (bf16[1536,2048]{1,0:T(8,128)(2,1)}, bf16[1536,512]{1,0:T(8,128)(2,1)}, bf16[1536,512]{1,0:T(8,128)(2,1)}, bf16[1536,512]{1,0:T(8,128)(2,1)}, b...) custom-call(bf16[2048,1536]{1,0:T(8,128)(2,1)} %get-tuple-element.329.refs_0_.refs_1_, ...), custom_call_target="tpu_custom_call" | custom-call | flops 1000 | bytes 1000 | tf_op jit(solution)/shard_map/weight_cols/pallas_call | solution.py:525
  450.3 19.1 %weight_cols.5 = (bf16[1536,512]{1,0:T(8,128)(2,1)}, bf16[1536,512]{1,0:T(8,128)(2,1)}, bf16[1536,512]{1,0:T(8,128)(2,1)}, bf16[1536,256]{1,0:T(8,128)(2,1)}, bf16[1536,256]{1,0:T(8,128)(2,1)}) custom-call(bf16[2048,1536]{1,0:T(8,128)(2,1)} %get-tuple-element.342.refs_0_.refs_2_, bf16[1024,2048]{1,0:T(8,128)(2,1)} %get-tuple-element.319.refs_0_.refs_4_.refs_1_, ...), custom_call_target="tpu_custom_call" | custom-call | flops 1000 | bytes 1000 | tf_op jit(solution)/shard_map/weight_cols/pallas_call | solution.py:525
  476.5 19.3 %to_hidden.13.refs_8_ = bf16[2048,1536]{1,0:T(8,128)(2,1)} custom-call(bf16[1024,2048]{1,0:T(8,128)(2,1)} %reorder.1.refs_0_.refs_1_, bf16[1024,2048]{1,0:T(8,128)(2,1)} %collective-permute-done.27.refs_1_.refs_2_, bf16[1536,512]{1,0:T(8,128)(2,1)} %all-gather.20.cloned.1.call-done.refs_2_.refs_7_, bf16[1536,512]{1,0:T(8,128)(2,1)} %copy-done.2, ...), custom_call_target="tpu_custom_call" | custom-call | flops 1000 | bytes 1000 | tf_op jit(solution)/shard_map/to_hidden/pallas_call | solution.py:525
  497.1 37.4 %ffn.3 = (bf16[2048,1536]{1,0:T(8,128)(2,1)}, bf16[2048,1536]{1,0:T(8,128)(2,1)}, bf16[2048,1536]{1,0:T(8,128)(2,1)}) custom-call(bf16[1024,2048]{1,0:T(8,128)(2,1)} %get-tuple-element.319.refs_0_.refs_4_.refs_1_, bf16[1024,2048]{1,0:T(8,128)(2,1)} %collective-permute-done.30.refs_1_.refs_5_.refs_2_, ...), custom_call_target="tpu_custom_call" | custom-call | flops 1000 | bytes 1000 | tf_op jit(solution)/shard_map/ffn/pallas_call | solution.py:525
  541.4 37.2 %weight_cols.6 = (bf16[1536,512]{1,0:T(8,128)(2,1)}, bf16[1536,512]{1,0:T(8,128)(2,1)}, bf16[1536,512]{1,0:T(8,128)(2,1)}, bf16[1536,256]{1,0:T(8,128)(2,1)}, bf...) custom-call(bf16[2048,1536]{1,0:T(8,128)(2,1)} %get-tuple-element.47, ...), custom_call_target="tpu_custom_call" | custom-call | flops 1000 | bytes 1000 | tf_op jit(solution)/shard_map/weight_cols/pallas_call | solution.py:525
  584.0 19.2 %weight_cols.7 = (bf16[1536,512]{1,0:T(8,128)(2,1)}, bf16[1536,512]{1,0:T(8,128)(2,1)}, bf16[1536,512]{1,0:T(8,128)(2,1)}, bf16[1536,512]{1,0:T(8,128)(2,1)}) custom-call(bf16[2048,1536]{1,0:T(8,128)(2,1)} %get-tuple-element.394.refs_0_.refs_4_, bf16[1024,2048]{1,0:T(8,128)(2,1)} %get-tuple-element.319.refs_0_.refs_4_.refs_1_, ...), custom_call_target="tpu_custom_call" | custom-call | flops 1000 | bytes 1000 | tf_op jit(solution)/shard_map/weight_cols/pallas_call | solution.py:525
  609.1 34.7 %to_model.10 = bf16[1024,2048]{1,0:T(8,128)(2,1)} custom-call(s32[8]{0:T(128)} %xor_add_fusion.refs_0_, bf16[2048,1536]{1,0:T(8,128)(2,1)} %get-tuple-element.330.refs_3_.refs_1_, bf16[2048,1536]{1,0:T(8,128)(2,1)} %get-tuple-element.342.refs_0_.refs_2_, bf16[2048,1536]{1,0:T(8,128)(2,1)} %get-tuple-element.412.refs_3_, ...), custom_call_target="tpu_custom_call" | custom-call | flops 1000 | bytes 1000 | tf_op jit(solution)/shard_map/to_model/pallas_call | solution.py:525
  649.4 34.6 %to_model.11.refs_2_ = bf16[1024,2048]{1,0:T(8,128)(2,1)} custom-call(s32[8]{0:T(128)} %xor_add_fusion.refs_0_, bf16[2048,1536]{1,0:T(8,128)(2,1)} %get-tuple-element.330.refs_3_.refs_1_, bf16[2048,1536]{1,0:T(8,128)(2,1)} %get-tuple-element.342.refs_0_.refs_2_, bf16[2048,1536]{1,0:T(8,128)(2,1)} %get-tuple-element.412.refs_3_, ...), custom_call_target="tpu_custom_call" | custom-call | flops 1000 | bytes 1000 | tf_op jit(solution)/shard_map/to_model/pallas_call | solution.py:525
  687.2 11.1 %norm_return.2 = (bf16[1024,2048]{1,0:T(8,128)(2,1)}, f32[8,2048]{1,0:T(8,128)}) custom-call(bf16[1024,2048]{1,0:T(8,128)(2,1)} %get-tuple-element.315.refs_0_, bf16[1024,2048]{1,0:T(8,128)(2,1)} %multiply_convert_fusion.1.refs_1_, bf16[1024,2048]{1,0:T(8,128)(2,1)} %to_model.11.refs_2_, bf16[1024,2048]{1,0:T(8,128)(2,1)} %collective-permute-done.51.refs_3_, ...), custom_call_target="tpu_custom_call" | custom-call | flops 1000 | bytes 1000 | tf_op jit(solution)/shard_map/norm_return/pallas_call | solution.py:525
  700.6 20.5 %to_model.12.refs_2_ = bf16[1024,2048]{1,0:T(8,128)(2,1)} custom-call(s32[8]{0:T(128)} %xor_add_fusion.refs_0_, bf16[2048,1536]{1,0:T(8,128)(2,1)} %get-tuple-element.329.refs_0_.refs_1_, bf16[2048,1536]{1,0:T(8,128)(2,1)} %get-tuple-element.471.refs_0_.refs_2_, bf16[1536,512]{1,0:T(8,128)(2,1)} %all-gather.16.cloned.1.call-done.refs_2_.refs_3_, ...), custom_call_target="tpu_custom_call" | custom-call | flops 1000 | bytes 1000 | tf_op jit(solution)/shard_map/to_model/pallas_call | solution.py:525
  742.6 33.5 %attend_back.2 = (bf16[1024,1024]{1,0:T(8,128)(2,1)}, bf16[1024,1024]{1,0:T(8,128)(2,1)}, bf16[1024,1024]{1,0:T(8,128)(2,1)}) custom-call(s32[2,9]{1,0:T(2,128)} %pad_add_fusion.refs_0_, bf16[1024,1024]{1,0:T(8,128)(2,1)} %make_heads.5.refs_2_.refs_1_, bf16[1024,1024]{1,0:T(8,128)(2,1)} %to_hidden.14.refs_2_, ...), custom_call_target="tpu_custom_call" | custom-call | flops 1000 | bytes 1000 | tf_op jit(solution)/shard_map/attend_back/pallas_call | solution.py:525
  776.1 14.5 %weight_rows.3 = (bf16[256,2048]{1,0:T(8,128)(2,1)}, bf16[256,2048]{1,0:T(8,128)(2,1)}, bf16[256,2048]{1,0:T(8,128)(2,1)}, bf16[256,2048]{1,0:T(8,128)(2,1)}) custom-call(bf16[1024,1024]{1,0:T(8,128)(2,1)} %get-tuple-element.300.refs_1_.refs_3_.refs_0_, bf16[1024,1024]{1,0:T(8,128)(2,1)} %get-tuple-element.311.refs_1_.refs_3_, ...), custom_call_target="tpu_custom_call" | custom-call | flops 1000 | bytes 1000 | tf_op jit(solution)/shard_map/weight_rows/pallas_call | solution.py:525
  790.6 17.5 %collective-permute-done.56 = bf16[1536,512]{1,0:T(8,128)(2,1)} collective-permute-done((bf16[1536,512]{1,0:T(8,128)(2,1)S(1)}, bf16[1536,512]{1,0:T(8,128)(2,1)}, u32[]{:S(2)}, u32[]{:S(2)}) %collective-permute-start.56) | collective-permute-done | bytes 1572896 | tf_op jit(solution)/shard_map/ppermute | solution.py:467
  830.4 33.6 %attend_back.3 = (bf16[1024,1024]{1,0:T(8,128)(2,1)}, bf16[1024,1024]{1,0:T(8,128)(2,1)}, bf16[1024,1024]{1,0:T(8,128)(2,1)}) custom-call(s32[2,9]{1,0:T(2,128)} %pad_add_fusion.refs_0_, bf16[1024,1024]{1,0:T(8,128)(2,1)} %make_heads.7.refs_2_.refs_1_, bf16[1024,1024]{1,0:T(8,128)(2,1)} %to_hidden.15.refs_2_, ...), custom_call_target="tpu_custom_call" | custom-call | flops 1000 | bytes 1000 | tf_op jit(solution)/shard_map/attend_back/pallas_call | solution.py:525
  882.6 14.4 %weight_rows.4 = (bf16[256,2048]{1,0:T(8,128)(2,1)}, bf16[256,2048]{1,0:T(8,128)(2,1)}, bf16[256,2048]{1,0:T(8,128)(2,1)}, bf16[256,2048]{1,0:T(8,128)(2,1)}) custom-call(bf16[1024,1024]{1,0:T(8,128)(2,1)} %get-tuple-element.467.refs_5_.refs_0_.refs_1_, bf16[1024,1024]{1,0:T(8,128)(2,1)} %get-tuple-element.468.refs_1_, ...), custom_call_target="tpu_custom_call" | custom-call | flops 1000 | bytes 1000 | tf_op jit(solution)/shard_map/weight_rows/pallas_call | solution.py:525
  897.2 20.6 %to_model.13.refs_6_ = bf16[1024,2048]{1,0:T(8,128)(2,1)} custom-call(s32[8]{0:T(128)} %xor_add_fusion.refs_0_, bf16[2048,1536]{1,0:T(8,128)(2,1)} %get-tuple-element.329.refs_0_.refs_1_, bf16[2048,1536]{1,0:T(8,128)(2,1)} %get-tuple-element.471.refs_0_.refs_2_, bf16[1536,512]{1,0:T(8,128)(2,1)} %all-gather.16.cloned.1.call-done.refs_2_.refs_3_, ...), custom_call_target="tpu_custom_call" | custom-call | flops 1000 | bytes 1000 | tf_op jit(solution)/shard_map/to_model/pallas_call | solution.py:525
  943.7 14.4 %weight_rows.5 = (bf16[256,2048]{1,0:T(8,128)(2,1)}, bf16[256,2048]{1,0:T(8,128)(2,1)}, bf16[256,2048]{1,0:T(8,128)(2,1)}, bf16[256,2048]{1,0:T(8,128)(2,1)}) custom-call(bf16[1024,1024]{1,0:T(8,128)(2,1)} %get-tuple-element.480.refs_0_.refs_2_, bf16[1024,1024]{1,0:T(8,128)(2,1)} %get-tuple-element.496.refs_1_.refs_2_, ...), custom_call_target="tpu_custom_call" | custom-call | flops 1000 | bytes 1000 | tf_op jit(solution)/shard_map/weight_rows/pallas_call | solution.py:525
  960.5 15.4 %to_model.14 = bf16[1024,2048]{1,0:T(8,128)(2,1)} custom-call(s32[8]{0:T(128)} %iota.44.refs_0_, bf16[1024,1024]{1,0:T(8,128)(2,1)} %get-tuple-element.468.refs_1_, bf16[1024,1024]{1,0:T(8,128)(2,1)} %get-tuple-element.496.refs_1_.refs_2_, bf16[1024,2048]{1,0:T(8,128)(2,1)} %constant_dynamic-update-slice_fusion.8.refs_1_.refs_3_, ...), custom_call_target="tpu_custom_call" | custom-call | flops 1000 | bytes 1000 | tf_op jit(solution)/shard_map/to_model/pallas_call | solution.py:525
  996.5 15.6 %to_model.15.refs_2_ = bf16[1024,2048]{1,0:T(8,128)(2,1)} custom-call(s32[8]{0:T(128)} %iota.45.refs_0_, bf16[1024,1024]{1,0:T(8,128)(2,1)} %get-tuple-element.467.refs_5_.refs_0_.refs_1_, bf16[1024,1024]{1,0:T(8,128)(2,1)} %get-tuple-element.480.refs_0_.refs_2_, bf16[1024,2048]{1,0:T(8,128)(2,1)} %constant_dynamic-update-slice_fusion.8.refs_1_.refs_3_, ...), custom_call_target="tpu_custom_call" | custom-call | flops 1000 | bytes 1000 | tf_op jit(solution)/shard_map/to_model/pallas_call | solution.py:525
  1021.8 12.2 %norm_return.3 = (f32[1024,2048]{1,0:T(8,128)}, f32[8,2048]{1,0:T(8,128)}) custom-call(bf16[1024,2048]{1,0:T(8,128)(2,1)} %refs_0_.1, bf16[1024,2048]{1,0:T(8,128)(2,1)} %get-tuple-element.421.refs_12_.refs_0_.refs_2_.refs_1_, bf16[1024,2048]{1,0:T(8,128)(2,1)} %to_model.15.refs_2_, bf16[1024,2048]{1,0:T(8,128)(2,1)} %collective-permute-done.74.refs_3_, ...), custom_call_target="tpu_custom_call" | custom-call | flops 1000 | bytes 1000 | tf_op jit(solution)/shard_map/norm_return/pallas_call | solution.py:525
  1044.5 10.8 collective-permute-start.82
  1055.3 10.8 collective-permute-start.81
  (501 shorter events, 402.8 us)
Async XLA Ops:
  8.9 60.9 %all-gather.12.cloned.1.call-start = ((), (), s32[]{:S(2)}) async-start(), calls=%async_computation.9 | async-start | bytes 1310720 | tf_op jit(solution)/shard_map/all_gather | solution.py:483
  9.7 89.2 %all-gather.14.cloned.1.call-start = ((), (), s32[]{:S(2)}) async-start(), calls=%async_computation.10 | async-start | bytes 1310720 | tf_op jit(solution)/shard_map/all_gather | solution.py:483
  12.6 168.3 %all-gather.16.cloned.1.call-start = ((), (), s32[]{:S(2)}) async-start(), calls=%async_computation.11 | async-start | bytes 1966080 | tf_op jit(solution)/shard_map/all_gather | solution.py:483
  32.7 132.0 %collective-permute-start.19 = (bf16[1024,2048]{1,0:T(8,128)(2,1)}, bf16[1024,2048]{1,0:T(8,128)(2,1)}, u32[]{:S(2)}, u32[]{:S(2)}) collective-permute-start(bf16[1024,2048]{1,0:T(8,128)(2,1)} %fusion.2.refs_0_.refs_2_), channel_id=1, source_target_pairs={{0,8},{8,0},{1,9},{9,1},{2,10},{10,2},{3,11},{11,3},{4,12},{12,4},... | collective-permute-start | bytes 12582920 | tf_op jit(solution)/shard_map/ppermute | solution.py:467
  46.7 207.7 %all-gather.18.cloned.1.call-start = ((), (), s32[]{:S(2)}) async-start(), calls=%async_computation.12 | async-start | bytes 1966080 | tf_op jit(solution)/shard_map/all_gather | solution.py:483
  143.8 218.7 %all-gather.20.cloned.1.call-start = ((), (), s32[]{:S(2)}) async-start(), calls=%async_computation.13 | async-start | bytes 1966080 | tf_op jit(solution)/shard_map/all_gather | solution.py:483
  145.5 219.3 %all-gather.22.cloned.1.call-start = ((), (), s32[]{:S(2)}) async-start(), calls=%async_computation.14 | async-start | bytes 7864320 | tf_op jit(solution)/shard_map/all_gather | solution.py:483
  193.7 215.1 %all-gather.24.cloned.1.call-start = ((), (), s32[]{:S(2)}) async-start(), calls=%async_computation.15 | async-start | bytes 1966080 | tf_op jit(solution)/shard_map/all_gather | solution.py:483
  232.6 264.4 %all-gather.26.cloned.1.call-start = ((), (), s32[]{:S(2)}) async-start(), calls=%async_computation.16 | async-start | bytes 7864320 | tf_op jit(solution)/shard_map/all_gather | solution.py:483
  277.4 55.8 %collective-permute-start.27 = (bf16[1024,2048]{1,0:T(8,128)(2,1)}, bf16[1024,2048]{1,0:T(8,128)(2,1)}, u32[]{:S(2)}, u32[]{:S(2)}) collective-permute-start(bf16[1024,2048]{1,0:T(8,128)(2,1)} %reorder.1.refs_0_.refs_1_), channel_id=1, source_target_pairs={{0,8},{8,0},{1,9},{9,1},{2,10},{10,2},{3,11},{11,3},{4,12},{12,4},... | collective-permute-start | bytes 12582920 | tf_op jit(solution)/shard_map/ppermute | solution.py:467
  316.6 492.7 %reduce-scatter.9.cloned.1.call-start = ((), (), s32[]{:S(2)}) async-start(), calls=%async_computation.17 | async-start | bytes 7864320 | tf_op jit(solution)/shard_map/reduce_scatter | solution.py:487
  447.1 539.0 %reduce-scatter.15.cloned.1.call-start = ((), (), s32[]{:S(2)}) async-start(), calls=%async_computation.20 | async-start | bytes 1966080 | tf_op jit(solution)/shard_map/reduce_scatter | solution.py:487
  473.6 60.9 %collective-permute-start.41 = (bf16[1536,256]{1,0:T(8,128)(2,1)}, bf16[1536,256]{1,0:T(8,128)(2,1)}, u32[]{:S(2)}, u32[]{:S(2)}) collective-permute-start(bf16[1536,256]{1,0:T(8,128)(2,1)} %get-tuple-element.357), channel_id=1, source_target_pairs={{0,16},{16,0},{1,17},{17,1},{2,18},{18,2},{3,19},{19,3},{4,20},{20... | collective-permute-start | bytes 2359304 | tf_op jit(solution)/shard_map/ppermute | solution.py:467
  475.0 59.5 %collective-permute-start.42 = (bf16[1536,256]{1,0:T(8,128)(2,1)}, bf16[1536,256]{1,0:T(8,128)(2,1)}, u32[]{:S(2)}, u32[]{:S(2)}) collective-permute-start(bf16[1536,256]{1,0:T(8,128)(2,1)} %get-tuple-element.358), channel_id=1, source_target_pairs={{0,4},{4,0},{1,5},{5,1},{2,6},{6,2},{3,7},{7,3},{8,12},{12,8},{9,1... | collective-permute-start | bytes 2359304 | tf_op jit(solution)/shard_map/ppermute | solution.py:467
  645.6 342.3 %reduce-scatter.19.cloned.1.call-start = ((), (), s32[]{:S(2)}) async-start(), calls=%async_computation.22 | async-start | bytes 1966080 | tf_op jit(solution)/shard_map/reduce_scatter | solution.py:487
  698.4 77.7 %collective-permute-start.58 = (bf16[1024,2048]{1,0:T(8,128)(2,1)}, bf16[1024,2048]{1,0:T(8,128)(2,1)}, u32[]{:S(2)}, u32[]{:S(2)}) collective-permute-start(bf16[1024,2048]{1,0:T(8,128)(2,1)} %get-tuple-element.421.refs_12_.refs_0_.refs_2_.refs_1_), channel_id=1, source_target_pairs={{0,8},{8,0},{1,9},{9,1},{2,10},{10,2},{3,11},{11,3},{4,12},{12,4},... | collective-permute-start | bytes 12582920 | tf_op jit(solution)/shard_map/ppermute | solution.py:467
  700.5 288.4 %reduce-scatter.17.cloned.1.call-start = ((), (), s32[]{:S(2)}) async-start(), calls=%async_computation.21 | async-start | bytes 1966080 | tf_op jit(solution)/shard_map/reduce_scatter | solution.py:487
  738.5 52.1 %collective-permute-start.54 = (bf16[1536,512]{1,0:T(8,128)(2,1)S(1)}, bf16[1536,512]{1,0:T(8,128)(2,1)S(1)}, u32[]{:S(2)}, u32[]{:S(2)}) collective-permute-start(bf16[1536,512]{1,0:T(8,128)(2,1)S(1)} %copy-done.66), channel_id=1, source_target_pairs={{0,16},{16,0},{1,17},{17,1},{2,18},{18,2},{3,19},{19,3},{4,20},{20... | collective-permute-start | bytes 4718600 | tf_op jit(solution)/shard_map/ppermute | solution.py:467
  740.0 50.6 %collective-permute-start.55 = (bf16[1536,512]{1,0:T(8,128)(2,1)S(1)}, bf16[1536,512]{1,0:T(8,128)(2,1)}, u32[]{:S(2)}, u32[]{:S(2)}) collective-permute-start(bf16[1536,512]{1,0:T(8,128)(2,1)S(1)} %add.264), channel_id=1, source_target_pairs={{0,4},{4,0},{1,5},{5,1},{2,6},{6,2},{3,7},{7,3},{8,12},{12,8},{9,1... | collective-permute-start | bytes 4718600 | tf_op jit(solution)/shard_map/ppermute | solution.py:467
  741.5 66.7 %collective-permute-start.56 = (bf16[1536,512]{1,0:T(8,128)(2,1)S(1)}, bf16[1536,512]{1,0:T(8,128)(2,1)}, u32[]{:S(2)}, u32[]{:S(2)}) collective-permute-start(bf16[1536,512]{1,0:T(8,128)(2,1)S(1)} %add.265), channel_id=1, source_target_pairs={{0,16},{16,0},{1,17},{17,1},{2,18},{18,2},{3,19},{19,3},{4,20},{20... | collective-permute-start | bytes 4718600 | tf_op jit(solution)/shard_map/ppermute | solution.py:467
  742.0 67.2 %collective-permute-start.57 = (bf16[1536,512]{1,0:T(8,128)(2,1)}, bf16[1536,512]{1,0:T(8,128)(2,1)}, u32[]{:S(2)}, u32[]{:S(2)}) collective-permute-start(bf16[1536,512]{1,0:T(8,128)(2,1)} %get-tuple-element.443), channel_id=1, source_target_pairs={{0,4},{4,0},{1,5},{5,1},{2,6},{6,2},{3,7},{7,3},{8,12},{12,8},{9,1... | collective-permute-start | bytes 4718600 | tf_op jit(solution)/shard_map/ppermute | solution.py:467
  812.1 181.9 %reduce-scatter.21.cloned.1.call-start = ((), (), s32[]{:S(2)}) async-start(), calls=%async_computation.23 | async-start | bytes 1966080 | tf_op jit(solution)/shard_map/reduce_scatter | solution.py:487
  812.1 59.0 %collective-permute-start.59 = (bf16[1024,1024]{1,0:T(8,128)(2,1)}, bf16[1024,1024]{1,0:T(8,128)(2,1)S(1)}, u32[]{:S(2)}, u32[]{:S(2)}) collective-permute-start(bf16[1024,1024]{1,0:T(8,128)(2,1)} %get-tuple-element.457), channel_id=1, source_target_pairs={{0,4},{4,0},{1,5},{5,1},{2,6},{6,2},{3,7},{7,3},{8,12},{12,8},{9,1... | collective-permute-start | bytes 6291464 | tf_op jit(solution)/shard_map/ppermute | solution.py:467
  813.7 57.4 %collective-permute-start.60 = (bf16[256,2048]{1,0:T(8,128)(2,1)}, bf16[256,2048]{1,0:T(8,128)(2,1)S(1)}, u32[]{:S(2)}, u32[]{:S(2)}) collective-permute-start(bf16[256,2048]{1,0:T(8,128)(2,1)} %get-tuple-element.460), channel_id=1, source_target_pairs={{0,16},{16,0},{1,17},{17,1},{2,18},{18,2},{3,19},{19,3},{4,20},{20... | collective-permute-start | bytes 3145736 | tf_op jit(solution)/shard_map/ppermute | solution.py:467
  818.0 195.4 %reduce-scatter.23.cloned.1.call-start = ((), (), s32[]{:S(2)}) async-start(), calls=%async_computation.24 | async-start | bytes 1966080 | tf_op jit(solution)/shard_map/reduce_scatter | solution.py:487
  819.4 51.7 %collective-permute-start.62 = (bf16[384,512]{1,0:T(8,128)(2,1)S(1)}, bf16[384,512]{1,0:T(8,128)(2,1)S(1)}, u32[]{:S(2)}, u32[]{:S(2)}) collective-permute-start(bf16[384,512]{1,0:T(8,128)(2,1)S(1)} %get-tuple-element.561), channel_id=1, source_target_pairs={{0,16},{16,0},{1,17},{17,1},{2,18},{18,2},{3,19},{19,3},{4,20},{20... | collective-permute-start | bytes 1179656 | tf_op jit(solution)/shard_map/ppermute | solution.py:467
  820.9 50.2 %collective-permute-start.61 = (bf16[384,512]{1,0:T(8,128)(2,1)S(1)}, bf16[384,512]{1,0:T(8,128)(2,1)S(1)}, u32[]{:S(2)}, u32[]{:S(2)}) collective-permute-start(bf16[384,512]{1,0:T(8,128)(2,1)S(1)} %get-tuple-element.563), channel_id=1, source_target_pairs={{0,16},{16,0},{1,17},{17,1},{2,18},{18,2},{3,19},{19,3},{4,20},{20... | collective-permute-start | bytes 1179656 | tf_op jit(solution)/shard_map/ppermute | solution.py:467
  871.1 55.3 %collective-permute-start.63 = (bf16[1024,1024]{1,0:T(8,128)(2,1)}, bf16[1024,1024]{1,0:T(8,128)(2,1)}, u32[]{:S(2)}, u32[]{:S(2)}) collective-permute-start(bf16[1024,1024]{1,0:T(8,128)(2,1)} %get-tuple-element.465), channel_id=1, source_target_pairs={{0,4},{4,0},{1,5},{5,1},{2,6},{6,2},{3,7},{7,3},{8,12},{12,8},{9,1... | collective-permute-start | bytes 6291464 | tf_op jit(solution)/shard_map/ppermute | solution.py:467
  928.4 116.1 %reduce-scatter.11.cloned.1.call-start = ((), (), s32[]{:S(2)}) async-start(), calls=%async_computation.18 | async-start | bytes 2621440 | tf_op jit(solution)/shard_map/reduce_scatter | solution.py:487
  928.8 47.0 %collective-permute-start.68 = (bf16[256,2048]{1,0:T(8,128)(2,1)S(1)}, bf16[256,2048]{1,0:T(8,128)(2,1)S(1)}, u32[]{:S(2)}, u32[]{:S(2)}) collective-permute-start(bf16[256,2048]{1,0:T(8,128)(2,1)S(1)} %add.272), channel_id=1, source_target_pairs={{0,4},{4,0},{1,5},{5,1},{2,6},{6,2},{3,7},{7,3},{8,12},{12,8},{9,1... | collective-permute-start | bytes 3145736 | tf_op jit(solution)/shard_map/ppermute | solution.py:467
  982.7 92.3 %reduce-scatter.13.cloned.1.call-start = ((), (), s32[]{:S(2)}) async-start(), calls=%async_computation.19 | async-start | bytes 1310720 | tf_op jit(solution)/shard_map/reduce_scatter | solution.py:487
  1016.8 49.3 %collective-permute-start.79 = (bf16[1024,2048]{1,0:T(8,128)(2,1)}, bf16[1024,2048]{1,0:T(8,128)(2,1)}, u32[]{:S(2)}, u32[]{:S(2)}) collective-permute-start(bf16[1024,2048]{1,0:T(8,128)(2,1)} %to_model.12.refs_2_), channel_id=1, source_target_pairs={{0,8},{8,0},{1,9},{9,1},{2,10},{10,2},{3,11},{11,3},{4,12},{12,4},... | collective-permute-start | bytes 12582920 | tf_op jit(solution)/shard_map/ppermute | solution.py:467
  (137 other events, 2691.9 us)
Sparse Core Ops, SparseCore 0:
  10.2 30.6 all-gather.9
  42.4 27.4 all-gather.11
  71.4 27.4 all-gather.13
  100.9 36.5 all-gather.15
  144.0 37.1 all-gather.17
  183.2 35.9 all-gather.19
  220.8 114.1 all-gather.21
  337.1 35.3 all-gather.23
  374.1 114.2 all-gather.25
  490.5 108.9 reduce-scatter.8
  645.7 39.2 reduce-scatter.14
  700.6 39.0 reduce-scatter.18
  812.2 38.9 reduce-scatter.16
  853.4 34.2 reduce-scatter.20
  928.5 44.9 reduce-scatter.22
  982.8 57.9 reduce-scatter.10
  1043.0 27.4 reduce-scatter.12

commit v6 on v5

--- a/solution.py
+++ b/solution.py
@@ -1332,31 +1332,30 @@
     ghi_x, ghi_y = swap(ghi_0, "x"), swap(ghi_0, "y")
 
     widths = [fourth, fourth, fourth, eighth, eighth]
-    dlo_grad, gl_0, gl_x, gl_y, gl_ca, gl_cb = weight_cols(
-        (act_lo, dy, [width]), (gg_lo, normed2, widths)
-    )
-    dlo_grad, gl_ca, gl_cb, ghi_x, ghi_y, ug_lo, dhi_x, dhi_y = sync(
-        dlo_grad, gl_ca, gl_cb, ghi_x, ghi_y, ug_lo, dhi_x, dhi_y
+    pieces = [fourth] * 4
+    dlo_grad, gl_0, gl_x, gl_y, gl_c = weight_cols(
+        (act_lo, dy, [width]), (gg_lo, normed2, pieces)
+    )
+    dlo_grad, gl_c, ghi_x, ghi_y, ug_lo, dhi_x, dhi_y = sync(
+        dlo_grad, gl_c, ghi_x, ghi_y, ug_lo, dhi_x, dhi_y
     )
     dlo_sum = scatter_z(dlo_grad)
     dhi_ca, dhi_cb = swap(dhi_y[:, :eighth], "x"), swap(dhi_x[:, eighth:], "y")
-    ul_0, ul_x, ul_y, ul_ca, ul_cb = weight_cols((ug_lo, normed2, widths))
-    dhi_ca, dhi_cb, ul_ca, ul_cb, ghi_x, ghi_y = sync(dhi_ca, dhi_cb, ul_ca, ul_cb, ghi_x, ghi_y)
+    ul_0, ul_x, ul_y, ul_c = weight_cols((ug_lo, normed2, pieces))
+    dhi_ca, dhi_cb, ul_c, ghi_x, ghi_y = sync(dhi_ca, dhi_cb, ul_c, ghi_x, ghi_y)
     dhi = [dhi_0, dhi_x, dhi_y, dhi_ca, dhi_cb]
     ghi_ca, ghi_cb = swap(ghi_y[:, :eighth], "x"), swap(ghi_x[:, eighth:], "y")
     d_act_hi = to_hidden(dy, dhi)
-    ghi_ca, ghi_cb, gl_ca, gl_cb, d_act_hi = sync(ghi_ca, ghi_cb, gl_ca, gl_cb, d_act_hi)
+    ghi_ca, ghi_cb, gl_c, ul_c, d_act_hi = sync(ghi_ca, ghi_cb, gl_c, ul_c, d_act_hi)
     ghi = [ghi_0, ghi_x, ghi_y, ghi_ca, ghi_cb]
-    from_a, from_b = swap(gl_ca, "x"), swap(gl_cb, "y")
-    from_ua, from_ub = swap(ul_ca, "x"), swap(ul_cb, "y")
+    from_g, from_u = swap(gl_c, "x"), swap(ul_c, "y")
     act_hi, gg_hi, ug_hi = ffn(normed2, ghi, uhi, d_act_hi)
-    gl_x, gl_y, from_a, from_b, ul_x, ul_y, from_ua, from_ub, act_hi, gg_hi, ug_hi = sync(
-        gl_x, gl_y, from_a, from_b, ul_x, ul_y, from_ua, from_ub, act_hi, gg_hi, ug_hi
-    )
-    gl_x, gl_y = add_halves(gl_x, gl_y, from_a, from_b)
+    gl_x, gl_y, from_g, ul_x, ul_y, from_u, act_hi, gg_hi, ug_hi = sync(
+        gl_x, gl_y, from_g, ul_x, ul_y, from_u, act_hi, gg_hi, ug_hi
+    )
+    gl_y = gl_y + from_g
     gl_x, gl_y, gg_hi = sync(gl_x, gl_y, gg_hi)
     got_x, got_y = swap(gl_x, "x"), swap(gl_y, "y")
-    pieces = [fourth] * 4
     dh_0, dh_x, dh_y, dh_ca, dh_cb, gh_0, gh_x, gh_y, gh_c = weight_cols(
         (act_hi, dy, widths), (gg_hi, normed2, pieces)
     )
@@ -1366,7 +1365,7 @@
     from_a, from_b = swap(dh_ca, "x"), swap(dh_cb, "y")
     glo_near = gl_0 + got_x + got_y
     glo_sum = scatter_z(glo_near)
-    ul_x, ul_y = add_halves(ul_x, ul_y, from_ua, from_ub)
+    ul_x = ul_x + from_u
     uh_0, uh_x, uh_y, uh_c = weight_cols(
         (ug_hi, normed2, pieces), after=[glo_near, ul_x]
     )
@@ -1409,8 +1408,9 @@
 
     dq0, dkv0, dkv0_far = attend_back(0, info, query[0], d_attn0, attn0, totals0, kv[0], kv_far0)
     o_0, o_x, o_y, o_c = weight_rows([attn0, attn1], [resid_here, resid_there], 4, [dq0])
-    gh_0, got_x, got_y, uh_0, got_ux, got_uy, resid_there, dkv0_far, dlo_sum, o_c = sync(
-        gh_0, got_x, got_y, uh_0, got_ux, got_uy, resid_there, dkv0_far, dlo_sum, o_c
+    d_attn1 = to_hidden([resid_there], [out_w], bf16, [o_0])
+    gh_0, got_x, got_y, uh_0, got_ux, got_uy, d_attn1, dkv0_far, dlo_sum, o_c = sync(
+        gh_0, got_x, got_y, uh_0, got_ux, got_uy, d_attn1, dkv0_far, dlo_sum, o_c
     )
     dkv0_back, from_o = swap(dkv0_far, "y"), swap(o_c, "x")
     dl_0, dl_x, dl_y, dl_c = (dlo_sum[:, i * fourth : (i + 1) * fourth] for i in range(4))
@@ -1418,8 +1418,9 @@
     ghi_near, uhi_near = gh_0 + got_x + got_y, uh_0 + got_ux + got_uy
     ghi_sum, uhi_sum = scatter_z(ghi_near), scatter_z(uhi_near)
     back = (cos_tab, sin_tab)
-    d_attn1 = to_hidden([resid_there], [out_w], bf16, [ghi_near, uhi_near])
-    dq1, dkv1, dkv1_far = attend_back(1, info, query[1], d_attn1, attn1, totals1, kv[1], kv_far1)
+    dq1, dkv1, dkv1_far = attend_back(
+        1, info, query[1], d_attn1, attn1, totals1, kv[1], kv_far1, [ghi_near, uhi_near]
+    )
     q_grad0, q_gain0 = heads_return(0, q_raw[0], dq0, [], *back, query_gain, 1, [dq1])
     dkv1_far, dkv0_back, o_x, o_y, from_o, got_lx, dl_y, from_l, q_grad0 = sync(
         dkv1_far, dkv0_back, o_x, o_y, from_o, got_lx, dl_y, from_l, q_grad0

time: 1090 us -> 1080 us (level)
  waiting for transfers between devices: 146 us -> 130 us
    ppermute x80 -> x78, waiting for transfers between devices: 101 us -> 85 us  [swap(): return lax.ppermute(array, axis, SWAP)]
    pallas_call x44 -> x42, Pallas kernels: 692 us -> 699 us  [call(): pl.pallas_call(body, grid_spec=pltpu.PrefetchScalarGridSpec(num_scalar_pr...]
    ppermute x80 -> x78, starting transfers between devices: 76 us -> 78 us  [swap(): return lax.ppermute(array, axis, SWAP)]
  transfers between devices with their start and end apart: 101 -> 99, of which waited for: 21 -> 19; matrix products, arithmetic and copies ran while one was open for 11% -> 12% of each run, Pallas kernels for 64% -> 65%
where the time goes in v6:
time: 1080 us
  Pallas kernels  699 us (65%)
  waiting for transfers between devices  130 us (12%)
  starting transfers between devices  94.1 us (9%)
  other arithmetic  83.9 us (8%)
  local copies, waits for them, and re-layouts  53 us (5%)
  between operations  15.4 us (1%)
    pallas_call x42, Pallas kernels, call(): pl.pallas_call(body, grid_spec=pltpu.PrefetchScalarGridSpec(num_scalar_pr...  699 us
    ppermute x78, waiting for transfers between devices, swap(): return lax.ppermute(array, axis, SWAP)  85 us
    ppermute x78, starting transfers between devices, swap(): return lax.ppermute(array, axis, SWAP)  78 us
    all_gather x9, waiting for transfers between devices, gather_z(): return lax.all_gather(array, 'z', axis=0, tiled=True)  43.9 us
    unnamed x151, local copies, waits for them, and re-layouts  25.1 us
  transfers between devices with their start and end apart: 99, of which 19 were waited for; matrix products, arithmetic and copies ran while one was open for 12% of the time, Pallas kernels for 65%

profile of v6, /device:TPU:0, one launch (start us, length us, event | category | flops | bytes accessed | tf_op | source)
XLA Modules:
  0.0 1075.8 jit_solution(8399331904625238396)
XLA Ops:
  50.0 19.9 %all-gather.12.cloned.1.call-done = bf16[256,2048]{1,0:T(8,128)(2,1)} async-done(((bf16[64,2048]{1,0:T(8,128)(2,1)}), bf16[256,2048]{1,0:T(8,128)(2,1)}) %all-gather.12.cloned.1.call-update) | async-done | bytes 1048592 | tf_op jit(solution)/shard_map/all_gather | solution.py:483
  81.4 17.5 %all-gather.14.cloned.1.call-done = bf16[256,2048]{1,0:T(8,128)(2,1)} async-done(((bf16[64,2048]{1,0:T(8,128)(2,1)}), bf16[256,2048]{1,0:T(8,128)(2,1)}) %all-gather.14.cloned.1.call-update) | async-done | bytes 1048592 | tf_op jit(solution)/shard_map/all_gather | solution.py:483
  98.9 9.5 collective-permute-done.6
  132.5 10.9 %collective-permute-done.11 = bf16[128,2048]{1,0:T(8,128)(2,1)S(1)} collective-permute-done((bf16[128,2048]{1,0:T(8,128)(2,1)S(1)}, bf16[128,2048]{1,0:T(8,128)(2,1)S(1)}, u32[]{:S(2)}, u32[]{:S(2)}) %collective-permute-start.11) | collective-permute-done | bytes 524320 | tf_op jit(solution)/shard_map/ppermute | solution.py:467
  198.0 28.2 %attend.2 = (bf16[1024,1024]{1,0:T(8,128)(2,1)}, f32[1024,512]{1,0:T(8,128)}) custom-call(s32[2,9]{1,0:T(2,128)} %pad_add_fusion.refs_0_, bf16[1024,1024]{1,0:T(8,128)(2,1)} %make_heads.5.refs_2_.refs_1_, bf16[1024,1024]{1,0:T(8,128)(2,1)} %make_heads.4.refs_2_.refs_5_, bf16[1024,1024]{1,0:T(8,128)(2,1)} %copy-done.9), custom_call_target="tpu_custom_call" | custom-call | flops 1000 | bytes 1000 | tf_op jit(solution)/shard_map/attend/pallas_call | solution.py:525
  262.6 11.5 %collective-permute-done.22.refs_3_.refs_6_ = bf16[1024,1024]{1,0:T(8,128)(2,1)} collective-permute-done((bf16[1024,1024]{1,0:T(8,128)(2,1)S(1)}, bf16[1024,1024]{1,0:T(8,128)(2,1)}, u32[]{:S(2)}, u32[]{:S(2)}) %collective-permute-start.22) | collective-permute-done | bytes 2097184 | tf_op jit(solution)/shard_map/ppermute | solution.py:467
  277.4 22.2 %attend.3 = (bf16[1024,1024]{1,0:T(8,128)(2,1)}, f32[1024,512]{1,0:T(8,128)}) custom-call(s32[2,9]{1,0:T(2,128)} %pad_add_fusion.refs_0_, bf16[1024,1024]{1,0:T(8,128)(2,1)} %make_heads.7.refs_2_.refs_1_, bf16[1024,1024]{1,0:T(8,128)(2,1)} %make_heads.6.refs_2_.refs_5_, bf16[1024,1024]{1,0:T(8,128)(2,1)} %collective-permute-done.22.refs_3_.refs_6_), custom_call_target="tpu_custom_call" | custom-call | flops 1000 | bytes 1000 | tf_op jit(solution)/shard_map/attend/pallas_call | solution.py:525
  306.4 10.4 to_model.8.refs_3_
  322.7 10.5 to_model.9.refs_6_.refs_2_
  333.2 19.2 %to_hidden.12.refs_5_.refs_8_ = bf16[2048,1536]{1,0:T(8,128)(2,1)} custom-call(bf16[1024,2048]{1,0:T(8,128)(2,1)} %reorder.1.refs_0_.refs_1_, bf16[1024,2048]{1,0:T(8,128)(2,1)} %collective-permute-done.27.refs_1_.refs_2_, bf16[1536,512]{1,0:T(8,128)(2,1)} %all-gather.16.cloned.1.call-done.refs_2_.refs_3_, bf16[1536,512]{1,0:T(8,128)(2,1)} %copy-done.6, ...), custom_call_target="tpu_custom_call" | custom-call | flops 1000 | bytes 1000 | tf_op jit(solution)/shard_map/to_hidden/pallas_call | solution.py:525
  352.4 10.0 resid_norm.1
  371.1 37.6 %ffn.2 = (bf16[2048,1536]{1,0:T(8,128)(2,1)}, bf16[2048,1536]{1,0:T(8,128)(2,1)}, bf16[2048,1536]{1,0:T(8,128)(2,1)}) custom-call(bf16[1024,2048]{1,0:T(8,128)(2,1)} %get-tuple-element.309.refs_0_.refs_4_.refs_1_, bf16[1024,2048]{1,0:T(8,128)(2,1)} %collective-permute-done.30.refs_1_.refs_5_.refs_2_, ...), custom_call_target="tpu_custom_call" | custom-call | flops 1000 | bytes 1000 | tf_op jit(solution)/shard_map/ffn/pallas_call | solution.py:525
  410.4 36.9 %weight_cols.4 = (bf16[1536,2048]{1,0:T(8,128)(2,1)}, bf16[1536,512]{1,0:T(8,128)(2,1)}, bf16[1536,512]{1,0:T(8,128)(2,1)}, bf16[1536,512]{1,0:T(8,128)(2,1)}, bf16[1536,512]{1,0:T(8,128)(2,1)}) custom-call(bf16[2048,1536]{1,0:T(8,128)(2,1)} %get-tuple-element.319.refs_0_.refs_1_, bf16[1024,2048]{1,0:T(8,128)(2,1)} %reorder.1.refs_0_.refs_1_, ...), custom_call_target="tpu_custom_call" | custom-call | flops 1000 | bytes 1000 | tf_op jit(solution)/shard_map/weight_cols/pallas_call | solution.py:525
  450.1 19.0 %weight_cols.5 = (bf16[1536,512]{1,0:T(8,128)(2,1)}, bf16[1536,512]{1,0:T(8,128)(2,1)}, bf16[1536,512]{1,0:T(8,128)(2,1)}, bf16[1536,512]{1,0:T(8,128)(2,1)}) custom-call(bf16[2048,1536]{1,0:T(8,128)(2,1)} %get-tuple-element.331.refs_0_.refs_2_, bf16[1024,2048]{1,0:T(8,128)(2,1)} %get-tuple-element.309.refs_0_.refs_4_.refs_1_, ...), custom_call_target="tpu_custom_call" | custom-call | flops 1000 | bytes 1000 | tf_op jit(solution)/shard_map/weight_cols/pallas_call | solution.py:525
  473.8 19.3 %to_hidden.13.refs_8_ = bf16[2048,1536]{1,0:T(8,128)(2,1)} custom-call(bf16[1024,2048]{1,0:T(8,128)(2,1)} %reorder.1.refs_0_.refs_1_, bf16[1024,2048]{1,0:T(8,128)(2,1)} %collective-permute-done.27.refs_1_.refs_2_, bf16[1536,512]{1,0:T(8,128)(2,1)} %all-gather.20.cloned.1.call-done.refs_2_.refs_7_, bf16[1536,512]{1,0:T(8,128)(2,1)} %copy-done.2, ...), custom_call_target="tpu_custom_call" | custom-call | flops 1000 | bytes 1000 | tf_op jit(solution)/shard_map/to_hidden/pallas_call | solution.py:525
  495.6 37.4 %ffn.3 = (bf16[2048,1536]{1,0:T(8,128)(2,1)}, bf16[2048,1536]{1,0:T(8,128)(2,1)}, bf16[2048,1536]{1,0:T(8,128)(2,1)}) custom-call(bf16[1024,2048]{1,0:T(8,128)(2,1)} %get-tuple-element.309.refs_0_.refs_4_.refs_1_, bf16[1024,2048]{1,0:T(8,128)(2,1)} %collective-permute-done.30.refs_1_.refs_5_.refs_2_, ...), custom_call_target="tpu_custom_call" | custom-call | flops 1000 | bytes 1000 | tf_op jit(solution)/shard_map/ffn/pallas_call | solution.py:525
  537.3 37.1 %weight_cols.6 = (bf16[1536,512]{1,0:T(8,128)(2,1)}, bf16[1536,512]{1,0:T(8,128)(2,1)}, bf16[1536,512]{1,0:T(8,128)(2,1)}, bf16[1536,256]{1,0:T(8,128)(2,1)}, bf...) custom-call(bf16[2048,1536]{1,0:T(8,128)(2,1)} %get-tuple-element.45, ...), custom_call_target="tpu_custom_call" | custom-call | flops 1000 | bytes 1000 | tf_op jit(solution)/shard_map/weight_cols/pallas_call | solution.py:525
  580.7 19.4 %weight_cols.7 = (bf16[1536,512]{1,0:T(8,128)(2,1)}, bf16[1536,512]{1,0:T(8,128)(2,1)}, bf16[1536,512]{1,0:T(8,128)(2,1)}, bf16[1536,512]{1,0:T(8,128)(2,1)}) custom-call(bf16[2048,1536]{1,0:T(8,128)(2,1)} %get-tuple-element.374.refs_0_.refs_4_, bf16[1024,2048]{1,0:T(8,128)(2,1)} %get-tuple-element.309.refs_0_.refs_4_.refs_1_, ...), custom_call_target="tpu_custom_call" | custom-call | flops 1000 | bytes 1000 | tf_op jit(solution)/shard_map/weight_cols/pallas_call | solution.py:525
  605.4 34.9 %to_model.10 = bf16[1024,2048]{1,0:T(8,128)(2,1)} custom-call(s32[8]{0:T(128)} %xor_add_fusion.refs_0_, bf16[2048,1536]{1,0:T(8,128)(2,1)} %get-tuple-element.320.refs_3_.refs_1_, bf16[2048,1536]{1,0:T(8,128)(2,1)} %get-tuple-element.331.refs_0_.refs_2_, bf16[2048,1536]{1,0:T(8,128)(2,1)} %get-tuple-element.392.refs_3_, ...), custom_call_target="tpu_custom_call" | custom-call | flops 1000 | bytes 1000 | tf_op jit(solution)/shard_map/to_model/pallas_call | solution.py:525
  646.8 34.6 %to_model.11.refs_2_ = bf16[1024,2048]{1,0:T(8,128)(2,1)} custom-call(s32[8]{0:T(128)} %xor_add_fusion.refs_0_, bf16[2048,1536]{1,0:T(8,128)(2,1)} %get-tuple-element.320.refs_3_.refs_1_, bf16[2048,1536]{1,0:T(8,128)(2,1)} %get-tuple-element.331.refs_0_.refs_2_, bf16[2048,1536]{1,0:T(8,128)(2,1)} %get-tuple-element.392.refs_3_, ...), custom_call_target="tpu_custom_call" | custom-call | flops 1000 | bytes 1000 | tf_op jit(solution)/shard_map/to_model/pallas_call | solution.py:525
  684.7 11.1 %norm_return.2 = (bf16[1024,2048]{1,0:T(8,128)(2,1)}, f32[8,2048]{1,0:T(8,128)}) custom-call(bf16[1024,2048]{1,0:T(8,128)(2,1)} %get-tuple-element.305.refs_0_, bf16[1024,2048]{1,0:T(8,128)(2,1)} %multiply_convert_fusion.1.refs_1_, bf16[1024,2048]{1,0:T(8,128)(2,1)} %to_model.11.refs_2_, bf16[1024,2048]{1,0:T(8,128)(2,1)} %collective-permute-done.49.refs_3_, ...), custom_call_target="tpu_custom_call" | custom-call | flops 1000 | bytes 1000 | tf_op jit(solution)/shard_map/norm_return/pallas_call | solution.py:525
  697.1 20.5 %to_model.12.refs_2_ = bf16[1024,2048]{1,0:T(8,128)(2,1)} custom-call(s32[8]{0:T(128)} %xor_add_fusion.refs_0_, bf16[2048,1536]{1,0:T(8,128)(2,1)} %get-tuple-element.319.refs_0_.refs_1_, bf16[2048,1536]{1,0:T(8,128)(2,1)} %get-tuple-element.452.refs_0_.refs_2_, bf16[1536,512]{1,0:T(8,128)(2,1)} %all-gather.16.cloned.1.call-done.refs_2_.refs_3_, ...), custom_call_target="tpu_custom_call" | custom-call | flops 1000 | bytes 1000 | tf_op jit(solution)/shard_map/to_model/pallas_call | solution.py:525
  740.1 41.6 %attend_back.2 = (bf16[1024,1024]{1,0:T(8,128)(2,1)}, bf16[1024,1024]{1,0:T(8,128)(2,1)}, bf16[1024,1024]{1,0:T(8,128)(2,1)}) custom-call(s32[2,9]{1,0:T(2,128)} %pad_add_fusion.refs_0_, bf16[1024,1024]{1,0:T(8,128)(2,1)} %make_heads.5.refs_2_.refs_1_, bf16[1024,1024]{1,0:T(8,128)(2,1)} %to_hidden.14.refs_2_, ...), custom_call_target="tpu_custom_call" | custom-call | flops 1000 | bytes 1000 | tf_op jit(solution)/shard_map/attend_back/pallas_call | solution.py:525
  781.7 14.4 %weight_rows.3 = (bf16[256,2048]{1,0:T(8,128)(2,1)}, bf16[256,2048]{1,0:T(8,128)(2,1)}, bf16[256,2048]{1,0:T(8,128)(2,1)}, bf16[256,2048]{1,0:T(8,128)(2,1)}) custom-call(bf16[1024,1024]{1,0:T(8,128)(2,1)} %get-tuple-element.290.refs_1_.refs_3_.refs_0_, bf16[1024,1024]{1,0:T(8,128)(2,1)} %get-tuple-element.301.refs_1_.refs_3_, ...), custom_call_target="tpu_custom_call" | custom-call | flops 1000 | bytes 1000 | tf_op jit(solution)/shard_map/weight_rows/pallas_call | solution.py:525
  819.5 34.2 %attend_back.3 = (bf16[1024,1024]{1,0:T(8,128)(2,1)}, bf16[1024,1024]{1,0:T(8,128)(2,1)}, bf16[1024,1024]{1,0:T(8,128)(2,1)}) custom-call(s32[2,9]{1,0:T(2,128)} %pad_add_fusion.refs_0_, bf16[1024,1024]{1,0:T(8,128)(2,1)} %make_heads.7.refs_2_.refs_1_, bf16[1024,1024]{1,0:T(8,128)(2,1)} %to_hidden.15.refs_2_, ...), custom_call_target="tpu_custom_call" | custom-call | flops 1000 | bytes 1000 | tf_op jit(solution)/shard_map/attend_back/pallas_call | solution.py:525
  877.0 14.4 %weight_rows.4 = (bf16[256,2048]{1,0:T(8,128)(2,1)}, bf16[256,2048]{1,0:T(8,128)(2,1)}, bf16[256,2048]{1,0:T(8,128)(2,1)}, bf16[256,2048]{1,0:T(8,128)(2,1)}) custom-call(bf16[1024,1024]{1,0:T(8,128)(2,1)} %get-tuple-element.448.refs_5_.refs_0_.refs_1_, bf16[1024,1024]{1,0:T(8,128)(2,1)} %get-tuple-element.449.refs_1_, ...), custom_call_target="tpu_custom_call" | custom-call | flops 1000 | bytes 1000 | tf_op jit(solution)/shard_map/weight_rows/pallas_call | solution.py:525
  893.4 20.3 %to_model.13.refs_6_ = bf16[1024,2048]{1,0:T(8,128)(2,1)} custom-call(s32[8]{0:T(128)} %xor_add_fusion.refs_0_, bf16[2048,1536]{1,0:T(8,128)(2,1)} %get-tuple-element.319.refs_0_.refs_1_, bf16[2048,1536]{1,0:T(8,128)(2,1)} %get-tuple-element.452.refs_0_.refs_2_, bf16[1536,512]{1,0:T(8,128)(2,1)} %all-gather.16.cloned.1.call-done.refs_2_.refs_3_, ...), custom_call_target="tpu_custom_call" | custom-call | flops 1000 | bytes 1000 | tf_op jit(solution)/shard_map/to_model/pallas_call | solution.py:525
  938.3 14.3 %weight_rows.5 = (bf16[256,2048]{1,0:T(8,128)(2,1)}, bf16[256,2048]{1,0:T(8,128)(2,1)}, bf16[256,2048]{1,0:T(8,128)(2,1)}, bf16[256,2048]{1,0:T(8,128)(2,1)}) custom-call(bf16[1024,1024]{1,0:T(8,128)(2,1)} %get-tuple-element.461.refs_0_.refs_2_, bf16[1024,1024]{1,0:T(8,128)(2,1)} %get-tuple-element.476.refs_1_.refs_2_, ...), custom_call_target="tpu_custom_call" | custom-call | flops 1000 | bytes 1000 | tf_op jit(solution)/shard_map/weight_rows/pallas_call | solution.py:525
  956.6 15.4 %to_model.14 = bf16[1024,2048]{1,0:T(8,128)(2,1)} custom-call(s32[8]{0:T(128)} %iota.44.refs_0_, bf16[1024,1024]{1,0:T(8,128)(2,1)} %get-tuple-element.449.refs_1_, bf16[1024,1024]{1,0:T(8,128)(2,1)} %get-tuple-element.476.refs_1_.refs_2_, bf16[1024,2048]{1,0:T(8,128)(2,1)} %constant_dynamic-update-slice_fusion.8.refs_1_.refs_3_, ...), custom_call_target="tpu_custom_call" | custom-call | flops 1000 | bytes 1000 | tf_op jit(solution)/shard_map/to_model/pallas_call | solution.py:525
  995.1 15.5 %to_model.15.refs_2_ = bf16[1024,2048]{1,0:T(8,128)(2,1)} custom-call(s32[8]{0:T(128)} %iota.45.refs_0_, bf16[1024,1024]{1,0:T(8,128)(2,1)} %get-tuple-element.448.refs_5_.refs_0_.refs_1_, bf16[1024,1024]{1,0:T(8,128)(2,1)} %get-tuple-element.461.refs_0_.refs_2_, bf16[1024,2048]{1,0:T(8,128)(2,1)} %constant_dynamic-update-slice_fusion.8.refs_1_.refs_3_, ...), custom_call_target="tpu_custom_call" | custom-call | flops 1000 | bytes 1000 | tf_op jit(solution)/shard_map/to_model/pallas_call | solution.py:525
  1021.2 12.1 %norm_return.3 = (f32[1024,2048]{1,0:T(8,128)}, f32[8,2048]{1,0:T(8,128)}) custom-call(bf16[1024,2048]{1,0:T(8,128)(2,1)} %refs_0_.1, bf16[1024,2048]{1,0:T(8,128)(2,1)} %get-tuple-element.401.refs_12_.refs_0_.refs_2_.refs_1_, bf16[1024,2048]{1,0:T(8,128)(2,1)} %to_model.15.refs_2_, bf16[1024,2048]{1,0:T(8,128)(2,1)} %collective-permute-done.72.refs_3_, ...), custom_call_target="tpu_custom_call" | custom-call | flops 1000 | bytes 1000 | tf_op jit(solution)/shard_map/norm_return/pallas_call | solution.py:525
  1043.8 12.7 %collective-permute-start.80 = (f32[1,4352]{1,0:T(1,128)S(1)}, f32[1,4352]{1,0:T(1,128)S(1)}, u32[]{:S(2)}, u32[]{:S(2)}) collective-permute-start(f32[1,4352]{1,0:T(1,128)S(1)} %add_add_fusion.10), channel_id=1, source_target_pairs={{0,3},{1,2},{2,1},{3,0},{4,7},{5,6},{6,5},{7,4},{8,11},{9,10},{10,... | collective-permute-start | bytes 52232 | tf_op jit(solution)/shard_map/ppermute | solution.py:1490
  (497 shorter events, 387.8 us)
Async XLA Ops:
  8.9 60.9 %all-gather.12.cloned.1.call-start = ((), (), s32[]{:S(2)}) async-start(), calls=%async_computation.9 | async-start | bytes 1310720 | tf_op jit(solution)/shard_map/all_gather | solution.py:483
  9.7 89.2 %all-gather.14.cloned.1.call-start = ((), (), s32[]{:S(2)}) async-start(), calls=%async_computation.10 | async-start | bytes 1310720 | tf_op jit(solution)/shard_map/all_gather | solution.py:483
  12.6 168.2 %all-gather.16.cloned.1.call-start = ((), (), s32[]{:S(2)}) async-start(), calls=%async_computation.11 | async-start | bytes 1966080 | tf_op jit(solution)/shard_map/all_gather | solution.py:483
  32.7 132.0 %collective-permute-start.19 = (bf16[1024,2048]{1,0:T(8,128)(2,1)}, bf16[1024,2048]{1,0:T(8,128)(2,1)}, u32[]{:S(2)}, u32[]{:S(2)}) collective-permute-start(bf16[1024,2048]{1,0:T(8,128)(2,1)} %fusion.2.refs_0_.refs_2_), channel_id=1, source_target_pairs={{0,8},{8,0},{1,9},{9,1},{2,10},{10,2},{3,11},{11,3},{4,12},{12,4},... | collective-permute-start | bytes 12582920 | tf_op jit(solution)/shard_map/ppermute | solution.py:467
  46.7 207.6 %all-gather.18.cloned.1.call-start = ((), (), s32[]{:S(2)}) async-start(), calls=%async_computation.12 | async-start | bytes 1966080 | tf_op jit(solution)/shard_map/all_gather | solution.py:483
  143.8 218.6 %all-gather.20.cloned.1.call-start = ((), (), s32[]{:S(2)}) async-start(), calls=%async_computation.13 | async-start | bytes 1966080 | tf_op jit(solution)/shard_map/all_gather | solution.py:483
  143.9 45.1 %collective-permute-start.15 = (bf16[1024,1024]{1,0:T(8,128)(2,1)}, bf16[1024,1024]{1,0:T(8,128)(2,1)S(1)}, u32[]{:S(2)}, u32[]{:S(2)}) collective-permute-start(bf16[1024,1024]{1,0:T(8,128)(2,1)} %make_heads.4.refs_2_.refs_5_), channel_id=1, source_target_pairs={{0,4},{4,0},{1,5},{5,1},{2,6},{6,2},{3,7},{7,3},{8,12},{12,8},{9,1... | collective-permute-start | bytes 6291464 | tf_op jit(solution)/shard_map/ppermute | solution.py:467
  145.5 219.6 %all-gather.22.cloned.1.call-start = ((), (), s32[]{:S(2)}) async-start(), calls=%async_computation.14 | async-start | bytes 7864320 | tf_op jit(solution)/shard_map/all_gather | solution.py:483
  193.7 215.0 %all-gather.24.cloned.1.call-start = ((), (), s32[]{:S(2)}) async-start(), calls=%async_computation.15 | async-start | bytes 1966080 | tf_op jit(solution)/shard_map/all_gather | solution.py:483
  230.2 43.9 %collective-permute-start.22 = (bf16[1024,1024]{1,0:T(8,128)(2,1)S(1)}, bf16[1024,1024]{1,0:T(8,128)(2,1)}, u32[]{:S(2)}, u32[]{:S(2)}) collective-permute-start(bf16[1024,1024]{1,0:T(8,128)(2,1)S(1)} %copy-done.5), channel_id=1, source_target_pairs={{0,4},{4,0},{1,5},{5,1},{2,6},{6,2},{3,7},{7,3},{8,12},{12,8},{9,1... | collective-permute-start | bytes 6291464 | tf_op jit(solution)/shard_map/ppermute | solution.py:467
  232.6 263.0 %all-gather.26.cloned.1.call-start = ((), (), s32[]{:S(2)}) async-start(), calls=%async_computation.16 | async-start | bytes 7864320 | tf_op jit(solution)/shard_map/all_gather | solution.py:483
  277.4 55.8 %collective-permute-start.27 = (bf16[1024,2048]{1,0:T(8,128)(2,1)}, bf16[1024,2048]{1,0:T(8,128)(2,1)}, u32[]{:S(2)}, u32[]{:S(2)}) collective-permute-start(bf16[1024,2048]{1,0:T(8,128)(2,1)} %reorder.1.refs_0_.refs_1_), channel_id=1, source_target_pairs={{0,8},{8,0},{1,9},{9,1},{2,10},{10,2},{3,11},{11,3},{4,12},{12,4},... | collective-permute-start | bytes 12582920 | tf_op jit(solution)/shard_map/ppermute | solution.py:467
  317.0 487.8 %reduce-scatter.9.cloned.1.call-start = ((), (), s32[]{:S(2)}) async-start(), calls=%async_computation.17 | async-start | bytes 7864320 | tf_op jit(solution)/shard_map/reduce_scatter | solution.py:487
  363.6 45.2 %collective-permute-start.32 = (bf16[1536,512]{1,0:T(8,128)(2,1)}, bf16[1536,512]{1,0:T(8,128)(2,1)S(1)}, u32[]{:S(2)}, u32[]{:S(2)}) collective-permute-start(bf16[1536,512]{1,0:T(8,128)(2,1)} %all-gather.20.cloned.1.call-done.refs_2_.refs_7_), channel_id=1, source_target_pairs={{0,4},{4,0},{1,5},{5,1},{2,6},{6,2},{3,7},{7,3},{8,12},{12,8},{9,1... | collective-permute-start | bytes 4718600 | tf_op jit(solution)/shard_map/ppermute | solution.py:467
  364.1 44.6 %collective-permute-start.31 = (bf16[1536,512]{1,0:T(8,128)(2,1)}, bf16[1536,512]{1,0:T(8,128)(2,1)S(1)}, u32[]{:S(2)}, u32[]{:S(2)}) collective-permute-start(bf16[1536,512]{1,0:T(8,128)(2,1)} %all-gather.20.cloned.1.call-done.refs_2_.refs_7_), channel_id=1, source_target_pairs={{0,16},{16,0},{1,17},{17,1},{2,18},{18,2},{3,19},{19,3},{4,20},{20... | collective-permute-start | bytes 4718600 | tf_op jit(solution)/shard_map/ppermute | solution.py:467
  447.4 537.4 %reduce-scatter.15.cloned.1.call-start = ((), (), s32[]{:S(2)}) async-start(), calls=%async_computation.20 | async-start | bytes 1966080 | tf_op jit(solution)/shard_map/reduce_scatter | solution.py:487
  640.3 44.4 %collective-permute-start.49 = (bf16[1024,2048]{1,0:T(8,128)(2,1)}, bf16[1024,2048]{1,0:T(8,128)(2,1)}, u32[]{:S(2)}, u32[]{:S(2)}) collective-permute-start(bf16[1024,2048]{1,0:T(8,128)(2,1)} %to_model.10), channel_id=1, source_target_pairs={{0,8},{8,0},{1,9},{9,1},{2,10},{10,2},{3,11},{11,3},{4,12},{12,4},... | collective-permute-start | bytes 12582920 | tf_op jit(solution)/shard_map/ppermute | solution.py:467
  643.0 343.5 %reduce-scatter.19.cloned.1.call-start = ((), (), s32[]{:S(2)}) async-start(), calls=%async_computation.22 | async-start | bytes 1966080 | tf_op jit(solution)/shard_map/reduce_scatter | solution.py:487
  695.8 85.9 %collective-permute-start.56 = (bf16[1024,2048]{1,0:T(8,128)(2,1)}, bf16[1024,2048]{1,0:T(8,128)(2,1)}, u32[]{:S(2)}, u32[]{:S(2)}) collective-permute-start(bf16[1024,2048]{1,0:T(8,128)(2,1)} %get-tuple-element.401.refs_12_.refs_0_.refs_2_.refs_1_), channel_id=1, source_target_pairs={{0,8},{8,0},{1,9},{9,1},{2,10},{10,2},{3,11},{11,3},{4,12},{12,4},... | collective-permute-start | bytes 12582920 | tf_op jit(solution)/shard_map/ppermute | solution.py:467
  697.0 290.5 %reduce-scatter.17.cloned.1.call-start = ((), (), s32[]{:S(2)}) async-start(), calls=%async_computation.21 | async-start | bytes 1966080 | tf_op jit(solution)/shard_map/reduce_scatter | solution.py:487
  736.0 68.8 %collective-permute-start.52 = (bf16[1536,512]{1,0:T(8,128)(2,1)}, bf16[1536,512]{1,0:T(8,128)(2,1)}, u32[]{:S(2)}, u32[]{:S(2)}) collective-permute-start(bf16[1536,512]{1,0:T(8,128)(2,1)} %get-tuple-element.419), channel_id=1, source_target_pairs={{0,16},{16,0},{1,17},{17,1},{2,18},{18,2},{3,19},{19,3},{4,20},{20... | collective-permute-start | bytes 4718600 | tf_op jit(solution)/shard_map/ppermute | solution.py:467
  737.8 67.0 %collective-permute-start.53 = (bf16[1536,512]{1,0:T(8,128)(2,1)}, bf16[1536,512]{1,0:T(8,128)(2,1)}, u32[]{:S(2)}, u32[]{:S(2)}) collective-permute-start(bf16[1536,512]{1,0:T(8,128)(2,1)} %add.272), channel_id=1, source_target_pairs={{0,4},{4,0},{1,5},{5,1},{2,6},{6,2},{3,7},{7,3},{8,12},{12,8},{9,1... | collective-permute-start | bytes 4718600 | tf_op jit(solution)/shard_map/ppermute | solution.py:467
  738.7 67.3 %collective-permute-start.54 = (bf16[1536,512]{1,0:T(8,128)(2,1)}, bf16[1536,512]{1,0:T(8,128)(2,1)S(1)}, u32[]{:S(2)}, u32[]{:S(2)}) collective-permute-start(bf16[1536,512]{1,0:T(8,128)(2,1)} %add.273), channel_id=1, source_target_pairs={{0,16},{16,0},{1,17},{17,1},{2,18},{18,2},{3,19},{19,3},{4,20},{20... | collective-permute-start | bytes 4718600 | tf_op jit(solution)/shard_map/ppermute | solution.py:467
  739.0 68.3 %collective-permute-start.55 = (bf16[1536,512]{1,0:T(8,128)(2,1)}, bf16[1536,512]{1,0:T(8,128)(2,1)}, u32[]{:S(2)}, u32[]{:S(2)}) collective-permute-start(bf16[1536,512]{1,0:T(8,128)(2,1)} %get-tuple-element.423), channel_id=1, source_target_pairs={{0,4},{4,0},{1,5},{5,1},{2,6},{6,2},{3,7},{7,3},{8,12},{12,8},{9,1... | collective-permute-start | bytes 4718600 | tf_op jit(solution)/shard_map/ppermute | solution.py:467
  810.5 182.1 %reduce-scatter.21.cloned.1.call-start = ((), (), s32[]{:S(2)}) async-start(), calls=%async_computation.23 | async-start | bytes 1966080 | tf_op jit(solution)/shard_map/reduce_scatter | solution.py:487
  810.6 50.1 %collective-permute-start.57 = (bf16[1024,1024]{1,0:T(8,128)(2,1)}, bf16[1024,1024]{1,0:T(8,128)(2,1)S(1)}, u32[]{:S(2)}, u32[]{:S(2)}) collective-permute-start(bf16[1024,1024]{1,0:T(8,128)(2,1)} %get-tuple-element.438), channel_id=1, source_target_pairs={{0,4},{4,0},{1,5},{5,1},{2,6},{6,2},{3,7},{7,3},{8,12},{12,8},{9,1... | collective-permute-start | bytes 6291464 | tf_op jit(solution)/shard_map/ppermute | solution.py:467
  811.6 49.1 %collective-permute-start.58 = (bf16[256,2048]{1,0:T(8,128)(2,1)}, bf16[256,2048]{1,0:T(8,128)(2,1)S(1)}, u32[]{:S(2)}, u32[]{:S(2)}) collective-permute-start(bf16[256,2048]{1,0:T(8,128)(2,1)} %get-tuple-element.441), channel_id=1, source_target_pairs={{0,16},{16,0},{1,17},{17,1},{2,18},{18,2},{3,19},{19,3},{4,20},{20... | collective-permute-start | bytes 3145736 | tf_op jit(solution)/shard_map/ppermute | solution.py:467
  816.0 196.8 %reduce-scatter.23.cloned.1.call-start = ((), (), s32[]{:S(2)}) async-start(), calls=%async_computation.24 | async-start | bytes 1966080 | tf_op jit(solution)/shard_map/reduce_scatter | solution.py:487
  860.7 62.0 %collective-permute-start.61 = (bf16[1024,1024]{1,0:T(8,128)(2,1)}, bf16[1024,1024]{1,0:T(8,128)(2,1)}, u32[]{:S(2)}, u32[]{:S(2)}) collective-permute-start(bf16[1024,1024]{1,0:T(8,128)(2,1)} %get-tuple-element.446), channel_id=1, source_target_pairs={{0,4},{4,0},{1,5},{5,1},{2,6},{6,2},{3,7},{7,3},{8,12},{12,8},{9,1... | collective-permute-start | bytes 6291464 | tf_op jit(solution)/shard_map/ppermute | solution.py:467
  922.9 120.9 %reduce-scatter.11.cloned.1.call-start = ((), (), s32[]{:S(2)}) async-start(), calls=%async_computation.18 | async-start | bytes 2621440 | tf_op jit(solution)/shard_map/reduce_scatter | solution.py:487
  923.5 48.4 %collective-permute-start.66 = (bf16[256,2048]{1,0:T(8,128)(2,1)S(1)}, bf16[256,2048]{1,0:T(8,128)(2,1)S(1)}, u32[]{:S(2)}, u32[]{:S(2)}) collective-permute-start(bf16[256,2048]{1,0:T(8,128)(2,1)S(1)} %add.280), channel_id=1, source_target_pairs={{0,4},{4,0},{1,5},{5,1},{2,6},{6,2},{3,7},{7,3},{8,12},{12,8},{9,1... | collective-permute-start | bytes 3145736 | tf_op jit(solution)/shard_map/ppermute | solution.py:467
  981.8 84.2 %reduce-scatter.13.cloned.1.call-start = ((), (), s32[]{:S(2)}) async-start(), calls=%async_computation.19 | async-start | bytes 1310720 | tf_op jit(solution)/shard_map/reduce_scatter | solution.py:487
  (135 other events, 2636.3 us)
Sparse Core Ops, SparseCore 0:
  10.2 30.6 all-gather.9
  42.4 27.4 all-gather.11
  71.4 27.4 all-gather.13
  100.9 36.5 all-gather.15
  144.0 37.1 all-gather.17
  183.2 35.9 all-gather.19
  220.8 114.1 all-gather.21
  337.1 35.3 all-gather.23
  374.1 114.1 all-gather.25
  490.5 108.9 reduce-scatter.8
  643.2 37.5 reduce-scatter.14
  697.2 39.5 reduce-scatter.18
  810.6 39.9 reduce-scatter.16
  852.8 34.2 reduce-scatter.20
  923.0 42.4 reduce-scatter.22
  981.9 52.1 reduce-scatter.10
  1036.4 27.5 reduce-scatter.12

commit v7 on v6

--- a/solution.py
+++ b/solution.py
@@ -1432,11 +1432,10 @@
     w_c, act_hi = sync(w_c, act_hi)
     from_w = swap(w_c, "x")
     mixed_own = to_model([act_lo, act_hi], [dlo, dhi], order, 0, rows)
-    dkv1_back, got_ox, from_w, mixed_own, o_y, dl_y, w_x, w_y = sync(
-        dkv1_back, got_ox, from_w, mixed_own, o_y + from_o, dl_y + from_l, w_x, w_y
+    dkv1_back, got_ox, mixed_own, o_y, dl_y, w_x = sync(
+        dkv1_back, got_ox, mixed_own, o_y + from_o, dl_y + from_l, w_x
     )
     got_oy, got_wx = swap(o_y, "y"), swap(w_x, "x")
-    got_wy = swap(w_y + from_w, "y")
 
     def halves(array):
         span = array.shape[0] // 2
@@ -1447,11 +1446,12 @@
         return stacked(x_a, x_b + from_b), stacked(y_a + from_a, y_b)
 
     kv_grad = [
-        heads_return(g, kv_raw[g], d, [e], *back, key_gain, 2, [mixed_own, w_y])
+        heads_return(g, kv_raw[g], d, [e], *back, key_gain, 2, [mixed_own, w_x])
         for g, (d, e) in enumerate(((dkv0, dkv0_back), (dkv1, dkv1_back)))
     ]
     k_gains = kv_grad[0][1] + kv_grad[1][1]
-    kv_grad = [kv_grad[0][0], kv_grad[1][0]]
+    *kv_grad, from_w, w_y = sync(kv_grad[0][0], kv_grad[1][0], from_w, w_y)
+    got_wy = swap(w_y + from_w, "y")
     kv_0, kv_x, kv_y, kv_c = weight_rows(kv_grad, normed1, 4)
     kv_c, kv_grad[1], got_oy, got_wx = sync(kv_c, kv_grad[1], got_oy, got_wx)
     kv_a, kv_b = halves(kv_c)

time: 1080 us -> 1080 us (level)
  transfers between devices with their start and end apart: 99 -> 99, of which waited for: 19 -> 18; matrix products, arithmetic and copies ran while one was open for 12% -> 12% of each run, Pallas kernels for 65% -> 64%
where the time goes in v7:
time: 1080 us; the launch traced here: 1070 us
  Pallas kernels  689 us (64%)
  waiting for transfers between devices  129 us (12%)
  starting transfers between devices  98.4 us (9%)
  other arithmetic  84.1 us (8%)
  local copies, waits for them, and re-layouts  53.6 us (5%)
  between operations  15.4 us (1%)
    pallas_call x42, Pallas kernels, call(): pl.pallas_call(body, grid_spec=pltpu.PrefetchScalarGridSpec(num_scalar_pr...  689 us
    ppermute x78, waiting for transfers between devices, swap(): return lax.ppermute(array, axis, SWAP)  84.5 us
    ppermute x78, starting transfers between devices, swap(): return lax.ppermute(array, axis, SWAP)  77.6 us
    all_gather x9, waiting for transfers between devices, gather_z(): return lax.all_gather(array, 'z', axis=0, tiled=True)  43.9 us
    unnamed x151, local copies, waits for them, and re-layouts  25.7 us
  transfers between devices with their start and end apart: 99, of which 18 were waited for; matrix products, arithmetic and copies ran while one was open for 12% of the time, Pallas kernels for 64%

profile of v7, /device:TPU:0, one launch (start us, length us, event | category | flops | bytes accessed | tf_op | source)
XLA Modules:
  0.0 1069.6 jit_solution(9759272826244032175)
XLA Ops:
  50.0 19.9 %all-gather.12.cloned.1.call-done = bf16[256,2048]{1,0:T(8,128)(2,1)} async-done(((bf16[64,2048]{1,0:T(8,128)(2,1)}), bf16[256,2048]{1,0:T(8,128)(2,1)}) %all-gather.12.cloned.1.call-update) | async-done | bytes 1048592 | tf_op jit(solution)/shard_map/all_gather | solution.py:483
  81.4 17.5 %all-gather.14.cloned.1.call-done = bf16[256,2048]{1,0:T(8,128)(2,1)} async-done(((bf16[64,2048]{1,0:T(8,128)(2,1)}), bf16[256,2048]{1,0:T(8,128)(2,1)}) %all-gather.14.cloned.1.call-update) | async-done | bytes 1048592 | tf_op jit(solution)/shard_map/all_gather | solution.py:483
  98.9 9.5 collective-permute-done.6
  132.5 10.9 %collective-permute-done.11 = bf16[128,2048]{1,0:T(8,128)(2,1)S(1)} collective-permute-done((bf16[128,2048]{1,0:T(8,128)(2,1)S(1)}, bf16[128,2048]{1,0:T(8,128)(2,1)S(1)}, u32[]{:S(2)}, u32[]{:S(2)}) %collective-permute-start.11) | collective-permute-done | bytes 524320 | tf_op jit(solution)/shard_map/ppermute | solution.py:467
  198.0 22.3 %attend.2 = (bf16[1024,1024]{1,0:T(8,128)(2,1)}, f32[1024,512]{1,0:T(8,128)}) custom-call(s32[2,9]{1,0:T(2,128)} %pad_add_fusion.refs_0_, bf16[1024,1024]{1,0:T(8,128)(2,1)} %make_heads.5.refs_2_.refs_1_, bf16[1024,1024]{1,0:T(8,128)(2,1)} %make_heads.4.refs_2_.refs_5_, bf16[1024,1024]{1,0:T(8,128)(2,1)} %copy-done.8), custom_call_target="tpu_custom_call" | custom-call | flops 1000 | bytes 1000 | tf_op jit(solution)/shard_map/attend/pallas_call | solution.py:525
  261.9 12.1 %collective-permute-done.22.refs_3_.refs_6_ = bf16[1024,1024]{1,0:T(8,128)(2,1)} collective-permute-done((bf16[1024,1024]{1,0:T(8,128)(2,1)S(1)}, bf16[1024,1024]{1,0:T(8,128)(2,1)}, u32[]{:S(2)}, u32[]{:S(2)}) %collective-permute-start.22) | collective-permute-done | bytes 2097184 | tf_op jit(solution)/shard_map/ppermute | solution.py:467
  275.9 23.4 %attend.3 = (bf16[1024,1024]{1,0:T(8,128)(2,1)}, f32[1024,512]{1,0:T(8,128)}) custom-call(s32[2,9]{1,0:T(2,128)} %pad_add_fusion.refs_0_, bf16[1024,1024]{1,0:T(8,128)(2,1)} %make_heads.7.refs_2_.refs_1_, bf16[1024,1024]{1,0:T(8,128)(2,1)} %make_heads.6.refs_2_.refs_5_, bf16[1024,1024]{1,0:T(8,128)(2,1)} %collective-permute-done.22.refs_3_.refs_6_), custom_call_target="tpu_custom_call" | custom-call | flops 1000 | bytes 1000 | tf_op jit(solution)/shard_map/attend/pallas_call | solution.py:525
  306.1 10.4 to_model.8.refs_3_
  322.7 10.5 to_model.9.refs_6_.refs_2_
  333.2 19.2 %to_hidden.12.refs_5_.refs_8_ = bf16[2048,1536]{1,0:T(8,128)(2,1)} custom-call(bf16[1024,2048]{1,0:T(8,128)(2,1)} %reorder.1.refs_0_.refs_1_, bf16[1024,2048]{1,0:T(8,128)(2,1)} %collective-permute-done.27.refs_1_.refs_2_, bf16[1536,512]{1,0:T(8,128)(2,1)} %all-gather.16.cloned.1.call-done.refs_2_.refs_3_, bf16[1536,512]{1,0:T(8,128)(2,1)} %copy-done.6, ...), custom_call_target="tpu_custom_call" | custom-call | flops 1000 | bytes 1000 | tf_op jit(solution)/shard_map/to_hidden/pallas_call | solution.py:525
  352.4 10.0 resid_norm.1
  371.1 37.6 %ffn.2 = (bf16[2048,1536]{1,0:T(8,128)(2,1)}, bf16[2048,1536]{1,0:T(8,128)(2,1)}, bf16[2048,1536]{1,0:T(8,128)(2,1)}) custom-call(bf16[1024,2048]{1,0:T(8,128)(2,1)} %get-tuple-element.311.refs_0_.refs_4_.refs_1_, bf16[1024,2048]{1,0:T(8,128)(2,1)} %collective-permute-done.30.refs_1_.refs_5_.refs_2_, ...), custom_call_target="tpu_custom_call" | custom-call | flops 1000 | bytes 1000 | tf_op jit(solution)/shard_map/ffn/pallas_call | solution.py:525
  410.0 36.9 %weight_cols.4 = (bf16[1536,2048]{1,0:T(8,128)(2,1)}, bf16[1536,512]{1,0:T(8,128)(2,1)}, bf16[1536,512]{1,0:T(8,128)(2,1)}, bf16[1536,512]{1,0:T(8,128)(2,1)}, bf16[1536,512]{1,0:T(8,128)(2,1)}) custom-call(bf16[2048,1536]{1,0:T(8,128)(2,1)} %get-tuple-element.321.refs_0_.refs_1_, bf16[1024,2048]{1,0:T(8,128)(2,1)} %reorder.1.refs_0_.refs_1_, ...), custom_call_target="tpu_custom_call" | custom-call | flops 1000 | bytes 1000 | tf_op jit(solution)/shard_map/weight_cols/pallas_call | solution.py:525
  450.1 19.0 %weight_cols.5 = (bf16[1536,512]{1,0:T(8,128)(2,1)}, bf16[1536,512]{1,0:T(8,128)(2,1)}, bf16[1536,512]{1,0:T(8,128)(2,1)}, bf16[1536,512]{1,0:T(8,128)(2,1)}) custom-call(bf16[2048,1536]{1,0:T(8,128)(2,1)} %get-tuple-element.333.refs_0_.refs_2_, bf16[1024,2048]{1,0:T(8,128)(2,1)} %get-tuple-element.311.refs_0_.refs_4_.refs_1_, ...), custom_call_target="tpu_custom_call" | custom-call | flops 1000 | bytes 1000 | tf_op jit(solution)/shard_map/weight_cols/pallas_call | solution.py:525
  473.3 19.3 %to_hidden.13.refs_8_ = bf16[2048,1536]{1,0:T(8,128)(2,1)} custom-call(bf16[1024,2048]{1,0:T(8,128)(2,1)} %reorder.1.refs_0_.refs_1_, bf16[1024,2048]{1,0:T(8,128)(2,1)} %collective-permute-done.27.refs_1_.refs_2_, bf16[1536,512]{1,0:T(8,128)(2,1)} %all-gather.20.cloned.1.call-done.refs_2_.refs_7_, bf16[1536,512]{1,0:T(8,128)(2,1)} %copy-done.2, ...), custom_call_target="tpu_custom_call" | custom-call | flops 1000 | bytes 1000 | tf_op jit(solution)/shard_map/to_hidden/pallas_call | solution.py:525
  495.6 37.4 %ffn.3 = (bf16[2048,1536]{1,0:T(8,128)(2,1)}, bf16[2048,1536]{1,0:T(8,128)(2,1)}, bf16[2048,1536]{1,0:T(8,128)(2,1)}) custom-call(bf16[1024,2048]{1,0:T(8,128)(2,1)} %get-tuple-element.311.refs_0_.refs_4_.refs_1_, bf16[1024,2048]{1,0:T(8,128)(2,1)} %collective-permute-done.30.refs_1_.refs_5_.refs_2_, ...), custom_call_target="tpu_custom_call" | custom-call | flops 1000 | bytes 1000 | tf_op jit(solution)/shard_map/ffn/pallas_call | solution.py:525
  537.1 37.2 %weight_cols.6 = (bf16[1536,512]{1,0:T(8,128)(2,1)}, bf16[1536,512]{1,0:T(8,128)(2,1)}, bf16[1536,512]{1,0:T(8,128)(2,1)}, bf16[1536,256]{1,0:T(8,128)(2,1)}, bf...) custom-call(bf16[2048,1536]{1,0:T(8,128)(2,1)} %get-tuple-element.45, ...), custom_call_target="tpu_custom_call" | custom-call | flops 1000 | bytes 1000 | tf_op jit(solution)/shard_map/weight_cols/pallas_call | solution.py:525
  580.7 19.4 %weight_cols.7 = (bf16[1536,512]{1,0:T(8,128)(2,1)}, bf16[1536,512]{1,0:T(8,128)(2,1)}, bf16[1536,512]{1,0:T(8,128)(2,1)}, bf16[1536,512]{1,0:T(8,128)(2,1)}) custom-call(bf16[2048,1536]{1,0:T(8,128)(2,1)} %get-tuple-element.376.refs_0_.refs_4_, bf16[1024,2048]{1,0:T(8,128)(2,1)} %get-tuple-element.311.refs_0_.refs_4_.refs_1_, ...), custom_call_target="tpu_custom_call" | custom-call | flops 1000 | bytes 1000 | tf_op jit(solution)/shard_map/weight_cols/pallas_call | solution.py:525
  605.2 34.9 %to_model.10 = bf16[1024,2048]{1,0:T(8,128)(2,1)} custom-call(s32[8]{0:T(128)} %xor_add_fusion.refs_0_, bf16[2048,1536]{1,0:T(8,128)(2,1)} %get-tuple-element.322.refs_3_.refs_1_, bf16[2048,1536]{1,0:T(8,128)(2,1)} %get-tuple-element.333.refs_0_.refs_2_, bf16[2048,1536]{1,0:T(8,128)(2,1)} %get-tuple-element.394.refs_3_, ...), custom_call_target="tpu_custom_call" | custom-call | flops 1000 | bytes 1000 | tf_op jit(solution)/shard_map/to_model/pallas_call | solution.py:525
  646.6 34.6 %to_model.11.refs_2_ = bf16[1024,2048]{1,0:T(8,128)(2,1)} custom-call(s32[8]{0:T(128)} %xor_add_fusion.refs_0_, bf16[2048,1536]{1,0:T(8,128)(2,1)} %get-tuple-element.322.refs_3_.refs_1_, bf16[2048,1536]{1,0:T(8,128)(2,1)} %get-tuple-element.333.refs_0_.refs_2_, bf16[2048,1536]{1,0:T(8,128)(2,1)} %get-tuple-element.394.refs_3_, ...), custom_call_target="tpu_custom_call" | custom-call | flops 1000 | bytes 1000 | tf_op jit(solution)/shard_map/to_model/pallas_call | solution.py:525
  684.4 11.1 %norm_return.2 = (bf16[1024,2048]{1,0:T(8,128)(2,1)}, f32[8,2048]{1,0:T(8,128)}) custom-call(bf16[1024,2048]{1,0:T(8,128)(2,1)} %get-tuple-element.307.refs_0_, bf16[1024,2048]{1,0:T(8,128)(2,1)} %multiply_convert_fusion.1.refs_1_, bf16[1024,2048]{1,0:T(8,128)(2,1)} %to_model.11.refs_2_, bf16[1024,2048]{1,0:T(8,128)(2,1)} %collective-permute-done.49.refs_3_, ...), custom_call_target="tpu_custom_call" | custom-call | flops 1000 | bytes 1000 | tf_op jit(solution)/shard_map/norm_return/pallas_call | solution.py:525
  696.9 20.5 %to_model.12.refs_2_ = bf16[1024,2048]{1,0:T(8,128)(2,1)} custom-call(s32[8]{0:T(128)} %xor_add_fusion.refs_0_, bf16[2048,1536]{1,0:T(8,128)(2,1)} %get-tuple-element.321.refs_0_.refs_1_, bf16[2048,1536]{1,0:T(8,128)(2,1)} %get-tuple-element.453.refs_0_.refs_2_, bf16[1536,512]{1,0:T(8,128)(2,1)} %all-gather.16.cloned.1.call-done.refs_2_.refs_3_, ...), custom_call_target="tpu_custom_call" | custom-call | flops 1000 | bytes 1000 | tf_op jit(solution)/shard_map/to_model/pallas_call | solution.py:525
  739.8 33.7 %attend_back.2 = (bf16[1024,1024]{1,0:T(8,128)(2,1)}, bf16[1024,1024]{1,0:T(8,128)(2,1)}, bf16[1024,1024]{1,0:T(8,128)(2,1)}) custom-call(s32[2,9]{1,0:T(2,128)} %pad_add_fusion.refs_0_, bf16[1024,1024]{1,0:T(8,128)(2,1)} %make_heads.5.refs_2_.refs_1_, bf16[1024,1024]{1,0:T(8,128)(2,1)} %to_hidden.14.refs_2_, ...), custom_call_target="tpu_custom_call" | custom-call | flops 1000 | bytes 1000 | tf_op jit(solution)/shard_map/attend_back/pallas_call | solution.py:525
  773.5 14.4 %weight_rows.3 = (bf16[256,2048]{1,0:T(8,128)(2,1)}, bf16[256,2048]{1,0:T(8,128)(2,1)}, bf16[256,2048]{1,0:T(8,128)(2,1)}, bf16[256,2048]{1,0:T(8,128)(2,1)}) custom-call(bf16[1024,1024]{1,0:T(8,128)(2,1)} %get-tuple-element.292.refs_1_.refs_3_.refs_0_, bf16[1024,1024]{1,0:T(8,128)(2,1)} %get-tuple-element.303.refs_1_.refs_3_, ...), custom_call_target="tpu_custom_call" | custom-call | flops 1000 | bytes 1000 | tf_op jit(solution)/shard_map/weight_rows/pallas_call | solution.py:525
  819.3 35.5 %attend_back.3 = (bf16[1024,1024]{1,0:T(8,128)(2,1)}, bf16[1024,1024]{1,0:T(8,128)(2,1)}, bf16[1024,1024]{1,0:T(8,128)(2,1)}) custom-call(s32[2,9]{1,0:T(2,128)} %pad_add_fusion.refs_0_, bf16[1024,1024]{1,0:T(8,128)(2,1)} %make_heads.7.refs_2_.refs_1_, bf16[1024,1024]{1,0:T(8,128)(2,1)} %to_hidden.15.refs_2_, ...), custom_call_target="tpu_custom_call" | custom-call | flops 1000 | bytes 1000 | tf_op jit(solution)/shard_map/attend_back/pallas_call | solution.py:525
  878.2 14.4 %weight_rows.4 = (bf16[256,2048]{1,0:T(8,128)(2,1)}, bf16[256,2048]{1,0:T(8,128)(2,1)}, bf16[256,2048]{1,0:T(8,128)(2,1)}, bf16[256,2048]{1,0:T(8,128)(2,1)}) custom-call(bf16[1024,1024]{1,0:T(8,128)(2,1)} %get-tuple-element.450.refs_5_.refs_0_.refs_1_, bf16[1024,1024]{1,0:T(8,128)(2,1)} %get-tuple-element.451.refs_1_, ...), custom_call_target="tpu_custom_call" | custom-call | flops 1000 | bytes 1000 | tf_op jit(solution)/shard_map/weight_rows/pallas_call | solution.py:525
  892.8 20.5 %to_model.13.refs_6_ = bf16[1024,2048]{1,0:T(8,128)(2,1)} custom-call(s32[8]{0:T(128)} %xor_add_fusion.refs_0_, bf16[2048,1536]{1,0:T(8,128)(2,1)} %get-tuple-element.321.refs_0_.refs_1_, bf16[2048,1536]{1,0:T(8,128)(2,1)} %get-tuple-element.453.refs_0_.refs_2_, bf16[1536,512]{1,0:T(8,128)(2,1)} %all-gather.16.cloned.1.call-done.refs_2_.refs_3_, ...), custom_call_target="tpu_custom_call" | custom-call | flops 1000 | bytes 1000 | tf_op jit(solution)/shard_map/to_model/pallas_call | solution.py:525
  932.9 14.3 %weight_rows.5 = (bf16[256,2048]{1,0:T(8,128)(2,1)}, bf16[256,2048]{1,0:T(8,128)(2,1)}, bf16[256,2048]{1,0:T(8,128)(2,1)}, bf16[256,2048]{1,0:T(8,128)(2,1)}) custom-call(bf16[1024,1024]{1,0:T(8,128)(2,1)} %get-tuple-element.467.refs_0_.refs_2_, bf16[1024,1024]{1,0:T(8,128)(2,1)} %get-tuple-element.480.refs_1_.refs_2_, ...), custom_call_target="tpu_custom_call" | custom-call | flops 1000 | bytes 1000 | tf_op jit(solution)/shard_map/weight_rows/pallas_call | solution.py:525
  950.2 15.4 %to_model.14 = bf16[1024,2048]{1,0:T(8,128)(2,1)} custom-call(s32[8]{0:T(128)} %iota.44.refs_0_, bf16[1024,1024]{1,0:T(8,128)(2,1)} %get-tuple-element.451.refs_1_, bf16[1024,1024]{1,0:T(8,128)(2,1)} %get-tuple-element.480.refs_1_.refs_2_, bf16[1024,2048]{1,0:T(8,128)(2,1)} %constant_dynamic-update-slice_fusion.8.refs_1_.refs_3_, ...), custom_call_target="tpu_custom_call" | custom-call | flops 1000 | bytes 1000 | tf_op jit(solution)/shard_map/to_model/pallas_call | solution.py:525
  985.0 15.6 %to_model.15.refs_2_ = bf16[1024,2048]{1,0:T(8,128)(2,1)} custom-call(s32[8]{0:T(128)} %iota.45.refs_0_, bf16[1024,1024]{1,0:T(8,128)(2,1)} %get-tuple-element.450.refs_5_.refs_0_.refs_1_, bf16[1024,1024]{1,0:T(8,128)(2,1)} %get-tuple-element.467.refs_0_.refs_2_, bf16[1024,2048]{1,0:T(8,128)(2,1)} %constant_dynamic-update-slice_fusion.8.refs_1_.refs_3_, ...), custom_call_target="tpu_custom_call" | custom-call | flops 1000 | bytes 1000 | tf_op jit(solution)/shard_map/to_model/pallas_call | solution.py:525
  1010.2 12.1 %norm_return.3 = (f32[1024,2048]{1,0:T(8,128)}, f32[8,2048]{1,0:T(8,128)}) custom-call(bf16[1024,2048]{1,0:T(8,128)(2,1)} %refs_0_.1, bf16[1024,2048]{1,0:T(8,128)(2,1)} %get-tuple-element.403.refs_12_.refs_0_.refs_2_.refs_1_, bf16[1024,2048]{1,0:T(8,128)(2,1)} %to_model.15.refs_2_, bf16[1024,2048]{1,0:T(8,128)(2,1)} %collective-permute-done.72.refs_3_, ...), custom_call_target="tpu_custom_call" | custom-call | flops 1000 | bytes 1000 | tf_op jit(solution)/shard_map/norm_return/pallas_call | solution.py:525
  1032.9 17.5 %collective-permute-start.80 = (f32[1,4352]{1,0:T(1,128)S(1)}, f32[1,4352]{1,0:T(1,128)S(1)}, u32[]{:S(2)}, u32[]{:S(2)}) collective-permute-start(f32[1,4352]{1,0:T(1,128)S(1)} %add_add_fusion.10), channel_id=1, source_target_pairs={{0,3},{1,2},{2,1},{3,0},{4,7},{5,6},{6,5},{7,4},{8,11},{9,10},{10,... | collective-permute-start | bytes 52232 | tf_op jit(solution)/shard_map/ppermute | solution.py:1490
  (497 shorter events, 387.1 us)
Async XLA Ops:
  8.9 60.9 %all-gather.12.cloned.1.call-start = ((), (), s32[]{:S(2)}) async-start(), calls=%async_computation.9 | async-start | bytes 1310720 | tf_op jit(solution)/shard_map/all_gather | solution.py:483
  9.7 89.2 %all-gather.14.cloned.1.call-start = ((), (), s32[]{:S(2)}) async-start(), calls=%async_computation.10 | async-start | bytes 1310720 | tf_op jit(solution)/shard_map/all_gather | solution.py:483
  12.6 168.2 %all-gather.16.cloned.1.call-start = ((), (), s32[]{:S(2)}) async-start(), calls=%async_computation.11 | async-start | bytes 1966080 | tf_op jit(solution)/shard_map/all_gather | solution.py:483
  32.7 132.0 %collective-permute-start.19 = (bf16[1024,2048]{1,0:T(8,128)(2,1)}, bf16[1024,2048]{1,0:T(8,128)(2,1)}, u32[]{:S(2)}, u32[]{:S(2)}) collective-permute-start(bf16[1024,2048]{1,0:T(8,128)(2,1)} %fusion.2.refs_0_.refs_2_), channel_id=1, source_target_pairs={{0,8},{8,0},{1,9},{9,1},{2,10},{10,2},{3,11},{11,3},{4,12},{12,4},... | collective-permute-start | bytes 12582920 | tf_op jit(solution)/shard_map/ppermute | solution.py:467
  46.7 206.6 %all-gather.18.cloned.1.call-start = ((), (), s32[]{:S(2)}) async-start(), calls=%async_computation.12 | async-start | bytes 1966080 | tf_op jit(solution)/shard_map/all_gather | solution.py:483
  143.8 218.6 %all-gather.20.cloned.1.call-start = ((), (), s32[]{:S(2)}) async-start(), calls=%async_computation.13 | async-start | bytes 1966080 | tf_op jit(solution)/shard_map/all_gather | solution.py:483
  143.9 45.1 %collective-permute-start.15 = (bf16[1024,1024]{1,0:T(8,128)(2,1)}, bf16[1024,1024]{1,0:T(8,128)(2,1)S(1)}, u32[]{:S(2)}, u32[]{:S(2)}) collective-permute-start(bf16[1024,1024]{1,0:T(8,128)(2,1)} %make_heads.4.refs_2_.refs_5_), channel_id=1, source_target_pairs={{0,4},{4,0},{1,5},{5,1},{2,6},{6,2},{3,7},{7,3},{8,12},{12,8},{9,1... | collective-permute-start | bytes 6291464 | tf_op jit(solution)/shard_map/ppermute | solution.py:467
  145.5 219.2 %all-gather.22.cloned.1.call-start = ((), (), s32[]{:S(2)}) async-start(), calls=%async_computation.14 | async-start | bytes 7864320 | tf_op jit(solution)/shard_map/all_gather | solution.py:483
  193.7 215.0 %all-gather.24.cloned.1.call-start = ((), (), s32[]{:S(2)}) async-start(), calls=%async_computation.15 | async-start | bytes 1966080 | tf_op jit(solution)/shard_map/all_gather | solution.py:483
  228.4 45.6 %collective-permute-start.22 = (bf16[1024,1024]{1,0:T(8,128)(2,1)S(1)}, bf16[1024,1024]{1,0:T(8,128)(2,1)}, u32[]{:S(2)}, u32[]{:S(2)}) collective-permute-start(bf16[1024,1024]{1,0:T(8,128)(2,1)S(1)} %copy-done.5), channel_id=1, source_target_pairs={{0,4},{4,0},{1,5},{5,1},{2,6},{6,2},{3,7},{7,3},{8,12},{12,8},{9,1... | collective-permute-start | bytes 6291464 | tf_op jit(solution)/shard_map/ppermute | solution.py:467
  231.6 264.0 %all-gather.26.cloned.1.call-start = ((), (), s32[]{:S(2)}) async-start(), calls=%async_computation.16 | async-start | bytes 7864320 | tf_op jit(solution)/shard_map/all_gather | solution.py:483
  275.9 57.3 %collective-permute-start.27 = (bf16[1024,2048]{1,0:T(8,128)(2,1)}, bf16[1024,2048]{1,0:T(8,128)(2,1)}, u32[]{:S(2)}, u32[]{:S(2)}) collective-permute-start(bf16[1024,2048]{1,0:T(8,128)(2,1)} %reorder.1.refs_0_.refs_1_), channel_id=1, source_target_pairs={{0,8},{8,0},{1,9},{9,1},{2,10},{10,2},{3,11},{11,3},{4,12},{12,4},... | collective-permute-start | bytes 12582920 | tf_op jit(solution)/shard_map/ppermute | solution.py:467
  316.6 480.0 %reduce-scatter.9.cloned.1.call-start = ((), (), s32[]{:S(2)}) async-start(), calls=%async_computation.17 | async-start | bytes 7864320 | tf_op jit(solution)/shard_map/reduce_scatter | solution.py:487
  363.6 45.2 %collective-permute-start.32 = (bf16[1536,512]{1,0:T(8,128)(2,1)}, bf16[1536,512]{1,0:T(8,128)(2,1)S(1)}, u32[]{:S(2)}, u32[]{:S(2)}) collective-permute-start(bf16[1536,512]{1,0:T(8,128)(2,1)} %all-gather.20.cloned.1.call-done.refs_2_.refs_7_), channel_id=1, source_target_pairs={{0,4},{4,0},{1,5},{5,1},{2,6},{6,2},{3,7},{7,3},{8,12},{12,8},{9,1... | collective-permute-start | bytes 4718600 | tf_op jit(solution)/shard_map/ppermute | solution.py:467
  446.9 528.4 %reduce-scatter.15.cloned.1.call-start = ((), (), s32[]{:S(2)}) async-start(), calls=%async_computation.20 | async-start | bytes 1966080 | tf_op jit(solution)/shard_map/reduce_scatter | solution.py:487
  642.8 334.3 %reduce-scatter.19.cloned.1.call-start = ((), (), s32[]{:S(2)}) async-start(), calls=%async_computation.22 | async-start | bytes 1966080 | tf_op jit(solution)/shard_map/reduce_scatter | solution.py:487
  695.6 77.9 %collective-permute-start.56 = (bf16[1024,2048]{1,0:T(8,128)(2,1)}, bf16[1024,2048]{1,0:T(8,128)(2,1)}, u32[]{:S(2)}, u32[]{:S(2)}) collective-permute-start(bf16[1024,2048]{1,0:T(8,128)(2,1)} %get-tuple-element.403.refs_12_.refs_0_.refs_2_.refs_1_), channel_id=1, source_target_pairs={{0,8},{8,0},{1,9},{9,1},{2,10},{10,2},{3,11},{11,3},{4,12},{12,4},... | collective-permute-start | bytes 12582920 | tf_op jit(solution)/shard_map/ppermute | solution.py:467
  696.9 281.3 %reduce-scatter.17.cloned.1.call-start = ((), (), s32[]{:S(2)}) async-start(), calls=%async_computation.21 | async-start | bytes 1966080 | tf_op jit(solution)/shard_map/reduce_scatter | solution.py:487
  735.8 60.8 %collective-permute-start.52 = (bf16[1536,512]{1,0:T(8,128)(2,1)}, bf16[1536,512]{1,0:T(8,128)(2,1)}, u32[]{:S(2)}, u32[]{:S(2)}) collective-permute-start(bf16[1536,512]{1,0:T(8,128)(2,1)} %get-tuple-element.421), channel_id=1, source_target_pairs={{0,16},{16,0},{1,17},{17,1},{2,18},{18,2},{3,19},{19,3},{4,20},{20... | collective-permute-start | bytes 4718600 | tf_op jit(solution)/shard_map/ppermute | solution.py:467
  737.5 59.1 %collective-permute-start.53 = (bf16[1536,512]{1,0:T(8,128)(2,1)}, bf16[1536,512]{1,0:T(8,128)(2,1)}, u32[]{:S(2)}, u32[]{:S(2)}) collective-permute-start(bf16[1536,512]{1,0:T(8,128)(2,1)} %add.272), channel_id=1, source_target_pairs={{0,4},{4,0},{1,5},{5,1},{2,6},{6,2},{3,7},{7,3},{8,12},{12,8},{9,1... | collective-permute-start | bytes 4718600 | tf_op jit(solution)/shard_map/ppermute | solution.py:467
  738.5 67.1 %collective-permute-start.54 = (bf16[1536,512]{1,0:T(8,128)(2,1)}, bf16[1536,512]{1,0:T(8,128)(2,1)S(1)}, u32[]{:S(2)}, u32[]{:S(2)}) collective-permute-start(bf16[1536,512]{1,0:T(8,128)(2,1)} %add.273), channel_id=1, source_target_pairs={{0,16},{16,0},{1,17},{17,1},{2,18},{18,2},{3,19},{19,3},{4,20},{20... | collective-permute-start | bytes 4718600 | tf_op jit(solution)/shard_map/ppermute | solution.py:467
  738.8 68.1 %collective-permute-start.55 = (bf16[1536,512]{1,0:T(8,128)(2,1)}, bf16[1536,512]{1,0:T(8,128)(2,1)}, u32[]{:S(2)}, u32[]{:S(2)}) collective-permute-start(bf16[1536,512]{1,0:T(8,128)(2,1)} %get-tuple-element.425), channel_id=1, source_target_pairs={{0,4},{4,0},{1,5},{5,1},{2,6},{6,2},{3,7},{7,3},{8,12},{12,8},{9,1... | collective-permute-start | bytes 4718600 | tf_op jit(solution)/shard_map/ppermute | solution.py:467
  810.2 172.3 %reduce-scatter.21.cloned.1.call-start = ((), (), s32[]{:S(2)}) async-start(), calls=%async_computation.23 | async-start | bytes 1966080 | tf_op jit(solution)/shard_map/reduce_scatter | solution.py:487
  810.2 51.7 %collective-permute-start.57 = (bf16[1024,1024]{1,0:T(8,128)(2,1)}, bf16[1024,1024]{1,0:T(8,128)(2,1)S(1)}, u32[]{:S(2)}, u32[]{:S(2)}) collective-permute-start(bf16[1024,1024]{1,0:T(8,128)(2,1)} %get-tuple-element.440), channel_id=1, source_target_pairs={{0,4},{4,0},{1,5},{5,1},{2,6},{6,2},{3,7},{7,3},{8,12},{12,8},{9,1... | collective-permute-start | bytes 6291464 | tf_op jit(solution)/shard_map/ppermute | solution.py:467
  811.4 50.5 %collective-permute-start.58 = (bf16[256,2048]{1,0:T(8,128)(2,1)}, bf16[256,2048]{1,0:T(8,128)(2,1)S(1)}, u32[]{:S(2)}, u32[]{:S(2)}) collective-permute-start(bf16[256,2048]{1,0:T(8,128)(2,1)} %get-tuple-element.443), channel_id=1, source_target_pairs={{0,16},{16,0},{1,17},{17,1},{2,18},{18,2},{3,19},{19,3},{4,20},{20... | collective-permute-start | bytes 3145736 | tf_op jit(solution)/shard_map/ppermute | solution.py:467
  815.9 186.0 %reduce-scatter.23.cloned.1.call-start = ((), (), s32[]{:S(2)}) async-start(), calls=%async_computation.24 | async-start | bytes 1966080 | tf_op jit(solution)/shard_map/reduce_scatter | solution.py:487
  817.2 44.7 %collective-permute-start.60 = (bf16[384,512]{1,0:T(8,128)(2,1)S(1)}, bf16[384,512]{1,0:T(8,128)(2,1)S(1)}, u32[]{:S(2)}, u32[]{:S(2)}) collective-permute-start(bf16[384,512]{1,0:T(8,128)(2,1)S(1)} %get-tuple-element.545), channel_id=1, source_target_pairs={{0,16},{16,0},{1,17},{17,1},{2,18},{18,2},{3,19},{19,3},{4,20},{20... | collective-permute-start | bytes 1179656 | tf_op jit(solution)/shard_map/ppermute | solution.py:467
  862.6 51.8 %collective-permute-start.61 = (bf16[1024,1024]{1,0:T(8,128)(2,1)}, bf16[1024,1024]{1,0:T(8,128)(2,1)S(1)}, u32[]{:S(2)}, u32[]{:S(2)}) collective-permute-start(bf16[1024,1024]{1,0:T(8,128)(2,1)} %get-tuple-element.448), channel_id=1, source_target_pairs={{0,4},{4,0},{1,5},{5,1},{2,6},{6,2},{3,7},{7,3},{8,12},{12,8},{9,1... | collective-permute-start | bytes 6291464 | tf_op jit(solution)/shard_map/ppermute | solution.py:467
  863.8 50.7 %collective-permute-start.62 = (bf16[256,2048]{1,0:T(8,128)(2,1)}, bf16[256,2048]{1,0:T(8,128)(2,1)}, u32[]{:S(2)}, u32[]{:S(2)}) collective-permute-start(bf16[256,2048]{1,0:T(8,128)(2,1)} %get-tuple-element.449), channel_id=1, source_target_pairs={{0,16},{16,0},{1,17},{17,1},{2,18},{18,2},{3,19},{19,3},{4,20},{20... | collective-permute-start | bytes 3145736 | tf_op jit(solution)/shard_map/ppermute | solution.py:467
  917.3 115.5 %reduce-scatter.11.cloned.1.call-start = ((), (), s32[]{:S(2)}) async-start(), calls=%async_computation.18 | async-start | bytes 2621440 | tf_op jit(solution)/shard_map/reduce_scatter | solution.py:487
  970.7 89.3 %reduce-scatter.13.cloned.1.call-start = ((), (), s32[]{:S(2)}) async-start(), calls=%async_computation.19 | async-start | bytes 1310720 | tf_op jit(solution)/shard_map/reduce_scatter | solution.py:487
  1005.2 45.8 %collective-permute-start.77 = (bf16[1024,2048]{1,0:T(8,128)(2,1)}, bf16[1024,2048]{1,0:T(8,128)(2,1)}, u32[]{:S(2)}, u32[]{:S(2)}) collective-permute-start(bf16[1024,2048]{1,0:T(8,128)(2,1)} %to_model.12.refs_2_), channel_id=1, source_target_pairs={{0,8},{8,0},{1,9},{9,1},{2,10},{10,2},{3,11},{11,3},{4,12},{12,4},... | collective-permute-start | bytes 12582920 | tf_op jit(solution)/shard_map/ppermute | solution.py:467
  (135 other events, 2604.2 us)
Sparse Core Ops, SparseCore 0:
  10.2 30.6 all-gather.9
  42.4 27.4 all-gather.11
  71.4 27.4 all-gather.13
  100.9 36.5 all-gather.15
  144.0 37.1 all-gather.17
  183.2 35.9 all-gather.19
  220.8 114.1 all-gather.21
  337.1 35.3 all-gather.23
  374.1 114.1 all-gather.25
  490.5 108.9 reduce-scatter.8
  642.9 37.0 reduce-scatter.14
  697.0 37.9 reduce-scatter.18
  810.3 37.2 reduce-scatter.16
  849.8 34.2 reduce-scatter.20
  917.4 40.5 reduce-scatter.22
  970.8 55.4 reduce-scatter.10
  1028.5 27.3 reduce-scatter.12
